TPU v7x, 32 devices: a whole 2x2x4 slice. The times are simulated.
32 devices in a mesh: groups: 2 (over x), req: 16 (over z, y, core).
Axes of the slice: x: 2, y: 2, z: 4, core: 2. Of those that a mesh axis runs over, the one named last changes fastest.
Arguments:
- queries: bfloat16 [64, 6, 4096], P(('groups', 'req')), parts along dimension 0, may hold values from -6 to 6
- keys: bfloat16 [64, 6, 4096], P(('groups', 'req')), parts along dimension 0, may hold values from -6 to 6
- values: bfloat16 [64, 6, 4096], P(('groups', 'req')), parts along dimension 0, may hold values from -6 to 6
- gates: bfloat16 [64, 6, 4096], P(('groups', 'req')), parts along dimension 0, may hold values from -6 to 6
- states: float32 [64, 32, 128, 128], P(('groups', 'req')), parts along dimension 0, may hold values from -12 to 12
- new_slot: int32 [64], P(('groups', 'req')), parts along dimension 0, may hold values from 0 to 31, as said below
- norm_gain: float32 [4096], replicated, may hold values from 0.1 to 1.9
Outputs:
- output: bfloat16 [64, 6, 4096], P(('groups', 'req')), parts along dimension 0
There are 2 independent parts, one for each index of `groups`. A program takes and returns all parts, laid end to end along the dimension named above; an argument that names none is the same for every part. Nothing has to cross between parts.
Inputs may be any that keep to these rules, and one draw needn't show every extreme that they name: `new_slot`: A permutation of the slots. On one device (its 2 slots) at most 1 request change slot, and exactly 1 do on some devices; a request that changes slot never keeps it.
All inputs are finite; a program needn't handle non-finite values.
Results may differ from a plain program's by a relative error of at most 0.001.
Values sent between devices are 32-bit elements; how exact they have to be, the bound alone decides.
No kernel may reach another device: no remote copies, remote signals or barrier semaphores. Data moves between devices by JAX's collectives and lax.ppermute only.
A program may use at most 64 MiB of HBM per device.

v0:
```python
import jax
import jax.numpy as jnp
from jax import lax
from jax.sharding import PartitionSpec as P

D_HEAD = 128
HEADS = 32
BEFORE = 3
STEPS = 6
MOVE_DEV = 1


def head_decay():
    order = jnp.arange(HEADS).astype(jnp.float32)
    slope = 2.0 ** (-8.0 * (order + 1.0) / (2.0 * HEADS))
    return jnp.exp(-slope)


def advance(current, query_row, key_row, value_row, gate_row, norm_gain):
    count = current.shape[0]
    query_act = jax.nn.silu(query_row.astype(jnp.float32)).reshape(count, HEADS, D_HEAD)
    key_act = jax.nn.silu(key_row.astype(jnp.float32)).reshape(count, HEADS, D_HEAD)
    value_act = jax.nn.silu(value_row.astype(jnp.float32)).reshape(count, HEADS, D_HEAD)
    current = (
        head_decay()[None, :, None, None] * current
        + key_act[:, :, :, None] * value_act[:, :, None, :]
    )
    mixed = jnp.einsum("nhi,nhij->nhj", query_act, current, precision=lax.Precision.HIGHEST)
    mixed = mixed.reshape(count, HEADS * D_HEAD)
    energy = jnp.mean(mixed * mixed, axis=-1, keepdims=True)
    output = (
        mixed
        * lax.rsqrt(energy + 1e-06)
        * norm_gain[None, :]
        * jax.nn.sigmoid(gate_row.astype(jnp.float32))
    )
    return (current, output.astype(jnp.bfloat16))


def on_device(queries, keys, values, gates, states, new_slot, norm_gain):
    slot_count = states.shape[0]
    peer_count = lax.axis_size("req")
    state_size = HEADS * D_HEAD * D_HEAD
    gathered = lax.all_gather(new_slot, "req", axis=0, tiled=True)
    current = states
    row_list = []
    for moment in range(BEFORE):
        current, row = advance(
            current,
            queries[:, moment],
            keys[:, moment],
            values[:, moment],
            gates[:, moment],
            norm_gain,
        )
        row_list.append(row[:, None, :])
    flat_state = current.reshape(slot_count, state_size)
    slot_total = slot_count * peer_count
    positions = jnp.arange(slot_total)
    inverse = jnp.zeros((slot_total,), jnp.int32).at[gathered].set(positions)
    leaving = (gathered != positions).reshape(peer_count, slot_count)
    rank_local = jnp.cumsum(leaving.astype(jnp.int32), axis=1) - 1
    leaving_flat = leaving.reshape(-1)
    rank_flat = rank_local.reshape(-1)
    own_index = lax.axis_index("req")
    mine_moving = lax.dynamic_slice_in_dim(leaving, own_index, 1, 0)[0]
    mine_rank = lax.dynamic_slice_in_dim(rank_local, own_index, 1, 0)[0]
    matches = mine_moving[None, :] & (mine_rank[None, :] == jnp.arange(MOVE_DEV)[:, None])
    picked = jnp.sum(jnp.where(matches, jnp.arange(slot_count)[None, :], 0), axis=1)
    pieces = lax.all_to_all(flat_state[picked], "req", split_axis=1, concat_axis=0, tiled=True)
    source_row = inverse // slot_count * MOVE_DEV + rank_flat[inverse]
    target = jnp.where(
        leaving_flat, positions // slot_count * MOVE_DEV + rank_flat, peer_count * MOVE_DEV
    )
    route_table = (
        jnp.zeros((peer_count * MOVE_DEV,), jnp.int32).at[target].set(source_row, mode="drop")
    )
    arrived = lax.all_to_all(pieces[route_table], "req", split_axis=0, concat_axis=1, tiled=True)
    slot_pick = jnp.maximum(mine_rank, 0)
    moved_state = jnp.where(mine_moving[:, None], arrived[slot_pick], flat_state)
    current = moved_state.reshape(slot_count, HEADS, D_HEAD, D_HEAD)
    for moment in range(BEFORE, STEPS):
        current, row = advance(
            current,
            queries[:, moment],
            keys[:, moment],
            values[:, moment],
            gates[:, moment],
            norm_gain,
        )
        row_list.append(row[:, None, :])
    return jnp.concatenate(row_list, axis=1)


def solution(mesh):
    in_specs = (
        P(("groups", "req"), None, None),
        P(("groups", "req"), None, None),
        P(("groups", "req"), None, None),
        P(("groups", "req"), None, None),
        P(("groups", "req"), None, None, None),
        P(("groups", "req")),
        P(),
    )
    out_specs = P(("groups", "req"), None, None)
    return jax.shard_map(
        on_device, mesh=mesh, in_specs=in_specs, out_specs=out_specs, check_vma=False
    )
```

profile of v0, /device:TPU:13, one launch (start us, length us, event | category | flops | bytes accessed | tf_op | source)
XLA Modules:
  0.0 192.6 jit_solution(7532482736330372226)
XLA Ops:
  0.0 0.9 convert_bitcast_fusion
  0.9 0.9 convert_bitcast_fusion.1
  1.9 6.8 %multiply_add_fusion.2 = f32[2,32,128,128]{3,2,1,0:T(8,128)S(1)} fusion(f32[2,32,128,128]{3,2,1,0:T(8,128)} %param.11, f32[2,32,128]{2,1,0:T(8,128)S(1)} %get-tuple-element.44, f32[2,32,128]{2,1,0:T(8,128)S(1)} %get-tuple-element.48, f32[2,32,128]{2,1,0:T(8,128)S(1)} %get-tuple-element.45, f32[2,32,128]{2,1,0:T(8,128)S(1)} %get-tuple-element.49, ...), kind=kLoop, calls=%fused_computation.11 | loop fusion | flops 9437184 | bytes 8585344 | tf_op jit(solution)/shard_map/add | solution.py:25
  8.7 1.9 copy-done.2
  10.6 16.1 %copy.62 = f32[1,2,4096,128]{3,1,2,0:T(2,128)} copy(f32[1,2,4096,128]{3,2,1,0:T(8,128)S(1)} %bitcast.329) | data formatting | bytes 8388608
  28.2 7.9 %all-reduce = s32[32]{0:T(128)S(1)} all-reduce(s32[32]{0:T(128)S(1)} %dynamic-update-slice.1), channel_id=1, replica_groups=mesh['groups'=2,'req'=16] {'req'}, use_global_device_ids=true, to_apply=%add | all-reduce | flops 32 | bytes 256
  39.0 5.1 %constant_dynamic-slice_fusion = f32[1,524288]{1,0:T(1,128)} fusion(f32[2,524288]{1,0:T(2,128)} %bitcast.331, s32[]{:T(128)} %bitcast.17), kind=kLoop, calls=%fused_computation.183 | loop fusion | bytes 4194308 | tf_op jit(solution)/shard_map/gather | solution.py:70
  44.1 9.3 %all-to-all-start = ((f32[1,16,32768]{2,0,1:T(1,128)}), f32[1,16,32768]{2,0,1:T(1,128)}, u32[]{:S(2)}, u32[]{:S(2)}) async-start(f32[1,16,32768]{2,0,1:T(1,128)} %bitcast.18), calls=%async_computation | async-start | bytes 4194304 | tf_op jit(solution)/shard_map/all_to_all | solution.py:70
  53.6 5.8 %fusion.4 = f32[2,32,1,128]{3,2,1,0:T(1,128)S(1)} fusion(f32[2,32,128,1]{2,3,1,0:T(1,128)S(1)} %bitcast.345, f32[2,32,128,128]{3,2,1,0:T(8,128)} %param.11, f32[2,32,128]{2,1,0:T(8,128)S(1)} %get-tuple-element.50, f32[2,32,128]{2,1,0:T(8,128)S(1)} %get-tuple-element.51, f32[32]{0:T(128)S(1)} %negate_exponential_fusion), kind=kOutput, calls=%fused_computation.14 | convolution fusion | flops 15728640 | bytes 4325504 | tf_op jit(solution)/shard_map/nhi,nhij->nhj/dot_general | solution.py:28
  59.5 6.9 %fusion.6 = f32[2,32,1,128]{3,2,1,0:T(1,128)S(1)} fusion(f32[2,32,128,1]{2,3,1,0:T(1,128)S(1)} %bitcast.351, f32[2,32,128,128]{3,2,1,0:T(8,128)} %param.11, f32[2,32,128]{2,1,0:T(8,128)S(1)} %get-tuple-element.45, f32[2,32,128]{2,1,0:T(8,128)S(1)} %get-tuple-element.49, f32[2,32,128]{2,1,0:T(8,128)S(1)} %get-tuple-element.50, ...), kind=kOutput, calls=%fused_computation.16 | convolution fusion | flops 18874368 | bytes 4391040 | tf_op jit(solution)/shard_map/nhi,nhij->nhj/dot_general | solution.py:28
  66.4 5.3 %fusion.98 = f32[2,32,1,128]{3,2,1,0:T(1,128)S(1)} fusion(f32[2,32,128,1]{2,3,1,0:T(1,128)S(1)} %bitcast.344, f32[2,32,128,128]{3,2,1,0:T(8,128)} %copy-done.2), kind=kOutput, calls=%fused_computation.203 | convolution fusion | flops 12582912 | bytes 4259840 | tf_op jit(solution)/shard_map/nhi,nhij->nhj/dot_general | solution.py:28
  74.2 26.7 %all-to-all-done = f32[1,16,32768]{2,0,1:T(1,128)} async-done(((f32[1,16,32768]{2,0,1:T(1,128)}), f32[1,16,32768]{2,0,1:T(1,128)}, u32[]{:S(2)}, u32[]{:S(2)}) %all-to-all-start) | async-done | bytes 2097184 | tf_op jit(solution)/shard_map/all_to_all | solution.py:70
  100.9 2.8 %copy.63 = f32[1,16,32768]{2,1,0:T(8,128)S(1)} copy(f32[1,16,32768]{2,0,1:T(1,128)} %all-to-all-done) | data formatting | bytes 4194304
  103.7 2.5 %gather_fusion.1 = f32[16,32768]{1,0:T(8,128)} fusion(f32[16,32768]{1,0:T(8,128)S(1)} %bitcast.328, s32[1024]{0:T(1024)S(1)} %pad_clamp_fusion), kind=kCustom, calls=%fused_computation.1 | custom fusion | bytes 4194368 | tf_op jit(solution)/shard_map/gather | solution.py:78
  106.2 5.1 %copy.8 = f32[16,1,32768]{2,1,0:T(1,128)} copy(f32[16,1,32768]{2,0,1:T(8,128)} %bitcast.333) | data formatting | bytes 4194304 | tf_op jit(solution)/shard_map/all_to_all | solution.py:78
  111.3 4.9 %all-to-all-start.1 = ((f32[16,1,32768]{2,1,0:T(1,128)}), f32[16,1,32768]{2,1,0:T(1,128)S(1)}, u32[]{:S(2)}, u32[]{:S(2)}) async-start(f32[16,1,32768]{2,1,0:T(1,128)} %copy.8), calls=%async_computation.1 | async-start | bytes 4194304 | tf_op jit(solution)/shard_map/all_to_all | solution.py:78
  116.7 46.9 %all-to-all-done.1 = f32[16,1,32768]{2,1,0:T(1,128)S(1)} async-done(((f32[16,1,32768]{2,1,0:T(1,128)}), f32[16,1,32768]{2,1,0:T(1,128)S(1)}, u32[]{:S(2)}, u32[]{:S(2)}) %all-to-all-start.1) | async-done | bytes 2097184 | tf_op jit(solution)/shard_map/all_to_all | solution.py:78
  163.6 1.5 broadcast_bitcast_fusion
  165.4 1.9 copy-done
  167.3 5.1 %multiply_add_fusion.1 = f32[2,32,128,128]{3,2,1,0:T(8,128)S(1)} fusion(f32[2,32,128,128]{3,2,1,0:T(8,128)S(1)} %bitcast.330, f32[2,32,128]{2,1,0:T(8,128)S(1)} %get-tuple-element.52, f32[2,32,128]{2,1,0:T(8,128)S(1)} %get-tuple-element.53, f32[32]{0:T(128)S(1)} %negate_exponential_fusion, pred[2]{0:T(512)(128)(4,1)S(1)} %fusion.97, ...), kind=kLoop, calls=%fused_computation.10 | loop fusion | flops 13631488 | bytes 12845186 | tf_op jit(solution)/shard_map/add | solution.py:25
  172.4 1.9 copy-done.1
  174.3 3.7 %fusion.99 = f32[2,32,1,128]{3,2,1,0:T(1,128)S(1)} fusion(f32[2,32,128,1]{2,3,1,0:T(1,128)S(1)} %bitcast.342, f32[2,32,128,128]{3,2,1,0:T(8,128)S(1)} %multiply_add_fusion.1), kind=kOutput, calls=%fused_computation.204 | convolution fusion | flops 12582912 | bytes 4259840 | tf_op jit(solution)/shard_map/nhi,nhij->nhj/dot_general | solution.py:28
  178.1 5.8 %fusion.5 = f32[2,32,1,128]{3,2,1,0:T(1,128)S(1)} fusion(f32[2,32,128,1]{2,3,1,0:T(1,128)S(1)} %bitcast.343, f32[2,32,128,128]{3,2,1,0:T(8,128)} %copy-done.1, f32[2,32,128]{2,1,0:T(8,128)S(1)} %get-tuple-element.43, f32[2,32,128]{2,1,0:T(8,128)S(1)} %get-tuple-element.47, f32[32]{0:T(128)S(1)} %negate_exponential_fusion), kind=kOutput, calls=%fused_computation.15 | convolution fusion | flops 15728640 | bytes 4325504 | tf_op jit(solution)/shard_map/nhi,nhij->nhj/dot_general | solution.py:28
  184.1 6.9 %fusion = f32[2,32,1,128]{3,2,1,0:T(1,128)S(1)} fusion(f32[2,32,128,1]{2,3,1,0:T(1,128)S(1)} %bitcast.350, f32[2,32,128,128]{3,2,1,0:T(8,128)} %copy-done.1, f32[2,32,128]{2,1,0:T(8,128)S(1)} %get-tuple-element.42, f32[2,32,128]{2,1,0:T(8,128)S(1)} %get-tuple-element.46, f32[2,32,128]{2,1,0:T(8,128)S(1)} %get-tuple-element.43, ...), kind=kOutput, calls=%fused_computation.5 | convolution fusion | flops 18874368 | bytes 4391040 | tf_op jit(solution)/shard_map/nhi,nhij->nhj/dot_general | solution.py:28
  (72 shorter events, 7.2 us)
Async XLA Ops:
  8.7 1.9 copy-start.2
  10.6 16.1 %copy-start.8 = (u32[32]{0:T(128)S(1)}, u32[32]{0:T(128)}, u32[]{:S(2)}) copy-start(u32[32]{0:T(128)} %constant.117) | copy-start | bytes 388
  10.6 17.4 %copy-start.7 = (s32[2]{0:T(128)S(1)}, s32[2]{0:T(128)}, u32[]{:S(2)}) copy-start(s32[2]{0:T(128)} %param.12) | copy-start | bytes 28
  39.0 14.5 %copy-start.5 = (bf16[2,6,4096]{2,0,1:T(2,128)(2,1)S(1)}, bf16[2,6,4096]{2,0,1:T(2,128)(2,1)}, u32[]{:S(2)}) copy-start(bf16[2,6,4096]{2,0,1:T(2,128)(2,1)} %param.7) | copy-start | bytes 294916
  44.1 56.8 %all-to-all-start = ((f32[1,16,32768]{2,0,1:T(1,128)}), f32[1,16,32768]{2,0,1:T(1,128)}, u32[]{:S(2)}, u32[]{:S(2)}) async-start(f32[1,16,32768]{2,0,1:T(1,128)} %bitcast.18), calls=%async_computation | async-start | bytes 4194304 | tf_op jit(solution)/shard_map/all_to_all | solution.py:70
  106.2 10.1 %copy-start.3 = (f32[4096]{0:T(1024)S(1)}, f32[4096]{0:T(1024)}, u32[]{:S(2)}) copy-start(f32[4096]{0:T(1024)} %param.13) | copy-start | bytes 49156
  106.2 10.2 %copy-start.4 = (bf16[2,6,4096]{2,0,1:T(2,128)(2,1)S(1)}, bf16[2,6,4096]{2,0,1:T(2,128)(2,1)}, u32[]{:S(2)}) copy-start(bf16[2,6,4096]{2,0,1:T(2,128)(2,1)} %param.10) | copy-start | bytes 294916
  111.3 52.3 %all-to-all-start.1 = ((f32[16,1,32768]{2,1,0:T(1,128)}), f32[16,1,32768]{2,1,0:T(1,128)S(1)}, u32[]{:S(2)}, u32[]{:S(2)}) async-start(f32[16,1,32768]{2,1,0:T(1,128)} %copy.8), calls=%async_computation.1 | async-start | bytes 4194304 | tf_op jit(solution)/shard_map/all_to_all | solution.py:78
  165.1 2.2 %copy-start = (f32[2,32,128,128]{3,2,1,0:T(8,128)S(1)}, f32[2,32,128,128]{3,2,1,0:T(8,128)}, u32[]{:S(2)}) copy-start(f32[2,32,128,128]{3,2,1,0:T(8,128)} %param.11) | copy-start | bytes 12582916
  172.4 1.9 copy-start.1
  191.3 0.6 copy-start.6
where the time goes:
time: 193 us
  waiting for transfers between devices  73.7 us (38%)
  local copies, waits for them, and re-layouts  42.9 us (22%)
  matrix products  34.3 us (18%)
  other arithmetic  16.7 us (9%)
  starting transfers between devices  14.2 us (7%)
  blocking collectives  7.89 us (4%)
  between operations  2.98 us (2%)
    all_to_all x1, waiting for transfers between devices, on_device(): lax.all_to_all(pieces[route_table], 'req', split_axis=0, concat_axis=1, t...  46.9 us
    dot_general x6, matrix products, advance(): jnp.einsum('nhi,nhij->nhj', query_act, current, precision=lax.Precision.H...  34.3 us
    unnamed x25, local copies, waits for them, and re-layouts  27.9 us
    all_to_all x1, waiting for transfers between devices, on_device(): lax.all_to_all(flat_state[picked], 'req', split_axis=1, concat_axis=0, ti...  26.7 us
    add x2, other arithmetic, advance(): head_decay()[None, :, None, None] * current  12 us
    all_to_all x1, starting transfers between devices, on_device(): lax.all_to_all(flat_state[picked], 'req', split_axis=1, concat_axis=0, ti...  9.29 us
    unnamed x1, blocking collectives  7.89 us
    gather x1, local copies, waits for them, and re-layouts, on_device(): flat_state[picked]  5.1 us
  transfers between devices with their start and end apart: 2, of which 2 were waited for; matrix products, arithmetic and copies ran while one was open for 11% of the time, Pallas kernels for 0%

commit v1 on v0

v1 whole, which is shorter than its diff:
```python
import functools

import jax
import jax.numpy as jnp
from jax import lax
from jax.experimental import pallas as pl
from jax.experimental.pallas import tpu as pltpu
from jax.sharding import PartitionSpec as P

BEFORE = 3
EPS = 1e-06
F32 = jnp.float32
BF16 = jnp.bfloat16
VMEM = pl.BlockSpec(memory_space=pltpu.VMEM)
SMEM = pl.BlockSpec(memory_space=pltpu.SMEM)
ANY = pl.BlockSpec(memory_space=pl.ANY)


def silu(x):
    return x / (1.0 + jnp.exp(-x))


def sigmoid(x):
    return 1.0 / (1.0 + jnp.exp(-x))


def moving_slot(slots_ref, count):
    base = lax.axis_index("req") * count
    place = jnp.int32(0)
    moves = slots_ref[0] != base
    for s in range(1, count):
        here = slots_ref[s] != base + s
        place = jnp.where(here, s, place)
        moves = jnp.logical_or(moves, here)
    return place, moves


def decay_power(heads, width, power):
    order = lax.broadcasted_iota(jnp.int32, (heads, width), 0).astype(F32)
    slope = jnp.exp2(-8.0 * (order + 1.0) / (2.0 * heads))
    return jnp.exp(slope * (-float(power)))


def split(x):
    high = x.astype(BF16)
    return high, (x - high.astype(F32)).astype(BF16)


def to_dense(source, target, slot, first, count, heads, width):
    for h in range(heads):
        rows = source[slot, :, h * width:(h + 1) * width].astype(F32)
        target[pl.ds(h, count, stride=heads), :] = rows[first:first + count]


def ask_kernel(slots_ref, queries_ref, out_ref, *, heads, width):
    count, steps, _ = queries_ref.shape
    place, _ = moving_slot(slots_ref, count)
    to_dense(queries_ref, out_ref, place, BEFORE, steps - BEFORE, heads, width)
    out_ref[...] = silu(out_ref[...])


def local_kernel(slots_ref, queries_ref, keys_ref, values_ref, gates_ref, gain_ref, states_ref,
                 out_ref, weight_ref, early_ref, late_ref,
                 state, qs, ks, vs, gs, lhs, prod, done, sems, *, heads, width, chunks):
    count, steps, _ = queries_ref.shape
    place, moves = moving_slot(slots_ref, count)
    order = [place] + [jnp.where(place == s, 0, s) for s in range(1, count)]
    size = heads // chunks

    def load(j, c):
        part = pl.ds(c * size, size)
        return pltpu.make_async_copy(
            states_ref.at[order[j], part], state.at[j, part], sems.at[j, c])

    for j in range(count):
        for c in range(chunks):
            load(j, c).start()
    decay = [decay_power(heads, width, p) for p in range(steps + 1)]
    gain = gain_ref[...]
    block = lambda ref, t: ref[t * heads:(t + 1) * heads, :]
    for j in range(count):
        slot = order[j]
        to_dense(queries_ref, qs, slot, 0, steps, heads, width)
        to_dense(keys_ref, ks, slot, 0, steps, heads, width)
        to_dense(values_ref, vs, slot, 0, steps, heads, width)
        to_dense(gates_ref, gs, slot, 0, steps, heads, width)
        q = [silu(block(qs, t)) for t in range(steps)]
        k = [silu(block(ks, t)) for t in range(steps)]
        v = [silu(block(vs, t)) for t in range(steps)]
        for t in range(steps):
            x = q[t] * decay[t + 1]
            high = x.astype(BF16).astype(F32)
            lhs[t * heads:(t + 1) * heads, :] = high
            lhs[(8 + t) * heads:(9 + t) * heads, :] = x - high
        mixed = []
        for t in range(steps):
            total = None
            far = None
            for s in range(t + 1):
                score = jnp.sum(q[t] * k[s], axis=1, keepdims=True)
                term = score * decay[t - s] * v[s]
                if t >= BEFORE and s < BEFORE:
                    far = term if far is None else far + term
                else:
                    total = term if total is None else total + term
            if j == 0 and t >= BEFORE:
                late_ref[0, (t - BEFORE) * heads:(t - BEFORE + 1) * heads, :] = total
            mixed.append(total if far is None else total + far)
        if j == 0:
            for s in range(BEFORE):
                early_ref[0, s * heads:(s + 1) * heads, :] = k[s]
                early_ref[1, s * heads:(s + 1) * heads, :] = v[s]
        for c in range(chunks):
            load(j, c).wait()
            for h in range(c * size, (c + 1) * size):
                high, low = split(state[j, h])
                weight = jnp.concatenate([high, low], axis=0)
                if j == 0:
                    weight_ref[h] = weight
                x = lhs[pl.ds(h, 16, stride=heads), :].astype(BF16)
                prod[pl.ds(h, 16, stride=heads), :] = jnp.dot(
                    jnp.concatenate([x, x], axis=1), weight, preferred_element_type=F32)
        for t in range(steps):
            x = mixed[t] + block(prod, t) + block(prod, 8 + t)
            energy = jnp.mean(x * x)
            scale = gain * sigmoid(block(gs, t))
            if j == 0 and t >= BEFORE:
                late_ref[1, (t - BEFORE) * heads:(t - BEFORE + 1) * heads, :] = scale
            done[t * heads:(t + 1) * heads, :] = x * lax.rsqrt(energy + EPS) * scale
        for h in range(heads):
            rows = done[pl.ds(h, steps, stride=heads), :]
            out_ref[slot, :, h * width:(h + 1) * width] = rows.astype(BF16)


def answer_kernel(ask_ref, weight_ref, early_ref, out_ref, lhs, prod, *, heads, width, late):
    block = lambda ref, t: ref[t * heads:(t + 1) * heads, :]
    q = [block(ask_ref, t) for t in range(late)]
    for t in range(late):
        x = q[t] * decay_power(heads, width, t + BEFORE + 1)
        high = x.astype(BF16).astype(F32)
        lhs[t * heads:(t + 1) * heads, :] = high
        lhs[(late + t) * heads:(late + t + 1) * heads, :] = x - high
    for h in range(heads):
        x = lhs[pl.ds(h, 2 * late, stride=heads), :].astype(BF16)
        prod[pl.ds(h, 2 * late, stride=heads), :] = jnp.dot(
            jnp.concatenate([x, x], axis=1), weight_ref[h], preferred_element_type=F32)
    for t in range(late):
        total = block(prod, t) + block(prod, late + t)
        for s in range(BEFORE):
            score = jnp.sum(q[t] * block(early_ref.at[0], s), axis=1, keepdims=True)
            total = total + score * decay_power(heads, width, t + BEFORE - s) * block(
                early_ref.at[1], s)
        out_ref[t * heads:(t + 1) * heads, :] = total


def finish_kernel(slots_ref, base_ref, late_ref, *refs, heads, width, late):
    parts, out_ref, done = refs[:-2], refs[-2], refs[-1]
    count, steps, _ = base_ref.shape
    place, moves = moving_slot(slots_ref, count)
    out_ref[...] = base_ref[...]

    @pl.when(moves)
    def _():
        for t in range(late):
            part = slice(t * heads, (t + 1) * heads)
            x = late_ref[0, part, :]
            for ref in parts:
                x = x + ref[part, :]
            energy = jnp.mean(x * x)
            row = (t + BEFORE) * heads
            done[row:row + heads, :] = x * lax.rsqrt(energy + EPS) * late_ref[1, part, :]
        fresh = lax.broadcasted_iota(jnp.int32, (steps, width), 0) >= BEFORE
        for h in range(heads):
            lanes = slice(h * width, (h + 1) * width)
            rows = done[pl.ds(h, steps, stride=heads), :]
            old = base_ref[place, :, lanes].astype(F32)
            out_ref[place, :, lanes] = jnp.where(fresh, rows, old).astype(BF16)


def near_square(total):
    inner = total
    for d in range(1, total + 1):
        if total % d == 0 and d * d >= total:
            inner = d
            break
    return inner, total // inner


def turn(position, step, size):
    return position ^ step if size & (size - 1) == 0 else (position + step) % size


def unturn(position, step, size):
    return position ^ step if size & (size - 1) == 0 else (position - step) % size


def on_device(queries, keys, values, gates, states, new_slot, norm_gain):
    count, steps, features = queries.shape
    heads, width = states.shape[1], states.shape[2]
    late = steps - BEFORE
    peers = lax.axis_size("req")
    inner, outer = near_square(peers)
    me = lax.axis_index("req")
    my_inner, my_outer = me % inner, me // inner

    def send_inner(x, k):
        return lax.ppermute(x, "req", [
            (o * inner + i, o * inner + turn(i, k, inner))
            for o in range(outer) for i in range(inner)])

    def send_outer(x, k):
        return lax.ppermute(x, "req", [
            (o * inner + i, turn(o, k, outer) * inner + i)
            for o in range(outer) for i in range(inner)])

    def target(slots, device):
        own = slots // count == device
        far = jnp.sum(jnp.where(own, 0, slots // count))
        return jnp.where(jnp.all(own), device, far)

    compact = dict(heads=heads, width=width)
    dense = jax.ShapeDtypeStruct((late * heads, width), F32)
    ask = pl.pallas_call(
        functools.partial(ask_kernel, **compact),
        out_shape=dense, in_specs=[SMEM, VMEM], out_specs=VMEM,
        name="ask",
    )(new_slot, queries)

    column = [ask] + [send_outer(ask, k) for k in range(1, outer)]
    wishes = [new_slot] + [send_inner(new_slot, k) for k in range(1, inner)]

    chunks = 4
    base, weight, early, late_parts = pl.pallas_call(
        functools.partial(local_kernel, chunks=chunks, **compact),
        out_shape=(
            jax.ShapeDtypeStruct((count, steps, features), BF16),
            jax.ShapeDtypeStruct((heads, 2 * width, width), BF16),
            jax.ShapeDtypeStruct((2, BEFORE * heads, width), F32),
            jax.ShapeDtypeStruct((2, late * heads, width), F32),
        ),
        in_specs=[SMEM, VMEM, VMEM, VMEM, VMEM, VMEM, ANY],
        out_specs=(VMEM, VMEM, VMEM, VMEM),
        scratch_shapes=[
            pltpu.VMEM((count, heads, width, width), F32),
            pltpu.VMEM((steps * heads, width), F32),
            pltpu.VMEM((steps * heads, width), F32),
            pltpu.VMEM((steps * heads, width), F32),
            pltpu.VMEM((steps * heads, width), F32),
            pltpu.VMEM((16 * heads, width), F32),
            pltpu.VMEM((16 * heads, width), F32),
            pltpu.VMEM((steps * heads, width), F32),
            pltpu.SemaphoreType.DMA((count, chunks)),
        ],
        compiler_params=pltpu.CompilerParams(vmem_limit_bytes=24 * 2**20),
        cost_estimate=pl.CostEstimate(
            flops=2 * count * heads * 16 * 2 * width * width,
            bytes_accessed=states.size * 4, transcendentals=0),
        name="local",
    )(new_slot, queries, keys, values, gates, norm_gain.reshape(heads, width), states)

    mates = [my_outer * inner + unturn(my_inner, k, inner) for k in range(inner)]
    wants = [target(wish, mate) for wish, mate in zip(wishes, mates)]

    def choose(options, index, size, mine):
        result = options[0]
        for k in range(1, size):
            result = jnp.where(unturn(mine, k, size) == index, options[k], result)
        return result

    def pick_outer(device):
        return choose(column, device // inner, outer, my_outer)

    sent = [pick_outer(wants[0])]
    for k in range(1, inner):
        back = [b for b in range(1, inner) if all(
            unturn(i, b, inner) == turn(i, k, inner) for i in range(inner))][0]
        sent.append(send_inner(pick_outer(wants[back]), k))
    found = choose(sent, wants[0] % inner, inner, my_inner)

    answer = pl.pallas_call(
        functools.partial(answer_kernel, late=late, **compact),
        out_shape=dense, in_specs=[VMEM, VMEM, VMEM], out_specs=VMEM,
        scratch_shapes=[
            pltpu.VMEM((2 * late * heads, width), F32),
            pltpu.VMEM((2 * late * heads, width), F32),
        ],
        compiler_params=pltpu.CompilerParams(vmem_limit_bytes=24 * 2**20),
        name="answer",
    )(found, weight, early)

    replies = [answer] + [send_inner(answer, k) for k in range(1, inner)]

    def reply_for(device):
        result = jnp.zeros_like(answer)
        for reply, want in zip(replies, wants):
            result = jnp.where(want == device, reply, result)
        return result

    parts = [reply_for(me)]
    for k in range(1, outer):
        parts.append(send_outer(reply_for(turn(my_outer, k, outer) * inner + my_inner), k))

    return pl.pallas_call(
        functools.partial(finish_kernel, late=late, **compact),
        out_shape=jax.ShapeDtypeStruct((count, steps, features), BF16),
        in_specs=[SMEM, VMEM, VMEM] + [VMEM] * outer, out_specs=VMEM,
        scratch_shapes=[pltpu.VMEM((steps * heads, width), F32)],
        name="finish",
    )(new_slot, base, late_parts, *parts)


def solution(mesh):
    rows = P(("groups", "req"), None, None)
    in_specs = (rows, rows, rows, rows, P(("groups", "req"), None, None, None),
                P(("groups", "req")), P())
    return jax.shard_map(
        on_device, mesh=mesh, in_specs=in_specs, out_specs=rows, check_vma=False)
```

time: 193 us -> 57.2 us (0.30)
  the two profiles are of different devices: /device:TPU:13 before, /device:TPU:0 now
where the time goes in v1:
time: 57.2 us; the launch traced here: 56.5 us
  starting transfers between devices  16.1 us (28%)
  local copies, waits for them, and re-layouts  11.2 us (20%)
  waiting for transfers between devices  8.9 us (16%)
  Pallas kernels  7.5 us (13%)
  other arithmetic  7.49 us (13%)
  between operations  5.35 us (9%)
    ppermute x6, starting transfers between devices, send_outer(): lax.ppermute(x, 'req', [(o * inner + i, turn(o, k, outer) * inner + i) fo...  10.1 us
    unnamed x24, local copies, waits for them, and re-layouts  9.56 us
    ppermute x9, starting transfers between devices, send_inner(): lax.ppermute(x, 'req', [(o * inner + i, o * inner + turn(i, k, inner)) fo...  5.99 us
    ppermute x6, waiting for transfers between devices, send_outer(): lax.ppermute(x, 'req', [(o * inner + i, turn(o, k, outer) * inner + i) fo...  5.03 us
    ppermute x9, waiting for transfers between devices, send_inner(): lax.ppermute(x, 'req', [(o * inner + i, o * inner + turn(i, k, inner)) fo...  3.87 us
    pallas_call x1, Pallas kernels, on_device(): pl.pallas_call(functools.partial(local_kernel, chunks=chunks, **compact),...  3.8 us
    reduce_sum x4, other arithmetic, target(): far = jnp.sum(jnp.where(own, 0, slots // count))  3.4 us
    reduce_and x4, other arithmetic, target(): return jnp.where(jnp.all(own), device, far)  2.58 us
  transfers between devices with their start and end apart: 15, of which 5 were waited for; matrix products, arithmetic and copies ran while one was open for 17% of the time, Pallas kernels for 7%

profile of v1, /device:TPU:0, one launch (start us, length us, event | category | flops | bytes accessed | tf_op | source)
XLA Modules:
  0.0 56.5 jit_solution(788593671237946420)
XLA Ops:
  0.0 1.6 %copy.8.queries_ref = bf16[2,6,4096]{2,1,0:T(8,128)(2,1)} copy(bf16[2,6,4096]{2,0,1:T(2,128)(2,1)} %param.7) | data formatting | bytes 196608 | tf_op args[0]
  1.6 1.6 %ask.1 = f32[96,128]{1,0:T(8,128)} custom-call(s32[2]{0:T(128)} %slots_ref.5, bf16[2,6,4096]{2,1,0:T(8,128)(2,1)} %copy.8.queries_ref), custom_call_target="tpu_custom_call" | custom-call | tf_op jit(solution)/shard_map/ask/pallas_call | solution.py:223
  3.2 5.0 %collective-permute-start.1 = (f32[96,128]{1,0:T(8,128)}, f32[96,128]{1,0:T(8,128)S(1)}, u32[]{:S(2)}, u32[]{:S(2)}) collective-permute-start(f32[96,128]{1,0:T(8,128)} %ask.1), channel_id=1, source_target_pairs={{0,12},{1,13},{2,14},{3,15},{4,8},{5,9},{6,10},{7,11},{8,4},{9,5},... | collective-permute-start | bytes 147464 | tf_op jit(solution)/shard_map/ppermute | solution.py:212
  8.8 1.7 %collective-permute-start.5 = (s32[2]{0:T(128)}, s32[2]{0:T(128)S(1)}, u32[]{:S(2)}, u32[]{:S(2)}) collective-permute-start(s32[2]{0:T(128)} %slots_ref.5), channel_id=1, source_target_pairs={{0,2},{1,3},{2,0},{3,1},{4,6},{5,7},{6,4},{7,5},{8,10},{9,11},{10,... | collective-permute-start | bytes 32 | tf_op jit(solution)/shard_map/ppermute | solution.py:207
  10.6 1.4 %fusion.1 = (s32[]{:T(128)}, s32[2]{0:T(128)S(1)}) fusion(s32[]{:T(128)S(6)} %add.39, s32[2]{0:T(128)} %slots_ref.5), kind=kLoop, calls=%fused_computation.33 | loop fusion | flops 35 | bytes 24 | tf_op jit(solution)/shard_map/reduce_sum | solution.py:218
  15.1 0.7 %fusion = (s32[]{:T(128)}, s32[2]{0:T(128)S(1)}) fusion(s32[]{:T(128)S(6)} %add.38, s32[2]{0:T(128)S(1)} %collective-permute-done), kind=kLoop, calls=%fused_computation.32 | loop fusion | flops 35 | bytes 24 | tf_op jit(solution)/shard_map/reduce_sum | solution.py:218
  20.3 0.8 %select_select_fusion.5 = (f32[96,128]{1,0:T(8,128)S(1)}, f32[96,128]{1,0:T(8,128)S(1)}, f32[96,128]{1,0:T(8,128)S(1)}) fusion(f32[96,128]{1,0:T(8,128)S(1)} %collective-permute-done.1, f32[96,128]{1,0:T(8,128)S(1)} %collective-permute-done.2, f32[96,128]{1,0:T(8,128)S(1)} %collective-permute-done.3, f32[96,128]{1,0:T(8,128)} %ask.1, pred[]{:T(512)S(6)} %eq.140, ...), kind=kLoop, calls=%fused_computation.5 | loop fusion | flops 110592 | bytes 344073 | tf_op jit(solution)/shard_map/jit(_where)/select_n | solution.py:267
  21.1 1.3 %collective-permute-start.4 = (f32[96,128]{1,0:T(8,128)S(1)}, f32[96,128]{1,0:T(8,128)S(1)}, u32[]{:S(2)}, u32[]{:S(2)}) collective-permute-start(f32[96,128]{1,0:T(8,128)S(1)} %get-tuple-element.26), channel_id=1, source_target_pairs={{0,3},{1,2},{2,1},{3,0},{4,7},{5,6},{6,5},{7,4},{8,11},{9,10},{10,... | collective-permute-start | bytes 147464 | tf_op jit(solution)/shard_map/ppermute | solution.py:207
  25.0 1.0 %copy.9.keys_ref = bf16[2,6,4096]{2,1,0:T(8,128)(2,1)S(1)} copy(bf16[2,6,4096]{2,0,1:T(2,128)(2,1)} %param.8) | data formatting | bytes 196608 | tf_op args[1]
  26.0 1.0 %copy.10.values_ref = bf16[2,6,4096]{2,1,0:T(8,128)(2,1)S(1)} copy(bf16[2,6,4096]{2,0,1:T(2,128)(2,1)} %param.9) | data formatting | bytes 196608 | tf_op args[2]
  27.0 1.0 %copy.11.gates_ref = bf16[2,6,4096]{2,1,0:T(8,128)(2,1)S(1)} copy(bf16[2,6,4096]{2,0,1:T(2,128)(2,1)} %param.10) | data formatting | bytes 196608 | tf_op args[3]
  27.9 2.2 %copy-done = f32[2,32,128,128]{3,2,1,0:T(8,128)S(1)} copy-done((f32[2,32,128,128]{3,2,1,0:T(8,128)S(1)}, f32[2,32,128,128]{3,2,1,0:T(8,128)}, u32[]{:S(2)}) %copy-start) | copy-done | bytes 4194328
  30.1 0.9 %copy-done.1 = bf16[2,6,4096]{2,1,0:T(8,128)(2,1)S(1)} copy-done((bf16[2,6,4096]{2,1,0:T(8,128)(2,1)S(1)}, bf16[2,6,4096]{2,1,0:T(8,128)(2,1)}, u32[]{:S(2)}) %copy-start.1) | copy-done | bytes 98328
  31.0 0.7 %copy-done.4 = f32[4096]{0:T(1024)S(1)} copy-done((f32[4096]{0:T(1024)S(1)}, f32[4096]{0:T(1024)}, u32[]{:S(2)}) %copy-start.4) | copy-done | bytes 16408
  32.4 3.8 %local.1 = (bf16[2,6,4096]{2,1,0:T(8,128)(2,1)S(1)}, bf16[32,256,128]{2,1,0:T(8,128)(2,1)S(1)}, f32[2,96,128]{2,1,0:T(8,128)S(1)}, f32[2,96,128]{2,1,0:T(8,128)S(1)}) custom-call(s32[2]{0:T(128)S(1)} %copy-done.5, bf16[2,6,4096]{2,1,0:T(8,128)(2,1)S(1)} %copy-done.1, bf16[2,6,4096]{2,1,0:T(8,128)(2,1)S(1)} %copy.9.keys_ref, ...), custom_call_target="tpu_custom_call" | custom-call | flops 67108864 | bytes 4194304 | tf_op jit(solution)/shard_map/local/pallas_call | solution.py:233
  36.7 1.6 %collective-permute-start.9 = (f32[96,128]{1,0:T(8,128)S(1)}, f32[96,128]{1,0:T(8,128)S(1)}, u32[]{:S(2)}, u32[]{:S(2)}) collective-permute-start(f32[96,128]{1,0:T(8,128)S(1)} %answer.1), channel_id=1, source_target_pairs={{0,3},{1,2},{2,1},{3,0},{4,7},{5,6},{6,5},{7,4},{8,11},{9,10},{10,... | collective-permute-start | bytes 147464 | tf_op jit(solution)/shard_map/ppermute | solution.py:207
  38.9 1.4 %collective-permute-done.9 = f32[96,128]{1,0:T(8,128)S(1)} collective-permute-done((f32[96,128]{1,0:T(8,128)S(1)}, f32[96,128]{1,0:T(8,128)S(1)}, u32[]{:S(2)}, u32[]{:S(2)}) %collective-permute-start.9) | collective-permute-done | bytes 49184 | tf_op jit(solution)/shard_map/ppermute | solution.py:207
  40.3 2.1 %collective-permute-done.10 = f32[96,128]{1,0:T(8,128)S(1)} collective-permute-done((f32[96,128]{1,0:T(8,128)S(1)}, f32[96,128]{1,0:T(8,128)S(1)}, u32[]{:S(2)}, u32[]{:S(2)}) %collective-permute-start.10) | collective-permute-done | bytes 49184 | tf_op jit(solution)/shard_map/ppermute | solution.py:207
  42.5 1.3 %collective-permute-start.12 = (f32[96,128]{1,0:T(8,128)S(1)}, f32[96,128]{1,0:T(8,128)S(1)}, u32[]{:S(2)}, u32[]{:S(2)}) collective-permute-start(f32[96,128]{1,0:T(8,128)S(1)} %get-tuple-element.23), channel_id=1, source_target_pairs={{0,4},{1,5},{2,6},{3,7},{4,0},{5,1},{6,2},{7,3},{8,12},{9,13},{10,... | collective-permute-start | bytes 147464 | tf_op jit(solution)/shard_map/ppermute | solution.py:212
  43.8 2.9 %collective-permute-start.13 = (f32[96,128]{1,0:T(8,128)S(1)}, f32[96,128]{1,0:T(8,128)S(1)}, u32[]{:S(2)}, u32[]{:S(2)}) collective-permute-start(f32[96,128]{1,0:T(8,128)S(1)} %get-tuple-element.22), channel_id=1, source_target_pairs={{0,8},{1,9},{2,10},{3,11},{4,12},{5,13},{6,14},{7,15},{8,0},{9,1},... | collective-permute-start | bytes 147464 | tf_op jit(solution)/shard_map/ppermute | solution.py:212
  47.5 1.7 %collective-permute-done.13.refs_2_ = f32[96,128]{1,0:T(8,128)S(1)} collective-permute-done((f32[96,128]{1,0:T(8,128)S(1)}, f32[96,128]{1,0:T(8,128)S(1)}, u32[]{:S(2)}, u32[]{:S(2)}) %collective-permute-start.13) | collective-permute-done | bytes 49184 | tf_op jit(solution)/shard_map/ppermute | solution.py:212
  49.3 3.3 %collective-permute-done.14.refs_3_ = f32[96,128]{1,0:T(8,128)S(1)} collective-permute-done((f32[96,128]{1,0:T(8,128)S(1)}, f32[96,128]{1,0:T(8,128)S(1)}, u32[]{:S(2)}, u32[]{:S(2)}) %collective-permute-start.14) | collective-permute-done | bytes 49184 | tf_op jit(solution)/shard_map/ppermute | solution.py:212
  53.2 1.7 %finish.1 = bf16[2,6,4096]{2,1,0:T(8,128)(2,1)} custom-call(s32[2]{0:T(128)} %slots_ref.5, bf16[2,6,4096]{2,1,0:T(8,128)(2,1)} %copy-done.2, f32[2,96,128]{2,1,0:T(8,128)} %copy-done.3, f32[96,128]{1,0:T(8,128)} %select_select_fusion.3.refs_0_, f32[96,128]{1,0:T(8,128)} %copy-done.7, f32[96,128]{1,0:T(8,128)} %copy-done.8, f32[96,128]{1,0:T(8,128)} %copy-done.9), custom_call_target="tpu_custom_call" | custom-call | tf_op jit(solution)/shard_map/finish/pallas_call | solution.py:303
  54.9 1.6 %copy.13 = bf16[2,6,4096]{2,0,1:T(2,128)(2,1)} copy(bf16[2,6,4096]{2,1,0:T(8,128)(2,1)} %finish.1) | data formatting | bytes 196608 | tf_op jit(solution)/shard_map/finish/pallas_call | solution.py:303
  (47 shorter events, 8.8 us)
Async XLA Ops:
  3.2 33.1 %copy-start.6 = (f32[96,128]{1,0:T(8,128)S(1)}, f32[96,128]{1,0:T(8,128)}, u32[]{:S(2)}) copy-start(f32[96,128]{1,0:T(8,128)} %ask.1) | copy-start | bytes 147460
  3.2 17.0 %collective-permute-start.1 = (f32[96,128]{1,0:T(8,128)}, f32[96,128]{1,0:T(8,128)S(1)}, u32[]{:S(2)}, u32[]{:S(2)}) collective-permute-start(f32[96,128]{1,0:T(8,128)} %ask.1), channel_id=1, source_target_pairs={{0,12},{1,13},{2,14},{3,15},{4,8},{5,9},{6,10},{7,11},{8,4},{9,5},... | collective-permute-start | bytes 147464 | tf_op jit(solution)/shard_map/ppermute | solution.py:212
  8.2 12.0 %collective-permute-start.2 = (f32[96,128]{1,0:T(8,128)}, f32[96,128]{1,0:T(8,128)S(1)}, u32[]{:S(2)}, u32[]{:S(2)}) collective-permute-start(f32[96,128]{1,0:T(8,128)} %ask.1), channel_id=1, source_target_pairs={{0,8},{1,9},{2,10},{3,11},{4,12},{5,13},{6,14},{7,15},{8,0},{9,1},... | collective-permute-start | bytes 147464 | tf_op jit(solution)/shard_map/ppermute | solution.py:212
  8.2 12.0 %collective-permute-start.3 = (f32[96,128]{1,0:T(8,128)}, f32[96,128]{1,0:T(8,128)S(1)}, u32[]{:S(2)}, u32[]{:S(2)}) collective-permute-start(f32[96,128]{1,0:T(8,128)} %ask.1), channel_id=1, source_target_pairs={{0,4},{1,5},{2,6},{3,7},{4,0},{5,1},{6,2},{7,3},{8,12},{9,13},{10,... | collective-permute-start | bytes 147464 | tf_op jit(solution)/shard_map/ppermute | solution.py:212
  8.8 3.2 %collective-permute-start.7 = (s32[2]{0:T(128)}, s32[2]{0:T(128)S(1)}, u32[]{:S(2)}, u32[]{:S(2)}) collective-permute-start(s32[2]{0:T(128)} %slots_ref.5), channel_id=1, source_target_pairs={{0,1},{1,0},{2,3},{3,2},{4,5},{5,4},{6,7},{7,6},{8,9},{9,8},{10,11... | collective-permute-start | bytes 32 | tf_op jit(solution)/shard_map/ppermute | solution.py:207
  8.8 4.5 %collective-permute-start.5 = (s32[2]{0:T(128)}, s32[2]{0:T(128)S(1)}, u32[]{:S(2)}, u32[]{:S(2)}) collective-permute-start(s32[2]{0:T(128)} %slots_ref.5), channel_id=1, source_target_pairs={{0,2},{1,3},{2,0},{3,1},{4,6},{5,7},{6,4},{7,5},{8,10},{9,11},{10,... | collective-permute-start | bytes 32 | tf_op jit(solution)/shard_map/ppermute | solution.py:207
  12.0 3.1 %collective-permute-start = (s32[2]{0:T(128)}, s32[2]{0:T(128)S(1)}, u32[]{:S(2)}, u32[]{:S(2)}) collective-permute-start(s32[2]{0:T(128)} %slots_ref.5), channel_id=1, source_target_pairs={{0,3},{1,2},{2,1},{3,0},{4,7},{5,6},{6,5},{7,4},{8,11},{9,10},{10,... | collective-permute-start | bytes 32 | tf_op jit(solution)/shard_map/ppermute | solution.py:207
  21.1 15.1 %collective-permute-start.4 = (f32[96,128]{1,0:T(8,128)S(1)}, f32[96,128]{1,0:T(8,128)S(1)}, u32[]{:S(2)}, u32[]{:S(2)}) collective-permute-start(f32[96,128]{1,0:T(8,128)S(1)} %get-tuple-element.26), channel_id=1, source_target_pairs={{0,3},{1,2},{2,1},{3,0},{4,7},{5,6},{6,5},{7,4},{8,11},{9,10},{10,... | collective-permute-start | bytes 147464 | tf_op jit(solution)/shard_map/ppermute | solution.py:207
  22.4 13.8 %collective-permute-start.6 = (f32[96,128]{1,0:T(8,128)S(1)}, f32[96,128]{1,0:T(8,128)S(1)}, u32[]{:S(2)}, u32[]{:S(2)}) collective-permute-start(f32[96,128]{1,0:T(8,128)S(1)} %get-tuple-element.25), channel_id=1, source_target_pairs={{0,2},{1,3},{2,0},{3,1},{4,6},{5,7},{6,4},{7,5},{8,10},{9,11},{10,... | collective-permute-start | bytes 147464 | tf_op jit(solution)/shard_map/ppermute | solution.py:207
  23.0 13.2 %collective-permute-start.8 = (f32[96,128]{1,0:T(8,128)S(1)}, f32[96,128]{1,0:T(8,128)S(1)}, u32[]{:S(2)}, u32[]{:S(2)}) collective-permute-start(f32[96,128]{1,0:T(8,128)S(1)} %get-tuple-element.24), channel_id=1, source_target_pairs={{0,1},{1,0},{2,3},{3,2},{4,5},{5,4},{6,7},{7,6},{8,9},{9,8},{10,11... | collective-permute-start | bytes 147464 | tf_op jit(solution)/shard_map/ppermute | solution.py:207
  27.9 2.2 %copy-start = (f32[2,32,128,128]{3,2,1,0:T(8,128)S(1)}, f32[2,32,128,128]{3,2,1,0:T(8,128)}, u32[]{:S(2)}) copy-start(f32[2,32,128,128]{3,2,1,0:T(8,128)} %states_ref.1) | copy-start | bytes 12582916
  30.1 0.9 %copy-start.1 = (bf16[2,6,4096]{2,1,0:T(8,128)(2,1)S(1)}, bf16[2,6,4096]{2,1,0:T(8,128)(2,1)}, u32[]{:S(2)}) copy-start(bf16[2,6,4096]{2,1,0:T(8,128)(2,1)} %copy.8.queries_ref) | copy-start | bytes 294916
  31.0 0.7 %copy-start.4 = (f32[4096]{0:T(1024)S(1)}, f32[4096]{0:T(1024)}, u32[]{:S(2)}) copy-start(f32[4096]{0:T(1024)} %param.13) | copy-start | bytes 49156
  31.7 0.7 %copy-start.5 = (s32[2]{0:T(128)S(1)}, s32[2]{0:T(128)}, u32[]{:S(2)}) copy-start(s32[2]{0:T(128)} %slots_ref.5) | copy-start | bytes 28
  36.2 2.1 %copy-start.2 = (bf16[2,6,4096]{2,1,0:T(8,128)(2,1)}, bf16[2,6,4096]{2,1,0:T(8,128)(2,1)S(1)}, u32[]{:S(2)}) copy-start(bf16[2,6,4096]{2,1,0:T(8,128)(2,1)S(1)} %get-tuple-element.9.base_ref) | copy-start | bytes 294916
  36.2 2.7 %copy-start.3 = (f32[2,96,128]{2,1,0:T(8,128)}, f32[2,96,128]{2,1,0:T(8,128)S(1)}, u32[]{:S(2)}) copy-start(f32[2,96,128]{2,1,0:T(8,128)S(1)} %get-tuple-element.10.late_ref) | copy-start | bytes 294916
  36.7 3.6 %collective-permute-start.9 = (f32[96,128]{1,0:T(8,128)S(1)}, f32[96,128]{1,0:T(8,128)S(1)}, u32[]{:S(2)}, u32[]{:S(2)}) collective-permute-start(f32[96,128]{1,0:T(8,128)S(1)} %answer.1), channel_id=1, source_target_pairs={{0,3},{1,2},{2,1},{3,0},{4,7},{5,6},{6,5},{7,4},{8,11},{9,10},{10,... | collective-permute-start | bytes 147464 | tf_op jit(solution)/shard_map/ppermute | solution.py:207
  38.3 4.1 %collective-permute-start.10 = (f32[96,128]{1,0:T(8,128)S(1)}, f32[96,128]{1,0:T(8,128)S(1)}, u32[]{:S(2)}, u32[]{:S(2)}) collective-permute-start(f32[96,128]{1,0:T(8,128)S(1)} %answer.1), channel_id=1, source_target_pairs={{0,2},{1,3},{2,0},{3,1},{4,6},{5,7},{6,4},{7,5},{8,10},{9,11},{10,... | collective-permute-start | bytes 147464 | tf_op jit(solution)/shard_map/ppermute | solution.py:207
  38.9 3.5 %collective-permute-start.11 = (f32[96,128]{1,0:T(8,128)S(1)}, f32[96,128]{1,0:T(8,128)S(1)}, u32[]{:S(2)}, u32[]{:S(2)}) collective-permute-start(f32[96,128]{1,0:T(8,128)S(1)} %answer.1), channel_id=1, source_target_pairs={{0,1},{1,0},{2,3},{3,2},{4,5},{5,4},{6,7},{7,6},{8,9},{9,8},{10,11... | collective-permute-start | bytes 147464 | tf_op jit(solution)/shard_map/ppermute | solution.py:207
  42.5 5.1 %collective-permute-start.12 = (f32[96,128]{1,0:T(8,128)S(1)}, f32[96,128]{1,0:T(8,128)S(1)}, u32[]{:S(2)}, u32[]{:S(2)}) collective-permute-start(f32[96,128]{1,0:T(8,128)S(1)} %get-tuple-element.23), channel_id=1, source_target_pairs={{0,4},{1,5},{2,6},{3,7},{4,0},{5,1},{6,2},{7,3},{8,12},{9,13},{10,... | collective-permute-start | bytes 147464 | tf_op jit(solution)/shard_map/ppermute | solution.py:212
  43.8 5.5 %collective-permute-start.13 = (f32[96,128]{1,0:T(8,128)S(1)}, f32[96,128]{1,0:T(8,128)S(1)}, u32[]{:S(2)}, u32[]{:S(2)}) collective-permute-start(f32[96,128]{1,0:T(8,128)S(1)} %get-tuple-element.22), channel_id=1, source_target_pairs={{0,8},{1,9},{2,10},{3,11},{4,12},{5,13},{6,14},{7,15},{8,0},{9,1},... | collective-permute-start | bytes 147464 | tf_op jit(solution)/shard_map/ppermute | solution.py:212
  46.7 5.9 %collective-permute-start.14 = (f32[96,128]{1,0:T(8,128)S(1)}, f32[96,128]{1,0:T(8,128)S(1)}, u32[]{:S(2)}, u32[]{:S(2)}) collective-permute-start(f32[96,128]{1,0:T(8,128)S(1)} %get-tuple-element.21), channel_id=1, source_target_pairs={{0,12},{1,13},{2,14},{3,15},{4,8},{5,9},{6,10},{7,11},{8,4},{9,5},... | collective-permute-start | bytes 147464 | tf_op jit(solution)/shard_map/ppermute | solution.py:212
  47.5 5.0 %copy-start.7 = (f32[96,128]{1,0:T(8,128)}, f32[96,128]{1,0:T(8,128)S(1)}, u32[]{:S(2)}) copy-start(f32[96,128]{1,0:T(8,128)S(1)} %collective-permute-done.12.refs_1_) | copy-start | bytes 147460
  49.3 3.3 %copy-start.8 = (f32[96,128]{1,0:T(8,128)}, f32[96,128]{1,0:T(8,128)S(1)}, u32[]{:S(2)}) copy-start(f32[96,128]{1,0:T(8,128)S(1)} %collective-permute-done.13.refs_2_) | copy-start | bytes 147460
  (1 other events, 0.6 us)

commit v2 on v0

v2 whole, which is shorter than its diff:
```python
import functools

import jax
import jax.numpy as jnp
from jax import lax
from jax.experimental import pallas as pl
from jax.experimental.pallas import tpu as pltpu
from jax.sharding import PartitionSpec as P

BEFORE = 3
EPS = 1e-06
F32 = jnp.float32
BF16 = jnp.bfloat16
MIB = 2**20
VMEM = pl.BlockSpec(memory_space=pltpu.VMEM)
SMEM = pl.BlockSpec(memory_space=pltpu.SMEM)
HBM = pl.BlockSpec(memory_space=pltpu.HBM)


def silu(x):
    return x / (1.0 + jnp.exp(-x))


def sigmoid(x):
    return 1.0 / (1.0 + jnp.exp(-x))


def moving_slot(slots_ref, count):
    base = lax.axis_index("req") * count
    place = jnp.int32(0)
    moves = slots_ref[0] != base
    for s in range(1, count):
        here = slots_ref[s] != base + s
        place = jnp.where(here, s, place)
        moves = jnp.logical_or(moves, here)
    return place, moves


def wanted_device(slots_ref, device, count):
    result = device
    for s in range(count):
        owner = lax.div(slots_ref[s], jnp.int32(count))
        result = jnp.where(owner != device, owner, result)
    return result


def head_slope(heads, width):
    order = lax.broadcasted_iota(jnp.int32, (heads, width), 0).astype(F32)
    return jnp.exp2(-8.0 * (order + 1.0) / (2.0 * heads))


def decay_power(slope, power):
    return jnp.exp(slope * (-float(power)))


def split(x):
    high = x.astype(BF16)
    return high, (x - high.astype(F32)).astype(BF16)


def extract(packed, place, count):
    rows = packed.shape[0] // count
    result = packed[pl.ds(0, rows, stride=count), :]
    for s in range(1, count):
        result = jnp.where(place == s, packed[pl.ds(s, rows, stride=count), :], result)
    return result


def turn(position, step, size):
    return position ^ step if size & (size - 1) == 0 else (position + step) % size


def unturn(position, step, size):
    return position ^ step if size & (size - 1) == 0 else (position - step) % size


def inverse_step(step, size):
    return step if size & (size - 1) == 0 else (size - step) % size


def choose(options, index, mine, size):
    result = options[0][...]
    for k in range(1, size):
        result = jnp.where(unturn(mine, k, size) == index, options[k][...], result)
    return result


def ask_kernel(slots_ref, queries_ref, out_ref, rows_ref, wide, sem, *, count):
    late = rows_ref.shape[0]
    first = queries_ref.shape[0] - late
    copy = pltpu.make_async_copy(queries_ref.at[pl.ds(first, late)], rows_ref, sem)
    copy.start()
    copy.wait()
    place, _ = moving_slot(slots_ref, count)
    wide[...] = rows_ref[...].astype(F32)
    out_ref[...] = silu(extract(wide, place, count))


def prepare_kernel(slots_ref, keys_ref, values_ref, states_ref, weight_ref, early_ref,
                   state, wide, sems, *, count, chunks):
    heads = states_ref.shape[1]
    size = heads // chunks
    place, _ = moving_slot(slots_ref, count)

    def load(c):
        part = pl.ds(c * size, size)
        return pltpu.make_async_copy(states_ref.at[place, part], state.at[part], sems.at[c])

    for c in range(chunks):
        load(c).start()
    rows = wide.shape[0]
    for n, ref in enumerate((keys_ref, values_ref)):
        wide[...] = ref[:rows, :].astype(F32)
        early_ref[n] = silu(extract(wide, place, count))
    for c in range(chunks):
        load(c).wait()
        for h in range(c * size, (c + 1) * size):
            weight_ref[h] = jnp.concatenate(split(state[h]), axis=0)


def route_kernel(*refs, inner, outer, count):
    wishes, column = refs[:inner], refs[inner:inner + outer]
    outs = refs[inner + outer:]
    me = lax.axis_index("req")
    my_inner, my_outer = lax.rem(me, inner), lax.div(me, inner)
    for k in range(inner):
        back = inverse_step(k, inner)
        mate = my_outer * inner + unturn(my_inner, back, inner)
        wanted = wanted_device(wishes[back], mate, count)
        outs[k][...] = choose(column, lax.div(wanted, inner), my_outer, outer)


def answer_kernel(slots_ref, *refs, inner, count, late, heads, width):
    found, (weight_ref, early_ref, out_ref, lhs, prod) = refs[:inner], refs[inner:]
    me = lax.axis_index("req")
    wanted = wanted_device(slots_ref, me, count)
    block = lambda ref, t: ref[t * heads:(t + 1) * heads, :]
    rows = choose(found, lax.rem(wanted, inner), lax.rem(me, inner), inner)
    q = [rows[t * heads:(t + 1) * heads, :] for t in range(late)]
    slope = head_slope(heads, width)
    for t in range(late):
        x = q[t] * decay_power(slope, t + BEFORE + 1)
        high = x.astype(BF16).astype(F32)
        lhs[t * heads:(t + 1) * heads, :] = high
        lhs[(late + t) * heads:(late + t + 1) * heads, :] = x - high
    for h in range(heads):
        x = lhs[pl.ds(h, 2 * late, stride=heads), :].astype(BF16)
        prod[pl.ds(h, 2 * late, stride=heads), :] = jnp.dot(
            jnp.concatenate([x, x], axis=1), weight_ref[h], preferred_element_type=F32)
    for t in range(late):
        total = block(prod, t) + block(prod, late + t)
        for s in range(BEFORE):
            score = jnp.sum(q[t] * block(early_ref.at[0], s), axis=1, keepdims=True)
            total = total + score * decay_power(slope, t + BEFORE - s) * block(
                early_ref.at[1], s)
        out_ref[t * heads:(t + 1) * heads, :] = total


def reply_kernel(*refs, inner, outer, count):
    wishes, replies = refs[:inner], refs[inner:2 * inner]
    outs = refs[2 * inner:]
    me = lax.axis_index("req")
    my_inner, my_outer = lax.rem(me, inner), lax.div(me, inner)
    wanted = [
        wanted_device(wishes[k], my_outer * inner + unturn(my_inner, k, inner), count)
        for k in range(inner)]
    for k in range(outer):
        device = turn(my_outer, k, outer) * inner + my_inner
        result = jnp.where(wanted[0] == device, replies[0][...], 0.0)
        for n in range(1, inner):
            result = jnp.where(wanted[n] == device, replies[n][...], result)
        outs[k][...] = result


def local_kernel(slots_ref, queries_ref, keys_ref, values_ref, gates_ref, gain_ref, own_ref,
                 states_ref, out_ref, late_ref, state, lhs, prod, wide, sems, *, count, chunks):
    heads, width = states_ref.shape[1], states_ref.shape[2]
    span = heads * count
    steps = queries_ref.shape[0] // span
    late = steps - BEFORE
    size = heads // chunks
    place, _ = moving_slot(slots_ref, count)

    def load(j, c):
        part = pl.ds(c * size, size)
        return pltpu.make_async_copy(states_ref.at[j, part], state.at[j, part], sems.at[j, c])

    for j in range(count):
        for c in range(chunks):
            load(j, c).start()

    def spread(x):
        for s in range(count):
            wide[pl.ds(s, heads, stride=count), :] = x
        return wide[:span, :]

    slope = spread(head_slope(heads, width))
    gain = spread(gain_ref[...])
    decay = [decay_power(slope, p) for p in range(steps + 1)]
    block = lambda ref, t: ref[t * span:(t + 1) * span, :]
    q = [silu(block(queries_ref, t).astype(F32)) for t in range(steps)]
    k = [silu(block(keys_ref, t).astype(F32)) for t in range(steps)]
    v = [silu(block(values_ref, t).astype(F32)) for t in range(steps)]
    for t in range(steps):
        x = q[t] * decay[t + 1]
        high = x.astype(BF16).astype(F32)
        lhs[t * span:(t + 1) * span, :] = high
        lhs[(8 + t) * span:(9 + t) * span, :] = x - high
    mixed = []
    for t in range(steps):
        total = None
        far = None
        for s in range(t + 1):
            score = jnp.sum(q[t] * k[s], axis=1, keepdims=True)
            term = score * decay[t - s] * v[s]
            if t >= BEFORE and s < BEFORE:
                far = term if far is None else far + term
            else:
                total = term if total is None else total + term
        if t >= BEFORE:
            wide[(t - BEFORE) * span:(t - BEFORE + 1) * span, :] = total
        mixed.append(total if far is None else total + far)
    late_ref[0] = extract(wide, place, count) + own_ref[...]
    scale = [gain * sigmoid(block(gates_ref, t).astype(F32)) for t in range(steps)]
    for t in range(late):
        wide[t * span:(t + 1) * span, :] = scale[BEFORE + t]
    late_ref[1] = extract(wide, place, count)
    for j in range(count):
        for c in range(chunks):
            load(j, c).wait()
            for h in range(c * size, (c + 1) * size):
                rows = pl.ds(h * count + j, 16, stride=span)
                x = lhs[rows, :].astype(BF16)
                prod[rows, :] = jnp.dot(
                    jnp.concatenate([x, x], axis=1),
                    jnp.concatenate(split(state[j, h]), axis=0),
                    preferred_element_type=F32)
    slot = lax.rem(lax.broadcasted_iota(jnp.int32, (span, 1), 0), jnp.int32(count))
    for t in range(steps):
        x = mixed[t] + block(prod, t) + block(prod, 8 + t)
        sums = jnp.sum(x * x, axis=1, keepdims=True)
        energy = jnp.zeros((span, 1), F32)
        for s in range(count):
            whole = jnp.sum(jnp.where(slot == s, sums, 0.0), axis=0, keepdims=True)
            energy = jnp.where(slot == s, whole, energy)
        factor = lax.rsqrt(energy * (1.0 / (heads * width)) + EPS)
        out_ref[t * span:(t + 1) * span, :] = (x * factor * scale[t]).astype(BF16)


def finish_kernel(slots_ref, base_ref, late_ref, *refs, count, heads):
    parts, out_ref, wide = refs[:-2], refs[-2], refs[-1]
    place, moves = moving_slot(slots_ref, count)
    rows = wide.shape[0]
    first = base_ref.shape[0] - rows
    single = rows // count
    wide[...] = base_ref[first:, :].astype(F32)
    for t in range(single // heads):
        part = slice(t * heads, (t + 1) * heads)
        x = late_ref[0, part, :]
        for ref in parts:
            x = x + ref[part, :]
        y = x * lax.rsqrt(jnp.mean(x * x) + EPS) * late_ref[1, part, :]
        for s in range(count):
            here = pl.ds(t * heads * count + s, heads, stride=count)
            use = jnp.logical_and(moves, place == s)
            wide[here, :] = jnp.where(use, y, wide[here, :])
    out_ref[:first, :] = base_ref[:first, :]
    out_ref[first:, :] = wide[...].astype(BF16)


def near_square(total):
    return next(
        (d, total // d) for d in range(1, total + 1) if total % d == 0 and d * d >= total)


def on_device(queries, keys, values, gates, states, new_slot, norm_gain):
    count, steps, features = queries.shape
    heads, width = states.shape[1], states.shape[2]
    late = steps - BEFORE
    packed_rows, single_rows = steps * heads * count, late * heads
    inner, outer = near_square(lax.axis_size("req"))

    def pack(x):
        return x.reshape(count, steps, heads, width).transpose(1, 2, 0, 3).reshape(
            packed_rows, width)

    def unpack(x):
        return x.reshape(steps, heads, count, width).transpose(2, 0, 1, 3).reshape(
            count, steps, features)

    def send_inner(x, k):
        return lax.ppermute(x, "req", [
            (o * inner + i, o * inner + int(turn(i, k, inner)))
            for o in range(outer) for i in range(inner)])

    def send_outer(x, k):
        return lax.ppermute(x, "req", [
            (o * inner + i, int(turn(o, k, outer)) * inner + i)
            for o in range(outer) for i in range(inner)])

    def params(limit):
        return pltpu.CompilerParams(vmem_limit_bytes=limit * MIB)

    queries, keys, values, gates = pack(queries), pack(keys), pack(values), pack(gates)
    single = jax.ShapeDtypeStruct((single_rows, width), F32)
    late_packed = pltpu.VMEM((late * heads * count, width), F32)

    ask = pl.pallas_call(
        functools.partial(ask_kernel, count=count),
        out_shape=single, in_specs=[SMEM, HBM], out_specs=VMEM,
        scratch_shapes=[pltpu.VMEM((late * heads * count, width), BF16), late_packed,
                        pltpu.SemaphoreType.DMA],
        compiler_params=params(4), name="ask",
    )(new_slot, queries)

    column = [ask] + [send_outer(ask, k) for k in range(1, outer)]
    wishes = [new_slot] + [send_inner(new_slot, k) for k in range(1, inner)]

    chunks = 8
    weight, early = pl.pallas_call(
        functools.partial(prepare_kernel, count=count, chunks=chunks),
        out_shape=(jax.ShapeDtypeStruct((heads, 2 * width, width), BF16),
                   jax.ShapeDtypeStruct((2, BEFORE * heads, width), F32)),
        in_specs=[SMEM, VMEM, VMEM, HBM], out_specs=(VMEM, VMEM),
        scratch_shapes=[pltpu.VMEM((heads, width, width), F32),
                        pltpu.VMEM((BEFORE * heads * count, width), F32),
                        pltpu.SemaphoreType.DMA((chunks,))],
        compiler_params=params(12), name="prepare",
    )(new_slot, keys, values, states)

    asked = pl.pallas_call(
        functools.partial(route_kernel, inner=inner, outer=outer, count=count),
        out_shape=(single,) * inner,
        in_specs=[SMEM] * inner + [VMEM] * outer, out_specs=(VMEM,) * inner,
        compiler_params=params(4), name="route",
    )(*wishes, *column)
    found = [asked[0]] + [send_inner(asked[k], k) for k in range(1, inner)]

    answer = pl.pallas_call(
        functools.partial(answer_kernel, inner=inner, count=count, late=late, heads=heads,
                          width=width),
        out_shape=single, in_specs=[SMEM] + [VMEM] * (inner + 2), out_specs=VMEM,
        scratch_shapes=[pltpu.VMEM((2 * late * heads, width), F32)] * 2,
        compiler_params=params(8), name="answer",
    )(new_slot, *found, weight, early)
    replies = [answer] + [send_inner(answer, k) for k in range(1, inner)]

    sorted_replies = pl.pallas_call(
        functools.partial(reply_kernel, inner=inner, outer=outer, count=count),
        out_shape=(single,) * outer,
        in_specs=[SMEM] * inner + [VMEM] * inner, out_specs=(VMEM,) * outer,
        compiler_params=params(4), name="reply",
    )(*wishes, *replies)
    parts = [send_outer(sorted_replies[k], k) for k in range(1, outer)]

    chunks = 4
    base, late_rows = pl.pallas_call(
        functools.partial(local_kernel, count=count, chunks=chunks),
        out_shape=(jax.ShapeDtypeStruct((packed_rows, width), BF16),
                   jax.ShapeDtypeStruct((2, single_rows, width), F32)),
        in_specs=[SMEM] + [VMEM] * 6 + [HBM], out_specs=(VMEM, VMEM),
        scratch_shapes=[
            pltpu.VMEM((count, heads, width, width), F32),
            pltpu.VMEM((16 * heads * count, width), F32),
            pltpu.VMEM((16 * heads * count, width), F32),
            late_packed,
            pltpu.SemaphoreType.DMA((count, chunks)),
        ],
        compiler_params=params(16), name="local",
    )(new_slot, queries, keys, values, gates, norm_gain.reshape(heads, width),
      sorted_replies[0], states)

    return unpack(pl.pallas_call(
        functools.partial(finish_kernel, count=count, heads=heads),
        out_shape=jax.ShapeDtypeStruct((packed_rows, width), BF16),
        in_specs=[SMEM, VMEM, VMEM] + [VMEM] * (outer - 1), out_specs=VMEM,
        scratch_shapes=[late_packed],
        compiler_params=params(4), name="finish",
    )(new_slot, base, late_rows, *parts))


def solution(mesh):
    rows = P(("groups", "req"), None, None)
    in_specs = (rows, rows, rows, rows, P(("groups", "req"), None, None, None),
                P(("groups", "req")), P())
    return jax.shard_map(
        on_device, mesh=mesh, in_specs=in_specs, out_specs=rows, check_vma=False)
```

time: 193 us -> 39.7 us (0.21)
  the two profiles are of different devices: /device:TPU:13 before, /device:TPU:0 now
where the time goes in v2:
time: 39.7 us; the launch traced here: 39.5 us
  starting transfers between devices  16.3 us (41%)
  Pallas kernels  8.42 us (21%)
  waiting for transfers between devices  8.42 us (21%)
  local copies, waits for them, and re-layouts  6.21 us (16%)
    ppermute x6, starting transfers between devices, send_outer(): lax.ppermute(x, 'req', [(o * inner + i, int(turn(o, k, outer)) * inner +...  10.2 us
    unnamed x26, local copies, waits for them, and re-layouts  6.21 us
    ppermute x9, starting transfers between devices, send_inner(): lax.ppermute(x, 'req', [(o * inner + i, o * inner + int(turn(i, k, inner)...  6.1 us
    ppermute x9, waiting for transfers between devices, send_inner(): lax.ppermute(x, 'req', [(o * inner + i, o * inner + int(turn(i, k, inner)...  5.62 us
    pallas_call x1, Pallas kernels, on_device(): pl.pallas_call(functools.partial(local_kernel, count=count, chunks=chunks...  3.03 us
    ppermute x6, waiting for transfers between devices, send_outer(): lax.ppermute(x, 'req', [(o * inner + i, int(turn(o, k, outer)) * inner +...  2.8 us
    pallas_call x1, Pallas kernels, on_device(): pl.pallas_call(functools.partial(finish_kernel, count=count, heads=heads)...  1.45 us
    pallas_call x1, Pallas kernels, on_device(): pl.pallas_call(functools.partial(prepare_kernel, count=count, chunks=chun...  1.06 us
  transfers between devices with their start and end apart: 15, of which 7 were waited for; matrix products, arithmetic and copies ran while one was open for 0% of the time, Pallas kernels for 10%

profile of v2, /device:TPU:0, one launch (start us, length us, event | category | flops | bytes accessed | tf_op | source)
XLA Modules:
  0.0 39.5 jit_solution(9106329640620806648)
XLA Ops:
  0.0 0.9 %copy-done.2 = bf16[2,6,4096]{2,0,1:T(2,128)(2,1)S(1)} copy-done((bf16[2,6,4096]{2,0,1:T(2,128)(2,1)S(1)}, bf16[2,6,4096]{2,0,1:T(2,128)(2,1)}, u32[]{:S(2)}) %copy-start.2) | copy-done | bytes 98328
  0.9 0.7 %copy-done.9 = s32[2]{0:T(128)S(1)} copy-done((s32[2]{0:T(128)S(1)}, s32[2]{0:T(128)}, u32[]{:S(2)}) %copy-start.9) | copy-done | bytes 32
  1.6 0.7 %ask.1.refs_4_ = f32[96,128]{1,0:T(8,128)S(1)} custom-call(s32[2]{0:T(128)S(1)} %copy-done.9, bf16[384,128]{1,0:T(8,128)(2,1)S(1)} %bitcast.26), custom_call_target="tpu_custom_call" | custom-call | tf_op jit(solution)/shard_map/ask/pallas_call | solution.py:308
  2.2 5.1 %collective-permute-start.5 = (f32[96,128]{1,0:T(8,128)S(1)}, f32[96,128]{1,0:T(8,128)S(1)}, u32[]{:S(2)}, u32[]{:S(2)}) collective-permute-start(f32[96,128]{1,0:T(8,128)S(1)} %ask.1.refs_4_), channel_id=1, source_target_pairs={{0,12},{1,13},{2,14},{3,15},{4,8},{5,9},{6,10},{7,11},{8,4},{9,5},... | collective-permute-start | bytes 147464 | tf_op jit(solution)/shard_map/ppermute | solution.py:297
  7.4 0.6 %collective-permute-start.3 = (f32[96,128]{1,0:T(8,128)S(1)}, f32[96,128]{1,0:T(8,128)S(1)}, u32[]{:S(2)}, u32[]{:S(2)}) collective-permute-start(f32[96,128]{1,0:T(8,128)S(1)} %ask.1.refs_4_), channel_id=1, source_target_pairs={{0,4},{1,5},{2,6},{3,7},{4,0},{5,1},{6,2},{7,3},{8,12},{9,13},{10,... | collective-permute-start | bytes 147464 | tf_op jit(solution)/shard_map/ppermute | solution.py:297
  8.4 1.3 %collective-permute-start.1 = (s32[2]{0:T(128)S(1)}, s32[2]{0:T(128)S(1)}, u32[]{:S(2)}, u32[]{:S(2)}) collective-permute-start(s32[2]{0:T(128)S(1)} %copy-done.9), channel_id=1, source_target_pairs={{0,2},{1,3},{2,0},{3,1},{4,6},{5,7},{6,4},{7,5},{8,10},{9,11},{10,... | collective-permute-start | bytes 32 | tf_op jit(solution)/shard_map/ppermute | solution.py:292
  9.7 1.3 %collective-permute-done.2.refs_3_ = s32[2]{0:T(128)S(1)} collective-permute-done((s32[2]{0:T(128)S(1)}, s32[2]{0:T(128)S(1)}, u32[]{:S(2)}, u32[]{:S(2)}) %collective-permute-start.2) | collective-permute-done | bytes 40 | tf_op jit(solution)/shard_map/ppermute | solution.py:292
  11.3 0.6 %collective-permute-done.1.refs_2_ = s32[2]{0:T(128)S(1)} collective-permute-done((s32[2]{0:T(128)S(1)}, s32[2]{0:T(128)S(1)}, u32[]{:S(2)}, u32[]{:S(2)}) %collective-permute-start.1) | collective-permute-done | bytes 40 | tf_op jit(solution)/shard_map/ppermute | solution.py:292
  13.2 1.5 %collective-permute-start.7 = (f32[96,128]{1,0:T(8,128)S(1)}, f32[96,128]{1,0:T(8,128)S(1)}, u32[]{:S(2)}, u32[]{:S(2)}) collective-permute-start(f32[96,128]{1,0:T(8,128)S(1)} %get-tuple-element.19), channel_id=1, source_target_pairs={{0,2},{1,3},{2,0},{3,1},{4,6},{5,7},{6,4},{7,5},{8,10},{9,11},{10,... | collective-permute-start | bytes 147464 | tf_op jit(solution)/shard_map/ppermute | solution.py:292
  14.9 2.2 %copy-done = f32[2,32,128,128]{3,2,1,0:T(8,128)S(1)} copy-done((f32[2,32,128,128]{3,2,1,0:T(8,128)S(1)}, f32[2,32,128,128]{3,2,1,0:T(8,128)}, u32[]{:S(2)}) %copy-start) | copy-done | bytes 4194328
  17.1 0.9 %copy-done.4 = bf16[2,6,4096]{2,0,1:T(2,128)(2,1)S(1)} copy-done((bf16[2,6,4096]{2,0,1:T(2,128)(2,1)S(1)}, bf16[2,6,4096]{2,0,1:T(2,128)(2,1)}, u32[]{:S(2)}) %copy-start.4) | copy-done | bytes 98328
  18.0 0.9 %copy-done.6 = bf16[2,6,4096]{2,0,1:T(2,128)(2,1)S(1)} copy-done((bf16[2,6,4096]{2,0,1:T(2,128)(2,1)S(1)}, bf16[2,6,4096]{2,0,1:T(2,128)(2,1)}, u32[]{:S(2)}) %copy-start.6) | copy-done | bytes 98328
  18.9 0.7 %copy-done.10 = s32[2]{0:T(128)S(1)} copy-done((s32[2]{0:T(128)S(1)}, s32[2]{0:T(128)}, u32[]{:S(2)}) %copy-start.10) | copy-done | bytes 32
  19.5 1.1 %prepare.1 = (bf16[32,256,128]{2,1,0:T(8,128)(2,1)S(1)}, f32[2,96,128]{2,1,0:T(8,128)S(1)}) custom-call(s32[2]{0:T(128)S(1)} %copy-done.10, bf16[384,128]{1,0:T(8,128)(2,1)S(1)} %bitcast.28, bf16[384,128]{1,0:T(8,128)(2,1)S(1)} %bitcast.30, f32[2,32,128,128]{3,2,1,0:T(8,128)S(1)} %copy-done), custom_call_target="tpu_custom_call" | custom-call | tf_op jit(solution)/shard_map/prepare/pallas_call | solution.py:320
  20.6 1.0 %answer.1.refs_4_ = f32[96,128]{1,0:T(8,128)S(1)} custom-call(s32[2]{0:T(128)S(1)} %copy-done.10, f32[96,128]{1,0:T(8,128)S(1)} %get-tuple-element.17.refs_0_, f32[96,128]{1,0:T(8,128)S(1)} %collective-permute-done.6.refs_1_, f32[96,128]{1,0:T(8,128)S(1)} %collective-permute-done.7.refs_2_, f32[96,128]{1,0:T(8,128)S(1)} %collective-permute-done.8.refs_3_, ...), custom_call_target="tpu_custom_call" | custom-call | tf_op jit(solution)/shard_map/answer/pallas_call | solution.py:339
  21.6 1.6 %collective-permute-start.11 = (f32[96,128]{1,0:T(8,128)S(1)}, f32[96,128]{1,0:T(8,128)S(1)}, u32[]{:S(2)}, u32[]{:S(2)}) collective-permute-start(f32[96,128]{1,0:T(8,128)S(1)} %answer.1.refs_4_), channel_id=1, source_target_pairs={{0,3},{1,2},{2,1},{3,0},{4,7},{5,6},{6,5},{7,4},{8,11},{9,10},{10,... | collective-permute-start | bytes 147464 | tf_op jit(solution)/shard_map/ppermute | solution.py:292
  23.8 1.5 %collective-permute-done.11.refs_7_ = f32[96,128]{1,0:T(8,128)S(1)} collective-permute-done((f32[96,128]{1,0:T(8,128)S(1)}, f32[96,128]{1,0:T(8,128)S(1)}, u32[]{:S(2)}, u32[]{:S(2)}) %collective-permute-start.11) | collective-permute-done | bytes 49184 | tf_op jit(solution)/shard_map/ppermute | solution.py:292
  25.3 2.0 %collective-permute-done.10.refs_6_ = f32[96,128]{1,0:T(8,128)S(1)} collective-permute-done((f32[96,128]{1,0:T(8,128)S(1)}, f32[96,128]{1,0:T(8,128)S(1)}, u32[]{:S(2)}, u32[]{:S(2)}) %collective-permute-start.10) | collective-permute-done | bytes 49184 | tf_op jit(solution)/shard_map/ppermute | solution.py:292
  27.3 0.6 %reply.1 = (f32[96,128]{1,0:T(8,128)S(1)}, f32[96,128]{1,0:T(8,128)S(1)}, f32[96,128]{1,0:T(8,128)S(1)}, f32[96,128]{1,0:T(8,128)S(1)}) custom-call(s32[2]{0:T(128)S(1)} %copy-done.10, s32[2]{0:T(128)S(1)} %collective-permute-done.refs_1_, s32[2]{0:T(128)S(1)} %collective-permute-done.1.refs_2_, s32[2]{0:T(128)S(1)} %collective-permute-done.2.refs_3_, ...), custom_call_target="tpu_custom_call" | custom-call | tf_op jit(solution)/shard_map/reply/pallas_call | solution.py:348
  27.9 1.3 %collective-permute-start.12 = (f32[96,128]{1,0:T(8,128)S(1)}, f32[96,128]{1,0:T(8,128)S(1)}, u32[]{:S(2)}, u32[]{:S(2)}) collective-permute-start(f32[96,128]{1,0:T(8,128)S(1)} %get-tuple-element.26), channel_id=1, source_target_pairs={{0,4},{1,5},{2,6},{3,7},{4,0},{5,1},{6,2},{7,3},{8,12},{9,13},{10,... | collective-permute-start | bytes 147464 | tf_op jit(solution)/shard_map/ppermute | solution.py:297
  29.2 2.9 %collective-permute-start.13 = (f32[96,128]{1,0:T(8,128)S(1)}, f32[96,128]{1,0:T(8,128)S(1)}, u32[]{:S(2)}, u32[]{:S(2)}) collective-permute-start(f32[96,128]{1,0:T(8,128)S(1)} %get-tuple-element.27), channel_id=1, source_target_pairs={{0,8},{1,9},{2,10},{3,11},{4,12},{5,13},{6,14},{7,15},{8,0},{9,1},... | collective-permute-start | bytes 147464 | tf_op jit(solution)/shard_map/ppermute | solution.py:297
  32.4 3.0 %local.1 = (bf16[384,128]{1,0:T(8,128)(2,1)S(1)}, f32[2,96,128]{2,1,0:T(8,128)S(1)}) custom-call(s32[2]{0:T(128)S(1)} %copy-done.11, bf16[384,128]{1,0:T(8,128)(2,1)S(1)} %bitcast.27, bf16[384,128]{1,0:T(8,128)(2,1)S(1)} %bitcast.29, bf16[384,128]{1,0:T(8,128)(2,1)S(1)} %bitcast.31, bf16[384,128]{1,0:T(8,128)(2,1)S(1)} %bitcast.32, f32[32,128]{1,0:T(8,128)S(1)} %bitcast.33, ...), custom_call_target="tpu_custom_call" | custom-call | tf_op jit(solution)/shard_map/local/pallas_call | solution.py:357
  35.5 2.6 %collective-permute-done.14.refs_2_ = f32[96,128]{1,0:T(8,128)S(1)} collective-permute-done((f32[96,128]{1,0:T(8,128)S(1)}, f32[96,128]{1,0:T(8,128)S(1)}, u32[]{:S(2)}, u32[]{:S(2)}) %collective-permute-start.14) | collective-permute-done | bytes 49184 | tf_op jit(solution)/shard_map/ppermute | solution.py:297
  38.0 1.4 %finish.1 = bf16[384,128]{1,0:T(8,128)(2,1)} custom-call(s32[2]{0:T(128)S(1)} %copy-done.11, bf16[384,128]{1,0:T(8,128)(2,1)S(1)} %get-tuple-element.24.base_ref, f32[2,96,128]{2,1,0:T(8,128)S(1)} %get-tuple-element.25.late_ref, f32[96,128]{1,0:T(8,128)S(1)} %collective-permute-done.12.refs_0_, f32[96,128]{1,0:T(8,128)S(1)} %collective-permute-done.13.refs_1_, ...), custom_call_target="tpu_custom_call" | custom-call | tf_op jit(solution)/shard_map/finish/pallas_call | solution.py:373
  (39 shorter events, 3.0 us)
Async XLA Ops:
  0.0 32.4 %copy-start.11 = (s32[2]{0:T(128)S(1)}, s32[2]{0:T(128)}, u32[]{:S(2)}) copy-start(s32[2]{0:T(128)} %slots_ref.9) | copy-start | bytes 28
  0.0 0.9 %copy-start.2 = (bf16[2,6,4096]{2,0,1:T(2,128)(2,1)S(1)}, bf16[2,6,4096]{2,0,1:T(2,128)(2,1)}, u32[]{:S(2)}) copy-start(bf16[2,6,4096]{2,0,1:T(2,128)(2,1)} %param.7) | copy-start | bytes 294916
  1.6 30.8 %copy-start.3 = (bf16[2,6,4096]{2,0,1:T(2,128)(2,1)S(1)}, bf16[2,6,4096]{2,0,1:T(2,128)(2,1)}, u32[]{:S(2)}) copy-start(bf16[2,6,4096]{2,0,1:T(2,128)(2,1)} %param.7) | copy-start | bytes 294916
  1.6 30.8 %copy-start.5 = (bf16[2,6,4096]{2,0,1:T(2,128)(2,1)S(1)}, bf16[2,6,4096]{2,0,1:T(2,128)(2,1)}, u32[]{:S(2)}) copy-start(bf16[2,6,4096]{2,0,1:T(2,128)(2,1)} %param.8) | copy-start | bytes 294916
  1.6 30.8 %copy-start.7 = (bf16[2,6,4096]{2,0,1:T(2,128)(2,1)S(1)}, bf16[2,6,4096]{2,0,1:T(2,128)(2,1)}, u32[]{:S(2)}) copy-start(bf16[2,6,4096]{2,0,1:T(2,128)(2,1)} %param.9) | copy-start | bytes 294916
  1.6 30.8 %copy-start.12 = (f32[4096]{0:T(1024)S(1)}, f32[4096]{0:T(1024)}, u32[]{:S(2)}) copy-start(f32[4096]{0:T(1024)} %param.13) | copy-start | bytes 49156
  2.2 9.9 %collective-permute-start.5 = (f32[96,128]{1,0:T(8,128)S(1)}, f32[96,128]{1,0:T(8,128)S(1)}, u32[]{:S(2)}, u32[]{:S(2)}) collective-permute-start(f32[96,128]{1,0:T(8,128)S(1)} %ask.1.refs_4_), channel_id=1, source_target_pairs={{0,12},{1,13},{2,14},{3,15},{4,8},{5,9},{6,10},{7,11},{8,4},{9,5},... | collective-permute-start | bytes 147464 | tf_op jit(solution)/shard_map/ppermute | solution.py:297
  7.4 5.0 %collective-permute-start.4 = (f32[96,128]{1,0:T(8,128)S(1)}, f32[96,128]{1,0:T(8,128)S(1)}, u32[]{:S(2)}, u32[]{:S(2)}) collective-permute-start(f32[96,128]{1,0:T(8,128)S(1)} %ask.1.refs_4_), channel_id=1, source_target_pairs={{0,8},{1,9},{2,10},{3,11},{4,12},{5,13},{6,14},{7,15},{8,0},{9,1},... | collective-permute-start | bytes 147464 | tf_op jit(solution)/shard_map/ppermute | solution.py:297
  7.4 5.0 %collective-permute-start.3 = (f32[96,128]{1,0:T(8,128)S(1)}, f32[96,128]{1,0:T(8,128)S(1)}, u32[]{:S(2)}, u32[]{:S(2)}) collective-permute-start(f32[96,128]{1,0:T(8,128)S(1)} %ask.1.refs_4_), channel_id=1, source_target_pairs={{0,4},{1,5},{2,6},{3,7},{4,0},{5,1},{6,2},{7,3},{8,12},{9,13},{10,... | collective-permute-start | bytes 147464 | tf_op jit(solution)/shard_map/ppermute | solution.py:297
  8.0 3.0 %collective-permute-start.2 = (s32[2]{0:T(128)S(1)}, s32[2]{0:T(128)S(1)}, u32[]{:S(2)}, u32[]{:S(2)}) collective-permute-start(s32[2]{0:T(128)S(1)} %copy-done.9), channel_id=1, source_target_pairs={{0,3},{1,2},{2,1},{3,0},{4,7},{5,6},{6,5},{7,4},{8,11},{9,10},{10,... | collective-permute-start | bytes 32 | tf_op jit(solution)/shard_map/ppermute | solution.py:292
  8.4 3.5 %collective-permute-start.1 = (s32[2]{0:T(128)S(1)}, s32[2]{0:T(128)S(1)}, u32[]{:S(2)}, u32[]{:S(2)}) collective-permute-start(s32[2]{0:T(128)S(1)} %copy-done.9), channel_id=1, source_target_pairs={{0,2},{1,3},{2,0},{3,1},{4,6},{5,7},{6,4},{7,5},{8,10},{9,11},{10,... | collective-permute-start | bytes 32 | tf_op jit(solution)/shard_map/ppermute | solution.py:292
  11.0 1.1 %collective-permute-start = (s32[2]{0:T(128)S(1)}, s32[2]{0:T(128)S(1)}, u32[]{:S(2)}, u32[]{:S(2)}) collective-permute-start(s32[2]{0:T(128)S(1)} %copy-done.9), channel_id=1, source_target_pairs={{0,1},{1,0},{2,3},{3,2},{4,5},{5,4},{6,7},{7,6},{8,9},{9,8},{10,11... | collective-permute-start | bytes 32 | tf_op jit(solution)/shard_map/ppermute | solution.py:292
  13.0 7.6 %collective-permute-start.6 = (f32[96,128]{1,0:T(8,128)S(1)}, f32[96,128]{1,0:T(8,128)S(1)}, u32[]{:S(2)}, u32[]{:S(2)}) collective-permute-start(f32[96,128]{1,0:T(8,128)S(1)} %get-tuple-element.18), channel_id=1, source_target_pairs={{0,1},{1,0},{2,3},{3,2},{4,5},{5,4},{6,7},{7,6},{8,9},{9,8},{10,11... | collective-permute-start | bytes 147464 | tf_op jit(solution)/shard_map/ppermute | solution.py:292
  13.2 7.4 %collective-permute-start.7 = (f32[96,128]{1,0:T(8,128)S(1)}, f32[96,128]{1,0:T(8,128)S(1)}, u32[]{:S(2)}, u32[]{:S(2)}) collective-permute-start(f32[96,128]{1,0:T(8,128)S(1)} %get-tuple-element.19), channel_id=1, source_target_pairs={{0,2},{1,3},{2,0},{3,1},{4,6},{5,7},{6,4},{7,5},{8,10},{9,11},{10,... | collective-permute-start | bytes 147464 | tf_op jit(solution)/shard_map/ppermute | solution.py:292
  14.7 6.0 %collective-permute-start.8 = (f32[96,128]{1,0:T(8,128)S(1)}, f32[96,128]{1,0:T(8,128)S(1)}, u32[]{:S(2)}, u32[]{:S(2)}) collective-permute-start(f32[96,128]{1,0:T(8,128)S(1)} %get-tuple-element.20), channel_id=1, source_target_pairs={{0,3},{1,2},{2,1},{3,0},{4,7},{5,6},{6,5},{7,4},{8,11},{9,10},{10,... | collective-permute-start | bytes 147464 | tf_op jit(solution)/shard_map/ppermute | solution.py:292
  14.9 2.2 %copy-start = (f32[2,32,128,128]{3,2,1,0:T(8,128)S(1)}, f32[2,32,128,128]{3,2,1,0:T(8,128)}, u32[]{:S(2)}) copy-start(f32[2,32,128,128]{3,2,1,0:T(8,128)} %states_ref.3) | copy-start | bytes 12582916
  19.5 12.9 %copy-start.1 = (f32[2,32,128,128]{3,2,1,0:T(8,128)S(1)}, f32[2,32,128,128]{3,2,1,0:T(8,128)}, u32[]{:S(2)}) copy-start(f32[2,32,128,128]{3,2,1,0:T(8,128)} %states_ref.3) | copy-start | bytes 12582916
  19.5 12.9 %copy-start.8 = (bf16[2,6,4096]{2,0,1:T(2,128)(2,1)S(1)}, bf16[2,6,4096]{2,0,1:T(2,128)(2,1)}, u32[]{:S(2)}) copy-start(bf16[2,6,4096]{2,0,1:T(2,128)(2,1)} %param.10) | copy-start | bytes 294916
  21.6 3.6 %collective-permute-start.11 = (f32[96,128]{1,0:T(8,128)S(1)}, f32[96,128]{1,0:T(8,128)S(1)}, u32[]{:S(2)}, u32[]{:S(2)}) collective-permute-start(f32[96,128]{1,0:T(8,128)S(1)} %answer.1.refs_4_), channel_id=1, source_target_pairs={{0,3},{1,2},{2,1},{3,0},{4,7},{5,6},{6,5},{7,4},{8,11},{9,10},{10,... | collective-permute-start | bytes 147464 | tf_op jit(solution)/shard_map/ppermute | solution.py:292
  23.2 4.1 %collective-permute-start.10 = (f32[96,128]{1,0:T(8,128)S(1)}, f32[96,128]{1,0:T(8,128)S(1)}, u32[]{:S(2)}, u32[]{:S(2)}) collective-permute-start(f32[96,128]{1,0:T(8,128)S(1)} %answer.1.refs_4_), channel_id=1, source_target_pairs={{0,2},{1,3},{2,0},{3,1},{4,6},{5,7},{6,4},{7,5},{8,10},{9,11},{10,... | collective-permute-start | bytes 147464 | tf_op jit(solution)/shard_map/ppermute | solution.py:292
  23.8 3.5 %collective-permute-start.9 = (f32[96,128]{1,0:T(8,128)S(1)}, f32[96,128]{1,0:T(8,128)S(1)}, u32[]{:S(2)}, u32[]{:S(2)}) collective-permute-start(f32[96,128]{1,0:T(8,128)S(1)} %answer.1.refs_4_), channel_id=1, source_target_pairs={{0,1},{1,0},{2,3},{3,2},{4,5},{5,4},{6,7},{7,6},{8,9},{9,8},{10,11... | collective-permute-start | bytes 147464 | tf_op jit(solution)/shard_map/ppermute | solution.py:292
  27.9 7.5 %collective-permute-start.12 = (f32[96,128]{1,0:T(8,128)S(1)}, f32[96,128]{1,0:T(8,128)S(1)}, u32[]{:S(2)}, u32[]{:S(2)}) collective-permute-start(f32[96,128]{1,0:T(8,128)S(1)} %get-tuple-element.26), channel_id=1, source_target_pairs={{0,4},{1,5},{2,6},{3,7},{4,0},{5,1},{6,2},{7,3},{8,12},{9,13},{10,... | collective-permute-start | bytes 147464 | tf_op jit(solution)/shard_map/ppermute | solution.py:297
  29.2 6.2 %collective-permute-start.13 = (f32[96,128]{1,0:T(8,128)S(1)}, f32[96,128]{1,0:T(8,128)S(1)}, u32[]{:S(2)}, u32[]{:S(2)}) collective-permute-start(f32[96,128]{1,0:T(8,128)S(1)} %get-tuple-element.27), channel_id=1, source_target_pairs={{0,8},{1,9},{2,10},{3,11},{4,12},{5,13},{6,14},{7,15},{8,0},{9,1},... | collective-permute-start | bytes 147464 | tf_op jit(solution)/shard_map/ppermute | solution.py:297
  32.2 5.9 %collective-permute-start.14 = (f32[96,128]{1,0:T(8,128)S(1)}, f32[96,128]{1,0:T(8,128)S(1)}, u32[]{:S(2)}, u32[]{:S(2)}) collective-permute-start(f32[96,128]{1,0:T(8,128)S(1)} %get-tuple-element.28), channel_id=1, source_target_pairs={{0,12},{1,13},{2,14},{3,15},{4,8},{5,9},{6,10},{7,11},{8,4},{9,5},... | collective-permute-start | bytes 147464 | tf_op jit(solution)/shard_map/ppermute | solution.py:297
  (4 other events, 3.1 us)

commit v3 on v2

--- a/solution.py
+++ b/solution.py
@@ -12,6 +12,7 @@
 F32 = jnp.float32
 BF16 = jnp.bfloat16
 MIB = 2**20
+LARGE = 61
 VMEM = pl.BlockSpec(memory_space=pltpu.VMEM)
 SMEM = pl.BlockSpec(memory_space=pltpu.SMEM)
 HBM = pl.BlockSpec(memory_space=pltpu.HBM)
@@ -36,12 +37,20 @@
     return place, moves
 
 
-def wanted_device(slots_ref, device, count):
+def wanted_device(slots_ref, count):
+    device = lax.axis_index("req")
     result = device
     for s in range(count):
         owner = lax.div(slots_ref[s], jnp.int32(count))
         result = jnp.where(owner != device, owner, result)
     return result
+
+
+OUTER, INNER, SLOT = 0, 1, 2
+
+
+def fact(ref, kind, rows):
+    return jnp.broadcast_to(ref[kind:kind + 1, :], (rows, ref.shape[1]))
 
 
 def head_slope(heads, width):
@@ -85,13 +94,17 @@
     return result
 
 
-def ask_kernel(slots_ref, queries_ref, out_ref, rows_ref, wide, sem, *, count):
+def ask_kernel(slots_ref, queries_ref, out_ref, facts_ref, rows_ref, wide, sem, *, count, inner):
     late = rows_ref.shape[0]
     first = queries_ref.shape[0] - late
     copy = pltpu.make_async_copy(queries_ref.at[pl.ds(first, late)], rows_ref, sem)
     copy.start()
+    place, moves = moving_slot(slots_ref, count)
+    wanted = wanted_device(slots_ref, count)
+    kind = lax.broadcasted_iota(jnp.int32, facts_ref.shape, 0)
+    facts = jnp.where(kind == INNER, lax.rem(wanted, inner), jnp.where(moves, place, count))
+    facts_ref[...] = jnp.where(kind == OUTER, lax.div(wanted, inner), facts)
     copy.wait()
-    place, _ = moving_slot(slots_ref, count)
     wide[...] = rows_ref[...].astype(F32)
     out_ref[...] = silu(extract(wide, place, count))
 
@@ -118,24 +131,20 @@
             weight_ref[h] = jnp.concatenate(split(state[h]), axis=0)
 
 
-def route_kernel(*refs, inner, outer, count):
+def route_kernel(*refs, inner, outer):
     wishes, column = refs[:inner], refs[inner:inner + outer]
     outs = refs[inner + outer:]
-    me = lax.axis_index("req")
-    my_inner, my_outer = lax.rem(me, inner), lax.div(me, inner)
+    my_outer = lax.div(lax.axis_index("req"), inner)
     for k in range(inner):
-        back = inverse_step(k, inner)
-        mate = my_outer * inner + unturn(my_inner, back, inner)
-        wanted = wanted_device(wishes[back], mate, count)
-        outs[k][...] = choose(column, lax.div(wanted, inner), my_outer, outer)
-
-
-def answer_kernel(slots_ref, *refs, inner, count, late, heads, width):
+        wish = fact(wishes[inverse_step(k, inner)], OUTER, outs[k].shape[0])
+        outs[k][...] = choose(column, wish, my_outer, outer)
+
+
+def answer_kernel(facts_ref, *refs, inner, late, heads, width):
     found, (weight_ref, early_ref, out_ref, lhs, prod) = refs[:inner], refs[inner:]
-    me = lax.axis_index("req")
-    wanted = wanted_device(slots_ref, me, count)
+    my_inner = lax.rem(lax.axis_index("req"), inner)
     block = lambda ref, t: ref[t * heads:(t + 1) * heads, :]
-    rows = choose(found, lax.rem(wanted, inner), lax.rem(me, inner), inner)
+    rows = choose(found, fact(facts_ref, INNER, late * heads), my_inner, inner)
     q = [rows[t * heads:(t + 1) * heads, :] for t in range(late)]
     slope = head_slope(heads, width)
     for t in range(late):
@@ -156,30 +165,30 @@
         out_ref[t * heads:(t + 1) * heads, :] = total
 
 
-def reply_kernel(*refs, inner, outer, count):
+def reply_kernel(*refs, inner, outer):
     wishes, replies = refs[:inner], refs[inner:2 * inner]
     outs = refs[2 * inner:]
     me = lax.axis_index("req")
     my_inner, my_outer = lax.rem(me, inner), lax.div(me, inner)
-    wanted = [
-        wanted_device(wishes[k], my_outer * inner + unturn(my_inner, k, inner), count)
-        for k in range(inner)]
+    rows = outs[0].shape[0]
+    owner = [
+        jnp.where(fact(wish, INNER, rows) == my_inner, fact(wish, OUTER, rows), -1)
+        for wish in wishes]
     for k in range(outer):
-        device = turn(my_outer, k, outer) * inner + my_inner
-        result = jnp.where(wanted[0] == device, replies[0][...], 0.0)
-        for n in range(1, inner):
-            result = jnp.where(wanted[n] == device, replies[n][...], result)
+        result = 0.0
+        for n in range(inner):
+            result = jnp.where(owner[n] == turn(my_outer, k, outer), replies[n][...], result)
         outs[k][...] = result
 
 
-def local_kernel(slots_ref, queries_ref, keys_ref, values_ref, gates_ref, gain_ref, own_ref,
-                 states_ref, out_ref, late_ref, state, lhs, prod, wide, sems, *, count, chunks):
+def local_kernel(facts_ref, queries_ref, keys_ref, values_ref, gates_ref, gain_ref, own_ref,
+                 states_ref, out_ref, last_ref, late_ref, state, lhs, prod, wide, sems, *, count, chunks):
     heads, width = states_ref.shape[1], states_ref.shape[2]
     span = heads * count
     steps = queries_ref.shape[0] // span
     late = steps - BEFORE
     size = heads // chunks
-    place, _ = moving_slot(slots_ref, count)
+    place = fact(facts_ref, SLOT, late * heads)
 
     def load(j, c):
         part = pl.ds(c * size, size)
@@ -244,17 +253,17 @@
             whole = jnp.sum(jnp.where(slot == s, sums, 0.0), axis=0, keepdims=True)
             energy = jnp.where(slot == s, whole, energy)
         factor = lax.rsqrt(energy * (1.0 / (heads * width)) + EPS)
-        out_ref[t * span:(t + 1) * span, :] = (x * factor * scale[t]).astype(BF16)
-
-
-def finish_kernel(slots_ref, base_ref, late_ref, *refs, count, heads):
-    parts, out_ref, wide = refs[:-2], refs[-2], refs[-1]
-    place, moves = moving_slot(slots_ref, count)
-    rows = wide.shape[0]
-    first = base_ref.shape[0] - rows
-    single = rows // count
-    wide[...] = base_ref[first:, :].astype(F32)
-    for t in range(single // heads):
+        y = (x * factor * scale[t]).astype(BF16)
+        out_ref[t * span:(t + 1) * span, :] = y
+        if t >= BEFORE:
+            last_ref[(t - BEFORE) * span:(t - BEFORE + 1) * span, :] = y
+
+
+def finish_kernel(facts_ref, base_ref, last_ref, late_ref, *refs, count, heads):
+    parts, (out_ref, rows_ref, wide, sem) = refs[:-4], refs[-4:]
+    wide[...] = last_ref[...].astype(F32)
+    place = fact(facts_ref, SLOT, heads)
+    for t in range(late_ref.shape[1] // heads):
         part = slice(t * heads, (t + 1) * heads)
         x = late_ref[0, part, :]
         for ref in parts:
@@ -262,10 +271,13 @@
         y = x * lax.rsqrt(jnp.mean(x * x) + EPS) * late_ref[1, part, :]
         for s in range(count):
             here = pl.ds(t * heads * count + s, heads, stride=count)
-            use = jnp.logical_and(moves, place == s)
-            wide[here, :] = jnp.where(use, y, wide[here, :])
-    out_ref[:first, :] = base_ref[:first, :]
-    out_ref[first:, :] = wide[...].astype(BF16)
+            wide[here, :] = jnp.where(place == s, y, wide[here, :])
+    rows_ref[...] = wide[...].astype(BF16)
+    rows = rows_ref.shape[0]
+    copy = pltpu.make_async_copy(
+        rows_ref, out_ref.at[pl.ds(out_ref.shape[0] - rows, rows)], sem)
+    copy.start()
+    copy.wait()
 
 
 def near_square(total):
@@ -305,16 +317,19 @@
     single = jax.ShapeDtypeStruct((single_rows, width), F32)
     late_packed = pltpu.VMEM((late * heads * count, width), F32)
 
-    ask = pl.pallas_call(
-        functools.partial(ask_kernel, count=count),
-        out_shape=single, in_specs=[SMEM, HBM], out_specs=VMEM,
-        scratch_shapes=[pltpu.VMEM((late * heads * count, width), BF16), late_packed,
-                        pltpu.SemaphoreType.DMA],
-        compiler_params=params(4), name="ask",
+    late_rows = jax.ShapeDtypeStruct((late * heads * count, width), BF16)
+    late_bf16 = pltpu.VMEM(late_rows.shape, BF16)
+
+    ask, facts = pl.pallas_call(
+        functools.partial(ask_kernel, count=count, inner=inner),
+        out_shape=(single, jax.ShapeDtypeStruct((8, width), jnp.int32)),
+        in_specs=[SMEM, HBM], out_specs=(VMEM, VMEM),
+        scratch_shapes=[late_bf16, late_packed, pltpu.SemaphoreType.DMA],
+        compiler_params=params(LARGE), name="ask",
     )(new_slot, queries)
 
     column = [ask] + [send_outer(ask, k) for k in range(1, outer)]
-    wishes = [new_slot] + [send_inner(new_slot, k) for k in range(1, inner)]
+    wishes = [facts] + [send_inner(facts, k) for k in range(1, inner)]
 
     chunks = 8
     weight, early = pl.pallas_call(
@@ -325,40 +340,39 @@
         scratch_shapes=[pltpu.VMEM((heads, width, width), F32),
                         pltpu.VMEM((BEFORE * heads * count, width), F32),
                         pltpu.SemaphoreType.DMA((chunks,))],
-        compiler_params=params(12), name="prepare",
+        compiler_params=params(LARGE), name="prepare",
     )(new_slot, keys, values, states)
 
     asked = pl.pallas_call(
-        functools.partial(route_kernel, inner=inner, outer=outer, count=count),
+        functools.partial(route_kernel, inner=inner, outer=outer),
         out_shape=(single,) * inner,
-        in_specs=[SMEM] * inner + [VMEM] * outer, out_specs=(VMEM,) * inner,
+        in_specs=[VMEM] * (inner + outer), out_specs=(VMEM,) * inner,
         compiler_params=params(4), name="route",
     )(*wishes, *column)
     found = [asked[0]] + [send_inner(asked[k], k) for k in range(1, inner)]
 
     answer = pl.pallas_call(
-        functools.partial(answer_kernel, inner=inner, count=count, late=late, heads=heads,
-                          width=width),
-        out_shape=single, in_specs=[SMEM] + [VMEM] * (inner + 2), out_specs=VMEM,
+        functools.partial(answer_kernel, inner=inner, late=late, heads=heads, width=width),
+        out_shape=single, in_specs=[VMEM] * (inner + 3), out_specs=VMEM,
         scratch_shapes=[pltpu.VMEM((2 * late * heads, width), F32)] * 2,
         compiler_params=params(8), name="answer",
-    )(new_slot, *found, weight, early)
+    )(facts, *found, weight, early)
     replies = [answer] + [send_inner(answer, k) for k in range(1, inner)]
 
     sorted_replies = pl.pallas_call(
-        functools.partial(reply_kernel, inner=inner, outer=outer, count=count),
+        functools.partial(reply_kernel, inner=inner, outer=outer),
         out_shape=(single,) * outer,
-        in_specs=[SMEM] * inner + [VMEM] * inner, out_specs=(VMEM,) * outer,
+        in_specs=[VMEM] * (2 * inner), out_specs=(VMEM,) * outer,
         compiler_params=params(4), name="reply",
     )(*wishes, *replies)
     parts = [send_outer(sorted_replies[k], k) for k in range(1, outer)]
 
     chunks = 4
-    base, late_rows = pl.pallas_call(
+    output = jax.ShapeDtypeStruct((packed_rows, width), BF16)
+    base, last, partial = pl.pallas_call(
         functools.partial(local_kernel, count=count, chunks=chunks),
-        out_shape=(jax.ShapeDtypeStruct((packed_rows, width), BF16),
-                   jax.ShapeDtypeStruct((2, single_rows, width), F32)),
-        in_specs=[SMEM] + [VMEM] * 6 + [HBM], out_specs=(VMEM, VMEM),
+        out_shape=(output, late_rows, jax.ShapeDtypeStruct((2, single_rows, width), F32)),
+        in_specs=[VMEM] * 7 + [HBM], out_specs=(VMEM, VMEM, VMEM),
         scratch_shapes=[
             pltpu.VMEM((count, heads, width, width), F32),
             pltpu.VMEM((16 * heads * count, width), F32),
@@ -366,17 +380,17 @@
             late_packed,
             pltpu.SemaphoreType.DMA((count, chunks)),
         ],
-        compiler_params=params(16), name="local",
-    )(new_slot, queries, keys, values, gates, norm_gain.reshape(heads, width),
+        compiler_params=params(LARGE), name="local",
+    )(facts, queries, keys, values, gates, norm_gain.reshape(heads, width),
       sorted_replies[0], states)
 
     return unpack(pl.pallas_call(
         functools.partial(finish_kernel, count=count, heads=heads),
-        out_shape=jax.ShapeDtypeStruct((packed_rows, width), BF16),
-        in_specs=[SMEM, VMEM, VMEM] + [VMEM] * (outer - 1), out_specs=VMEM,
-        scratch_shapes=[late_packed],
+        out_shape=output, in_specs=[VMEM, HBM] + [VMEM] * (outer + 1), out_specs=HBM,
+        scratch_shapes=[late_bf16, late_packed, pltpu.SemaphoreType.DMA],
+        input_output_aliases={1: 0},
         compiler_params=params(4), name="finish",
-    )(new_slot, base, late_rows, *parts))
+    )(facts, base, last, partial, *parts))
 
 
 def solution(mesh):

time: 39.7 us -> 42.6 us (1.073)
  Pallas kernels: 8.42 us -> 12.1 us
  waiting for transfers between devices: 8.42 us -> 7.22 us
    pallas_call x1, Pallas kernels: 1.06 us -> 3.91 us  [on_device(): pl.pallas_call(functools.partial(prepare_kernel, count=count, chunks=chun...]
    ppermute x6, waiting for transfers between devices: 2.8 us -> 1.06 us  [send_outer(): lax.ppermute(x, 'req', [(o * inner + i, int(turn(o, k, outer)) * inner +...]
    pallas_call x1, Pallas kernels: 3.03 us -> 4.59 us  [on_device(): pl.pallas_call(functools.partial(local_kernel, count=count, chunks=chunks...]
    pallas_call x1, Pallas kernels: 1.45 us -> 0.9 us  [on_device(): pl.pallas_call(functools.partial(finish_kernel, count=count, heads=heads)...]
    ppermute x9, waiting for transfers between devices: 5.62 us -> 6.16 us  [send_inner(): lax.ppermute(x, 'req', [(o * inner + i, o * inner + int(turn(i, k, inner)...]
    unnamed x26 -> x18, local copies, waits for them, and re-layouts: 6.21 us -> 6.25 us
  transfers between devices with their start and end apart: 15 -> 15, of which waited for: 7 -> 6; matrix products, arithmetic and copies ran while one was open for 0% -> 0% of each run, Pallas kernels for 10% -> 20%
where the time goes in v3:
time: 42.6 us; the launch traced here: 42.1 us
  starting transfers between devices  16.4 us (38%)
  Pallas kernels  12.1 us (28%)
  waiting for transfers between devices  7.22 us (17%)
  local copies, waits for them, and re-layouts  6.25 us (15%)
    ppermute x6, starting transfers between devices, send_outer(): lax.ppermute(x, 'req', [(o * inner + i, int(turn(o, k, outer)) * inner +...  10.1 us
    ppermute x9, starting transfers between devices, send_inner(): lax.ppermute(x, 'req', [(o * inner + i, o * inner + int(turn(i, k, inner)...  6.26 us
    unnamed x18, local copies, waits for them, and re-layouts  6.25 us
    ppermute x9, waiting for transfers between devices, send_inner(): lax.ppermute(x, 'req', [(o * inner + i, o * inner + int(turn(i, k, inner)...  6.16 us
    pallas_call x1, Pallas kernels, on_device(): pl.pallas_call(functools.partial(local_kernel, count=count, chunks=chunks...  4.59 us
    pallas_call x1, Pallas kernels, on_device(): pl.pallas_call(functools.partial(prepare_kernel, count=count, chunks=chun...  3.91 us
    pallas_call x1, Pallas kernels, on_device(): pl.pallas_call(functools.partial(ask_kernel, count=count, inner=inner), o...  2.13 us
    ppermute x6, waiting for transfers between devices, send_outer(): lax.ppermute(x, 'req', [(o * inner + i, int(turn(o, k, outer)) * inner +...  1.06 us
  transfers between devices with their start and end apart: 15, of which 6 were waited for; matrix products, arithmetic and copies ran while one was open for 0% of the time, Pallas kernels for 20%

profile of v3, /device:TPU:0, one launch (start us, length us, event | category | flops | bytes accessed | tf_op | source)
XLA Modules:
  0.0 42.1 jit_solution(7496029428662741812)
XLA Ops:
  0.0 2.1 %ask.1 = (f32[96,128]{1,0:T(8,128)}, s32[8,128]{1,0:T(8,128)}) custom-call(s32[2]{0:T(128)} %slots_ref.3, bf16[384,128]{1,0:T(8,128)(2,1)} %bitcast.26), custom_call_target="tpu_custom_call" | custom-call | tf_op jit(solution)/shard_map/ask/pallas_call | solution.py:323
  2.1 5.1 %collective-permute-start.5 = (f32[96,128]{1,0:T(8,128)}, f32[96,128]{1,0:T(8,128)S(1)}, u32[]{:S(2)}, u32[]{:S(2)}) collective-permute-start(f32[96,128]{1,0:T(8,128)} %get-tuple-element.21.refs_4_), channel_id=1, source_target_pairs={{0,12},{1,13},{2,14},{3,15},{4,8},{5,9},{6,10},{7,11},{8,4},{9,5},... | collective-permute-start | bytes 147464 | tf_op jit(solution)/shard_map/ppermute | solution.py:309
  7.3 0.6 %collective-permute-start.3 = (f32[96,128]{1,0:T(8,128)}, f32[96,128]{1,0:T(8,128)S(1)}, u32[]{:S(2)}, u32[]{:S(2)}) collective-permute-start(f32[96,128]{1,0:T(8,128)} %get-tuple-element.21.refs_4_), channel_id=1, source_target_pairs={{0,4},{1,5},{2,6},{3,7},{4,0},{5,1},{6,2},{7,3},{8,12},{9,13},{10,... | collective-permute-start | bytes 147464 | tf_op jit(solution)/shard_map/ppermute | solution.py:309
  8.3 1.3 %collective-permute-start.1 = (s32[8,128]{1,0:T(8,128)}, s32[8,128]{1,0:T(8,128)S(1)}, u32[]{:S(2)}, u32[]{:S(2)}) collective-permute-start(s32[8,128]{1,0:T(8,128)} %get-tuple-element.20.refs_0_.facts_ref), channel_id=1, source_target_pairs={{0,2},{1,3},{2,0},{3,1},{4,6},{5,7},{6,4},{7,5},{8,10},{9,11},{10,... | collective-permute-start | bytes 12296 | tf_op jit(solution)/shard_map/ppermute | solution.py:304
  9.6 1.5 %collective-permute-done.2.refs_3_ = s32[8,128]{1,0:T(8,128)S(1)} collective-permute-done((s32[8,128]{1,0:T(8,128)}, s32[8,128]{1,0:T(8,128)S(1)}, u32[]{:S(2)}, u32[]{:S(2)}) %collective-permute-start.2) | collective-permute-done | bytes 4128 | tf_op jit(solution)/shard_map/ppermute | solution.py:304
  11.5 0.6 %collective-permute-done.1.refs_2_ = s32[8,128]{1,0:T(8,128)S(1)} collective-permute-done((s32[8,128]{1,0:T(8,128)}, s32[8,128]{1,0:T(8,128)S(1)}, u32[]{:S(2)}, u32[]{:S(2)}) %collective-permute-start.1) | collective-permute-done | bytes 4128 | tf_op jit(solution)/shard_map/ppermute | solution.py:304
  12.5 0.7 %copy-done.1 = s32[8,128]{1,0:T(8,128)S(1)} copy-done((s32[8,128]{1,0:T(8,128)S(1)}, s32[8,128]{1,0:T(8,128)}, u32[]{:S(2)}) %copy-start.1) | copy-done | bytes 4120
  13.2 0.8 %copy-done.7 = f32[96,128]{1,0:T(8,128)S(1)} copy-done((f32[96,128]{1,0:T(8,128)S(1)}, f32[96,128]{1,0:T(8,128)}, u32[]{:S(2)}) %copy-start.7) | copy-done | bytes 49176
  14.4 1.5 %collective-permute-start.7 = (f32[96,128]{1,0:T(8,128)S(1)}, f32[96,128]{1,0:T(8,128)S(1)}, u32[]{:S(2)}, u32[]{:S(2)}) collective-permute-start(f32[96,128]{1,0:T(8,128)S(1)} %get-tuple-element.24), channel_id=1, source_target_pairs={{0,2},{1,3},{2,0},{3,1},{4,6},{5,7},{6,4},{7,5},{8,10},{9,11},{10,... | collective-permute-start | bytes 147464 | tf_op jit(solution)/shard_map/ppermute | solution.py:304
  16.0 3.9 %prepare.1 = (bf16[32,256,128]{2,1,0:T(8,128)(2,1)}, f32[2,96,128]{2,1,0:T(8,128)}) custom-call(s32[2]{0:T(128)} %slots_ref.3, bf16[384,128]{1,0:T(8,128)(2,1)} %bitcast.28, bf16[384,128]{1,0:T(8,128)(2,1)} %bitcast.30, f32[2,32,128,128]{3,2,1,0:T(8,128)} %states_ref.3), custom_call_target="tpu_custom_call" | custom-call | tf_op jit(solution)/shard_map/prepare/pallas_call | solution.py:335
  20.0 1.6 %copy-done = bf16[32,256,128]{2,1,0:T(8,128)(2,1)S(1)} copy-done((bf16[32,256,128]{2,1,0:T(8,128)(2,1)S(1)}, bf16[32,256,128]{2,1,0:T(8,128)(2,1)}, u32[]{:S(2)}) %copy-start) | copy-done | bytes 2097176
  21.6 0.9 %copy-done.4 = f32[2,96,128]{2,1,0:T(8,128)S(1)} copy-done((f32[2,96,128]{2,1,0:T(8,128)S(1)}, f32[2,96,128]{2,1,0:T(8,128)}, u32[]{:S(2)}) %copy-start.4) | copy-done | bytes 98328
  22.9 1.8 %collective-permute-start.11 = (f32[96,128]{1,0:T(8,128)S(1)}, f32[96,128]{1,0:T(8,128)S(1)}, u32[]{:S(2)}, u32[]{:S(2)}) collective-permute-start(f32[96,128]{1,0:T(8,128)S(1)} %answer.1.refs_4_), channel_id=1, source_target_pairs={{0,3},{1,2},{2,1},{3,0},{4,7},{5,6},{6,5},{7,4},{8,11},{9,10},{10,... | collective-permute-start | bytes 147464 | tf_op jit(solution)/shard_map/ppermute | solution.py:304
  24.7 0.5 %collective-permute-start.10 = (f32[96,128]{1,0:T(8,128)S(1)}, f32[96,128]{1,0:T(8,128)S(1)}, u32[]{:S(2)}, u32[]{:S(2)}) collective-permute-start(f32[96,128]{1,0:T(8,128)S(1)} %answer.1.refs_4_), channel_id=1, source_target_pairs={{0,2},{1,3},{2,0},{3,1},{4,6},{5,7},{6,4},{7,5},{8,10},{9,11},{10,... | collective-permute-start | bytes 147464 | tf_op jit(solution)/shard_map/ppermute | solution.py:304
  25.2 1.5 %collective-permute-done.11.refs_7_ = f32[96,128]{1,0:T(8,128)S(1)} collective-permute-done((f32[96,128]{1,0:T(8,128)S(1)}, f32[96,128]{1,0:T(8,128)S(1)}, u32[]{:S(2)}, u32[]{:S(2)}) %collective-permute-start.11) | collective-permute-done | bytes 49184 | tf_op jit(solution)/shard_map/ppermute | solution.py:304
  26.7 2.0 %collective-permute-done.10.refs_6_ = f32[96,128]{1,0:T(8,128)S(1)} collective-permute-done((f32[96,128]{1,0:T(8,128)S(1)}, f32[96,128]{1,0:T(8,128)S(1)}, u32[]{:S(2)}, u32[]{:S(2)}) %collective-permute-start.10) | collective-permute-done | bytes 49184 | tf_op jit(solution)/shard_map/ppermute | solution.py:304
  28.8 0.6 %copy-done.6 = f32[96,128]{1,0:T(8,128)} copy-done((f32[96,128]{1,0:T(8,128)}, f32[96,128]{1,0:T(8,128)S(1)}, u32[]{:S(2)}) %copy-start.6) | copy-done | bytes 49176
  29.4 1.2 %collective-permute-start.12 = (f32[96,128]{1,0:T(8,128)S(1)}, f32[96,128]{1,0:T(8,128)S(1)}, u32[]{:S(2)}, u32[]{:S(2)}) collective-permute-start(f32[96,128]{1,0:T(8,128)S(1)} %get-tuple-element.32), channel_id=1, source_target_pairs={{0,4},{1,5},{2,6},{3,7},{4,0},{5,1},{6,2},{7,3},{8,12},{9,13},{10,... | collective-permute-start | bytes 147464 | tf_op jit(solution)/shard_map/ppermute | solution.py:309
  30.7 2.9 %collective-permute-start.13 = (f32[96,128]{1,0:T(8,128)S(1)}, f32[96,128]{1,0:T(8,128)S(1)}, u32[]{:S(2)}, u32[]{:S(2)}) collective-permute-start(f32[96,128]{1,0:T(8,128)S(1)} %get-tuple-element.33), channel_id=1, source_target_pairs={{0,8},{1,9},{2,10},{3,11},{4,12},{5,13},{6,14},{7,15},{8,0},{9,1},... | collective-permute-start | bytes 147464 | tf_op jit(solution)/shard_map/ppermute | solution.py:309
  33.8 4.6 %local.1 = (bf16[384,128]{1,0:T(8,128)(2,1)}, bf16[192,128]{1,0:T(8,128)(2,1)}, f32[2,96,128]{2,1,0:T(8,128)}) custom-call(s32[8,128]{1,0:T(8,128)} %get-tuple-element.20.refs_0_.facts_ref, bf16[384,128]{1,0:T(8,128)(2,1)} %bitcast.27, bf16[384,128]{1,0:T(8,128)(2,1)} %bitcast.29, bf16[384,128]{1,0:T(8,128)(2,1)} %bitcast.31, bf16[384,128]{1,0:T(8,128)(2,1)} %bitcast.32, ...), custom_call_target="tpu_custom_call" | custom-call | tf_op jit(solution)/shard_map/local/pallas_call | solution.py:372
  38.4 1.1 %collective-permute-done.14.refs_2_ = f32[96,128]{1,0:T(8,128)S(1)} collective-permute-done((f32[96,128]{1,0:T(8,128)S(1)}, f32[96,128]{1,0:T(8,128)S(1)}, u32[]{:S(2)}, u32[]{:S(2)}) %collective-permute-start.14) | collective-permute-done | bytes 49184 | tf_op jit(solution)/shard_map/ppermute | solution.py:309
  39.5 0.9 %copy-done.5 = f32[2,96,128]{2,1,0:T(8,128)S(1)} copy-done((f32[2,96,128]{2,1,0:T(8,128)S(1)}, f32[2,96,128]{2,1,0:T(8,128)}, u32[]{:S(2)}) %copy-start.5) | copy-done | bytes 98328
  40.4 0.8 %copy-done.8 = bf16[192,128]{1,0:T(8,128)(2,1)S(1)} copy-done((bf16[192,128]{1,0:T(8,128)(2,1)S(1)}, bf16[192,128]{1,0:T(8,128)(2,1)}, u32[]{:S(2)}) %copy-start.8) | copy-done | bytes 49176
  41.2 0.9 %finish.1 = bf16[384,128]{1,0:T(8,128)(2,1)} custom-call(s32[8,128]{1,0:T(8,128)S(1)} %copy-done.3, bf16[384,128]{1,0:T(8,128)(2,1)} %get-tuple-element.29.base_ref, bf16[192,128]{1,0:T(8,128)(2,1)S(1)} %copy-done.8, f32[2,96,128]{2,1,0:T(8,128)S(1)} %copy-done.5, f32[96,128]{1,0:T(8,128)S(1)} %collective-permute-done.12.refs_0_, ...), custom_call_target="tpu_custom_call", output_to_operand_aliasing={{}: (1, {})} | custom-call | tf_op jit(solution)/shard_map/finish/pallas_call | solution.py:387
  (31 shorter events, 2.4 us)
Async XLA Ops:
  2.1 10.4 %collective-permute-start.5 = (f32[96,128]{1,0:T(8,128)}, f32[96,128]{1,0:T(8,128)S(1)}, u32[]{:S(2)}, u32[]{:S(2)}) collective-permute-start(f32[96,128]{1,0:T(8,128)} %get-tuple-element.21.refs_4_), channel_id=1, source_target_pairs={{0,12},{1,13},{2,14},{3,15},{4,8},{5,9},{6,10},{7,11},{8,4},{9,5},... | collective-permute-start | bytes 147464 | tf_op jit(solution)/shard_map/ppermute | solution.py:309
  7.2 5.3 %collective-permute-start.4 = (f32[96,128]{1,0:T(8,128)}, f32[96,128]{1,0:T(8,128)S(1)}, u32[]{:S(2)}, u32[]{:S(2)}) collective-permute-start(f32[96,128]{1,0:T(8,128)} %get-tuple-element.21.refs_4_), channel_id=1, source_target_pairs={{0,8},{1,9},{2,10},{3,11},{4,12},{5,13},{6,14},{7,15},{8,0},{9,1},... | collective-permute-start | bytes 147464 | tf_op jit(solution)/shard_map/ppermute | solution.py:309
  7.3 5.3 %collective-permute-start.3 = (f32[96,128]{1,0:T(8,128)}, f32[96,128]{1,0:T(8,128)S(1)}, u32[]{:S(2)}, u32[]{:S(2)}) collective-permute-start(f32[96,128]{1,0:T(8,128)} %get-tuple-element.21.refs_4_), channel_id=1, source_target_pairs={{0,4},{1,5},{2,6},{3,7},{4,0},{5,1},{6,2},{7,3},{8,12},{9,13},{10,... | collective-permute-start | bytes 147464 | tf_op jit(solution)/shard_map/ppermute | solution.py:309
  7.9 3.2 %collective-permute-start.2 = (s32[8,128]{1,0:T(8,128)}, s32[8,128]{1,0:T(8,128)S(1)}, u32[]{:S(2)}, u32[]{:S(2)}) collective-permute-start(s32[8,128]{1,0:T(8,128)} %get-tuple-element.20.refs_0_.facts_ref), channel_id=1, source_target_pairs={{0,3},{1,2},{2,1},{3,0},{4,7},{5,6},{6,5},{7,4},{8,11},{9,10},{10,... | collective-permute-start | bytes 12296 | tf_op jit(solution)/shard_map/ppermute | solution.py:304
  8.3 3.8 %collective-permute-start.1 = (s32[8,128]{1,0:T(8,128)}, s32[8,128]{1,0:T(8,128)S(1)}, u32[]{:S(2)}, u32[]{:S(2)}) collective-permute-start(s32[8,128]{1,0:T(8,128)} %get-tuple-element.20.refs_0_.facts_ref), channel_id=1, source_target_pairs={{0,2},{1,3},{2,0},{3,1},{4,6},{5,7},{6,4},{7,5},{8,10},{9,11},{10,... | collective-permute-start | bytes 12296 | tf_op jit(solution)/shard_map/ppermute | solution.py:304
  11.1 1.4 %collective-permute-start = (s32[8,128]{1,0:T(8,128)}, s32[8,128]{1,0:T(8,128)S(1)}, u32[]{:S(2)}, u32[]{:S(2)}) collective-permute-start(s32[8,128]{1,0:T(8,128)} %get-tuple-element.20.refs_0_.facts_ref), channel_id=1, source_target_pairs={{0,1},{1,0},{2,3},{3,2},{4,5},{5,4},{6,7},{7,6},{8,9},{9,8},{10,11... | collective-permute-start | bytes 12296 | tf_op jit(solution)/shard_map/ppermute | solution.py:304
  12.5 0.7 %copy-start.1 = (s32[8,128]{1,0:T(8,128)S(1)}, s32[8,128]{1,0:T(8,128)}, u32[]{:S(2)}) copy-start(s32[8,128]{1,0:T(8,128)} %get-tuple-element.20.refs_0_.facts_ref) | copy-start | bytes 12292
  13.2 0.8 %copy-start.7 = (f32[96,128]{1,0:T(8,128)S(1)}, f32[96,128]{1,0:T(8,128)}, u32[]{:S(2)}) copy-start(f32[96,128]{1,0:T(8,128)} %get-tuple-element.21.refs_4_) | copy-start | bytes 147460
  14.0 5.9 %copy-start.2 = (s32[8,128]{1,0:T(8,128)S(1)}, s32[8,128]{1,0:T(8,128)}, u32[]{:S(2)}) copy-start(s32[8,128]{1,0:T(8,128)} %get-tuple-element.20.refs_0_.facts_ref) | copy-start | bytes 12292
  14.0 5.9 %collective-permute-start.6 = (f32[96,128]{1,0:T(8,128)S(1)}, f32[96,128]{1,0:T(8,128)S(1)}, u32[]{:S(2)}, u32[]{:S(2)}) collective-permute-start(f32[96,128]{1,0:T(8,128)S(1)} %get-tuple-element.23), channel_id=1, source_target_pairs={{0,1},{1,0},{2,3},{3,2},{4,5},{5,4},{6,7},{7,6},{8,9},{9,8},{10,11... | collective-permute-start | bytes 147464 | tf_op jit(solution)/shard_map/ppermute | solution.py:304
  14.4 5.5 %collective-permute-start.7 = (f32[96,128]{1,0:T(8,128)S(1)}, f32[96,128]{1,0:T(8,128)S(1)}, u32[]{:S(2)}, u32[]{:S(2)}) collective-permute-start(f32[96,128]{1,0:T(8,128)S(1)} %get-tuple-element.24), channel_id=1, source_target_pairs={{0,2},{1,3},{2,0},{3,1},{4,6},{5,7},{6,4},{7,5},{8,10},{9,11},{10,... | collective-permute-start | bytes 147464 | tf_op jit(solution)/shard_map/ppermute | solution.py:304
  15.9 4.0 %collective-permute-start.8 = (f32[96,128]{1,0:T(8,128)S(1)}, f32[96,128]{1,0:T(8,128)S(1)}, u32[]{:S(2)}, u32[]{:S(2)}) collective-permute-start(f32[96,128]{1,0:T(8,128)S(1)} %get-tuple-element.25), channel_id=1, source_target_pairs={{0,3},{1,2},{2,1},{3,0},{4,7},{5,6},{6,5},{7,4},{8,11},{9,10},{10,... | collective-permute-start | bytes 147464 | tf_op jit(solution)/shard_map/ppermute | solution.py:304
  19.9 19.6 %copy-start.3 = (s32[8,128]{1,0:T(8,128)S(1)}, s32[8,128]{1,0:T(8,128)}, u32[]{:S(2)}) copy-start(s32[8,128]{1,0:T(8,128)} %get-tuple-element.20.refs_0_.facts_ref) | copy-start | bytes 12292
  20.0 1.6 %copy-start = (bf16[32,256,128]{2,1,0:T(8,128)(2,1)S(1)}, bf16[32,256,128]{2,1,0:T(8,128)(2,1)}, u32[]{:S(2)}) copy-start(bf16[32,256,128]{2,1,0:T(8,128)(2,1)} %get-tuple-element.26.refs_4_) | copy-start | bytes 6291460
  21.6 0.9 %copy-start.4 = (f32[2,96,128]{2,1,0:T(8,128)S(1)}, f32[2,96,128]{2,1,0:T(8,128)}, u32[]{:S(2)}) copy-start(f32[2,96,128]{2,1,0:T(8,128)} %get-tuple-element.27.refs_5_) | copy-start | bytes 294916
  22.9 3.8 %collective-permute-start.11 = (f32[96,128]{1,0:T(8,128)S(1)}, f32[96,128]{1,0:T(8,128)S(1)}, u32[]{:S(2)}, u32[]{:S(2)}) collective-permute-start(f32[96,128]{1,0:T(8,128)S(1)} %answer.1.refs_4_), channel_id=1, source_target_pairs={{0,3},{1,2},{2,1},{3,0},{4,7},{5,6},{6,5},{7,4},{8,11},{9,10},{10,... | collective-permute-start | bytes 147464 | tf_op jit(solution)/shard_map/ppermute | solution.py:304
  24.7 4.1 %collective-permute-start.10 = (f32[96,128]{1,0:T(8,128)S(1)}, f32[96,128]{1,0:T(8,128)S(1)}, u32[]{:S(2)}, u32[]{:S(2)}) collective-permute-start(f32[96,128]{1,0:T(8,128)S(1)} %answer.1.refs_4_), channel_id=1, source_target_pairs={{0,2},{1,3},{2,0},{3,1},{4,6},{5,7},{6,4},{7,5},{8,10},{9,11},{10,... | collective-permute-start | bytes 147464 | tf_op jit(solution)/shard_map/ppermute | solution.py:304
  25.2 3.6 %collective-permute-start.9 = (f32[96,128]{1,0:T(8,128)S(1)}, f32[96,128]{1,0:T(8,128)S(1)}, u32[]{:S(2)}, u32[]{:S(2)}) collective-permute-start(f32[96,128]{1,0:T(8,128)S(1)} %answer.1.refs_4_), channel_id=1, source_target_pairs={{0,1},{1,0},{2,3},{3,2},{4,5},{5,4},{6,7},{7,6},{8,9},{9,8},{10,11... | collective-permute-start | bytes 147464 | tf_op jit(solution)/shard_map/ppermute | solution.py:304
  28.8 0.6 %copy-start.6 = (f32[96,128]{1,0:T(8,128)}, f32[96,128]{1,0:T(8,128)S(1)}, u32[]{:S(2)}) copy-start(f32[96,128]{1,0:T(8,128)S(1)} %get-tuple-element.28.own_ref) | copy-start | bytes 147460
  29.4 9.0 %collective-permute-start.12 = (f32[96,128]{1,0:T(8,128)S(1)}, f32[96,128]{1,0:T(8,128)S(1)}, u32[]{:S(2)}, u32[]{:S(2)}) collective-permute-start(f32[96,128]{1,0:T(8,128)S(1)} %get-tuple-element.32), channel_id=1, source_target_pairs={{0,4},{1,5},{2,6},{3,7},{4,0},{5,1},{6,2},{7,3},{8,12},{9,13},{10,... | collective-permute-start | bytes 147464 | tf_op jit(solution)/shard_map/ppermute | solution.py:309
  30.7 7.8 %collective-permute-start.13 = (f32[96,128]{1,0:T(8,128)S(1)}, f32[96,128]{1,0:T(8,128)S(1)}, u32[]{:S(2)}, u32[]{:S(2)}) collective-permute-start(f32[96,128]{1,0:T(8,128)S(1)} %get-tuple-element.33), channel_id=1, source_target_pairs={{0,8},{1,9},{2,10},{3,11},{4,12},{5,13},{6,14},{7,15},{8,0},{9,1},... | collective-permute-start | bytes 147464 | tf_op jit(solution)/shard_map/ppermute | solution.py:309
  33.6 5.9 %collective-permute-start.14 = (f32[96,128]{1,0:T(8,128)S(1)}, f32[96,128]{1,0:T(8,128)S(1)}, u32[]{:S(2)}, u32[]{:S(2)}) collective-permute-start(f32[96,128]{1,0:T(8,128)S(1)} %get-tuple-element.34), channel_id=1, source_target_pairs={{0,12},{1,13},{2,14},{3,15},{4,8},{5,9},{6,10},{7,11},{8,4},{9,5},... | collective-permute-start | bytes 147464 | tf_op jit(solution)/shard_map/ppermute | solution.py:309
  39.5 0.9 %copy-start.5 = (f32[2,96,128]{2,1,0:T(8,128)S(1)}, f32[2,96,128]{2,1,0:T(8,128)}, u32[]{:S(2)}) copy-start(f32[2,96,128]{2,1,0:T(8,128)} %get-tuple-element.31.late_ref) | copy-start | bytes 294916
  40.4 0.8 %copy-start.8 = (bf16[192,128]{1,0:T(8,128)(2,1)S(1)}, bf16[192,128]{1,0:T(8,128)(2,1)}, u32[]{:S(2)}) copy-start(bf16[192,128]{1,0:T(8,128)(2,1)} %get-tuple-element.30.last_ref) | copy-start | bytes 147460

commit v4 on v3

--- a/solution.py
+++ b/solution.py
@@ -12,7 +12,6 @@
 F32 = jnp.float32
 BF16 = jnp.bfloat16
 MIB = 2**20
-LARGE = 61
 VMEM = pl.BlockSpec(memory_space=pltpu.VMEM)
 SMEM = pl.BlockSpec(memory_space=pltpu.SMEM)
 HBM = pl.BlockSpec(memory_space=pltpu.HBM)
@@ -110,10 +109,16 @@
 
 
 def prepare_kernel(slots_ref, keys_ref, values_ref, states_ref, weight_ref, early_ref,
-                   state, wide, sems, *, count, chunks):
+                   state, rows_ref, wide, sems, row_sems, *, count, chunks):
     heads = states_ref.shape[1]
     size = heads // chunks
     place, _ = moving_slot(slots_ref, count)
+    copies = [
+        pltpu.make_async_copy(
+            ref.at[pl.ds(0, wide.shape[0])], rows_ref.at[n], row_sems.at[n])
+        for n, ref in enumerate((keys_ref, values_ref))]
+    for copy in copies:
+        copy.start()
 
     def load(c):
         part = pl.ds(c * size, size)
@@ -121,9 +126,9 @@
 
     for c in range(chunks):
         load(c).start()
-    rows = wide.shape[0]
-    for n, ref in enumerate((keys_ref, values_ref)):
-        wide[...] = ref[:rows, :].astype(F32)
+    for n, copy in enumerate(copies):
+        copy.wait()
+        wide[...] = rows_ref[n].astype(F32)
         early_ref[n] = silu(extract(wide, place, count))
     for c in range(chunks):
         load(c).wait()
@@ -280,6 +285,10 @@
     copy.wait()
 
 
+def in_hbm(x):
+    return pltpu.with_memory_space_constraint(x, pltpu.HBM)
+
+
 def near_square(total):
     return next(
         (d, total // d) for d in range(1, total + 1) if total % d == 0 and d * d >= total)
@@ -325,8 +334,8 @@
         out_shape=(single, jax.ShapeDtypeStruct((8, width), jnp.int32)),
         in_specs=[SMEM, HBM], out_specs=(VMEM, VMEM),
         scratch_shapes=[late_bf16, late_packed, pltpu.SemaphoreType.DMA],
-        compiler_params=params(LARGE), name="ask",
-    )(new_slot, queries)
+        compiler_params=params(4), name="ask",
+    )(in_hbm(new_slot), in_hbm(queries))
 
     column = [ask] + [send_outer(ask, k) for k in range(1, outer)]
     wishes = [facts] + [send_inner(facts, k) for k in range(1, inner)]
@@ -336,12 +345,14 @@
         functools.partial(prepare_kernel, count=count, chunks=chunks),
         out_shape=(jax.ShapeDtypeStruct((heads, 2 * width, width), BF16),
                    jax.ShapeDtypeStruct((2, BEFORE * heads, width), F32)),
-        in_specs=[SMEM, VMEM, VMEM, HBM], out_specs=(VMEM, VMEM),
+        in_specs=[SMEM, HBM, HBM, HBM], out_specs=(VMEM, VMEM),
         scratch_shapes=[pltpu.VMEM((heads, width, width), F32),
+                        pltpu.VMEM((2, BEFORE * heads * count, width), BF16),
                         pltpu.VMEM((BEFORE * heads * count, width), F32),
-                        pltpu.SemaphoreType.DMA((chunks,))],
-        compiler_params=params(LARGE), name="prepare",
-    )(new_slot, keys, values, states)
+                        pltpu.SemaphoreType.DMA((chunks,)),
+                        pltpu.SemaphoreType.DMA((2,))],
+        compiler_params=params(12), name="prepare",
+    )(in_hbm(new_slot), in_hbm(keys), in_hbm(values), in_hbm(states))
 
     asked = pl.pallas_call(
         functools.partial(route_kernel, inner=inner, outer=outer),
@@ -371,7 +382,7 @@
     output = jax.ShapeDtypeStruct((packed_rows, width), BF16)
     base, last, partial = pl.pallas_call(
         functools.partial(local_kernel, count=count, chunks=chunks),
-        out_shape=(output, late_rows, jax.ShapeDtypeStruct((2, single_rows, width), F32)),
+        out_shape=(pltpu.HBM(output.shape, output.dtype), late_rows, jax.ShapeDtypeStruct((2, single_rows, width), F32)),
         in_specs=[VMEM] * 7 + [HBM], out_specs=(VMEM, VMEM, VMEM),
         scratch_shapes=[
             pltpu.VMEM((count, heads, width, width), F32),
@@ -380,9 +391,9 @@
             late_packed,
             pltpu.SemaphoreType.DMA((count, chunks)),
         ],
-        compiler_params=params(LARGE), name="local",
+        compiler_params=params(16), name="local",
     )(facts, queries, keys, values, gates, norm_gain.reshape(heads, width),
-      sorted_replies[0], states)
+      sorted_replies[0], in_hbm(states))
 
     return unpack(pl.pallas_call(
         functools.partial(finish_kernel, count=count, heads=heads),
@@ -390,7 +401,7 @@
         scratch_shapes=[late_bf16, late_packed, pltpu.SemaphoreType.DMA],
         input_output_aliases={1: 0},
         compiler_params=params(4), name="finish",
-    )(facts, base, last, partial, *parts))
+    )(facts, in_hbm(base), last, partial, *parts))
 
 
 def solution(mesh):

time: 42.6 us -> 34.3 us (0.81)
  local copies, waits for them, and re-layouts: 6.25 us -> 0.02 us
  Pallas kernels: 12.1 us -> 8.95 us
  waiting for transfers between devices: 7.22 us -> 8.85 us
    unnamed x18 -> x10, local copies, waits for them, and re-layouts: 6.25 us -> 0.02 us
    pallas_call x1, Pallas kernels: 3.91 us -> 2.41 us  [on_device(): pl.pallas_call(functools.partial(prepare_kernel, count=count, chunks=chun...]
    ppermute x6, waiting for transfers between devices: 1.06 us -> 2.27 us  [send_outer(): lax.ppermute(x, 'req', [(o * inner + i, int(turn(o, k, outer)) * inner +...]
    pallas_call x1, Pallas kernels: 4.59 us -> 3.49 us  [on_device(): pl.pallas_call(functools.partial(local_kernel, count=count, chunks=chunks...]
    pallas_call x1, Pallas kernels: 2.13 us -> 1.64 us  [on_device(): pl.pallas_call(functools.partial(ask_kernel, count=count, inner=inner), o...]
  transfers between devices with their start and end apart: 15 -> 15, of which waited for: 6 -> 8; matrix products, arithmetic and copies ran while one was open for 0% -> 0% of each run, Pallas kernels for 20% -> 17%
where the time goes in v4:
time: 34.3 us; the launch traced here: 34.1 us
  starting transfers between devices  16.1 us (47%)
  Pallas kernels  8.95 us (26%)
  waiting for transfers between devices  8.85 us (26%)
    ppermute x6, starting transfers between devices, send_outer(): lax.ppermute(x, 'req', [(o * inner + i, int(turn(o, k, outer)) * inner +...  10.2 us
    ppermute x9, waiting for transfers between devices, send_inner(): lax.ppermute(x, 'req', [(o * inner + i, o * inner + int(turn(i, k, inner)...  6.57 us
    ppermute x9, starting transfers between devices, send_inner(): lax.ppermute(x, 'req', [(o * inner + i, o * inner + int(turn(i, k, inner)...  5.91 us
    pallas_call x1, Pallas kernels, on_device(): pl.pallas_call(functools.partial(local_kernel, count=count, chunks=chunks...  3.49 us
    pallas_call x1, Pallas kernels, on_device(): pl.pallas_call(functools.partial(prepare_kernel, count=count, chunks=chun...  2.41 us
    ppermute x6, waiting for transfers between devices, send_outer(): lax.ppermute(x, 'req', [(o * inner + i, int(turn(o, k, outer)) * inner +...  2.27 us
    pallas_call x1, Pallas kernels, on_device(): pl.pallas_call(functools.partial(ask_kernel, count=count, inner=inner), o...  1.64 us
    pallas_call x1, Pallas kernels, on_device(): pl.pallas_call(functools.partial(finish_kernel, count=count, heads=heads)...  0.9 us
  transfers between devices with their start and end apart: 15, of which 8 were waited for; matrix products, arithmetic and copies ran while one was open for 0% of the time, Pallas kernels for 17%

profile of v4, /device:TPU:0, one launch (start us, length us, event | category | flops | bytes accessed | tf_op | source)
XLA Modules:
  0.0 34.1 jit_solution(8022709685529419961)
XLA Ops:
  0.0 1.6 %ask.1 = (f32[96,128]{1,0:T(8,128)S(1)}, s32[8,128]{1,0:T(8,128)S(1)}) custom-call(s32[2]{0:T(128)} %slots_ref.3, bf16[384,128]{1,0:T(8,128)(2,1)} %bitcast.26), custom_call_target="tpu_custom_call" | custom-call | tf_op jit(solution)/shard_map/ask/pallas_call | solution.py:332
  1.7 5.1 %collective-permute-start.5 = (f32[96,128]{1,0:T(8,128)S(1)}, f32[96,128]{1,0:T(8,128)S(1)}, u32[]{:S(2)}, u32[]{:S(2)}) collective-permute-start(f32[96,128]{1,0:T(8,128)S(1)} %get-tuple-element.21.refs_4_), channel_id=1, source_target_pairs={{0,12},{1,13},{2,14},{3,15},{4,8},{5,9},{6,10},{7,11},{8,4},{9,5},... | collective-permute-start | bytes 147464 | tf_op jit(solution)/shard_map/ppermute | solution.py:318
  6.8 0.6 %collective-permute-start.3 = (f32[96,128]{1,0:T(8,128)S(1)}, f32[96,128]{1,0:T(8,128)S(1)}, u32[]{:S(2)}, u32[]{:S(2)}) collective-permute-start(f32[96,128]{1,0:T(8,128)S(1)} %get-tuple-element.21.refs_4_), channel_id=1, source_target_pairs={{0,4},{1,5},{2,6},{3,7},{4,0},{5,1},{6,2},{7,3},{8,12},{9,13},{10,... | collective-permute-start | bytes 147464 | tf_op jit(solution)/shard_map/ppermute | solution.py:318
  7.4 0.4 %collective-permute-start.2 = (s32[8,128]{1,0:T(8,128)S(1)}, s32[8,128]{1,0:T(8,128)S(1)}, u32[]{:S(2)}, u32[]{:S(2)}) collective-permute-start(s32[8,128]{1,0:T(8,128)S(1)} %get-tuple-element.20.refs_0_.facts_ref), channel_id=1, source_target_pairs={{0,3},{1,2},{2,1},{3,0},{4,7},{5,6},{6,5},{7,4},{8,11},{9,10},{10,... | collective-permute-start | bytes 12296 | tf_op jit(solution)/shard_map/ppermute | solution.py:313
  7.8 1.3 %collective-permute-start.1 = (s32[8,128]{1,0:T(8,128)S(1)}, s32[8,128]{1,0:T(8,128)S(1)}, u32[]{:S(2)}, u32[]{:S(2)}) collective-permute-start(s32[8,128]{1,0:T(8,128)S(1)} %get-tuple-element.20.refs_0_.facts_ref), channel_id=1, source_target_pairs={{0,2},{1,3},{2,0},{3,1},{4,6},{5,7},{6,4},{7,5},{8,10},{9,11},{10,... | collective-permute-start | bytes 12296 | tf_op jit(solution)/shard_map/ppermute | solution.py:313
  9.1 1.3 %collective-permute-done.2.refs_3_ = s32[8,128]{1,0:T(8,128)S(1)} collective-permute-done((s32[8,128]{1,0:T(8,128)S(1)}, s32[8,128]{1,0:T(8,128)S(1)}, u32[]{:S(2)}, u32[]{:S(2)}) %collective-permute-start.2) | collective-permute-done | bytes 4128 | tf_op jit(solution)/shard_map/ppermute | solution.py:313
  10.5 0.3 collective-permute-start
  10.8 0.6 %collective-permute-done.1.refs_2_ = s32[8,128]{1,0:T(8,128)S(1)} collective-permute-done((s32[8,128]{1,0:T(8,128)S(1)}, s32[8,128]{1,0:T(8,128)S(1)}, u32[]{:S(2)}, u32[]{:S(2)}) %collective-permute-start.1) | collective-permute-done | bytes 4128 | tf_op jit(solution)/shard_map/ppermute | solution.py:313
  11.4 0.2 collective-permute-done.refs_1_
  11.8 0.3 collective-permute-start.6
  12.1 1.5 %collective-permute-start.7 = (f32[96,128]{1,0:T(8,128)S(1)}, f32[96,128]{1,0:T(8,128)S(1)}, u32[]{:S(2)}, u32[]{:S(2)}) collective-permute-start(f32[96,128]{1,0:T(8,128)S(1)} %get-tuple-element.24), channel_id=1, source_target_pairs={{0,2},{1,3},{2,0},{3,1},{4,6},{5,7},{6,4},{7,5},{8,10},{9,11},{10,... | collective-permute-start | bytes 147464 | tf_op jit(solution)/shard_map/ppermute | solution.py:313
  13.8 2.4 %prepare.1 = (bf16[32,256,128]{2,1,0:T(8,128)(2,1)S(1)}, f32[2,96,128]{2,1,0:T(8,128)S(1)}) custom-call(s32[2]{0:T(128)} %slots_ref.3, bf16[384,128]{1,0:T(8,128)(2,1)} %bitcast.28, bf16[384,128]{1,0:T(8,128)(2,1)} %bitcast.30, f32[2,32,128,128]{3,2,1,0:T(8,128)} %states_ref.3), custom_call_target="tpu_custom_call" | custom-call | tf_op jit(solution)/shard_map/prepare/pallas_call | solution.py:344
  16.2 1.2 %collective-permute-done.8.refs_3_ = f32[96,128]{1,0:T(8,128)S(1)} collective-permute-done((f32[96,128]{1,0:T(8,128)S(1)}, f32[96,128]{1,0:T(8,128)S(1)}, u32[]{:S(2)}, u32[]{:S(2)}) %collective-permute-start.8) | collective-permute-done | bytes 49184 | tf_op jit(solution)/shard_map/ppermute | solution.py:313
  17.4 0.4 %answer.1.refs_4_ = f32[96,128]{1,0:T(8,128)S(1)} custom-call(s32[8,128]{1,0:T(8,128)S(1)} %get-tuple-element.20.refs_0_.facts_ref, f32[96,128]{1,0:T(8,128)S(1)} %get-tuple-element.22.refs_0_, f32[96,128]{1,0:T(8,128)S(1)} %collective-permute-done.6.refs_1_, f32[96,128]{1,0:T(8,128)S(1)} %collective-permute-done.7.refs_2_, ...), custom_call_target="tpu_custom_call" | custom-call | tf_op jit(solution)/shard_map/answer/pallas_call | solution.py:365
  17.8 0.8 %collective-permute-start.11 = (f32[96,128]{1,0:T(8,128)S(1)}, f32[96,128]{1,0:T(8,128)S(1)}, u32[]{:S(2)}, u32[]{:S(2)}) collective-permute-start(f32[96,128]{1,0:T(8,128)S(1)} %answer.1.refs_4_), channel_id=1, source_target_pairs={{0,3},{1,2},{2,1},{3,0},{4,7},{5,6},{6,5},{7,4},{8,11},{9,10},{10,... | collective-permute-start | bytes 147464 | tf_op jit(solution)/shard_map/ppermute | solution.py:313
  18.6 1.0 %collective-permute-start.10 = (f32[96,128]{1,0:T(8,128)S(1)}, f32[96,128]{1,0:T(8,128)S(1)}, u32[]{:S(2)}, u32[]{:S(2)}) collective-permute-start(f32[96,128]{1,0:T(8,128)S(1)} %answer.1.refs_4_), channel_id=1, source_target_pairs={{0,2},{1,3},{2,0},{3,1},{4,6},{5,7},{6,4},{7,5},{8,10},{9,11},{10,... | collective-permute-start | bytes 147464 | tf_op jit(solution)/shard_map/ppermute | solution.py:313
  19.8 1.8 %collective-permute-done.11.refs_7_ = f32[96,128]{1,0:T(8,128)S(1)} collective-permute-done((f32[96,128]{1,0:T(8,128)S(1)}, f32[96,128]{1,0:T(8,128)S(1)}, u32[]{:S(2)}, u32[]{:S(2)}) %collective-permute-start.11) | collective-permute-done | bytes 49184 | tf_op jit(solution)/shard_map/ppermute | solution.py:313
  21.6 1.3 %collective-permute-done.10.refs_6_ = f32[96,128]{1,0:T(8,128)S(1)} collective-permute-done((f32[96,128]{1,0:T(8,128)S(1)}, f32[96,128]{1,0:T(8,128)S(1)}, u32[]{:S(2)}, u32[]{:S(2)}) %collective-permute-start.10) | collective-permute-done | bytes 49184 | tf_op jit(solution)/shard_map/ppermute | solution.py:313
  23.0 1.3 %collective-permute-start.12 = (f32[96,128]{1,0:T(8,128)S(1)}, f32[96,128]{1,0:T(8,128)S(1)}, u32[]{:S(2)}, u32[]{:S(2)}) collective-permute-start(f32[96,128]{1,0:T(8,128)S(1)} %get-tuple-element.32), channel_id=1, source_target_pairs={{0,4},{1,5},{2,6},{3,7},{4,0},{5,1},{6,2},{7,3},{8,12},{9,13},{10,... | collective-permute-start | bytes 147464 | tf_op jit(solution)/shard_map/ppermute | solution.py:318
  24.4 2.9 %collective-permute-start.13 = (f32[96,128]{1,0:T(8,128)S(1)}, f32[96,128]{1,0:T(8,128)S(1)}, u32[]{:S(2)}, u32[]{:S(2)}) collective-permute-start(f32[96,128]{1,0:T(8,128)S(1)} %get-tuple-element.33), channel_id=1, source_target_pairs={{0,8},{1,9},{2,10},{3,11},{4,12},{5,13},{6,14},{7,15},{8,0},{9,1},... | collective-permute-start | bytes 147464 | tf_op jit(solution)/shard_map/ppermute | solution.py:318
  27.3 0.2 collective-permute-start.14
  27.5 3.5 %local.1 = (bf16[384,128]{1,0:T(8,128)(2,1)}, bf16[192,128]{1,0:T(8,128)(2,1)S(1)}, f32[2,96,128]{2,1,0:T(8,128)S(1)}) custom-call(s32[8,128]{1,0:T(8,128)S(1)} %get-tuple-element.20.refs_0_.facts_ref, bf16[384,128]{1,0:T(8,128)(2,1)S(1)} %bitcast.27, bf16[384,128]{1,0:T(8,128)(2,1)S(1)} %bitcast.29, bf16[384,128]{1,0:T(8,128)(2,1)S(1)} %bitcast.31, ...), custom_call_target="tpu_custom_call" | custom-call | tf_op jit(solution)/shard_map/local/pallas_call | solution.py:383
  31.0 2.1 %collective-permute-done.14.refs_2_ = f32[96,128]{1,0:T(8,128)S(1)} collective-permute-done((f32[96,128]{1,0:T(8,128)S(1)}, f32[96,128]{1,0:T(8,128)S(1)}, u32[]{:S(2)}, u32[]{:S(2)}) %collective-permute-start.14) | collective-permute-done | bytes 49184 | tf_op jit(solution)/shard_map/ppermute | solution.py:318
  33.2 0.9 %finish.1 = bf16[384,128]{1,0:T(8,128)(2,1)} custom-call(s32[8,128]{1,0:T(8,128)S(1)} %get-tuple-element.20.refs_0_.facts_ref, bf16[384,128]{1,0:T(8,128)(2,1)} %get-tuple-element.29.base_ref, bf16[192,128]{1,0:T(8,128)(2,1)S(1)} %get-tuple-element.30.last_ref, f32[2,96,128]{2,1,0:T(8,128)S(1)} %get-tuple-element.31.late_ref, ...), custom_call_target="tpu_custom_call", output_to_operand_aliasing={{}: (1, {})} | custom-call | tf_op jit(solution)/shard_map/finish/pallas_call | solution.py:398
  (23 shorter events, 0.6 us)
Async XLA Ops:
  0.0 27.5 %copy-start = (bf16[2,6,4096]{2,0,1:T(2,128)(2,1)S(1)}, bf16[2,6,4096]{2,0,1:T(2,128)(2,1)}, u32[]{:S(2)}) copy-start(bf16[2,6,4096]{2,0,1:T(2,128)(2,1)} %param.7) | copy-start | bytes 294916
  0.0 27.5 %copy-start.2 = (bf16[2,6,4096]{2,0,1:T(2,128)(2,1)S(1)}, bf16[2,6,4096]{2,0,1:T(2,128)(2,1)}, u32[]{:S(2)}) copy-start(bf16[2,6,4096]{2,0,1:T(2,128)(2,1)} %param.9) | copy-start | bytes 294916
  0.0 27.5 %copy-start.1 = (bf16[2,6,4096]{2,0,1:T(2,128)(2,1)S(1)}, bf16[2,6,4096]{2,0,1:T(2,128)(2,1)}, u32[]{:S(2)}) copy-start(bf16[2,6,4096]{2,0,1:T(2,128)(2,1)} %param.8) | copy-start | bytes 294916
  0.0 27.5 %copy-start.4 = (f32[4096]{0:T(1024)S(1)}, f32[4096]{0:T(1024)}, u32[]{:S(2)}) copy-start(f32[4096]{0:T(1024)} %param.13) | copy-start | bytes 49156
  0.0 27.5 %copy-start.3 = (bf16[2,6,4096]{2,0,1:T(2,128)(2,1)S(1)}, bf16[2,6,4096]{2,0,1:T(2,128)(2,1)}, u32[]{:S(2)}) copy-start(bf16[2,6,4096]{2,0,1:T(2,128)(2,1)} %param.10) | copy-start | bytes 294916
  1.7 10.0 %collective-permute-start.5 = (f32[96,128]{1,0:T(8,128)S(1)}, f32[96,128]{1,0:T(8,128)S(1)}, u32[]{:S(2)}, u32[]{:S(2)}) collective-permute-start(f32[96,128]{1,0:T(8,128)S(1)} %get-tuple-element.21.refs_4_), channel_id=1, source_target_pairs={{0,12},{1,13},{2,14},{3,15},{4,8},{5,9},{6,10},{7,11},{8,4},{9,5},... | collective-permute-start | bytes 147464 | tf_op jit(solution)/shard_map/ppermute | solution.py:318
  6.8 5.0 %collective-permute-start.4 = (f32[96,128]{1,0:T(8,128)S(1)}, f32[96,128]{1,0:T(8,128)S(1)}, u32[]{:S(2)}, u32[]{:S(2)}) collective-permute-start(f32[96,128]{1,0:T(8,128)S(1)} %get-tuple-element.21.refs_4_), channel_id=1, source_target_pairs={{0,8},{1,9},{2,10},{3,11},{4,12},{5,13},{6,14},{7,15},{8,0},{9,1},... | collective-permute-start | bytes 147464 | tf_op jit(solution)/shard_map/ppermute | solution.py:318
  6.8 5.0 %collective-permute-start.3 = (f32[96,128]{1,0:T(8,128)S(1)}, f32[96,128]{1,0:T(8,128)S(1)}, u32[]{:S(2)}, u32[]{:S(2)}) collective-permute-start(f32[96,128]{1,0:T(8,128)S(1)} %get-tuple-element.21.refs_4_), channel_id=1, source_target_pairs={{0,4},{1,5},{2,6},{3,7},{4,0},{5,1},{6,2},{7,3},{8,12},{9,13},{10,... | collective-permute-start | bytes 147464 | tf_op jit(solution)/shard_map/ppermute | solution.py:318
  7.4 3.0 %collective-permute-start.2 = (s32[8,128]{1,0:T(8,128)S(1)}, s32[8,128]{1,0:T(8,128)S(1)}, u32[]{:S(2)}, u32[]{:S(2)}) collective-permute-start(s32[8,128]{1,0:T(8,128)S(1)} %get-tuple-element.20.refs_0_.facts_ref), channel_id=1, source_target_pairs={{0,3},{1,2},{2,1},{3,0},{4,7},{5,6},{6,5},{7,4},{8,11},{9,10},{10,... | collective-permute-start | bytes 12296 | tf_op jit(solution)/shard_map/ppermute | solution.py:313
  7.8 3.6 %collective-permute-start.1 = (s32[8,128]{1,0:T(8,128)S(1)}, s32[8,128]{1,0:T(8,128)S(1)}, u32[]{:S(2)}, u32[]{:S(2)}) collective-permute-start(s32[8,128]{1,0:T(8,128)S(1)} %get-tuple-element.20.refs_0_.facts_ref), channel_id=1, source_target_pairs={{0,2},{1,3},{2,0},{3,1},{4,6},{5,7},{6,4},{7,5},{8,10},{9,11},{10,... | collective-permute-start | bytes 12296 | tf_op jit(solution)/shard_map/ppermute | solution.py:313
  10.5 1.2 %collective-permute-start = (s32[8,128]{1,0:T(8,128)S(1)}, s32[8,128]{1,0:T(8,128)S(1)}, u32[]{:S(2)}, u32[]{:S(2)}) collective-permute-start(s32[8,128]{1,0:T(8,128)S(1)} %get-tuple-element.20.refs_0_.facts_ref), channel_id=1, source_target_pairs={{0,1},{1,0},{2,3},{3,2},{4,5},{5,4},{6,7},{7,6},{8,9},{9,8},{10,11... | collective-permute-start | bytes 12296 | tf_op jit(solution)/shard_map/ppermute | solution.py:313
  11.8 4.3 %collective-permute-start.6 = (f32[96,128]{1,0:T(8,128)S(1)}, f32[96,128]{1,0:T(8,128)S(1)}, u32[]{:S(2)}, u32[]{:S(2)}) collective-permute-start(f32[96,128]{1,0:T(8,128)S(1)} %get-tuple-element.23), channel_id=1, source_target_pairs={{0,1},{1,0},{2,3},{3,2},{4,5},{5,4},{6,7},{7,6},{8,9},{9,8},{10,11... | collective-permute-start | bytes 147464 | tf_op jit(solution)/shard_map/ppermute | solution.py:313
  12.1 4.1 %collective-permute-start.7 = (f32[96,128]{1,0:T(8,128)S(1)}, f32[96,128]{1,0:T(8,128)S(1)}, u32[]{:S(2)}, u32[]{:S(2)}) collective-permute-start(f32[96,128]{1,0:T(8,128)S(1)} %get-tuple-element.24), channel_id=1, source_target_pairs={{0,2},{1,3},{2,0},{3,1},{4,6},{5,7},{6,4},{7,5},{8,10},{9,11},{10,... | collective-permute-start | bytes 147464 | tf_op jit(solution)/shard_map/ppermute | solution.py:313
  13.6 3.8 %collective-permute-start.8 = (f32[96,128]{1,0:T(8,128)S(1)}, f32[96,128]{1,0:T(8,128)S(1)}, u32[]{:S(2)}, u32[]{:S(2)}) collective-permute-start(f32[96,128]{1,0:T(8,128)S(1)} %get-tuple-element.25), channel_id=1, source_target_pairs={{0,3},{1,2},{2,1},{3,0},{4,7},{5,6},{6,5},{7,4},{8,11},{9,10},{10,... | collective-permute-start | bytes 147464 | tf_op jit(solution)/shard_map/ppermute | solution.py:313
  17.8 3.8 %collective-permute-start.11 = (f32[96,128]{1,0:T(8,128)S(1)}, f32[96,128]{1,0:T(8,128)S(1)}, u32[]{:S(2)}, u32[]{:S(2)}) collective-permute-start(f32[96,128]{1,0:T(8,128)S(1)} %answer.1.refs_4_), channel_id=1, source_target_pairs={{0,3},{1,2},{2,1},{3,0},{4,7},{5,6},{6,5},{7,4},{8,11},{9,10},{10,... | collective-permute-start | bytes 147464 | tf_op jit(solution)/shard_map/ppermute | solution.py:313
  18.6 4.4 %collective-permute-start.10 = (f32[96,128]{1,0:T(8,128)S(1)}, f32[96,128]{1,0:T(8,128)S(1)}, u32[]{:S(2)}, u32[]{:S(2)}) collective-permute-start(f32[96,128]{1,0:T(8,128)S(1)} %answer.1.refs_4_), channel_id=1, source_target_pairs={{0,2},{1,3},{2,0},{3,1},{4,6},{5,7},{6,4},{7,5},{8,10},{9,11},{10,... | collective-permute-start | bytes 147464 | tf_op jit(solution)/shard_map/ppermute | solution.py:313
  19.6 3.4 %collective-permute-start.9 = (f32[96,128]{1,0:T(8,128)S(1)}, f32[96,128]{1,0:T(8,128)S(1)}, u32[]{:S(2)}, u32[]{:S(2)}) collective-permute-start(f32[96,128]{1,0:T(8,128)S(1)} %answer.1.refs_4_), channel_id=1, source_target_pairs={{0,1},{1,0},{2,3},{3,2},{4,5},{5,4},{6,7},{7,6},{8,9},{9,8},{10,11... | collective-permute-start | bytes 147464 | tf_op jit(solution)/shard_map/ppermute | solution.py:313
  23.0 8.0 %collective-permute-start.12 = (f32[96,128]{1,0:T(8,128)S(1)}, f32[96,128]{1,0:T(8,128)S(1)}, u32[]{:S(2)}, u32[]{:S(2)}) collective-permute-start(f32[96,128]{1,0:T(8,128)S(1)} %get-tuple-element.32), channel_id=1, source_target_pairs={{0,4},{1,5},{2,6},{3,7},{4,0},{5,1},{6,2},{7,3},{8,12},{9,13},{10,... | collective-permute-start | bytes 147464 | tf_op jit(solution)/shard_map/ppermute | solution.py:318
  24.4 6.7 %collective-permute-start.13 = (f32[96,128]{1,0:T(8,128)S(1)}, f32[96,128]{1,0:T(8,128)S(1)}, u32[]{:S(2)}, u32[]{:S(2)}) collective-permute-start(f32[96,128]{1,0:T(8,128)S(1)} %get-tuple-element.33), channel_id=1, source_target_pairs={{0,8},{1,9},{2,10},{3,11},{4,12},{5,13},{6,14},{7,15},{8,0},{9,1},... | collective-permute-start | bytes 147464 | tf_op jit(solution)/shard_map/ppermute | solution.py:318
  27.3 5.9 %collective-permute-start.14 = (f32[96,128]{1,0:T(8,128)S(1)}, f32[96,128]{1,0:T(8,128)S(1)}, u32[]{:S(2)}, u32[]{:S(2)}) collective-permute-start(f32[96,128]{1,0:T(8,128)S(1)} %get-tuple-element.34), channel_id=1, source_target_pairs={{0,12},{1,13},{2,14},{3,15},{4,8},{5,9},{6,10},{7,11},{8,4},{9,5},... | collective-permute-start | bytes 147464 | tf_op jit(solution)/shard_map/ppermute | solution.py:318

commit v5 on v4

--- a/solution.py
+++ b/solution.py
@@ -45,11 +45,12 @@
     return result
 
 
-OUTER, INNER, SLOT = 0, 1, 2
-
-
-def fact(ref, kind, rows):
-    return jnp.broadcast_to(ref[kind:kind + 1, :], (rows, ref.shape[1]))
+OUTER, INNER, SLOT, FACTS = 0, 1, 2, 8
+
+
+def fact(ref, step, kind, rows):
+    row = step * FACTS + kind
+    return jnp.broadcast_to(ref[row:row + 1, :], (rows, ref.shape[1]))
 
 
 def head_slope(heads, width):
@@ -93,11 +94,15 @@
     return result
 
 
-def ask_kernel(slots_ref, queries_ref, out_ref, facts_ref, rows_ref, wide, sem, *, count, inner):
+def ask_kernel(new_slot_ref, queries_ref, out_ref, facts_ref, slots_ref, rows_ref, wide, sems, *,
+               count, inner):
     late = rows_ref.shape[0]
     first = queries_ref.shape[0] - late
-    copy = pltpu.make_async_copy(queries_ref.at[pl.ds(first, late)], rows_ref, sem)
+    slots_copy = pltpu.make_async_copy(new_slot_ref, slots_ref, sems.at[0])
+    slots_copy.start()
+    copy = pltpu.make_async_copy(queries_ref.at[pl.ds(first, late)], rows_ref, sems.at[1])
     copy.start()
+    slots_copy.wait()
     place, moves = moving_slot(slots_ref, count)
     wanted = wanted_device(slots_ref, count)
     kind = lax.broadcasted_iota(jnp.int32, facts_ref.shape, 0)
@@ -136,12 +141,11 @@
             weight_ref[h] = jnp.concatenate(split(state[h]), axis=0)
 
 
-def route_kernel(*refs, inner, outer):
-    wishes, column = refs[:inner], refs[inner:inner + outer]
-    outs = refs[inner + outer:]
+def route_kernel(wishes_ref, *refs, inner, outer):
+    column, outs = refs[:outer], refs[outer:]
     my_outer = lax.div(lax.axis_index("req"), inner)
     for k in range(inner):
-        wish = fact(wishes[inverse_step(k, inner)], OUTER, outs[k].shape[0])
+        wish = fact(wishes_ref, inverse_step(k, inner), OUTER, outs[k].shape[0])
         outs[k][...] = choose(column, wish, my_outer, outer)
 
 
@@ -149,7 +153,7 @@
     found, (weight_ref, early_ref, out_ref, lhs, prod) = refs[:inner], refs[inner:]
     my_inner = lax.rem(lax.axis_index("req"), inner)
     block = lambda ref, t: ref[t * heads:(t + 1) * heads, :]
-    rows = choose(found, fact(facts_ref, INNER, late * heads), my_inner, inner)
+    rows = choose(found, fact(facts_ref, 0, INNER, late * heads), my_inner, inner)
     q = [rows[t * heads:(t + 1) * heads, :] for t in range(late)]
     slope = head_slope(heads, width)
     for t in range(late):
@@ -170,15 +174,15 @@
         out_ref[t * heads:(t + 1) * heads, :] = total
 
 
-def reply_kernel(*refs, inner, outer):
-    wishes, replies = refs[:inner], refs[inner:2 * inner]
-    outs = refs[2 * inner:]
+def reply_kernel(wishes_ref, *refs, inner, outer):
+    replies, outs = refs[:inner], refs[inner:]
     me = lax.axis_index("req")
     my_inner, my_outer = lax.rem(me, inner), lax.div(me, inner)
     rows = outs[0].shape[0]
     owner = [
-        jnp.where(fact(wish, INNER, rows) == my_inner, fact(wish, OUTER, rows), -1)
-        for wish in wishes]
+        jnp.where(fact(wishes_ref, k, INNER, rows) == my_inner,
+                  fact(wishes_ref, k, OUTER, rows), -1)
+        for k in range(inner)]
     for k in range(outer):
         result = 0.0
         for n in range(inner):
@@ -193,7 +197,7 @@
     steps = queries_ref.shape[0] // span
     late = steps - BEFORE
     size = heads // chunks
-    place = fact(facts_ref, SLOT, late * heads)
+    place = fact(facts_ref, 0, SLOT, late * heads)
 
     def load(j, c):
         part = pl.ds(c * size, size)
@@ -267,7 +271,7 @@
 def finish_kernel(facts_ref, base_ref, last_ref, late_ref, *refs, count, heads):
     parts, (out_ref, rows_ref, wide, sem) = refs[:-4], refs[-4:]
     wide[...] = last_ref[...].astype(F32)
-    place = fact(facts_ref, SLOT, heads)
+    place = fact(facts_ref, 0, SLOT, heads)
     for t in range(late_ref.shape[1] // heads):
         part = slice(t * heads, (t + 1) * heads)
         x = late_ref[0, part, :]
@@ -319,6 +323,15 @@
             (o * inner + i, int(turn(o, k, outer)) * inner + i)
             for o in range(outer) for i in range(inner)])
 
+    def gather_inner(x):
+        if inner & (inner - 1):
+            return jnp.concatenate([x] + [send_inner(x, k) for k in range(1, inner)])
+        step = 1
+        while step < inner:
+            x = jnp.concatenate([x, send_inner(x, step)])
+            step *= 2
+        return x
+
     def params(limit):
         return pltpu.CompilerParams(vmem_limit_bytes=limit * MIB)
 
@@ -331,14 +344,15 @@
 
     ask, facts = pl.pallas_call(
         functools.partial(ask_kernel, count=count, inner=inner),
-        out_shape=(single, jax.ShapeDtypeStruct((8, width), jnp.int32)),
-        in_specs=[SMEM, HBM], out_specs=(VMEM, VMEM),
-        scratch_shapes=[late_bf16, late_packed, pltpu.SemaphoreType.DMA],
+        out_shape=(single, jax.ShapeDtypeStruct((FACTS, width), jnp.int32)),
+        in_specs=[HBM, HBM], out_specs=(VMEM, VMEM),
+        scratch_shapes=[pltpu.SMEM((count,), jnp.int32), late_bf16, late_packed,
+                        pltpu.SemaphoreType.DMA((2,))],
         compiler_params=params(4), name="ask",
     )(in_hbm(new_slot), in_hbm(queries))
 
     column = [ask] + [send_outer(ask, k) for k in range(1, outer)]
-    wishes = [facts] + [send_inner(facts, k) for k in range(1, inner)]
+    wishes = gather_inner(facts)
 
     chunks = 8
     weight, early = pl.pallas_call(
@@ -357,10 +371,10 @@
     asked = pl.pallas_call(
         functools.partial(route_kernel, inner=inner, outer=outer),
         out_shape=(single,) * inner,
-        in_specs=[VMEM] * (inner + outer), out_specs=(VMEM,) * inner,
+        in_specs=[VMEM] * (1 + outer), out_specs=(VMEM,) * inner,
         compiler_params=params(4), name="route",
-    )(*wishes, *column)
-    found = [asked[0]] + [send_inner(asked[k], k) for k in range(1, inner)]
+    )(wishes, *column)
+    found = [asked[0]] + [send_inner(asked[k], k) for k in range(inner - 1, 0, -1)][::-1]
 
     answer = pl.pallas_call(
         functools.partial(answer_kernel, inner=inner, late=late, heads=heads, width=width),
@@ -373,10 +387,10 @@
     sorted_replies = pl.pallas_call(
         functools.partial(reply_kernel, inner=inner, outer=outer),
         out_shape=(single,) * outer,
-        in_specs=[VMEM] * (2 * inner), out_specs=(VMEM,) * outer,
+        in_specs=[VMEM] * (1 + inner), out_specs=(VMEM,) * outer,
         compiler_params=params(4), name="reply",
-    )(*wishes, *replies)
-    parts = [send_outer(sorted_replies[k], k) for k in range(1, outer)]
+    )(wishes, *replies)
+    parts = [send_outer(sorted_replies[k], k) for k in range(outer - 1, 0, -1)]
 
     chunks = 4
     output = jax.ShapeDtypeStruct((packed_rows, width), BF16)

time: 34.3 us -> 32.5 us (0.948)
  Pallas kernels: 8.95 us -> 8.23 us
  waiting for transfers between devices: 8.85 us -> 8.19 us
  starting transfers between devices: 16.1 us -> 15.7 us
    ppermute x6, waiting for transfers between devices: 2.27 us -> 0.68 us  [send_outer(): lax.ppermute(x, 'req', [(o * inner + i, int(turn(o, k, outer)) * inner +...]
    ppermute x9 -> x8, waiting for transfers between devices: 6.57 us -> 7.51 us  [send_inner(): lax.ppermute(x, 'req', [(o * inner + i, o * inner + int(turn(i, k, inner)...]
    pallas_call x1, Pallas kernels: 1.64 us -> 0.91 us  [on_device(): pl.pallas_call(functools.partial(ask_kernel, count=count, inner=inner), o...]
    ppermute x9 -> x8, starting transfers between devices: 5.91 us -> 5.52 us  [send_inner(): lax.ppermute(x, 'req', [(o * inner + i, o * inner + int(turn(i, k, inner)...]
  transfers between devices with their start and end apart: 15 -> 14, of which waited for: 8 -> 6; matrix products, arithmetic and copies ran while one was open for 0% -> 0% of each run, Pallas kernels for 17% -> 18%
where the time goes in v5:
time: 32.5 us; the launch traced here: 32.3 us
  starting transfers between devices  15.7 us (48%)
  Pallas kernels  8.23 us (25%)
  waiting for transfers between devices  8.19 us (25%)
    ppermute x6, starting transfers between devices, send_outer(): lax.ppermute(x, 'req', [(o * inner + i, int(turn(o, k, outer)) * inner +...  10.2 us
    ppermute x8, waiting for transfers between devices, send_inner(): lax.ppermute(x, 'req', [(o * inner + i, o * inner + int(turn(i, k, inner)...  7.51 us
    ppermute x8, starting transfers between devices, send_inner(): lax.ppermute(x, 'req', [(o * inner + i, o * inner + int(turn(i, k, inner)...  5.52 us
    pallas_call x1, Pallas kernels, on_device(): pl.pallas_call(functools.partial(local_kernel, count=count, chunks=chunks...  3.49 us
    pallas_call x1, Pallas kernels, on_device(): pl.pallas_call(functools.partial(prepare_kernel, count=count, chunks=chun...  2.41 us
    pallas_call x1, Pallas kernels, on_device(): pl.pallas_call(functools.partial(ask_kernel, count=count, inner=inner), o...  0.91 us
    pallas_call x1, Pallas kernels, on_device(): pl.pallas_call(functools.partial(finish_kernel, count=count, heads=heads)...  0.9 us
    ppermute x6, waiting for transfers between devices, send_outer(): lax.ppermute(x, 'req', [(o * inner + i, int(turn(o, k, outer)) * inner +...  0.68 us
  transfers between devices with their start and end apart: 14, of which 6 were waited for; matrix products, arithmetic and copies ran while one was open for 0% of the time, Pallas kernels for 18%

profile of v5, /device:TPU:0, one launch (start us, length us, event | category | flops | bytes accessed | tf_op | source)
XLA Modules:
  0.0 32.3 jit_solution(10624846437598456602)
XLA Ops:
  0.0 0.9 %ask.1 = (f32[96,128]{1,0:T(8,128)S(1)}, s32[8,128]{1,0:T(8,128)S(1)}) custom-call(s32[2]{0:T(128)} %slots_ref.1, bf16[384,128]{1,0:T(8,128)(2,1)} %bitcast.26), custom_call_target="tpu_custom_call" | custom-call | tf_op jit(solution)/shard_map/ask/pallas_call | solution.py:345
  0.9 5.1 %collective-permute-start.4 = (f32[96,128]{1,0:T(8,128)S(1)}, f32[96,128]{1,0:T(8,128)S(1)}, u32[]{:S(2)}, u32[]{:S(2)}) collective-permute-start(f32[96,128]{1,0:T(8,128)S(1)} %get-tuple-element.21.refs_0_), channel_id=1, source_target_pairs={{0,12},{1,13},{2,14},{3,15},{4,8},{5,9},{6,10},{7,11},{8,4},{9,5},... | collective-permute-start | bytes 147464 | tf_op jit(solution)/shard_map/ppermute | solution.py:322
  6.1 0.6 %collective-permute-start.2 = (f32[96,128]{1,0:T(8,128)S(1)}, f32[96,128]{1,0:T(8,128)S(1)}, u32[]{:S(2)}, u32[]{:S(2)}) collective-permute-start(f32[96,128]{1,0:T(8,128)S(1)} %get-tuple-element.21.refs_0_), channel_id=1, source_target_pairs={{0,4},{1,5},{2,6},{3,7},{4,0},{5,1},{6,2},{7,3},{8,12},{9,13},{10,... | collective-permute-start | bytes 147464 | tf_op jit(solution)/shard_map/ppermute | solution.py:322
  6.7 1.2 %collective-permute-done = s32[8,128]{1,0:T(8,128)S(1)} collective-permute-done((s32[8,128]{1,0:T(8,128)S(1)}, s32[8,128]{1,0:T(8,128)S(1)}, u32[]{:S(2)}, u32[]{:S(2)}) %collective-permute-start) | collective-permute-done | bytes 4128 | tf_op jit(solution)/shard_map/ppermute | solution.py:317
  7.9 1.7 %collective-permute-start.1 = (s32[16,128]{1,0:T(8,128)S(1)}, s32[16,128]{1,0:T(8,128)S(1)}, u32[]{:S(2)}, u32[]{:S(2)}) collective-permute-start(s32[16,128]{1,0:T(8,128)S(1)} %pad_add_fusion), channel_id=1, source_target_pairs={{0,2},{1,3},{2,0},{3,1},{4,6},{5,7},{6,4},{7,5},{8,10},{9,11},{10,... | collective-permute-start | bytes 24584 | tf_op jit(solution)/shard_map/ppermute | solution.py:317
  9.5 2.0 %collective-permute-done.1 = s32[16,128]{1,0:T(8,128)S(1)} collective-permute-done((s32[16,128]{1,0:T(8,128)S(1)}, s32[16,128]{1,0:T(8,128)S(1)}, u32[]{:S(2)}, u32[]{:S(2)}) %collective-permute-start.1) | collective-permute-done | bytes 8224 | tf_op jit(solution)/shard_map/ppermute | solution.py:317
  11.5 0.0 collective-permute-done.4.refs_3_
  11.5 0.0 collective-permute-done.3.refs_2_
  11.6 0.1 collective-permute-start.5
  11.7 1.7 %collective-permute-start.6 = (f32[96,128]{1,0:T(8,128)S(1)}, f32[96,128]{1,0:T(8,128)S(1)}, u32[]{:S(2)}, u32[]{:S(2)}) collective-permute-start(f32[96,128]{1,0:T(8,128)S(1)} %get-tuple-element.24), channel_id=1, source_target_pairs={{0,2},{1,3},{2,0},{3,1},{4,6},{5,7},{6,4},{7,5},{8,10},{9,11},{10,... | collective-permute-start | bytes 147464 | tf_op jit(solution)/shard_map/ppermute | solution.py:317
  13.4 0.1 collective-permute-start.7
  13.5 2.4 %prepare.1 = (bf16[32,256,128]{2,1,0:T(8,128)(2,1)S(1)}, f32[2,96,128]{2,1,0:T(8,128)S(1)}) custom-call(s32[2]{0:T(128)} %slots_ref.1, bf16[384,128]{1,0:T(8,128)(2,1)} %bitcast.28, bf16[384,128]{1,0:T(8,128)(2,1)} %bitcast.30, f32[2,32,128,128]{3,2,1,0:T(8,128)} %states_ref.3), custom_call_target="tpu_custom_call" | custom-call | tf_op jit(solution)/shard_map/prepare/pallas_call | solution.py:358
  16.0 1.1 %collective-permute-done.7.refs_3_ = f32[96,128]{1,0:T(8,128)S(1)} collective-permute-done((f32[96,128]{1,0:T(8,128)S(1)}, f32[96,128]{1,0:T(8,128)S(1)}, u32[]{:S(2)}, u32[]{:S(2)}) %collective-permute-start.7) | collective-permute-done | bytes 49184 | tf_op jit(solution)/shard_map/ppermute | solution.py:317
  17.1 0.4 %answer.1.refs_0_ = f32[96,128]{1,0:T(8,128)S(1)} custom-call(s32[8,128]{1,0:T(8,128)S(1)} %get-tuple-element.20.facts_ref, f32[96,128]{1,0:T(8,128)S(1)} %get-tuple-element.22.refs_0_, f32[96,128]{1,0:T(8,128)S(1)} %collective-permute-done.5.refs_1_, f32[96,128]{1,0:T(8,128)S(1)} %collective-permute-done.6.refs_2_, ...), custom_call_target="tpu_custom_call" | custom-call | tf_op jit(solution)/shard_map/answer/pallas_call | solution.py:379
  17.5 0.9 %collective-permute-start.10 = (f32[96,128]{1,0:T(8,128)S(1)}, f32[96,128]{1,0:T(8,128)S(1)}, u32[]{:S(2)}, u32[]{:S(2)}) collective-permute-start(f32[96,128]{1,0:T(8,128)S(1)} %answer.1.refs_0_), channel_id=1, source_target_pairs={{0,3},{1,2},{2,1},{3,0},{4,7},{5,6},{6,5},{7,4},{8,11},{9,10},{10,... | collective-permute-start | bytes 147464 | tf_op jit(solution)/shard_map/ppermute | solution.py:317
  18.5 0.9 %collective-permute-start.9 = (f32[96,128]{1,0:T(8,128)S(1)}, f32[96,128]{1,0:T(8,128)S(1)}, u32[]{:S(2)}, u32[]{:S(2)}) collective-permute-start(f32[96,128]{1,0:T(8,128)S(1)} %answer.1.refs_0_), channel_id=1, source_target_pairs={{0,2},{1,3},{2,0},{3,1},{4,6},{5,7},{6,4},{7,5},{8,10},{9,11},{10,... | collective-permute-start | bytes 147464 | tf_op jit(solution)/shard_map/ppermute | solution.py:317
  19.4 0.1 collective-permute-start.8
  19.5 1.9 %collective-permute-done.10.refs_3_ = f32[96,128]{1,0:T(8,128)S(1)} collective-permute-done((f32[96,128]{1,0:T(8,128)S(1)}, f32[96,128]{1,0:T(8,128)S(1)}, u32[]{:S(2)}, u32[]{:S(2)}) %collective-permute-start.10) | collective-permute-done | bytes 49184 | tf_op jit(solution)/shard_map/ppermute | solution.py:317
  21.4 1.3 %collective-permute-done.9.refs_2_ = f32[96,128]{1,0:T(8,128)S(1)} collective-permute-done((f32[96,128]{1,0:T(8,128)S(1)}, f32[96,128]{1,0:T(8,128)S(1)}, u32[]{:S(2)}, u32[]{:S(2)}) %collective-permute-start.9) | collective-permute-done | bytes 49184 | tf_op jit(solution)/shard_map/ppermute | solution.py:317
  22.8 3.7 %collective-permute-start.11 = (f32[96,128]{1,0:T(8,128)S(1)}, f32[96,128]{1,0:T(8,128)S(1)}, u32[]{:S(2)}, u32[]{:S(2)}) collective-permute-start(f32[96,128]{1,0:T(8,128)S(1)} %get-tuple-element.32), channel_id=1, source_target_pairs={{0,12},{1,13},{2,14},{3,15},{4,8},{5,9},{6,10},{7,11},{8,4},{9,5},... | collective-permute-start | bytes 147464 | tf_op jit(solution)/shard_map/ppermute | solution.py:322
  26.4 0.8 %collective-permute-start.13 = (f32[96,128]{1,0:T(8,128)S(1)}, f32[96,128]{1,0:T(8,128)S(1)}, u32[]{:S(2)}, u32[]{:S(2)}) collective-permute-start(f32[96,128]{1,0:T(8,128)S(1)} %get-tuple-element.34), channel_id=1, source_target_pairs={{0,4},{1,5},{2,6},{3,7},{4,0},{5,1},{6,2},{7,3},{8,12},{9,13},{10,... | collective-permute-start | bytes 147464 | tf_op jit(solution)/shard_map/ppermute | solution.py:322
  27.2 3.5 %local.1 = (bf16[384,128]{1,0:T(8,128)(2,1)}, bf16[192,128]{1,0:T(8,128)(2,1)S(1)}, f32[2,96,128]{2,1,0:T(8,128)S(1)}) custom-call(s32[8,128]{1,0:T(8,128)S(1)} %get-tuple-element.20.facts_ref, bf16[384,128]{1,0:T(8,128)(2,1)S(1)} %bitcast.27, bf16[384,128]{1,0:T(8,128)(2,1)S(1)} %bitcast.29, bf16[384,128]{1,0:T(8,128)(2,1)S(1)} %bitcast.31, ...), custom_call_target="tpu_custom_call" | custom-call | tf_op jit(solution)/shard_map/local/pallas_call | solution.py:397
  30.7 0.7 %collective-permute-done.12.refs_1_ = f32[96,128]{1,0:T(8,128)S(1)} collective-permute-done((f32[96,128]{1,0:T(8,128)S(1)}, f32[96,128]{1,0:T(8,128)S(1)}, u32[]{:S(2)}, u32[]{:S(2)}) %collective-permute-start.12) | collective-permute-done | bytes 49184 | tf_op jit(solution)/shard_map/ppermute | solution.py:322
  31.4 0.9 %finish.1 = bf16[384,128]{1,0:T(8,128)(2,1)} custom-call(s32[8,128]{1,0:T(8,128)S(1)} %get-tuple-element.20.facts_ref, bf16[384,128]{1,0:T(8,128)(2,1)} %get-tuple-element.29.base_ref, bf16[192,128]{1,0:T(8,128)(2,1)S(1)} %get-tuple-element.30.last_ref, f32[2,96,128]{2,1,0:T(8,128)S(1)} %get-tuple-element.31.late_ref, ...), custom_call_target="tpu_custom_call", output_to_operand_aliasing={{}: (1, {})} | custom-call | tf_op jit(solution)/shard_map/finish/pallas_call | solution.py:412
  (25 shorter events, 0.1 us)
Async XLA Ops:
  0.0 27.2 %copy-start = (bf16[2,6,4096]{2,0,1:T(2,128)(2,1)S(1)}, bf16[2,6,4096]{2,0,1:T(2,128)(2,1)}, u32[]{:S(2)}) copy-start(bf16[2,6,4096]{2,0,1:T(2,128)(2,1)} %param.7) | copy-start | bytes 294916
  0.0 27.2 %copy-start.2 = (bf16[2,6,4096]{2,0,1:T(2,128)(2,1)S(1)}, bf16[2,6,4096]{2,0,1:T(2,128)(2,1)}, u32[]{:S(2)}) copy-start(bf16[2,6,4096]{2,0,1:T(2,128)(2,1)} %param.9) | copy-start | bytes 294916
  0.0 27.2 %copy-start.1 = (bf16[2,6,4096]{2,0,1:T(2,128)(2,1)S(1)}, bf16[2,6,4096]{2,0,1:T(2,128)(2,1)}, u32[]{:S(2)}) copy-start(bf16[2,6,4096]{2,0,1:T(2,128)(2,1)} %param.8) | copy-start | bytes 294916
  0.0 27.2 %copy-start.4 = (f32[4096]{0:T(1024)S(1)}, f32[4096]{0:T(1024)}, u32[]{:S(2)}) copy-start(f32[4096]{0:T(1024)} %param.13) | copy-start | bytes 49156
  0.0 27.2 %copy-start.3 = (bf16[2,6,4096]{2,0,1:T(2,128)(2,1)S(1)}, bf16[2,6,4096]{2,0,1:T(2,128)(2,1)}, u32[]{:S(2)}) copy-start(bf16[2,6,4096]{2,0,1:T(2,128)(2,1)} %param.10) | copy-start | bytes 294916
  0.9 10.6 %collective-permute-start.4 = (f32[96,128]{1,0:T(8,128)S(1)}, f32[96,128]{1,0:T(8,128)S(1)}, u32[]{:S(2)}, u32[]{:S(2)}) collective-permute-start(f32[96,128]{1,0:T(8,128)S(1)} %get-tuple-element.21.refs_0_), channel_id=1, source_target_pairs={{0,12},{1,13},{2,14},{3,15},{4,8},{5,9},{6,10},{7,11},{8,4},{9,5},... | collective-permute-start | bytes 147464 | tf_op jit(solution)/shard_map/ppermute | solution.py:322
  6.1 5.5 %collective-permute-start.3 = (f32[96,128]{1,0:T(8,128)S(1)}, f32[96,128]{1,0:T(8,128)S(1)}, u32[]{:S(2)}, u32[]{:S(2)}) collective-permute-start(f32[96,128]{1,0:T(8,128)S(1)} %get-tuple-element.21.refs_0_), channel_id=1, source_target_pairs={{0,8},{1,9},{2,10},{3,11},{4,12},{5,13},{6,14},{7,15},{8,0},{9,1},... | collective-permute-start | bytes 147464 | tf_op jit(solution)/shard_map/ppermute | solution.py:322
  6.1 5.5 %collective-permute-start.2 = (f32[96,128]{1,0:T(8,128)S(1)}, f32[96,128]{1,0:T(8,128)S(1)}, u32[]{:S(2)}, u32[]{:S(2)}) collective-permute-start(f32[96,128]{1,0:T(8,128)S(1)} %get-tuple-element.21.refs_0_), channel_id=1, source_target_pairs={{0,4},{1,5},{2,6},{3,7},{4,0},{5,1},{6,2},{7,3},{8,12},{9,13},{10,... | collective-permute-start | bytes 147464 | tf_op jit(solution)/shard_map/ppermute | solution.py:322
  6.7 1.2 %collective-permute-start = (s32[8,128]{1,0:T(8,128)S(1)}, s32[8,128]{1,0:T(8,128)S(1)}, u32[]{:S(2)}, u32[]{:S(2)}) collective-permute-start(s32[8,128]{1,0:T(8,128)S(1)} %get-tuple-element.20.facts_ref), channel_id=1, source_target_pairs={{0,1},{1,0},{2,3},{3,2},{4,5},{5,4},{6,7},{7,6},{8,9},{9,8},{10,11... | collective-permute-start | bytes 12296 | tf_op jit(solution)/shard_map/ppermute | solution.py:317
  7.9 3.7 %collective-permute-start.1 = (s32[16,128]{1,0:T(8,128)S(1)}, s32[16,128]{1,0:T(8,128)S(1)}, u32[]{:S(2)}, u32[]{:S(2)}) collective-permute-start(s32[16,128]{1,0:T(8,128)S(1)} %pad_add_fusion), channel_id=1, source_target_pairs={{0,2},{1,3},{2,0},{3,1},{4,6},{5,7},{6,4},{7,5},{8,10},{9,11},{10,... | collective-permute-start | bytes 24584 | tf_op jit(solution)/shard_map/ppermute | solution.py:317
  11.6 4.4 %collective-permute-start.5 = (f32[96,128]{1,0:T(8,128)S(1)}, f32[96,128]{1,0:T(8,128)S(1)}, u32[]{:S(2)}, u32[]{:S(2)}) collective-permute-start(f32[96,128]{1,0:T(8,128)S(1)} %get-tuple-element.23), channel_id=1, source_target_pairs={{0,1},{1,0},{2,3},{3,2},{4,5},{5,4},{6,7},{7,6},{8,9},{9,8},{10,11... | collective-permute-start | bytes 147464 | tf_op jit(solution)/shard_map/ppermute | solution.py:317
  11.7 4.3 %collective-permute-start.6 = (f32[96,128]{1,0:T(8,128)S(1)}, f32[96,128]{1,0:T(8,128)S(1)}, u32[]{:S(2)}, u32[]{:S(2)}) collective-permute-start(f32[96,128]{1,0:T(8,128)S(1)} %get-tuple-element.24), channel_id=1, source_target_pairs={{0,2},{1,3},{2,0},{3,1},{4,6},{5,7},{6,4},{7,5},{8,10},{9,11},{10,... | collective-permute-start | bytes 147464 | tf_op jit(solution)/shard_map/ppermute | solution.py:317
  13.4 3.7 %collective-permute-start.7 = (f32[96,128]{1,0:T(8,128)S(1)}, f32[96,128]{1,0:T(8,128)S(1)}, u32[]{:S(2)}, u32[]{:S(2)}) collective-permute-start(f32[96,128]{1,0:T(8,128)S(1)} %get-tuple-element.25), channel_id=1, source_target_pairs={{0,3},{1,2},{2,1},{3,0},{4,7},{5,6},{6,5},{7,4},{8,11},{9,10},{10,... | collective-permute-start | bytes 147464 | tf_op jit(solution)/shard_map/ppermute | solution.py:317
  17.5 3.8 %collective-permute-start.10 = (f32[96,128]{1,0:T(8,128)S(1)}, f32[96,128]{1,0:T(8,128)S(1)}, u32[]{:S(2)}, u32[]{:S(2)}) collective-permute-start(f32[96,128]{1,0:T(8,128)S(1)} %answer.1.refs_0_), channel_id=1, source_target_pairs={{0,3},{1,2},{2,1},{3,0},{4,7},{5,6},{6,5},{7,4},{8,11},{9,10},{10,... | collective-permute-start | bytes 147464 | tf_op jit(solution)/shard_map/ppermute | solution.py:317
  18.5 4.2 %collective-permute-start.9 = (f32[96,128]{1,0:T(8,128)S(1)}, f32[96,128]{1,0:T(8,128)S(1)}, u32[]{:S(2)}, u32[]{:S(2)}) collective-permute-start(f32[96,128]{1,0:T(8,128)S(1)} %answer.1.refs_0_), channel_id=1, source_target_pairs={{0,2},{1,3},{2,0},{3,1},{4,6},{5,7},{6,4},{7,5},{8,10},{9,11},{10,... | collective-permute-start | bytes 147464 | tf_op jit(solution)/shard_map/ppermute | solution.py:317
  19.4 3.3 %collective-permute-start.8 = (f32[96,128]{1,0:T(8,128)S(1)}, f32[96,128]{1,0:T(8,128)S(1)}, u32[]{:S(2)}, u32[]{:S(2)}) collective-permute-start(f32[96,128]{1,0:T(8,128)S(1)} %answer.1.refs_0_), channel_id=1, source_target_pairs={{0,1},{1,0},{2,3},{3,2},{4,5},{5,4},{6,7},{7,6},{8,9},{9,8},{10,11... | collective-permute-start | bytes 147464 | tf_op jit(solution)/shard_map/ppermute | solution.py:317
  22.8 8.0 %collective-permute-start.11 = (f32[96,128]{1,0:T(8,128)S(1)}, f32[96,128]{1,0:T(8,128)S(1)}, u32[]{:S(2)}, u32[]{:S(2)}) collective-permute-start(f32[96,128]{1,0:T(8,128)S(1)} %get-tuple-element.32), channel_id=1, source_target_pairs={{0,12},{1,13},{2,14},{3,15},{4,8},{5,9},{6,10},{7,11},{8,4},{9,5},... | collective-permute-start | bytes 147464 | tf_op jit(solution)/shard_map/ppermute | solution.py:322
  26.4 5.0 %collective-permute-start.12 = (f32[96,128]{1,0:T(8,128)S(1)}, f32[96,128]{1,0:T(8,128)S(1)}, u32[]{:S(2)}, u32[]{:S(2)}) collective-permute-start(f32[96,128]{1,0:T(8,128)S(1)} %get-tuple-element.33), channel_id=1, source_target_pairs={{0,8},{1,9},{2,10},{3,11},{4,12},{5,13},{6,14},{7,15},{8,0},{9,1},... | collective-permute-start | bytes 147464 | tf_op jit(solution)/shard_map/ppermute | solution.py:322
  26.4 5.0 %collective-permute-start.13 = (f32[96,128]{1,0:T(8,128)S(1)}, f32[96,128]{1,0:T(8,128)S(1)}, u32[]{:S(2)}, u32[]{:S(2)}) collective-permute-start(f32[96,128]{1,0:T(8,128)S(1)} %get-tuple-element.34), channel_id=1, source_target_pairs={{0,4},{1,5},{2,6},{3,7},{4,0},{5,1},{6,2},{7,3},{8,12},{9,13},{10,... | collective-permute-start | bytes 147464 | tf_op jit(solution)/shard_map/ppermute | solution.py:322

commit v6 on v5

--- a/solution.py
+++ b/solution.py
@@ -48,8 +48,17 @@
 OUTER, INNER, SLOT, FACTS = 0, 1, 2, 8
 
 
-def fact(ref, step, kind, rows):
-    row = step * FACTS + kind
+def wish_steps(inner):
+    if inner & (inner - 1):
+        return list(range(inner))
+    steps, step = [0], inner // 2
+    while step:
+        steps, step = steps + [s ^ step for s in steps], step // 2
+    return steps
+
+
+def fact(ref, place, kind, rows):
+    row = place * FACTS + kind
     return jnp.broadcast_to(ref[row:row + 1, :], (rows, ref.shape[1]))
 
 
@@ -145,12 +154,13 @@
     column, outs = refs[:outer], refs[outer:]
     my_outer = lax.div(lax.axis_index("req"), inner)
     for k in range(inner):
-        wish = fact(wishes_ref, inverse_step(k, inner), OUTER, outs[k].shape[0])
+        back = wish_steps(inner).index(inverse_step(k, inner))
+        wish = fact(wishes_ref, back, OUTER, outs[k].shape[0])
         outs[k][...] = choose(column, wish, my_outer, outer)
 
 
 def answer_kernel(facts_ref, *refs, inner, late, heads, width):
-    found, (weight_ref, early_ref, out_ref, lhs, prod) = refs[:inner], refs[inner:]
+    found, (weight_ref, early_ref, out_ref, lhs, prod) = refs[:inner][::-1], refs[inner:]
     my_inner = lax.rem(lax.axis_index("req"), inner)
     block = lambda ref, t: ref[t * heads:(t + 1) * heads, :]
     rows = choose(found, fact(facts_ref, 0, INNER, late * heads), my_inner, inner)
@@ -180,9 +190,9 @@
     my_inner, my_outer = lax.rem(me, inner), lax.div(me, inner)
     rows = outs[0].shape[0]
     owner = [
-        jnp.where(fact(wishes_ref, k, INNER, rows) == my_inner,
-                  fact(wishes_ref, k, OUTER, rows), -1)
-        for k in range(inner)]
+        jnp.where(fact(wishes_ref, n, INNER, rows) == my_inner,
+                  fact(wishes_ref, n, OUTER, rows), -1)
+        for n in map(wish_steps(inner).index, range(inner))]
     for k in range(outer):
         result = 0.0
         for n in range(inner):
@@ -269,24 +279,30 @@
 
 
 def finish_kernel(facts_ref, base_ref, last_ref, late_ref, *refs, count, heads):
-    parts, (out_ref, rows_ref, wide, sem) = refs[:-4], refs[-4:]
-    wide[...] = last_ref[...].astype(F32)
+    parts, (out_ref, rows_ref, wide, sems) = refs[:-4], refs[-4:]
     place = fact(facts_ref, 0, SLOT, heads)
-    for t in range(late_ref.shape[1] // heads):
+    span = heads * count
+    steps = late_ref.shape[1] // heads
+    first = out_ref.shape[0] - steps * span
+    copies = []
+    for t in range(steps):
         part = slice(t * heads, (t + 1) * heads)
         x = late_ref[0, part, :]
         for ref in parts:
             x = x + ref[part, :]
         y = x * lax.rsqrt(jnp.mean(x * x) + EPS) * late_ref[1, part, :]
+        rows = slice(t * span, (t + 1) * span)
+        wide[rows, :] = last_ref[rows, :].astype(F32)
         for s in range(count):
-            here = pl.ds(t * heads * count + s, heads, stride=count)
+            here = pl.ds(t * span + s, heads, stride=count)
             wide[here, :] = jnp.where(place == s, y, wide[here, :])
-    rows_ref[...] = wide[...].astype(BF16)
-    rows = rows_ref.shape[0]
-    copy = pltpu.make_async_copy(
-        rows_ref, out_ref.at[pl.ds(out_ref.shape[0] - rows, rows)], sem)
-    copy.start()
-    copy.wait()
+        rows_ref[rows, :] = wide[rows, :].astype(BF16)
+        copies.append(pltpu.make_async_copy(
+            rows_ref.at[pl.ds(t * span, span)], out_ref.at[pl.ds(first + t * span, span)],
+            sems.at[t]))
+        copies[t].start()
+    for copy in copies:
+        copy.wait()
 
 
 def in_hbm(x):
@@ -326,10 +342,9 @@
     def gather_inner(x):
         if inner & (inner - 1):
             return jnp.concatenate([x] + [send_inner(x, k) for k in range(1, inner)])
-        step = 1
-        while step < inner:
-            x = jnp.concatenate([x, send_inner(x, step)])
-            step *= 2
+        step = inner // 2
+        while step:
+            x, step = jnp.concatenate([x, send_inner(x, step)]), step // 2
         return x
 
     def params(limit):
@@ -374,7 +389,7 @@
         in_specs=[VMEM] * (1 + outer), out_specs=(VMEM,) * inner,
         compiler_params=params(4), name="route",
     )(wishes, *column)
-    found = [asked[0]] + [send_inner(asked[k], k) for k in range(inner - 1, 0, -1)][::-1]
+    found = [send_inner(asked[k], k) for k in range(inner - 1, 0, -1)] + [asked[0]]
 
     answer = pl.pallas_call(
         functools.partial(answer_kernel, inner=inner, late=late, heads=heads, width=width),
@@ -412,7 +427,7 @@
     return unpack(pl.pallas_call(
         functools.partial(finish_kernel, count=count, heads=heads),
         out_shape=output, in_specs=[VMEM, HBM] + [VMEM] * (outer + 1), out_specs=HBM,
-        scratch_shapes=[late_bf16, late_packed, pltpu.SemaphoreType.DMA],
+        scratch_shapes=[late_bf16, late_packed, pltpu.SemaphoreType.DMA((late,))],
         input_output_aliases={1: 0},
         compiler_params=params(4), name="finish",
     )(facts, in_hbm(base), last, partial, *parts))

time: 32.5 us -> 32.6 us (level)
  transfers between devices with their start and end apart: 14 -> 14, of which waited for: 6 -> 7; matrix products, arithmetic and copies ran while one was open for 0% -> 0% of each run, Pallas kernels for 18% -> 18%
where the time goes in v6:
time: 32.6 us; the launch traced here: 32.4 us
  starting transfers between devices  15.7 us (48%)
  waiting for transfers between devices  8.28 us (25%)
  Pallas kernels  8.23 us (25%)
    ppermute x6, starting transfers between devices, send_outer(): lax.ppermute(x, 'req', [(o * inner + i, int(turn(o, k, outer)) * inner +...  10.2 us
    ppermute x8, waiting for transfers between devices, send_inner(): lax.ppermute(x, 'req', [(o * inner + i, o * inner + int(turn(i, k, inner)...  7.48 us
    ppermute x8, starting transfers between devices, send_inner(): lax.ppermute(x, 'req', [(o * inner + i, o * inner + int(turn(i, k, inner)...  5.52 us
    pallas_call x1, Pallas kernels, on_device(): pl.pallas_call(functools.partial(local_kernel, count=count, chunks=chunks...  3.49 us
    pallas_call x1, Pallas kernels, on_device(): pl.pallas_call(functools.partial(prepare_kernel, count=count, chunks=chun...  2.41 us
    pallas_call x1, Pallas kernels, on_device(): pl.pallas_call(functools.partial(ask_kernel, count=count, inner=inner), o...  0.91 us
    pallas_call x1, Pallas kernels, on_device(): pl.pallas_call(functools.partial(finish_kernel, count=count, heads=heads)...  0.9 us
    ppermute x6, waiting for transfers between devices, send_outer(): lax.ppermute(x, 'req', [(o * inner + i, int(turn(o, k, outer)) * inner +...  0.8 us
  transfers between devices with their start and end apart: 14, of which 7 were waited for; matrix products, arithmetic and copies ran while one was open for 0% of the time, Pallas kernels for 18%

profile of v6, /device:TPU:0, one launch (start us, length us, event | category | flops | bytes accessed | tf_op | source)
XLA Modules:
  0.0 32.4 jit_solution(5161228305455361704)
XLA Ops:
  0.0 0.9 %ask.1 = (f32[96,128]{1,0:T(8,128)S(1)}, s32[8,128]{1,0:T(8,128)S(1)}) custom-call(s32[2]{0:T(128)} %slots_ref.1, bf16[384,128]{1,0:T(8,128)(2,1)} %bitcast.26), custom_call_target="tpu_custom_call" | custom-call | tf_op jit(solution)/shard_map/ask/pallas_call | solution.py:360
  0.9 5.1 %collective-permute-start.4 = (f32[96,128]{1,0:T(8,128)S(1)}, f32[96,128]{1,0:T(8,128)S(1)}, u32[]{:S(2)}, u32[]{:S(2)}) collective-permute-start(f32[96,128]{1,0:T(8,128)S(1)} %get-tuple-element.21.refs_0_), channel_id=1, source_target_pairs={{0,12},{1,13},{2,14},{3,15},{4,8},{5,9},{6,10},{7,11},{8,4},{9,5},... | collective-permute-start | bytes 147464 | tf_op jit(solution)/shard_map/ppermute | solution.py:338
  6.1 0.6 %collective-permute-start.2 = (f32[96,128]{1,0:T(8,128)S(1)}, f32[96,128]{1,0:T(8,128)S(1)}, u32[]{:S(2)}, u32[]{:S(2)}) collective-permute-start(f32[96,128]{1,0:T(8,128)S(1)} %get-tuple-element.21.refs_0_), channel_id=1, source_target_pairs={{0,4},{1,5},{2,6},{3,7},{4,0},{5,1},{6,2},{7,3},{8,12},{9,13},{10,... | collective-permute-start | bytes 147464 | tf_op jit(solution)/shard_map/ppermute | solution.py:338
  6.7 1.7 %collective-permute-start = (s32[8,128]{1,0:T(8,128)S(1)}, s32[8,128]{1,0:T(8,128)S(1)}, u32[]{:S(2)}, u32[]{:S(2)}) collective-permute-start(s32[8,128]{1,0:T(8,128)S(1)} %get-tuple-element.20.facts_ref), channel_id=1, source_target_pairs={{0,2},{1,3},{2,0},{3,1},{4,6},{5,7},{6,4},{7,5},{8,10},{9,11},{10,... | collective-permute-start | bytes 12296 | tf_op jit(solution)/shard_map/ppermute | solution.py:333
  8.4 1.9 %collective-permute-done = s32[8,128]{1,0:T(8,128)S(1)} collective-permute-done((s32[8,128]{1,0:T(8,128)S(1)}, s32[8,128]{1,0:T(8,128)S(1)}, u32[]{:S(2)}, u32[]{:S(2)}) %collective-permute-start) | collective-permute-done | bytes 4128 | tf_op jit(solution)/shard_map/ppermute | solution.py:333
  10.3 1.2 %collective-permute-done.1 = s32[16,128]{1,0:T(8,128)S(1)} collective-permute-done((s32[16,128]{1,0:T(8,128)S(1)}, s32[16,128]{1,0:T(8,128)S(1)}, u32[]{:S(2)}, u32[]{:S(2)}) %collective-permute-start.1) | collective-permute-done | bytes 8224 | tf_op jit(solution)/shard_map/ppermute | solution.py:333
  11.5 0.0 collective-permute-done.4.refs_3_
  11.5 1.5 %collective-permute-start.5 = (f32[96,128]{1,0:T(8,128)S(1)}, f32[96,128]{1,0:T(8,128)S(1)}, u32[]{:S(2)}, u32[]{:S(2)}) collective-permute-start(f32[96,128]{1,0:T(8,128)S(1)} %get-tuple-element.22), channel_id=1, source_target_pairs={{0,3},{1,2},{2,1},{3,0},{4,7},{5,6},{6,5},{7,4},{8,11},{9,10},{10,... | collective-permute-start | bytes 147464 | tf_op jit(solution)/shard_map/ppermute | solution.py:333
  13.0 0.4 %collective-permute-start.6 = (f32[96,128]{1,0:T(8,128)S(1)}, f32[96,128]{1,0:T(8,128)S(1)}, u32[]{:S(2)}, u32[]{:S(2)}) collective-permute-start(f32[96,128]{1,0:T(8,128)S(1)} %get-tuple-element.23), channel_id=1, source_target_pairs={{0,2},{1,3},{2,0},{3,1},{4,6},{5,7},{6,4},{7,5},{8,10},{9,11},{10,... | collective-permute-start | bytes 147464 | tf_op jit(solution)/shard_map/ppermute | solution.py:333
  13.4 0.1 collective-permute-start.7
  13.5 2.4 %prepare.1 = (bf16[32,256,128]{2,1,0:T(8,128)(2,1)S(1)}, f32[2,96,128]{2,1,0:T(8,128)S(1)}) custom-call(s32[2]{0:T(128)} %slots_ref.1, bf16[384,128]{1,0:T(8,128)(2,1)} %bitcast.28, bf16[384,128]{1,0:T(8,128)(2,1)} %bitcast.30, f32[2,32,128,128]{3,2,1,0:T(8,128)} %states_ref.3), custom_call_target="tpu_custom_call" | custom-call | tf_op jit(solution)/shard_map/prepare/pallas_call | solution.py:373
  15.9 1.2 %collective-permute-done.6.refs_1_ = f32[96,128]{1,0:T(8,128)S(1)} collective-permute-done((f32[96,128]{1,0:T(8,128)S(1)}, f32[96,128]{1,0:T(8,128)S(1)}, u32[]{:S(2)}, u32[]{:S(2)}) %collective-permute-start.6) | collective-permute-done | bytes 49184 | tf_op jit(solution)/shard_map/ppermute | solution.py:333
  17.1 0.4 %answer.1.refs_0_ = f32[96,128]{1,0:T(8,128)S(1)} custom-call(s32[8,128]{1,0:T(8,128)S(1)} %get-tuple-element.20.facts_ref, f32[96,128]{1,0:T(8,128)S(1)} %collective-permute-done.5.refs_0_, f32[96,128]{1,0:T(8,128)S(1)} %collective-permute-done.6.refs_1_, f32[96,128]{1,0:T(8,128)S(1)} %collective-permute-done.7.refs_2_, ...), custom_call_target="tpu_custom_call" | custom-call | tf_op jit(solution)/shard_map/answer/pallas_call | solution.py:394
  17.6 0.7 %collective-permute-start.10 = (f32[96,128]{1,0:T(8,128)S(1)}, f32[96,128]{1,0:T(8,128)S(1)}, u32[]{:S(2)}, u32[]{:S(2)}) collective-permute-start(f32[96,128]{1,0:T(8,128)S(1)} %answer.1.refs_0_), channel_id=1, source_target_pairs={{0,3},{1,2},{2,1},{3,0},{4,7},{5,6},{6,5},{7,4},{8,11},{9,10},{10,... | collective-permute-start | bytes 147464 | tf_op jit(solution)/shard_map/ppermute | solution.py:333
  18.3 0.7 %collective-permute-start.9 = (f32[96,128]{1,0:T(8,128)S(1)}, f32[96,128]{1,0:T(8,128)S(1)}, u32[]{:S(2)}, u32[]{:S(2)}) collective-permute-start(f32[96,128]{1,0:T(8,128)S(1)} %answer.1.refs_0_), channel_id=1, source_target_pairs={{0,2},{1,3},{2,0},{3,1},{4,6},{5,7},{6,4},{7,5},{8,10},{9,11},{10,... | collective-permute-start | bytes 147464 | tf_op jit(solution)/shard_map/ppermute | solution.py:333
  19.0 0.5 %collective-permute-start.8 = (f32[96,128]{1,0:T(8,128)S(1)}, f32[96,128]{1,0:T(8,128)S(1)}, u32[]{:S(2)}, u32[]{:S(2)}) collective-permute-start(f32[96,128]{1,0:T(8,128)S(1)} %answer.1.refs_0_), channel_id=1, source_target_pairs={{0,1},{1,0},{2,3},{3,2},{4,5},{5,4},{6,7},{7,6},{8,9},{9,8},{10,11... | collective-permute-start | bytes 147464 | tf_op jit(solution)/shard_map/ppermute | solution.py:333
  19.5 2.0 %collective-permute-done.10.refs_3_ = f32[96,128]{1,0:T(8,128)S(1)} collective-permute-done((f32[96,128]{1,0:T(8,128)S(1)}, f32[96,128]{1,0:T(8,128)S(1)}, u32[]{:S(2)}, u32[]{:S(2)}) %collective-permute-start.10) | collective-permute-done | bytes 49184 | tf_op jit(solution)/shard_map/ppermute | solution.py:333
  21.5 1.2 %collective-permute-done.9.refs_2_ = f32[96,128]{1,0:T(8,128)S(1)} collective-permute-done((f32[96,128]{1,0:T(8,128)S(1)}, f32[96,128]{1,0:T(8,128)S(1)}, u32[]{:S(2)}, u32[]{:S(2)}) %collective-permute-start.9) | collective-permute-done | bytes 49184 | tf_op jit(solution)/shard_map/ppermute | solution.py:333
  22.7 3.7 %collective-permute-start.11 = (f32[96,128]{1,0:T(8,128)S(1)}, f32[96,128]{1,0:T(8,128)S(1)}, u32[]{:S(2)}, u32[]{:S(2)}) collective-permute-start(f32[96,128]{1,0:T(8,128)S(1)} %get-tuple-element.32), channel_id=1, source_target_pairs={{0,12},{1,13},{2,14},{3,15},{4,8},{5,9},{6,10},{7,11},{8,4},{9,5},... | collective-permute-start | bytes 147464 | tf_op jit(solution)/shard_map/ppermute | solution.py:338
  26.4 0.8 %collective-permute-start.13 = (f32[96,128]{1,0:T(8,128)S(1)}, f32[96,128]{1,0:T(8,128)S(1)}, u32[]{:S(2)}, u32[]{:S(2)}) collective-permute-start(f32[96,128]{1,0:T(8,128)S(1)} %get-tuple-element.34), channel_id=1, source_target_pairs={{0,4},{1,5},{2,6},{3,7},{4,0},{5,1},{6,2},{7,3},{8,12},{9,13},{10,... | collective-permute-start | bytes 147464 | tf_op jit(solution)/shard_map/ppermute | solution.py:338
  27.2 3.5 %local.1 = (bf16[384,128]{1,0:T(8,128)(2,1)}, bf16[192,128]{1,0:T(8,128)(2,1)S(1)}, f32[2,96,128]{2,1,0:T(8,128)S(1)}) custom-call(s32[8,128]{1,0:T(8,128)S(1)} %get-tuple-element.20.facts_ref, bf16[384,128]{1,0:T(8,128)(2,1)S(1)} %bitcast.27, bf16[384,128]{1,0:T(8,128)(2,1)S(1)} %bitcast.29, bf16[384,128]{1,0:T(8,128)(2,1)S(1)} %bitcast.31, ...), custom_call_target="tpu_custom_call" | custom-call | tf_op jit(solution)/shard_map/local/pallas_call | solution.py:412
  30.7 0.7 %collective-permute-done.12.refs_1_ = f32[96,128]{1,0:T(8,128)S(1)} collective-permute-done((f32[96,128]{1,0:T(8,128)S(1)}, f32[96,128]{1,0:T(8,128)S(1)}, u32[]{:S(2)}, u32[]{:S(2)}) %collective-permute-start.12) | collective-permute-done | bytes 49184 | tf_op jit(solution)/shard_map/ppermute | solution.py:338
  31.4 0.1 collective-permute-done.13.refs_2_
  31.5 0.9 %finish.1 = bf16[384,128]{1,0:T(8,128)(2,1)} custom-call(s32[8,128]{1,0:T(8,128)S(1)} %get-tuple-element.20.facts_ref, bf16[384,128]{1,0:T(8,128)(2,1)} %get-tuple-element.29.base_ref, bf16[192,128]{1,0:T(8,128)(2,1)S(1)} %get-tuple-element.30.last_ref, f32[2,96,128]{2,1,0:T(8,128)S(1)} %get-tuple-element.31.late_ref, ...), custom_call_target="tpu_custom_call", output_to_operand_aliasing={{}: (1, {})} | custom-call | tf_op jit(solution)/shard_map/finish/pallas_call | solution.py:427
  (25 shorter events, 0.1 us)
Async XLA Ops:
  0.0 27.2 %copy-start = (bf16[2,6,4096]{2,0,1:T(2,128)(2,1)S(1)}, bf16[2,6,4096]{2,0,1:T(2,128)(2,1)}, u32[]{:S(2)}) copy-start(bf16[2,6,4096]{2,0,1:T(2,128)(2,1)} %param.7) | copy-start | bytes 294916
  0.0 27.2 %copy-start.2 = (bf16[2,6,4096]{2,0,1:T(2,128)(2,1)S(1)}, bf16[2,6,4096]{2,0,1:T(2,128)(2,1)}, u32[]{:S(2)}) copy-start(bf16[2,6,4096]{2,0,1:T(2,128)(2,1)} %param.9) | copy-start | bytes 294916
  0.0 27.2 %copy-start.1 = (bf16[2,6,4096]{2,0,1:T(2,128)(2,1)S(1)}, bf16[2,6,4096]{2,0,1:T(2,128)(2,1)}, u32[]{:S(2)}) copy-start(bf16[2,6,4096]{2,0,1:T(2,128)(2,1)} %param.8) | copy-start | bytes 294916
  0.0 27.2 %copy-start.4 = (f32[4096]{0:T(1024)S(1)}, f32[4096]{0:T(1024)}, u32[]{:S(2)}) copy-start(f32[4096]{0:T(1024)} %param.13) | copy-start | bytes 49156
  0.0 27.2 %copy-start.3 = (bf16[2,6,4096]{2,0,1:T(2,128)(2,1)S(1)}, bf16[2,6,4096]{2,0,1:T(2,128)(2,1)}, u32[]{:S(2)}) copy-start(bf16[2,6,4096]{2,0,1:T(2,128)(2,1)} %param.10) | copy-start | bytes 294916
  0.9 10.6 %collective-permute-start.4 = (f32[96,128]{1,0:T(8,128)S(1)}, f32[96,128]{1,0:T(8,128)S(1)}, u32[]{:S(2)}, u32[]{:S(2)}) collective-permute-start(f32[96,128]{1,0:T(8,128)S(1)} %get-tuple-element.21.refs_0_), channel_id=1, source_target_pairs={{0,12},{1,13},{2,14},{3,15},{4,8},{5,9},{6,10},{7,11},{8,4},{9,5},... | collective-permute-start | bytes 147464 | tf_op jit(solution)/shard_map/ppermute | solution.py:338
  6.1 5.4 %collective-permute-start.3 = (f32[96,128]{1,0:T(8,128)S(1)}, f32[96,128]{1,0:T(8,128)S(1)}, u32[]{:S(2)}, u32[]{:S(2)}) collective-permute-start(f32[96,128]{1,0:T(8,128)S(1)} %get-tuple-element.21.refs_0_), channel_id=1, source_target_pairs={{0,8},{1,9},{2,10},{3,11},{4,12},{5,13},{6,14},{7,15},{8,0},{9,1},... | collective-permute-start | bytes 147464 | tf_op jit(solution)/shard_map/ppermute | solution.py:338
  6.1 5.4 %collective-permute-start.2 = (f32[96,128]{1,0:T(8,128)S(1)}, f32[96,128]{1,0:T(8,128)S(1)}, u32[]{:S(2)}, u32[]{:S(2)}) collective-permute-start(f32[96,128]{1,0:T(8,128)S(1)} %get-tuple-element.21.refs_0_), channel_id=1, source_target_pairs={{0,4},{1,5},{2,6},{3,7},{4,0},{5,1},{6,2},{7,3},{8,12},{9,13},{10,... | collective-permute-start | bytes 147464 | tf_op jit(solution)/shard_map/ppermute | solution.py:338
  6.7 3.6 %collective-permute-start = (s32[8,128]{1,0:T(8,128)S(1)}, s32[8,128]{1,0:T(8,128)S(1)}, u32[]{:S(2)}, u32[]{:S(2)}) collective-permute-start(s32[8,128]{1,0:T(8,128)S(1)} %get-tuple-element.20.facts_ref), channel_id=1, source_target_pairs={{0,2},{1,3},{2,0},{3,1},{4,6},{5,7},{6,4},{7,5},{8,10},{9,11},{10,... | collective-permute-start | bytes 12296 | tf_op jit(solution)/shard_map/ppermute | solution.py:333
  10.3 1.2 %collective-permute-start.1 = (s32[16,128]{1,0:T(8,128)S(1)}, s32[16,128]{1,0:T(8,128)S(1)}, u32[]{:S(2)}, u32[]{:S(2)}) collective-permute-start(s32[16,128]{1,0:T(8,128)S(1)} %pad_add_fusion), channel_id=1, source_target_pairs={{0,1},{1,0},{2,3},{3,2},{4,5},{5,4},{6,7},{7,6},{8,9},{9,8},{10,11... | collective-permute-start | bytes 24584 | tf_op jit(solution)/shard_map/ppermute | solution.py:333
  11.5 4.3 %collective-permute-start.5 = (f32[96,128]{1,0:T(8,128)S(1)}, f32[96,128]{1,0:T(8,128)S(1)}, u32[]{:S(2)}, u32[]{:S(2)}) collective-permute-start(f32[96,128]{1,0:T(8,128)S(1)} %get-tuple-element.22), channel_id=1, source_target_pairs={{0,3},{1,2},{2,1},{3,0},{4,7},{5,6},{6,5},{7,4},{8,11},{9,10},{10,... | collective-permute-start | bytes 147464 | tf_op jit(solution)/shard_map/ppermute | solution.py:333
  13.0 4.1 %collective-permute-start.6 = (f32[96,128]{1,0:T(8,128)S(1)}, f32[96,128]{1,0:T(8,128)S(1)}, u32[]{:S(2)}, u32[]{:S(2)}) collective-permute-start(f32[96,128]{1,0:T(8,128)S(1)} %get-tuple-element.23), channel_id=1, source_target_pairs={{0,2},{1,3},{2,0},{3,1},{4,6},{5,7},{6,4},{7,5},{8,10},{9,11},{10,... | collective-permute-start | bytes 147464 | tf_op jit(solution)/shard_map/ppermute | solution.py:333
  13.4 3.7 %collective-permute-start.7 = (f32[96,128]{1,0:T(8,128)S(1)}, f32[96,128]{1,0:T(8,128)S(1)}, u32[]{:S(2)}, u32[]{:S(2)}) collective-permute-start(f32[96,128]{1,0:T(8,128)S(1)} %get-tuple-element.24), channel_id=1, source_target_pairs={{0,1},{1,0},{2,3},{3,2},{4,5},{5,4},{6,7},{7,6},{8,9},{9,8},{10,11... | collective-permute-start | bytes 147464 | tf_op jit(solution)/shard_map/ppermute | solution.py:333
  17.6 3.9 %collective-permute-start.10 = (f32[96,128]{1,0:T(8,128)S(1)}, f32[96,128]{1,0:T(8,128)S(1)}, u32[]{:S(2)}, u32[]{:S(2)}) collective-permute-start(f32[96,128]{1,0:T(8,128)S(1)} %answer.1.refs_0_), channel_id=1, source_target_pairs={{0,3},{1,2},{2,1},{3,0},{4,7},{5,6},{6,5},{7,4},{8,11},{9,10},{10,... | collective-permute-start | bytes 147464 | tf_op jit(solution)/shard_map/ppermute | solution.py:333
  18.3 4.4 %collective-permute-start.9 = (f32[96,128]{1,0:T(8,128)S(1)}, f32[96,128]{1,0:T(8,128)S(1)}, u32[]{:S(2)}, u32[]{:S(2)}) collective-permute-start(f32[96,128]{1,0:T(8,128)S(1)} %answer.1.refs_0_), channel_id=1, source_target_pairs={{0,2},{1,3},{2,0},{3,1},{4,6},{5,7},{6,4},{7,5},{8,10},{9,11},{10,... | collective-permute-start | bytes 147464 | tf_op jit(solution)/shard_map/ppermute | solution.py:333
  19.0 3.7 %collective-permute-start.8 = (f32[96,128]{1,0:T(8,128)S(1)}, f32[96,128]{1,0:T(8,128)S(1)}, u32[]{:S(2)}, u32[]{:S(2)}) collective-permute-start(f32[96,128]{1,0:T(8,128)S(1)} %answer.1.refs_0_), channel_id=1, source_target_pairs={{0,1},{1,0},{2,3},{3,2},{4,5},{5,4},{6,7},{7,6},{8,9},{9,8},{10,11... | collective-permute-start | bytes 147464 | tf_op jit(solution)/shard_map/ppermute | solution.py:333
  22.7 8.0 %collective-permute-start.11 = (f32[96,128]{1,0:T(8,128)S(1)}, f32[96,128]{1,0:T(8,128)S(1)}, u32[]{:S(2)}, u32[]{:S(2)}) collective-permute-start(f32[96,128]{1,0:T(8,128)S(1)} %get-tuple-element.32), channel_id=1, source_target_pairs={{0,12},{1,13},{2,14},{3,15},{4,8},{5,9},{6,10},{7,11},{8,4},{9,5},... | collective-permute-start | bytes 147464 | tf_op jit(solution)/shard_map/ppermute | solution.py:338
  26.4 5.0 %collective-permute-start.12 = (f32[96,128]{1,0:T(8,128)S(1)}, f32[96,128]{1,0:T(8,128)S(1)}, u32[]{:S(2)}, u32[]{:S(2)}) collective-permute-start(f32[96,128]{1,0:T(8,128)S(1)} %get-tuple-element.33), channel_id=1, source_target_pairs={{0,8},{1,9},{2,10},{3,11},{4,12},{5,13},{6,14},{7,15},{8,0},{9,1},... | collective-permute-start | bytes 147464 | tf_op jit(solution)/shard_map/ppermute | solution.py:338
  26.4 5.1 %collective-permute-start.13 = (f32[96,128]{1,0:T(8,128)S(1)}, f32[96,128]{1,0:T(8,128)S(1)}, u32[]{:S(2)}, u32[]{:S(2)}) collective-permute-start(f32[96,128]{1,0:T(8,128)S(1)} %get-tuple-element.34), channel_id=1, source_target_pairs={{0,4},{1,5},{2,6},{3,7},{4,0},{5,1},{6,2},{7,3},{8,12},{9,13},{10,... | collective-permute-start | bytes 147464 | tf_op jit(solution)/shard_map/ppermute | solution.py:338

commit v7 on v6

--- a/solution.py
+++ b/solution.py
@@ -51,9 +51,9 @@
 def wish_steps(inner):
     if inner & (inner - 1):
         return list(range(inner))
-    steps, step = [0], inner // 2
-    while step:
-        steps, step = steps + [s ^ step for s in steps], step // 2
+    steps, step = [0], 1
+    while step < inner:
+        steps, step = steps + [s ^ step for s in steps], step * 2
     return steps
 
 
@@ -94,6 +94,13 @@
 
 def inverse_step(step, size):
     return step if size & (size - 1) == 0 else (size - step) % size
+
+
+def in_steps(refs, order):
+    result = [refs[0]] * len(refs)
+    for step, ref in zip(order, refs[1:]):
+        result[step] = ref
+    return result
 
 
 def choose(options, index, mine, size):
@@ -150,8 +157,8 @@
             weight_ref[h] = jnp.concatenate(split(state[h]), axis=0)
 
 
-def route_kernel(wishes_ref, *refs, inner, outer):
-    column, outs = refs[:outer], refs[outer:]
+def route_kernel(wishes_ref, *refs, inner, outer, order):
+    column, outs = in_steps(refs[:outer], order), refs[outer:]
     my_outer = lax.div(lax.axis_index("req"), inner)
     for k in range(inner):
         back = wish_steps(inner).index(inverse_step(k, inner))
@@ -159,8 +166,9 @@
         outs[k][...] = choose(column, wish, my_outer, outer)
 
 
-def answer_kernel(facts_ref, *refs, inner, late, heads, width):
-    found, (weight_ref, early_ref, out_ref, lhs, prod) = refs[:inner][::-1], refs[inner:]
+def answer_kernel(facts_ref, *refs, inner, late, heads, width, order):
+    found, (weight_ref, early_ref, out_ref, lhs, prod) = refs[:inner], refs[inner:]
+    found = in_steps(found, order)
     my_inner = lax.rem(lax.axis_index("req"), inner)
     block = lambda ref, t: ref[t * heads:(t + 1) * heads, :]
     rows = choose(found, fact(facts_ref, 0, INNER, late * heads), my_inner, inner)
@@ -184,8 +192,8 @@
         out_ref[t * heads:(t + 1) * heads, :] = total
 
 
-def reply_kernel(wishes_ref, *refs, inner, outer):
-    replies, outs = refs[:inner], refs[inner:]
+def reply_kernel(wishes_ref, *refs, inner, outer, order):
+    replies, outs = in_steps(refs[:inner], order), refs[inner:]
     me = lax.axis_index("req")
     my_inner, my_outer = lax.rem(me, inner), lax.div(me, inner)
     rows = outs[0].shape[0]
@@ -342,9 +350,11 @@
     def gather_inner(x):
         if inner & (inner - 1):
             return jnp.concatenate([x] + [send_inner(x, k) for k in range(1, inner)])
-        step = inner // 2
-        while step:
-            x, step = jnp.concatenate([x, send_inner(x, step)]), step // 2
+        own, step = x[:FACTS], 1
+        x = jnp.concatenate([own, send_inner(x, step)[:FACTS]])
+        while 2 * step < inner:
+            step *= 2
+            x = jnp.concatenate([x, send_inner(x, step)])
         return x
 
     def params(limit):
@@ -366,7 +376,10 @@
         compiler_params=params(4), name="ask",
     )(in_hbm(new_slot), in_hbm(queries))
 
-    column = [ask] + [send_outer(ask, k) for k in range(1, outer)]
+    up, half = list(range(1, outer)), outer // 2
+    z1, z2 = up, up[half - 1:] + up[:half - 1]
+    q1, q2 = list(range(inner - 1, 0, -1)), list(range(1, inner))
+    column = [ask] + [send_outer(ask, k) for k in z1]
     wishes = gather_inner(facts)
 
     chunks = 8
@@ -384,28 +397,29 @@
     )(in_hbm(new_slot), in_hbm(keys), in_hbm(values), in_hbm(states))
 
     asked = pl.pallas_call(
-        functools.partial(route_kernel, inner=inner, outer=outer),
+        functools.partial(route_kernel, inner=inner, outer=outer, order=z1),
         out_shape=(single,) * inner,
         in_specs=[VMEM] * (1 + outer), out_specs=(VMEM,) * inner,
         compiler_params=params(4), name="route",
     )(wishes, *column)
-    found = [send_inner(asked[k], k) for k in range(inner - 1, 0, -1)] + [asked[0]]
+    found = [asked[0]] + [send_inner(asked[k], k) for k in q1]
 
     answer = pl.pallas_call(
-        functools.partial(answer_kernel, inner=inner, late=late, heads=heads, width=width),
+        functools.partial(answer_kernel, inner=inner, late=late, heads=heads, width=width,
+                          order=q1),
         out_shape=single, in_specs=[VMEM] * (inner + 3), out_specs=VMEM,
         scratch_shapes=[pltpu.VMEM((2 * late * heads, width), F32)] * 2,
         compiler_params=params(8), name="answer",
     )(facts, *found, weight, early)
-    replies = [answer] + [send_inner(answer, k) for k in range(1, inner)]
+    replies = [answer] + [send_inner(answer, k) for k in q2]
 
     sorted_replies = pl.pallas_call(
-        functools.partial(reply_kernel, inner=inner, outer=outer),
+        functools.partial(reply_kernel, inner=inner, outer=outer, order=q2),
         out_shape=(single,) * outer,
         in_specs=[VMEM] * (1 + inner), out_specs=(VMEM,) * outer,
         compiler_params=params(4), name="reply",
     )(wishes, *replies)
-    parts = [send_outer(sorted_replies[k], k) for k in range(outer - 1, 0, -1)]
+    parts = [send_outer(sorted_replies[k], k) for k in z2]
 
     chunks = 4
     output = jax.ShapeDtypeStruct((packed_rows, width), BF16)

time: 32.6 us -> 31.8 us (0.975)
  waiting for transfers between devices: 8.28 us -> 7.61 us
    ppermute x8, waiting for transfers between devices: 7.48 us -> 7 us  [send_inner(): lax.ppermute(x, 'req', [(o * inner + i, o * inner + int(turn(i, k, inner)...]
  transfers between devices with their start and end apart: 14 -> 14, of which waited for: 7 -> 7; matrix products, arithmetic and copies ran while one was open for 0% -> 0% of each run, Pallas kernels for 18% -> 19%
where the time goes in v7:
time: 31.8 us; the launch traced here: 31.6 us
  starting transfers between devices  15.6 us (49%)
  Pallas kernels  8.23 us (26%)
  waiting for transfers between devices  7.61 us (24%)
    ppermute x6, starting transfers between devices, send_outer(): lax.ppermute(x, 'req', [(o * inner + i, int(turn(o, k, outer)) * inner +...  10.1 us
    ppermute x8, waiting for transfers between devices, send_inner(): lax.ppermute(x, 'req', [(o * inner + i, o * inner + int(turn(i, k, inner)...  7 us
    ppermute x8, starting transfers between devices, send_inner(): lax.ppermute(x, 'req', [(o * inner + i, o * inner + int(turn(i, k, inner)...  5.58 us
    pallas_call x1, Pallas kernels, on_device(): pl.pallas_call(functools.partial(local_kernel, count=count, chunks=chunks...  3.49 us
    pallas_call x1, Pallas kernels, on_device(): pl.pallas_call(functools.partial(prepare_kernel, count=count, chunks=chun...  2.41 us
    pallas_call x1, Pallas kernels, on_device(): pl.pallas_call(functools.partial(ask_kernel, count=count, inner=inner), o...  0.91 us
    pallas_call x1, Pallas kernels, on_device(): pl.pallas_call(functools.partial(finish_kernel, count=count, heads=heads)...  0.9 us
  transfers between devices with their start and end apart: 14, of which 7 were waited for; matrix products, arithmetic and copies ran while one was open for 0% of the time, Pallas kernels for 19%

profile of v7, /device:TPU:0, one launch (start us, length us, event | category | flops | bytes accessed | tf_op | source)
XLA Modules:
  0.0 31.6 jit_solution(5495029577657787806)
XLA Ops:
  0.0 0.9 %ask.1 = (f32[96,128]{1,0:T(8,128)S(1)}, s32[8,128]{1,0:T(8,128)S(1)}) custom-call(s32[2]{0:T(128)} %slots_ref.1, bf16[384,128]{1,0:T(8,128)(2,1)} %bitcast.26), custom_call_target="tpu_custom_call" | custom-call | tf_op jit(solution)/shard_map/ask/pallas_call | solution.py:370
  0.9 5.1 %collective-permute-start.4 = (f32[96,128]{1,0:T(8,128)S(1)}, f32[96,128]{1,0:T(8,128)S(1)}, u32[]{:S(2)}, u32[]{:S(2)}) collective-permute-start(f32[96,128]{1,0:T(8,128)S(1)} %get-tuple-element.21.refs_0_), channel_id=1, source_target_pairs={{0,12},{1,13},{2,14},{3,15},{4,8},{5,9},{6,10},{7,11},{8,4},{9,5},... | collective-permute-start | bytes 147464 | tf_op jit(solution)/shard_map/ppermute | solution.py:346
  6.1 0.6 %collective-permute-start.2 = (f32[96,128]{1,0:T(8,128)S(1)}, f32[96,128]{1,0:T(8,128)S(1)}, u32[]{:S(2)}, u32[]{:S(2)}) collective-permute-start(f32[96,128]{1,0:T(8,128)S(1)} %get-tuple-element.21.refs_0_), channel_id=1, source_target_pairs={{0,4},{1,5},{2,6},{3,7},{4,0},{5,1},{6,2},{7,3},{8,12},{9,13},{10,... | collective-permute-start | bytes 147464 | tf_op jit(solution)/shard_map/ppermute | solution.py:346
  6.7 1.2 %collective-permute-done = s32[8,128]{1,0:T(8,128)S(1)} collective-permute-done((s32[8,128]{1,0:T(8,128)S(1)}, s32[8,128]{1,0:T(8,128)S(1)}, u32[]{:S(2)}, u32[]{:S(2)}) %collective-permute-start) | collective-permute-done | bytes 4128 | tf_op jit(solution)/shard_map/ppermute | solution.py:341
  7.9 1.7 %collective-permute-start.1 = (s32[16,128]{1,0:T(8,128)S(1)}, s32[16,128]{1,0:T(8,128)S(1)}, u32[]{:S(2)}, u32[]{:S(2)}) collective-permute-start(s32[16,128]{1,0:T(8,128)S(1)} %pad_add_fusion), channel_id=1, source_target_pairs={{0,2},{1,3},{2,0},{3,1},{4,6},{5,7},{6,4},{7,5},{8,10},{9,11},{10,... | collective-permute-start | bytes 24584 | tf_op jit(solution)/shard_map/ppermute | solution.py:341
  9.5 2.0 %collective-permute-done.1 = s32[16,128]{1,0:T(8,128)S(1)} collective-permute-done((s32[16,128]{1,0:T(8,128)S(1)}, s32[16,128]{1,0:T(8,128)S(1)}, u32[]{:S(2)}, u32[]{:S(2)}) %collective-permute-start.1) | collective-permute-done | bytes 8224 | tf_op jit(solution)/shard_map/ppermute | solution.py:341
  11.6 0.6 %collective-permute-start.5 = (f32[96,128]{1,0:T(8,128)S(1)}, f32[96,128]{1,0:T(8,128)S(1)}, u32[]{:S(2)}, u32[]{:S(2)}) collective-permute-start(f32[96,128]{1,0:T(8,128)S(1)} %get-tuple-element.23), channel_id=1, source_target_pairs={{0,3},{1,2},{2,1},{3,0},{4,7},{5,6},{6,5},{7,4},{8,11},{9,10},{10,... | collective-permute-start | bytes 147464 | tf_op jit(solution)/shard_map/ppermute | solution.py:341
  12.2 1.2 %collective-permute-start.6 = (f32[96,128]{1,0:T(8,128)S(1)}, f32[96,128]{1,0:T(8,128)S(1)}, u32[]{:S(2)}, u32[]{:S(2)}) collective-permute-start(f32[96,128]{1,0:T(8,128)S(1)} %get-tuple-element.24), channel_id=1, source_target_pairs={{0,2},{1,3},{2,0},{3,1},{4,6},{5,7},{6,4},{7,5},{8,10},{9,11},{10,... | collective-permute-start | bytes 147464 | tf_op jit(solution)/shard_map/ppermute | solution.py:341
  13.4 0.1 collective-permute-start.7
  13.5 2.4 %prepare.1 = (bf16[32,256,128]{2,1,0:T(8,128)(2,1)S(1)}, f32[2,96,128]{2,1,0:T(8,128)S(1)}) custom-call(s32[2]{0:T(128)} %slots_ref.1, bf16[384,128]{1,0:T(8,128)(2,1)} %bitcast.28, bf16[384,128]{1,0:T(8,128)(2,1)} %bitcast.30, f32[2,32,128,128]{3,2,1,0:T(8,128)} %states_ref.3), custom_call_target="tpu_custom_call" | custom-call | tf_op jit(solution)/shard_map/prepare/pallas_call | solution.py:386
  16.0 0.6 %collective-permute-done.6.refs_2_ = f32[96,128]{1,0:T(8,128)S(1)} collective-permute-done((f32[96,128]{1,0:T(8,128)S(1)}, f32[96,128]{1,0:T(8,128)S(1)}, u32[]{:S(2)}, u32[]{:S(2)}) %collective-permute-start.6) | collective-permute-done | bytes 49184 | tf_op jit(solution)/shard_map/ppermute | solution.py:341
  16.6 0.4 %answer.1.refs_0_ = f32[96,128]{1,0:T(8,128)S(1)} custom-call(s32[8,128]{1,0:T(8,128)S(1)} %get-tuple-element.20.facts_ref, f32[96,128]{1,0:T(8,128)S(1)} %get-tuple-element.22.refs_0_, f32[96,128]{1,0:T(8,128)S(1)} %collective-permute-done.5.refs_1_, f32[96,128]{1,0:T(8,128)S(1)} %collective-permute-done.6.refs_2_, ...), custom_call_target="tpu_custom_call" | custom-call | tf_op jit(solution)/shard_map/answer/pallas_call | solution.py:407
  17.1 1.0 %collective-permute-start.10 = (f32[96,128]{1,0:T(8,128)S(1)}, f32[96,128]{1,0:T(8,128)S(1)}, u32[]{:S(2)}, u32[]{:S(2)}) collective-permute-start(f32[96,128]{1,0:T(8,128)S(1)} %answer.1.refs_0_), channel_id=1, source_target_pairs={{0,3},{1,2},{2,1},{3,0},{4,7},{5,6},{6,5},{7,4},{8,11},{9,10},{10,... | collective-permute-start | bytes 147464 | tf_op jit(solution)/shard_map/ppermute | solution.py:341
  18.1 0.8 %collective-permute-start.9 = (f32[96,128]{1,0:T(8,128)S(1)}, f32[96,128]{1,0:T(8,128)S(1)}, u32[]{:S(2)}, u32[]{:S(2)}) collective-permute-start(f32[96,128]{1,0:T(8,128)S(1)} %answer.1.refs_0_), channel_id=1, source_target_pairs={{0,2},{1,3},{2,0},{3,1},{4,6},{5,7},{6,4},{7,5},{8,10},{9,11},{10,... | collective-permute-start | bytes 147464 | tf_op jit(solution)/shard_map/ppermute | solution.py:341
  18.9 0.1 collective-permute-start.8
  19.0 1.8 %collective-permute-done.10.refs_3_ = f32[96,128]{1,0:T(8,128)S(1)} collective-permute-done((f32[96,128]{1,0:T(8,128)S(1)}, f32[96,128]{1,0:T(8,128)S(1)}, u32[]{:S(2)}, u32[]{:S(2)}) %collective-permute-start.10) | collective-permute-done | bytes 49184 | tf_op jit(solution)/shard_map/ppermute | solution.py:341
  20.9 1.3 %collective-permute-done.9.refs_2_ = f32[96,128]{1,0:T(8,128)S(1)} collective-permute-done((f32[96,128]{1,0:T(8,128)S(1)}, f32[96,128]{1,0:T(8,128)S(1)}, u32[]{:S(2)}, u32[]{:S(2)}) %collective-permute-start.9) | collective-permute-done | bytes 49184 | tf_op jit(solution)/shard_map/ppermute | solution.py:341
  22.3 2.3 %collective-permute-start.11 = (f32[96,128]{1,0:T(8,128)S(1)}, f32[96,128]{1,0:T(8,128)S(1)}, u32[]{:S(2)}, u32[]{:S(2)}) collective-permute-start(f32[96,128]{1,0:T(8,128)S(1)} %get-tuple-element.32), channel_id=1, source_target_pairs={{0,8},{1,9},{2,10},{3,11},{4,12},{5,13},{6,14},{7,15},{8,0},{9,1},... | collective-permute-start | bytes 147464 | tf_op jit(solution)/shard_map/ppermute | solution.py:346
  24.5 1.5 %collective-permute-start.12 = (f32[96,128]{1,0:T(8,128)S(1)}, f32[96,128]{1,0:T(8,128)S(1)}, u32[]{:S(2)}, u32[]{:S(2)}) collective-permute-start(f32[96,128]{1,0:T(8,128)S(1)} %get-tuple-element.33), channel_id=1, source_target_pairs={{0,12},{1,13},{2,14},{3,15},{4,8},{5,9},{6,10},{7,11},{8,4},{9,5},... | collective-permute-start | bytes 147464 | tf_op jit(solution)/shard_map/ppermute | solution.py:346
  26.1 0.5 %collective-permute-start.13 = (f32[96,128]{1,0:T(8,128)S(1)}, f32[96,128]{1,0:T(8,128)S(1)}, u32[]{:S(2)}, u32[]{:S(2)}) collective-permute-start(f32[96,128]{1,0:T(8,128)S(1)} %get-tuple-element.34), channel_id=1, source_target_pairs={{0,4},{1,5},{2,6},{3,7},{4,0},{5,1},{6,2},{7,3},{8,12},{9,13},{10,... | collective-permute-start | bytes 147464 | tf_op jit(solution)/shard_map/ppermute | solution.py:346
  26.6 3.5 %local.1 = (bf16[384,128]{1,0:T(8,128)(2,1)}, bf16[192,128]{1,0:T(8,128)(2,1)S(1)}, f32[2,96,128]{2,1,0:T(8,128)S(1)}) custom-call(s32[8,128]{1,0:T(8,128)S(1)} %get-tuple-element.20.facts_ref, bf16[384,128]{1,0:T(8,128)(2,1)S(1)} %bitcast.27, bf16[384,128]{1,0:T(8,128)(2,1)S(1)} %bitcast.29, bf16[384,128]{1,0:T(8,128)(2,1)S(1)} %bitcast.31, ...), custom_call_target="tpu_custom_call" | custom-call | tf_op jit(solution)/shard_map/local/pallas_call | solution.py:426
  30.1 0.5 %collective-permute-done.12.refs_1_ = f32[96,128]{1,0:T(8,128)S(1)} collective-permute-done((f32[96,128]{1,0:T(8,128)S(1)}, f32[96,128]{1,0:T(8,128)S(1)}, u32[]{:S(2)}, u32[]{:S(2)}) %collective-permute-start.12) | collective-permute-done | bytes 49184 | tf_op jit(solution)/shard_map/ppermute | solution.py:346
  30.6 0.1 collective-permute-done.13.refs_2_
  30.7 0.9 %finish.1 = bf16[384,128]{1,0:T(8,128)(2,1)} custom-call(s32[8,128]{1,0:T(8,128)S(1)} %get-tuple-element.20.facts_ref, bf16[384,128]{1,0:T(8,128)(2,1)} %get-tuple-element.29.base_ref, bf16[192,128]{1,0:T(8,128)(2,1)S(1)} %get-tuple-element.30.last_ref, f32[2,96,128]{2,1,0:T(8,128)S(1)} %get-tuple-element.31.late_ref, ...), custom_call_target="tpu_custom_call", output_to_operand_aliasing={{}: (1, {})} | custom-call | tf_op jit(solution)/shard_map/finish/pallas_call | solution.py:441
  (25 shorter events, 0.1 us)
Async XLA Ops:
  0.0 26.6 %copy-start = (bf16[2,6,4096]{2,0,1:T(2,128)(2,1)S(1)}, bf16[2,6,4096]{2,0,1:T(2,128)(2,1)}, u32[]{:S(2)}) copy-start(bf16[2,6,4096]{2,0,1:T(2,128)(2,1)} %param.7) | copy-start | bytes 294916
  0.0 26.6 %copy-start.2 = (bf16[2,6,4096]{2,0,1:T(2,128)(2,1)S(1)}, bf16[2,6,4096]{2,0,1:T(2,128)(2,1)}, u32[]{:S(2)}) copy-start(bf16[2,6,4096]{2,0,1:T(2,128)(2,1)} %param.9) | copy-start | bytes 294916
  0.0 26.6 %copy-start.1 = (bf16[2,6,4096]{2,0,1:T(2,128)(2,1)S(1)}, bf16[2,6,4096]{2,0,1:T(2,128)(2,1)}, u32[]{:S(2)}) copy-start(bf16[2,6,4096]{2,0,1:T(2,128)(2,1)} %param.8) | copy-start | bytes 294916
  0.0 26.6 %copy-start.4 = (f32[4096]{0:T(1024)S(1)}, f32[4096]{0:T(1024)}, u32[]{:S(2)}) copy-start(f32[4096]{0:T(1024)} %param.13) | copy-start | bytes 49156
  0.0 26.6 %copy-start.3 = (bf16[2,6,4096]{2,0,1:T(2,128)(2,1)S(1)}, bf16[2,6,4096]{2,0,1:T(2,128)(2,1)}, u32[]{:S(2)}) copy-start(bf16[2,6,4096]{2,0,1:T(2,128)(2,1)} %param.10) | copy-start | bytes 294916
  0.9 10.6 %collective-permute-start.4 = (f32[96,128]{1,0:T(8,128)S(1)}, f32[96,128]{1,0:T(8,128)S(1)}, u32[]{:S(2)}, u32[]{:S(2)}) collective-permute-start(f32[96,128]{1,0:T(8,128)S(1)} %get-tuple-element.21.refs_0_), channel_id=1, source_target_pairs={{0,12},{1,13},{2,14},{3,15},{4,8},{5,9},{6,10},{7,11},{8,4},{9,5},... | collective-permute-start | bytes 147464 | tf_op jit(solution)/shard_map/ppermute | solution.py:346
  6.1 5.5 %collective-permute-start.3 = (f32[96,128]{1,0:T(8,128)S(1)}, f32[96,128]{1,0:T(8,128)S(1)}, u32[]{:S(2)}, u32[]{:S(2)}) collective-permute-start(f32[96,128]{1,0:T(8,128)S(1)} %get-tuple-element.21.refs_0_), channel_id=1, source_target_pairs={{0,8},{1,9},{2,10},{3,11},{4,12},{5,13},{6,14},{7,15},{8,0},{9,1},... | collective-permute-start | bytes 147464 | tf_op jit(solution)/shard_map/ppermute | solution.py:346
  6.1 5.5 %collective-permute-start.2 = (f32[96,128]{1,0:T(8,128)S(1)}, f32[96,128]{1,0:T(8,128)S(1)}, u32[]{:S(2)}, u32[]{:S(2)}) collective-permute-start(f32[96,128]{1,0:T(8,128)S(1)} %get-tuple-element.21.refs_0_), channel_id=1, source_target_pairs={{0,4},{1,5},{2,6},{3,7},{4,0},{5,1},{6,2},{7,3},{8,12},{9,13},{10,... | collective-permute-start | bytes 147464 | tf_op jit(solution)/shard_map/ppermute | solution.py:346
  6.7 1.2 %collective-permute-start = (s32[8,128]{1,0:T(8,128)S(1)}, s32[8,128]{1,0:T(8,128)S(1)}, u32[]{:S(2)}, u32[]{:S(2)}) collective-permute-start(s32[8,128]{1,0:T(8,128)S(1)} %get-tuple-element.20.facts_ref), channel_id=1, source_target_pairs={{0,1},{1,0},{2,3},{3,2},{4,5},{5,4},{6,7},{7,6},{8,9},{9,8},{10,11... | collective-permute-start | bytes 12296 | tf_op jit(solution)/shard_map/ppermute | solution.py:341
  7.9 3.7 %collective-permute-start.1 = (s32[16,128]{1,0:T(8,128)S(1)}, s32[16,128]{1,0:T(8,128)S(1)}, u32[]{:S(2)}, u32[]{:S(2)}) collective-permute-start(s32[16,128]{1,0:T(8,128)S(1)} %pad_add_fusion), channel_id=1, source_target_pairs={{0,2},{1,3},{2,0},{3,1},{4,6},{5,7},{6,4},{7,5},{8,10},{9,11},{10,... | collective-permute-start | bytes 24584 | tf_op jit(solution)/shard_map/ppermute | solution.py:341
  11.6 4.4 %collective-permute-start.5 = (f32[96,128]{1,0:T(8,128)S(1)}, f32[96,128]{1,0:T(8,128)S(1)}, u32[]{:S(2)}, u32[]{:S(2)}) collective-permute-start(f32[96,128]{1,0:T(8,128)S(1)} %get-tuple-element.23), channel_id=1, source_target_pairs={{0,3},{1,2},{2,1},{3,0},{4,7},{5,6},{6,5},{7,4},{8,11},{9,10},{10,... | collective-permute-start | bytes 147464 | tf_op jit(solution)/shard_map/ppermute | solution.py:341
  12.2 4.4 %collective-permute-start.6 = (f32[96,128]{1,0:T(8,128)S(1)}, f32[96,128]{1,0:T(8,128)S(1)}, u32[]{:S(2)}, u32[]{:S(2)}) collective-permute-start(f32[96,128]{1,0:T(8,128)S(1)} %get-tuple-element.24), channel_id=1, source_target_pairs={{0,2},{1,3},{2,0},{3,1},{4,6},{5,7},{6,4},{7,5},{8,10},{9,11},{10,... | collective-permute-start | bytes 147464 | tf_op jit(solution)/shard_map/ppermute | solution.py:341
  13.4 3.2 %collective-permute-start.7 = (f32[96,128]{1,0:T(8,128)S(1)}, f32[96,128]{1,0:T(8,128)S(1)}, u32[]{:S(2)}, u32[]{:S(2)}) collective-permute-start(f32[96,128]{1,0:T(8,128)S(1)} %get-tuple-element.25), channel_id=1, source_target_pairs={{0,1},{1,0},{2,3},{3,2},{4,5},{5,4},{6,7},{7,6},{8,9},{9,8},{10,11... | collective-permute-start | bytes 147464 | tf_op jit(solution)/shard_map/ppermute | solution.py:341
  17.1 3.8 %collective-permute-start.10 = (f32[96,128]{1,0:T(8,128)S(1)}, f32[96,128]{1,0:T(8,128)S(1)}, u32[]{:S(2)}, u32[]{:S(2)}) collective-permute-start(f32[96,128]{1,0:T(8,128)S(1)} %answer.1.refs_0_), channel_id=1, source_target_pairs={{0,3},{1,2},{2,1},{3,0},{4,7},{5,6},{6,5},{7,4},{8,11},{9,10},{10,... | collective-permute-start | bytes 147464 | tf_op jit(solution)/shard_map/ppermute | solution.py:341
  18.1 4.2 %collective-permute-start.9 = (f32[96,128]{1,0:T(8,128)S(1)}, f32[96,128]{1,0:T(8,128)S(1)}, u32[]{:S(2)}, u32[]{:S(2)}) collective-permute-start(f32[96,128]{1,0:T(8,128)S(1)} %answer.1.refs_0_), channel_id=1, source_target_pairs={{0,2},{1,3},{2,0},{3,1},{4,6},{5,7},{6,4},{7,5},{8,10},{9,11},{10,... | collective-permute-start | bytes 147464 | tf_op jit(solution)/shard_map/ppermute | solution.py:341
  18.9 3.4 %collective-permute-start.8 = (f32[96,128]{1,0:T(8,128)S(1)}, f32[96,128]{1,0:T(8,128)S(1)}, u32[]{:S(2)}, u32[]{:S(2)}) collective-permute-start(f32[96,128]{1,0:T(8,128)S(1)} %answer.1.refs_0_), channel_id=1, source_target_pairs={{0,1},{1,0},{2,3},{3,2},{4,5},{5,4},{6,7},{7,6},{8,9},{9,8},{10,11... | collective-permute-start | bytes 147464 | tf_op jit(solution)/shard_map/ppermute | solution.py:341
  22.3 7.8 %collective-permute-start.11 = (f32[96,128]{1,0:T(8,128)S(1)}, f32[96,128]{1,0:T(8,128)S(1)}, u32[]{:S(2)}, u32[]{:S(2)}) collective-permute-start(f32[96,128]{1,0:T(8,128)S(1)} %get-tuple-element.32), channel_id=1, source_target_pairs={{0,8},{1,9},{2,10},{3,11},{4,12},{5,13},{6,14},{7,15},{8,0},{9,1},... | collective-permute-start | bytes 147464 | tf_op jit(solution)/shard_map/ppermute | solution.py:346
  24.5 6.0 %collective-permute-start.12 = (f32[96,128]{1,0:T(8,128)S(1)}, f32[96,128]{1,0:T(8,128)S(1)}, u32[]{:S(2)}, u32[]{:S(2)}) collective-permute-start(f32[96,128]{1,0:T(8,128)S(1)} %get-tuple-element.33), channel_id=1, source_target_pairs={{0,12},{1,13},{2,14},{3,15},{4,8},{5,9},{6,10},{7,11},{8,4},{9,5},... | collective-permute-start | bytes 147464 | tf_op jit(solution)/shard_map/ppermute | solution.py:346
  26.1 4.6 %collective-permute-start.13 = (f32[96,128]{1,0:T(8,128)S(1)}, f32[96,128]{1,0:T(8,128)S(1)}, u32[]{:S(2)}, u32[]{:S(2)}) collective-permute-start(f32[96,128]{1,0:T(8,128)S(1)} %get-tuple-element.34), channel_id=1, source_target_pairs={{0,4},{1,5},{2,6},{3,7},{4,0},{5,1},{6,2},{7,3},{8,12},{9,13},{10,... | collective-permute-start | bytes 147464 | tf_op jit(solution)/shard_map/ppermute | solution.py:346

commit v8 on v7

--- a/solution.py
+++ b/solution.py
@@ -104,14 +104,15 @@
 
 
 def choose(options, index, mine, size):
-    result = options[0][...]
+    rows = index.shape[0]
+    result = options[0][:rows, :]
     for k in range(1, size):
-        result = jnp.where(unturn(mine, k, size) == index, options[k][...], result)
+        result = jnp.where(unturn(mine, k, size) == index, options[k][:rows, :], result)
     return result
 
 
-def ask_kernel(new_slot_ref, queries_ref, out_ref, facts_ref, slots_ref, rows_ref, wide, sems, *,
-               count, inner):
+def ask_kernel(new_slot_ref, queries_ref, out_ref, long_ref, facts_ref, slots_ref, rows_ref, wide,
+               sems, *, count, inner):
     late = rows_ref.shape[0]
     first = queries_ref.shape[0] - late
     slots_copy = pltpu.make_async_copy(new_slot_ref, slots_ref, sems.at[0])
@@ -126,7 +127,16 @@
     facts_ref[...] = jnp.where(kind == OUTER, lax.div(wanted, inner), facts)
     copy.wait()
     wide[...] = rows_ref[...].astype(F32)
-    out_ref[...] = silu(extract(wide, place, count))
+    rows = silu(extract(wide, place, count))
+    out_ref[...] = rows
+    long_ref[:rows.shape[0], :] = rows
+    long_ref[rows.shape[0]:, :] = jnp.zeros_like(long_ref[rows.shape[0]:, :])
+
+
+def pair_kernel(near_ref, far_ref, out_ref):
+    rows = out_ref.shape[0] // 2
+    out_ref[:rows, :] = near_ref[:rows, :]
+    out_ref[rows:, :] = far_ref[:rows, :]
 
 
 def prepare_kernel(slots_ref, keys_ref, values_ref, states_ref, weight_ref, early_ref,
@@ -349,13 +359,17 @@
 
     def gather_inner(x):
         if inner & (inner - 1):
+            x = x[:FACTS]
             return jnp.concatenate([x] + [send_inner(x, k) for k in range(1, inner)])
-        own, step = x[:FACTS], 1
-        x = jnp.concatenate([own, send_inner(x, step)[:FACTS]])
-        while 2 * step < inner:
+        step, result = 1, x
+        while step < inner:
+            result = pl.pallas_call(
+                pair_kernel,
+                out_shape=jax.ShapeDtypeStruct((2 * step * FACTS, width), jnp.int32),
+                in_specs=[VMEM, VMEM], out_specs=VMEM, compiler_params=params(4), name="pair",
+            )(result, send_inner(result, step))
             step *= 2
-            x = jnp.concatenate([x, send_inner(x, step)])
-        return x
+        return result
 
     def params(limit):
         return pltpu.CompilerParams(vmem_limit_bytes=limit * MIB)
@@ -367,10 +381,12 @@
     late_rows = jax.ShapeDtypeStruct((late * heads * count, width), BF16)
     late_bf16 = pltpu.VMEM(late_rows.shape, BF16)
 
-    ask, facts = pl.pallas_call(
+    long = jax.ShapeDtypeStruct((single_rows + FACTS, width), F32)
+    facts_rows = max(single_rows * 5 // (6 * FACTS), 1) * FACTS
+    ask, ask_long, facts = pl.pallas_call(
         functools.partial(ask_kernel, count=count, inner=inner),
-        out_shape=(single, jax.ShapeDtypeStruct((FACTS, width), jnp.int32)),
-        in_specs=[HBM, HBM], out_specs=(VMEM, VMEM),
+        out_shape=(single, long, jax.ShapeDtypeStruct((facts_rows, width), jnp.int32)),
+        in_specs=[HBM, HBM], out_specs=(VMEM, VMEM, VMEM),
         scratch_shapes=[pltpu.SMEM((count,), jnp.int32), late_bf16, late_packed,
                         pltpu.SemaphoreType.DMA((2,))],
         compiler_params=params(4), name="ask",
@@ -379,7 +395,7 @@
     up, half = list(range(1, outer)), outer // 2
     z1, z2 = up, up[half - 1:] + up[:half - 1]
     q1, q2 = list(range(inner - 1, 0, -1)), list(range(1, inner))
-    column = [ask] + [send_outer(ask, k) for k in z1]
+    column = [ask] + [send_outer(ask_long if k == outer - 1 else ask, k) for k in z1]
     wishes = gather_inner(facts)
 
     chunks = 8

time: 31.8 us -> 30.9 us (0.972)
  starting transfers between devices: 15.6 us -> 14.8 us
    ppermute x6, starting transfers between devices: 10.1 us -> 9.39 us  [send_outer(): lax.ppermute(x, 'req', [(o * inner + i, int(turn(o, k, outer)) * inner +...]
where the time goes in v8:
time: 30.9 us; the launch traced here: 30.8 us
  starting transfers between devices  14.8 us (48%)
  Pallas kernels  8.23 us (27%)
  waiting for transfers between devices  7.65 us (25%)
    ppermute x6, starting transfers between devices, send_outer(): lax.ppermute(x, 'req', [(o * inner + i, int(turn(o, k, outer)) * inner +...  9.39 us
    ppermute x8, waiting for transfers between devices, send_inner(): lax.ppermute(x, 'req', [(o * inner + i, o * inner + int(turn(i, k, inner)...  6.86 us
    ppermute x8, starting transfers between devices, send_inner(): lax.ppermute(x, 'req', [(o * inner + i, o * inner + int(turn(i, k, inner)...  5.37 us
    pallas_call x1, Pallas kernels, on_device(): pl.pallas_call(functools.partial(local_kernel, count=count, chunks=chunks...  3.49 us
    pallas_call x1, Pallas kernels, on_device(): pl.pallas_call(functools.partial(prepare_kernel, count=count, chunks=chun...  2.41 us
    pallas_call x1, Pallas kernels, on_device(): pl.pallas_call(functools.partial(ask_kernel, count=count, inner=inner), o...  0.91 us
    pallas_call x1, Pallas kernels, on_device(): pl.pallas_call(functools.partial(finish_kernel, count=count, heads=heads)...  0.9 us
    ppermute x6, waiting for transfers between devices, send_outer(): lax.ppermute(x, 'req', [(o * inner + i, int(turn(o, k, outer)) * inner +...  0.78 us
  transfers between devices with their start and end apart: 14, of which 7 were waited for; matrix products, arithmetic and copies ran while one was open for 0% of the time, Pallas kernels for 19%

profile of v8, /device:TPU:0, one launch (start us, length us, event | category | flops | bytes accessed | tf_op | source)
XLA Modules:
  0.0 30.8 jit_solution(5986447896577754734)
XLA Ops:
  0.0 0.9 %ask.1 = (f32[96,128]{1,0:T(8,128)S(1)}, f32[104,128]{1,0:T(8,128)S(1)}, s32[80,128]{1,0:T(8,128)S(1)}) custom-call(s32[2]{0:T(128)} %slots_ref.1, bf16[384,128]{1,0:T(8,128)(2,1)} %bitcast.26), custom_call_target="tpu_custom_call" | custom-call | tf_op jit(solution)/shard_map/ask/pallas_call | solution.py:386
  0.9 5.1 %collective-permute-start.4 = (f32[104,128]{1,0:T(8,128)S(1)}, f32[104,128]{1,0:T(8,128)S(1)}, u32[]{:S(2)}, u32[]{:S(2)}) collective-permute-start(f32[104,128]{1,0:T(8,128)S(1)} %get-tuple-element.23), channel_id=1, source_target_pairs={{0,12},{1,13},{2,14},{3,15},{4,8},{5,9},{6,10},{7,11},{8,4},{9,5},... | collective-permute-start | bytes 159752 | tf_op jit(solution)/shard_map/ppermute | solution.py:356
  6.1 0.7 %collective-permute-start.2 = (f32[96,128]{1,0:T(8,128)S(1)}, f32[96,128]{1,0:T(8,128)S(1)}, u32[]{:S(2)}, u32[]{:S(2)}) collective-permute-start(f32[96,128]{1,0:T(8,128)S(1)} %get-tuple-element.22.refs_0_), channel_id=1, source_target_pairs={{0,4},{1,5},{2,6},{3,7},{4,0},{5,1},{6,2},{7,3},{8,12},{9,13},{10,... | collective-permute-start | bytes 147464 | tf_op jit(solution)/shard_map/ppermute | solution.py:356
  6.8 0.5 %collective-permute-done.far_ref = s32[80,128]{1,0:T(8,128)S(1)} collective-permute-done((s32[80,128]{1,0:T(8,128)S(1)}, s32[80,128]{1,0:T(8,128)S(1)}, u32[]{:S(2)}, u32[]{:S(2)}) %collective-permute-start) | collective-permute-done | bytes 40992 | tf_op jit(solution)/shard_map/ppermute | solution.py:351
  7.3 1.5 %collective-permute-start.1 = (s32[16,128]{1,0:T(8,128)S(1)}, s32[16,128]{1,0:T(8,128)S(1)}, u32[]{:S(2)}, u32[]{:S(2)}) collective-permute-start(s32[16,128]{1,0:T(8,128)S(1)} %pair.2.near_ref), channel_id=1, source_target_pairs={{0,2},{1,3},{2,0},{3,1},{4,6},{5,7},{6,4},{7,5},{8,10},{9,11},{10,... | collective-permute-start | bytes 24584 | tf_op jit(solution)/shard_map/ppermute | solution.py:351
  8.8 2.1 %collective-permute-done.1.far_ref = s32[16,128]{1,0:T(8,128)S(1)} collective-permute-done((s32[16,128]{1,0:T(8,128)S(1)}, s32[16,128]{1,0:T(8,128)S(1)}, u32[]{:S(2)}, u32[]{:S(2)}) %collective-permute-start.1) | collective-permute-done | bytes 8224 | tf_op jit(solution)/shard_map/ppermute | solution.py:351
  10.9 0.3 %collective-permute-done.3.refs_2_ = f32[96,128]{1,0:T(8,128)S(1)} collective-permute-done((f32[96,128]{1,0:T(8,128)S(1)}, f32[96,128]{1,0:T(8,128)S(1)}, u32[]{:S(2)}, u32[]{:S(2)}) %collective-permute-start.3) | collective-permute-done | bytes 49184 | tf_op jit(solution)/shard_map/ppermute | solution.py:356
  11.3 0.8 %collective-permute-start.5 = (f32[96,128]{1,0:T(8,128)S(1)}, f32[96,128]{1,0:T(8,128)S(1)}, u32[]{:S(2)}, u32[]{:S(2)}) collective-permute-start(f32[96,128]{1,0:T(8,128)S(1)} %get-tuple-element.25), channel_id=1, source_target_pairs={{0,3},{1,2},{2,1},{3,0},{4,7},{5,6},{6,5},{7,4},{8,11},{9,10},{10,... | collective-permute-start | bytes 147464 | tf_op jit(solution)/shard_map/ppermute | solution.py:351
  12.2 0.8 %collective-permute-start.6 = (f32[96,128]{1,0:T(8,128)S(1)}, f32[96,128]{1,0:T(8,128)S(1)}, u32[]{:S(2)}, u32[]{:S(2)}) collective-permute-start(f32[96,128]{1,0:T(8,128)S(1)} %get-tuple-element.26), channel_id=1, source_target_pairs={{0,2},{1,3},{2,0},{3,1},{4,6},{5,7},{6,4},{7,5},{8,10},{9,11},{10,... | collective-permute-start | bytes 147464 | tf_op jit(solution)/shard_map/ppermute | solution.py:351
  13.0 0.3 collective-permute-start.7
  13.2 2.4 %prepare.1 = (bf16[32,256,128]{2,1,0:T(8,128)(2,1)S(1)}, f32[2,96,128]{2,1,0:T(8,128)S(1)}) custom-call(s32[2]{0:T(128)} %slots_ref.1, bf16[384,128]{1,0:T(8,128)(2,1)} %bitcast.28, bf16[384,128]{1,0:T(8,128)(2,1)} %bitcast.30, f32[2,32,128,128]{3,2,1,0:T(8,128)} %states_ref.3), custom_call_target="tpu_custom_call" | custom-call | tf_op jit(solution)/shard_map/prepare/pallas_call | solution.py:402
  15.7 1.0 %collective-permute-done.6.refs_2_ = f32[96,128]{1,0:T(8,128)S(1)} collective-permute-done((f32[96,128]{1,0:T(8,128)S(1)}, f32[96,128]{1,0:T(8,128)S(1)}, u32[]{:S(2)}, u32[]{:S(2)}) %collective-permute-start.6) | collective-permute-done | bytes 49184 | tf_op jit(solution)/shard_map/ppermute | solution.py:351
  16.7 0.4 %answer.1.refs_0_ = f32[96,128]{1,0:T(8,128)S(1)} custom-call(s32[80,128]{1,0:T(8,128)S(1)} %get-tuple-element.21.near_ref.facts_ref, f32[96,128]{1,0:T(8,128)S(1)} %get-tuple-element.24.refs_0_, f32[96,128]{1,0:T(8,128)S(1)} %collective-permute-done.5.refs_1_, f32[96,128]{1,0:T(8,128)S(1)} %collective-permute-done.6.refs_2_, ...), custom_call_target="tpu_custom_call" | custom-call | tf_op jit(solution)/shard_map/answer/pallas_call | solution.py:423
  17.1 0.8 %collective-permute-start.10 = (f32[96,128]{1,0:T(8,128)S(1)}, f32[96,128]{1,0:T(8,128)S(1)}, u32[]{:S(2)}, u32[]{:S(2)}) collective-permute-start(f32[96,128]{1,0:T(8,128)S(1)} %answer.1.refs_0_), channel_id=1, source_target_pairs={{0,3},{1,2},{2,1},{3,0},{4,7},{5,6},{6,5},{7,4},{8,11},{9,10},{10,... | collective-permute-start | bytes 147464 | tf_op jit(solution)/shard_map/ppermute | solution.py:351
  17.9 0.9 %collective-permute-start.9 = (f32[96,128]{1,0:T(8,128)S(1)}, f32[96,128]{1,0:T(8,128)S(1)}, u32[]{:S(2)}, u32[]{:S(2)}) collective-permute-start(f32[96,128]{1,0:T(8,128)S(1)} %answer.1.refs_0_), channel_id=1, source_target_pairs={{0,2},{1,3},{2,0},{3,1},{4,6},{5,7},{6,4},{7,5},{8,10},{9,11},{10,... | collective-permute-start | bytes 147464 | tf_op jit(solution)/shard_map/ppermute | solution.py:351
  18.8 0.2 collective-permute-start.8
  19.0 2.0 %collective-permute-done.10.refs_3_ = f32[96,128]{1,0:T(8,128)S(1)} collective-permute-done((f32[96,128]{1,0:T(8,128)S(1)}, f32[96,128]{1,0:T(8,128)S(1)}, u32[]{:S(2)}, u32[]{:S(2)}) %collective-permute-start.10) | collective-permute-done | bytes 49184 | tf_op jit(solution)/shard_map/ppermute | solution.py:351
  21.0 1.2 %collective-permute-done.9.refs_2_ = f32[96,128]{1,0:T(8,128)S(1)} collective-permute-done((f32[96,128]{1,0:T(8,128)S(1)}, f32[96,128]{1,0:T(8,128)S(1)}, u32[]{:S(2)}, u32[]{:S(2)}) %collective-permute-start.9) | collective-permute-done | bytes 49184 | tf_op jit(solution)/shard_map/ppermute | solution.py:351
  22.3 1.5 %collective-permute-start.11 = (f32[96,128]{1,0:T(8,128)S(1)}, f32[96,128]{1,0:T(8,128)S(1)}, u32[]{:S(2)}, u32[]{:S(2)}) collective-permute-start(f32[96,128]{1,0:T(8,128)S(1)} %get-tuple-element.34), channel_id=1, source_target_pairs={{0,8},{1,9},{2,10},{3,11},{4,12},{5,13},{6,14},{7,15},{8,0},{9,1},... | collective-permute-start | bytes 147464 | tf_op jit(solution)/shard_map/ppermute | solution.py:356
  23.9 1.3 %collective-permute-start.12 = (f32[96,128]{1,0:T(8,128)S(1)}, f32[96,128]{1,0:T(8,128)S(1)}, u32[]{:S(2)}, u32[]{:S(2)}) collective-permute-start(f32[96,128]{1,0:T(8,128)S(1)} %get-tuple-element.35), channel_id=1, source_target_pairs={{0,12},{1,13},{2,14},{3,15},{4,8},{5,9},{6,10},{7,11},{8,4},{9,5},... | collective-permute-start | bytes 147464 | tf_op jit(solution)/shard_map/ppermute | solution.py:356
  25.2 0.7 %collective-permute-start.13 = (f32[96,128]{1,0:T(8,128)S(1)}, f32[96,128]{1,0:T(8,128)S(1)}, u32[]{:S(2)}, u32[]{:S(2)}) collective-permute-start(f32[96,128]{1,0:T(8,128)S(1)} %get-tuple-element.36), channel_id=1, source_target_pairs={{0,4},{1,5},{2,6},{3,7},{4,0},{5,1},{6,2},{7,3},{8,12},{9,13},{10,... | collective-permute-start | bytes 147464 | tf_op jit(solution)/shard_map/ppermute | solution.py:356
  25.9 3.5 %local.1 = (bf16[384,128]{1,0:T(8,128)(2,1)}, bf16[192,128]{1,0:T(8,128)(2,1)S(1)}, f32[2,96,128]{2,1,0:T(8,128)S(1)}) custom-call(s32[80,128]{1,0:T(8,128)S(1)} %get-tuple-element.21.near_ref.facts_ref, bf16[384,128]{1,0:T(8,128)(2,1)S(1)} %bitcast.27, bf16[384,128]{1,0:T(8,128)(2,1)S(1)} %bitcast.29, bf16[384,128]{1,0:T(8,128)(2,1)S(1)} %bitcast.31, ...), custom_call_target="tpu_custom_call" | custom-call | tf_op jit(solution)/shard_map/local/pallas_call | solution.py:442
  29.4 0.4 %collective-permute-done.12.refs_1_ = f32[96,128]{1,0:T(8,128)S(1)} collective-permute-done((f32[96,128]{1,0:T(8,128)S(1)}, f32[96,128]{1,0:T(8,128)S(1)}, u32[]{:S(2)}, u32[]{:S(2)}) %collective-permute-start.12) | collective-permute-done | bytes 49184 | tf_op jit(solution)/shard_map/ppermute | solution.py:356
  29.9 0.9 %finish.1 = bf16[384,128]{1,0:T(8,128)(2,1)} custom-call(s32[80,128]{1,0:T(8,128)S(1)} %get-tuple-element.21.near_ref.facts_ref, bf16[384,128]{1,0:T(8,128)(2,1)} %get-tuple-element.31.base_ref, bf16[192,128]{1,0:T(8,128)(2,1)S(1)} %get-tuple-element.32.last_ref, f32[2,96,128]{2,1,0:T(8,128)S(1)} %get-tuple-element.33.late_ref, ...), custom_call_target="tpu_custom_call", output_to_operand_aliasing={{}: (1, {})} | custom-call | tf_op jit(solution)/shard_map/finish/pallas_call | solution.py:457
  (23 shorter events, 0.1 us)
Async XLA Ops:
  0.0 25.9 %copy-start = (bf16[2,6,4096]{2,0,1:T(2,128)(2,1)S(1)}, bf16[2,6,4096]{2,0,1:T(2,128)(2,1)}, u32[]{:S(2)}) copy-start(bf16[2,6,4096]{2,0,1:T(2,128)(2,1)} %param.7) | copy-start | bytes 294916
  0.0 25.9 %copy-start.2 = (bf16[2,6,4096]{2,0,1:T(2,128)(2,1)S(1)}, bf16[2,6,4096]{2,0,1:T(2,128)(2,1)}, u32[]{:S(2)}) copy-start(bf16[2,6,4096]{2,0,1:T(2,128)(2,1)} %param.9) | copy-start | bytes 294916
  0.0 25.9 %copy-start.1 = (bf16[2,6,4096]{2,0,1:T(2,128)(2,1)S(1)}, bf16[2,6,4096]{2,0,1:T(2,128)(2,1)}, u32[]{:S(2)}) copy-start(bf16[2,6,4096]{2,0,1:T(2,128)(2,1)} %param.8) | copy-start | bytes 294916
  0.0 25.9 %copy-start.4 = (f32[4096]{0:T(1024)S(1)}, f32[4096]{0:T(1024)}, u32[]{:S(2)}) copy-start(f32[4096]{0:T(1024)} %param.13) | copy-start | bytes 49156
  0.0 25.9 %copy-start.3 = (bf16[2,6,4096]{2,0,1:T(2,128)(2,1)S(1)}, bf16[2,6,4096]{2,0,1:T(2,128)(2,1)}, u32[]{:S(2)}) copy-start(bf16[2,6,4096]{2,0,1:T(2,128)(2,1)} %param.10) | copy-start | bytes 294916
  0.9 10.3 %collective-permute-start.4 = (f32[104,128]{1,0:T(8,128)S(1)}, f32[104,128]{1,0:T(8,128)S(1)}, u32[]{:S(2)}, u32[]{:S(2)}) collective-permute-start(f32[104,128]{1,0:T(8,128)S(1)} %get-tuple-element.23), channel_id=1, source_target_pairs={{0,12},{1,13},{2,14},{3,15},{4,8},{5,9},{6,10},{7,11},{8,4},{9,5},... | collective-permute-start | bytes 159752 | tf_op jit(solution)/shard_map/ppermute | solution.py:356
  6.1 1.2 %collective-permute-start = (s32[80,128]{1,0:T(8,128)S(1)}, s32[80,128]{1,0:T(8,128)S(1)}, u32[]{:S(2)}, u32[]{:S(2)}) collective-permute-start(s32[80,128]{1,0:T(8,128)S(1)} %get-tuple-element.21.near_ref.facts_ref), channel_id=1, source_target_pairs={{0,1},{1,0},{2,3},{3,2},{4,5},{5,4},{6,7},{7,6},{8,9},{9,8},{10,11... | collective-permute-start | bytes 122888 | tf_op jit(solution)/shard_map/ppermute | solution.py:351
  6.1 5.2 %collective-permute-start.3 = (f32[96,128]{1,0:T(8,128)S(1)}, f32[96,128]{1,0:T(8,128)S(1)}, u32[]{:S(2)}, u32[]{:S(2)}) collective-permute-start(f32[96,128]{1,0:T(8,128)S(1)} %get-tuple-element.22.refs_0_), channel_id=1, source_target_pairs={{0,8},{1,9},{2,10},{3,11},{4,12},{5,13},{6,14},{7,15},{8,0},{9,1},... | collective-permute-start | bytes 147464 | tf_op jit(solution)/shard_map/ppermute | solution.py:356
  6.1 5.2 %collective-permute-start.2 = (f32[96,128]{1,0:T(8,128)S(1)}, f32[96,128]{1,0:T(8,128)S(1)}, u32[]{:S(2)}, u32[]{:S(2)}) collective-permute-start(f32[96,128]{1,0:T(8,128)S(1)} %get-tuple-element.22.refs_0_), channel_id=1, source_target_pairs={{0,4},{1,5},{2,6},{3,7},{4,0},{5,1},{6,2},{7,3},{8,12},{9,13},{10,... | collective-permute-start | bytes 147464 | tf_op jit(solution)/shard_map/ppermute | solution.py:356
  7.3 3.7 %collective-permute-start.1 = (s32[16,128]{1,0:T(8,128)S(1)}, s32[16,128]{1,0:T(8,128)S(1)}, u32[]{:S(2)}, u32[]{:S(2)}) collective-permute-start(s32[16,128]{1,0:T(8,128)S(1)} %pair.2.near_ref), channel_id=1, source_target_pairs={{0,2},{1,3},{2,0},{3,1},{4,6},{5,7},{6,4},{7,5},{8,10},{9,11},{10,... | collective-permute-start | bytes 24584 | tf_op jit(solution)/shard_map/ppermute | solution.py:351
  11.3 4.3 %collective-permute-start.5 = (f32[96,128]{1,0:T(8,128)S(1)}, f32[96,128]{1,0:T(8,128)S(1)}, u32[]{:S(2)}, u32[]{:S(2)}) collective-permute-start(f32[96,128]{1,0:T(8,128)S(1)} %get-tuple-element.25), channel_id=1, source_target_pairs={{0,3},{1,2},{2,1},{3,0},{4,7},{5,6},{6,5},{7,4},{8,11},{9,10},{10,... | collective-permute-start | bytes 147464 | tf_op jit(solution)/shard_map/ppermute | solution.py:351
  12.2 4.5 %collective-permute-start.6 = (f32[96,128]{1,0:T(8,128)S(1)}, f32[96,128]{1,0:T(8,128)S(1)}, u32[]{:S(2)}, u32[]{:S(2)}) collective-permute-start(f32[96,128]{1,0:T(8,128)S(1)} %get-tuple-element.26), channel_id=1, source_target_pairs={{0,2},{1,3},{2,0},{3,1},{4,6},{5,7},{6,4},{7,5},{8,10},{9,11},{10,... | collective-permute-start | bytes 147464 | tf_op jit(solution)/shard_map/ppermute | solution.py:351
  13.0 3.7 %collective-permute-start.7 = (f32[96,128]{1,0:T(8,128)S(1)}, f32[96,128]{1,0:T(8,128)S(1)}, u32[]{:S(2)}, u32[]{:S(2)}) collective-permute-start(f32[96,128]{1,0:T(8,128)S(1)} %get-tuple-element.27), channel_id=1, source_target_pairs={{0,1},{1,0},{2,3},{3,2},{4,5},{5,4},{6,7},{7,6},{8,9},{9,8},{10,11... | collective-permute-start | bytes 147464 | tf_op jit(solution)/shard_map/ppermute | solution.py:351
  17.1 3.9 %collective-permute-start.10 = (f32[96,128]{1,0:T(8,128)S(1)}, f32[96,128]{1,0:T(8,128)S(1)}, u32[]{:S(2)}, u32[]{:S(2)}) collective-permute-start(f32[96,128]{1,0:T(8,128)S(1)} %answer.1.refs_0_), channel_id=1, source_target_pairs={{0,3},{1,2},{2,1},{3,0},{4,7},{5,6},{6,5},{7,4},{8,11},{9,10},{10,... | collective-permute-start | bytes 147464 | tf_op jit(solution)/shard_map/ppermute | solution.py:351
  17.9 4.4 %collective-permute-start.9 = (f32[96,128]{1,0:T(8,128)S(1)}, f32[96,128]{1,0:T(8,128)S(1)}, u32[]{:S(2)}, u32[]{:S(2)}) collective-permute-start(f32[96,128]{1,0:T(8,128)S(1)} %answer.1.refs_0_), channel_id=1, source_target_pairs={{0,2},{1,3},{2,0},{3,1},{4,6},{5,7},{6,4},{7,5},{8,10},{9,11},{10,... | collective-permute-start | bytes 147464 | tf_op jit(solution)/shard_map/ppermute | solution.py:351
  18.8 3.5 %collective-permute-start.8 = (f32[96,128]{1,0:T(8,128)S(1)}, f32[96,128]{1,0:T(8,128)S(1)}, u32[]{:S(2)}, u32[]{:S(2)}) collective-permute-start(f32[96,128]{1,0:T(8,128)S(1)} %answer.1.refs_0_), channel_id=1, source_target_pairs={{0,1},{1,0},{2,3},{3,2},{4,5},{5,4},{6,7},{7,6},{8,9},{9,8},{10,11... | collective-permute-start | bytes 147464 | tf_op jit(solution)/shard_map/ppermute | solution.py:351
  22.3 7.1 %collective-permute-start.11 = (f32[96,128]{1,0:T(8,128)S(1)}, f32[96,128]{1,0:T(8,128)S(1)}, u32[]{:S(2)}, u32[]{:S(2)}) collective-permute-start(f32[96,128]{1,0:T(8,128)S(1)} %get-tuple-element.34), channel_id=1, source_target_pairs={{0,8},{1,9},{2,10},{3,11},{4,12},{5,13},{6,14},{7,15},{8,0},{9,1},... | collective-permute-start | bytes 147464 | tf_op jit(solution)/shard_map/ppermute | solution.py:356
  23.9 6.0 %collective-permute-start.12 = (f32[96,128]{1,0:T(8,128)S(1)}, f32[96,128]{1,0:T(8,128)S(1)}, u32[]{:S(2)}, u32[]{:S(2)}) collective-permute-start(f32[96,128]{1,0:T(8,128)S(1)} %get-tuple-element.35), channel_id=1, source_target_pairs={{0,12},{1,13},{2,14},{3,15},{4,8},{5,9},{6,10},{7,11},{8,4},{9,5},... | collective-permute-start | bytes 147464 | tf_op jit(solution)/shard_map/ppermute | solution.py:356
  25.2 4.7 %collective-permute-start.13 = (f32[96,128]{1,0:T(8,128)S(1)}, f32[96,128]{1,0:T(8,128)S(1)}, u32[]{:S(2)}, u32[]{:S(2)}) collective-permute-start(f32[96,128]{1,0:T(8,128)S(1)} %get-tuple-element.36), channel_id=1, source_target_pairs={{0,4},{1,5},{2,6},{3,7},{4,0},{5,1},{6,2},{7,3},{8,12},{9,13},{10,... | collective-permute-start | bytes 147464 | tf_op jit(solution)/shard_map/ppermute | solution.py:356

commit v9 on v8

--- a/solution.py
+++ b/solution.py
@@ -15,6 +15,7 @@
 VMEM = pl.BlockSpec(memory_space=pltpu.VMEM)
 SMEM = pl.BlockSpec(memory_space=pltpu.SMEM)
 HBM = pl.BlockSpec(memory_space=pltpu.HBM)
+ANY = pl.BlockSpec(memory_space=pl.ANY)
 
 
 def silu(x):
@@ -202,7 +203,7 @@
         out_ref[t * heads:(t + 1) * heads, :] = total
 
 
-def reply_kernel(wishes_ref, *refs, inner, outer, order):
+def reply_kernel(wishes_ref, after_ref, *refs, inner, outer, order):
     replies, outs = in_steps(refs[:inner], order), refs[inner:]
     me = lax.axis_index("req")
     my_inner, my_outer = lax.rem(me, inner), lax.div(me, inner)
@@ -218,22 +219,52 @@
         outs[k][...] = result
 
 
-def local_kernel(facts_ref, queries_ref, keys_ref, values_ref, gates_ref, gain_ref, own_ref,
-                 states_ref, out_ref, last_ref, late_ref, state, lhs, prod, wide, sems, *, count, chunks):
+def load_states(states_ref, state, sems, slots, chunks):
+    size = states_ref.shape[1] // chunks
+
+    def load(n, c):
+        part = pl.ds(c * size, size)
+        return pltpu.make_async_copy(
+            states_ref.at[slots[n], part], state.at[n, part], sems.at[n, c])
+
+    for n in range(len(slots)):
+        for c in range(chunks):
+            load(n, c).start()
+    return load
+
+
+def times_states(load, state, lhs, prod, slots, count, chunks):
+    heads = state.shape[1]
+    size = heads // chunks
+    for n, slot in enumerate(slots):
+        for c in range(chunks):
+            load(n, c).wait()
+            for h in range(c * size, (c + 1) * size):
+                rows = pl.ds(h * count + slot, 16, stride=heads * count)
+                x = lhs[rows, :].astype(BF16)
+                prod[rows, :] = jnp.dot(
+                    jnp.concatenate([x, x], axis=1),
+                    jnp.concatenate(split(state[n, h]), axis=0),
+                    preferred_element_type=F32)
+
+
+def row_slot(span, count):
+    return lax.rem(lax.broadcasted_iota(jnp.int32, (span, 1), 0), jnp.int32(count))
+
+
+def block(ref, t, rows):
+    return ref[t * rows:(t + 1) * rows, :]
+
+
+def scores_kernel(facts_ref, queries_ref, keys_ref, values_ref, gates_ref, gain_ref, after_ref,
+                  states_ref, mixed_ref, scale_ref, late_ref, lhs, state, prod, wide, sems,
+                  *, slots, count, chunks):
     heads, width = states_ref.shape[1], states_ref.shape[2]
     span = heads * count
     steps = queries_ref.shape[0] // span
     late = steps - BEFORE
-    size = heads // chunks
     place = fact(facts_ref, 0, SLOT, late * heads)
-
-    def load(j, c):
-        part = pl.ds(c * size, size)
-        return pltpu.make_async_copy(states_ref.at[j, part], state.at[j, part], sems.at[j, c])
-
-    for j in range(count):
-        for c in range(chunks):
-            load(j, c).start()
+    load = load_states(states_ref, state, sems, slots, chunks)
 
     def spread(x):
         for s in range(count):
@@ -243,16 +274,14 @@
     slope = spread(head_slope(heads, width))
     gain = spread(gain_ref[...])
     decay = [decay_power(slope, p) for p in range(steps + 1)]
-    block = lambda ref, t: ref[t * span:(t + 1) * span, :]
-    q = [silu(block(queries_ref, t).astype(F32)) for t in range(steps)]
-    k = [silu(block(keys_ref, t).astype(F32)) for t in range(steps)]
-    v = [silu(block(values_ref, t).astype(F32)) for t in range(steps)]
+    q = [silu(block(queries_ref, t, span).astype(F32)) for t in range(steps)]
+    k = [silu(block(keys_ref, t, span).astype(F32)) for t in range(steps)]
+    v = [silu(block(values_ref, t, span).astype(F32)) for t in range(steps)]
     for t in range(steps):
         x = q[t] * decay[t + 1]
         high = x.astype(BF16).astype(F32)
         lhs[t * span:(t + 1) * span, :] = high
         lhs[(8 + t) * span:(9 + t) * span, :] = x - high
-    mixed = []
     for t in range(steps):
         total = None
         far = None
@@ -265,32 +294,42 @@
                 total = term if total is None else total + term
         if t >= BEFORE:
             wide[(t - BEFORE) * span:(t - BEFORE + 1) * span, :] = total
-        mixed.append(total if far is None else total + far)
-    late_ref[0] = extract(wide, place, count) + own_ref[...]
-    scale = [gain * sigmoid(block(gates_ref, t).astype(F32)) for t in range(steps)]
-    for t in range(late):
-        wide[t * span:(t + 1) * span, :] = scale[BEFORE + t]
+        mixed_ref[t * span:(t + 1) * span, :] = total if far is None else total + far
+    late_ref[0] = extract(wide, place, count)
+    for t in range(steps):
+        scale = gain * sigmoid(block(gates_ref, t, span).astype(F32))
+        scale_ref[t * span:(t + 1) * span, :] = scale
+        if t >= BEFORE:
+            wide[(t - BEFORE) * span:(t - BEFORE + 1) * span, :] = scale
     late_ref[1] = extract(wide, place, count)
-    for j in range(count):
-        for c in range(chunks):
-            load(j, c).wait()
-            for h in range(c * size, (c + 1) * size):
-                rows = pl.ds(h * count + j, 16, stride=span)
-                x = lhs[rows, :].astype(BF16)
-                prod[rows, :] = jnp.dot(
-                    jnp.concatenate([x, x], axis=1),
-                    jnp.concatenate(split(state[j, h]), axis=0),
-                    preferred_element_type=F32)
-    slot = lax.rem(lax.broadcasted_iota(jnp.int32, (span, 1), 0), jnp.int32(count))
+    times_states(load, state, lhs, prod, slots, count, chunks)
+    slot = row_slot(span, count)
     for t in range(steps):
-        x = mixed[t] + block(prod, t) + block(prod, 8 + t)
+        x = block(prod, t, span) + block(prod, 8 + t, span)
+        for s in slots:
+            rows = slice(t * span, (t + 1) * span)
+            mixed_ref[rows, :] = mixed_ref[rows, :] + jnp.where(slot == s, x, 0.0)
+
+
+def local_kernel(mixed_ref, scale_ref, lhs, after_ref, states_ref, out_ref, last_ref, state, prod,
+                 sems, *, slots, count, chunks):
+    heads, width = states_ref.shape[1], states_ref.shape[2]
+    span = heads * count
+    steps = mixed_ref.shape[0] // span
+    load = load_states(states_ref, state, sems, slots, chunks)
+    times_states(load, state, lhs, prod, slots, count, chunks)
+    slot = row_slot(span, count)
+    for t in range(steps):
+        x = block(mixed_ref, t, span)
+        for s in slots:
+            x = x + jnp.where(slot == s, block(prod, t, span) + block(prod, 8 + t, span), 0.0)
         sums = jnp.sum(x * x, axis=1, keepdims=True)
         energy = jnp.zeros((span, 1), F32)
         for s in range(count):
             whole = jnp.sum(jnp.where(slot == s, sums, 0.0), axis=0, keepdims=True)
             energy = jnp.where(slot == s, whole, energy)
         factor = lax.rsqrt(energy * (1.0 / (heads * width)) + EPS)
-        y = (x * factor * scale[t]).astype(BF16)
+        y = (x * factor * block(scale_ref, t, span)).astype(BF16)
         out_ref[t * span:(t + 1) * span, :] = y
         if t >= BEFORE:
             last_ref[(t - BEFORE) * span:(t - BEFORE + 1) * span, :] = y
@@ -308,7 +347,8 @@
         x = late_ref[0, part, :]
         for ref in parts:
             x = x + ref[part, :]
-        y = x * lax.rsqrt(jnp.mean(x * x) + EPS) * late_ref[1, part, :]
+        energy = jnp.sum(jnp.sum(x * x, axis=0, keepdims=True), axis=1, keepdims=True)
+        y = x * lax.rsqrt(energy * (1.0 / x.size) + EPS) * late_ref[1, part, :]
         rows = slice(t * span, (t + 1) * span)
         wide[rows, :] = last_ref[rows, :].astype(F32)
         for s in range(count):
@@ -429,38 +469,52 @@
     )(facts, *found, weight, early)
     replies = [answer] + [send_inner(answer, k) for k in q2]
 
+    chunks = 4
+    first_slots, last_slots = list(range(count // 2)), list(range(count // 2, count))
+    packed = jax.ShapeDtypeStruct((packed_rows, width), F32)
+    products = jax.ShapeDtypeStruct((16 * heads * count, width), F32)
+    mixed, scale, partial, lhs = pl.pallas_call(
+        functools.partial(scores_kernel, slots=first_slots, count=count, chunks=chunks),
+        out_shape=(packed, packed, jax.ShapeDtypeStruct((2, single_rows, width), F32), products),
+        in_specs=[VMEM] * 6 + [ANY, HBM], out_specs=(VMEM,) * 4,
+        scratch_shapes=[
+            pltpu.VMEM((max(len(first_slots), 1), heads, width, width), F32),
+            pltpu.VMEM(products.shape, F32),
+            late_packed,
+            pltpu.SemaphoreType.DMA((max(len(first_slots), 1), chunks)),
+        ],
+        compiler_params=params(16), name="scores",
+    )(facts, queries, keys, values, gates, norm_gain.reshape(heads, width), answer,
+      in_hbm(states))
+
     sorted_replies = pl.pallas_call(
         functools.partial(reply_kernel, inner=inner, outer=outer, order=q2),
         out_shape=(single,) * outer,
-        in_specs=[VMEM] * (1 + inner), out_specs=(VMEM,) * outer,
+        in_specs=[VMEM, ANY] + [VMEM] * inner, out_specs=(VMEM,) * outer,
         compiler_params=params(4), name="reply",
-    )(wishes, *replies)
+    )(wishes, partial, *replies)
     parts = [send_outer(sorted_replies[k], k) for k in z2]
 
-    chunks = 4
     output = jax.ShapeDtypeStruct((packed_rows, width), BF16)
-    base, last, partial = pl.pallas_call(
-        functools.partial(local_kernel, count=count, chunks=chunks),
-        out_shape=(pltpu.HBM(output.shape, output.dtype), late_rows, jax.ShapeDtypeStruct((2, single_rows, width), F32)),
-        in_specs=[VMEM] * 7 + [HBM], out_specs=(VMEM, VMEM, VMEM),
+    base, last = pl.pallas_call(
+        functools.partial(local_kernel, slots=last_slots, count=count, chunks=chunks),
+        out_shape=(pltpu.HBM(output.shape, output.dtype), late_rows),
+        in_specs=[VMEM] * 3 + [ANY, HBM], out_specs=(VMEM, VMEM),
         scratch_shapes=[
-            pltpu.VMEM((count, heads, width, width), F32),
-            pltpu.VMEM((16 * heads * count, width), F32),
-            pltpu.VMEM((16 * heads * count, width), F32),
-            late_packed,
-            pltpu.SemaphoreType.DMA((count, chunks)),
+            pltpu.VMEM((len(last_slots), heads, width, width), F32),
+            pltpu.VMEM(products.shape, F32),
+            pltpu.SemaphoreType.DMA((len(last_slots), chunks)),
         ],
         compiler_params=params(16), name="local",
-    )(facts, queries, keys, values, gates, norm_gain.reshape(heads, width),
-      sorted_replies[0], in_hbm(states))
+    )(mixed, scale, lhs, sorted_replies[0], in_hbm(states))
 
     return unpack(pl.pallas_call(
         functools.partial(finish_kernel, count=count, heads=heads),
-        out_shape=output, in_specs=[VMEM, HBM] + [VMEM] * (outer + 1), out_specs=HBM,
+        out_shape=output, in_specs=[VMEM, HBM] + [VMEM] * (outer + 2), out_specs=HBM,
         scratch_shapes=[late_bf16, late_packed, pltpu.SemaphoreType.DMA((late,))],
         input_output_aliases={1: 0},
         compiler_params=params(4), name="finish",
-    )(facts, in_hbm(base), last, partial, *parts))
+    )(facts, in_hbm(base), last, partial, sorted_replies[0], *parts))
 
 
 def solution(mesh):

time: 30.9 us -> 30.8 us (level)
  waiting for transfers between devices: 7.65 us -> 6.54 us
  Pallas kernels: 8.23 us -> 9.21 us
    ppermute x8, waiting for transfers between devices: 6.86 us -> 4.9 us  [send_inner(): lax.ppermute(x, 'req', [(o * inner + i, o * inner + int(turn(i, k, inner)...]
    pallas_call x1 -> x2, Pallas kernels: 3.49 us -> 4.6 us  [the longest x1 2.67 us: on_device(): pl.pallas_call(functools.partial(local_kernel, slots=last_slots, count=co...]
    ppermute x6, waiting for transfers between devices: 0.78 us -> 1.64 us  [send_outer(): lax.ppermute(x, 'req', [(o * inner + i, int(turn(o, k, outer)) * inner +...]
  transfers between devices with their start and end apart: 14 -> 14, of which waited for: 7 -> 7; matrix products, arithmetic and copies ran while one was open for 0% -> 0% of each run, Pallas kernels for 19% -> 23%
where the time goes in v9:
time: 30.8 us; the launch traced here: 30.6 us
  starting transfers between devices  14.8 us (48%)
  Pallas kernels  9.21 us (30%)
  waiting for transfers between devices  6.54 us (21%)
    ppermute x6, starting transfers between devices, send_outer(): lax.ppermute(x, 'req', [(o * inner + i, int(turn(o, k, outer)) * inner +...  9.39 us
    ppermute x8, starting transfers between devices, send_inner(): lax.ppermute(x, 'req', [(o * inner + i, o * inner + int(turn(i, k, inner)...  5.37 us
    ppermute x8, waiting for transfers between devices, send_inner(): lax.ppermute(x, 'req', [(o * inner + i, o * inner + int(turn(i, k, inner)...  4.9 us
    pallas_call x1, Pallas kernels, on_device(): pl.pallas_call(functools.partial(local_kernel, slots=last_slots, count=co...  2.67 us
    pallas_call x1, Pallas kernels, on_device(): pl.pallas_call(functools.partial(prepare_kernel, count=count, chunks=chun...  2.41 us
    pallas_call x1, Pallas kernels, on_device(): pl.pallas_call(functools.partial(scores_kernel, slots=first_slots, count=...  1.93 us
    ppermute x6, waiting for transfers between devices, send_outer(): lax.ppermute(x, 'req', [(o * inner + i, int(turn(o, k, outer)) * inner +...  1.64 us
    pallas_call x1, Pallas kernels, on_device(): pl.pallas_call(functools.partial(ask_kernel, count=count, inner=inner), o...  0.91 us
  transfers between devices with their start and end apart: 14, of which 7 were waited for; matrix products, arithmetic and copies ran while one was open for 0% of the time, Pallas kernels for 23%

profile of v9, /device:TPU:0, one launch (start us, length us, event | category | flops | bytes accessed | tf_op | source)
XLA Modules:
  0.0 30.6 jit_solution(15973873790103197462)
XLA Ops:
  0.0 0.9 %ask.1 = (f32[96,128]{1,0:T(8,128)S(1)}, f32[104,128]{1,0:T(8,128)S(1)}, s32[80,128]{1,0:T(8,128)S(1)}) custom-call(s32[2]{0:T(128)} %slots_ref.1, bf16[384,128]{1,0:T(8,128)(2,1)} %bitcast.26), custom_call_target="tpu_custom_call" | custom-call | tf_op jit(solution)/shard_map/ask/pallas_call | solution.py:426
  0.9 5.1 %collective-permute-start.4 = (f32[104,128]{1,0:T(8,128)S(1)}, f32[104,128]{1,0:T(8,128)S(1)}, u32[]{:S(2)}, u32[]{:S(2)}) collective-permute-start(f32[104,128]{1,0:T(8,128)S(1)} %get-tuple-element.26), channel_id=1, source_target_pairs={{0,12},{1,13},{2,14},{3,15},{4,8},{5,9},{6,10},{7,11},{8,4},{9,5},... | collective-permute-start | bytes 159752 | tf_op jit(solution)/shard_map/ppermute | solution.py:396
  6.1 0.7 %collective-permute-start.2 = (f32[96,128]{1,0:T(8,128)S(1)}, f32[96,128]{1,0:T(8,128)S(1)}, u32[]{:S(2)}, u32[]{:S(2)}) collective-permute-start(f32[96,128]{1,0:T(8,128)S(1)} %get-tuple-element.25.refs_0_), channel_id=1, source_target_pairs={{0,4},{1,5},{2,6},{3,7},{4,0},{5,1},{6,2},{7,3},{8,12},{9,13},{10,... | collective-permute-start | bytes 147464 | tf_op jit(solution)/shard_map/ppermute | solution.py:396
  6.8 0.5 %collective-permute-done.far_ref = s32[80,128]{1,0:T(8,128)S(1)} collective-permute-done((s32[80,128]{1,0:T(8,128)S(1)}, s32[80,128]{1,0:T(8,128)S(1)}, u32[]{:S(2)}, u32[]{:S(2)}) %collective-permute-start) | collective-permute-done | bytes 40992 | tf_op jit(solution)/shard_map/ppermute | solution.py:391
  7.3 1.5 %collective-permute-start.1 = (s32[16,128]{1,0:T(8,128)S(1)}, s32[16,128]{1,0:T(8,128)S(1)}, u32[]{:S(2)}, u32[]{:S(2)}) collective-permute-start(s32[16,128]{1,0:T(8,128)S(1)} %pair.2.near_ref), channel_id=1, source_target_pairs={{0,2},{1,3},{2,0},{3,1},{4,6},{5,7},{6,4},{7,5},{8,10},{9,11},{10,... | collective-permute-start | bytes 24584 | tf_op jit(solution)/shard_map/ppermute | solution.py:391
  8.8 2.1 %collective-permute-done.1.far_ref = s32[16,128]{1,0:T(8,128)S(1)} collective-permute-done((s32[16,128]{1,0:T(8,128)S(1)}, s32[16,128]{1,0:T(8,128)S(1)}, u32[]{:S(2)}, u32[]{:S(2)}) %collective-permute-start.1) | collective-permute-done | bytes 8224 | tf_op jit(solution)/shard_map/ppermute | solution.py:391
  10.9 0.3 %collective-permute-done.3.refs_2_ = f32[96,128]{1,0:T(8,128)S(1)} collective-permute-done((f32[96,128]{1,0:T(8,128)S(1)}, f32[96,128]{1,0:T(8,128)S(1)}, u32[]{:S(2)}, u32[]{:S(2)}) %collective-permute-start.3) | collective-permute-done | bytes 49184 | tf_op jit(solution)/shard_map/ppermute | solution.py:396
  11.3 0.8 %collective-permute-start.5 = (f32[96,128]{1,0:T(8,128)S(1)}, f32[96,128]{1,0:T(8,128)S(1)}, u32[]{:S(2)}, u32[]{:S(2)}) collective-permute-start(f32[96,128]{1,0:T(8,128)S(1)} %get-tuple-element.28), channel_id=1, source_target_pairs={{0,3},{1,2},{2,1},{3,0},{4,7},{5,6},{6,5},{7,4},{8,11},{9,10},{10,... | collective-permute-start | bytes 147464 | tf_op jit(solution)/shard_map/ppermute | solution.py:391
  12.2 0.8 %collective-permute-start.6 = (f32[96,128]{1,0:T(8,128)S(1)}, f32[96,128]{1,0:T(8,128)S(1)}, u32[]{:S(2)}, u32[]{:S(2)}) collective-permute-start(f32[96,128]{1,0:T(8,128)S(1)} %get-tuple-element.29), channel_id=1, source_target_pairs={{0,2},{1,3},{2,0},{3,1},{4,6},{5,7},{6,4},{7,5},{8,10},{9,11},{10,... | collective-permute-start | bytes 147464 | tf_op jit(solution)/shard_map/ppermute | solution.py:391
  13.0 0.3 collective-permute-start.7
  13.2 2.4 %prepare.1 = (bf16[32,256,128]{2,1,0:T(8,128)(2,1)S(1)}, f32[2,96,128]{2,1,0:T(8,128)S(1)}) custom-call(s32[2]{0:T(128)} %slots_ref.1, bf16[384,128]{1,0:T(8,128)(2,1)} %bitcast.28, bf16[384,128]{1,0:T(8,128)(2,1)} %bitcast.30, f32[2,32,128,128]{3,2,1,0:T(8,128)} %states_ref.5), custom_call_target="tpu_custom_call" | custom-call | tf_op jit(solution)/shard_map/prepare/pallas_call | solution.py:442
  15.7 1.0 %collective-permute-done.6.refs_2_ = f32[96,128]{1,0:T(8,128)S(1)} collective-permute-done((f32[96,128]{1,0:T(8,128)S(1)}, f32[96,128]{1,0:T(8,128)S(1)}, u32[]{:S(2)}, u32[]{:S(2)}) %collective-permute-start.6) | collective-permute-done | bytes 49184 | tf_op jit(solution)/shard_map/ppermute | solution.py:391
  16.7 0.5 %answer.1.after_ref.refs_0_ = f32[96,128]{1,0:T(8,128)S(1)} custom-call(s32[80,128]{1,0:T(8,128)S(1)} %get-tuple-element.24.near_ref.facts_ref, f32[96,128]{1,0:T(8,128)S(1)} %get-tuple-element.27.refs_0_, f32[96,128]{1,0:T(8,128)S(1)} %collective-permute-done.5.refs_1_, f32[96,128]{1,0:T(8,128)S(1)} %collective-permute-done.6.refs_2_, ...), custom_call_target="tpu_custom_call" | custom-call | tf_op jit(solution)/shard_map/answer/pallas_call | solution.py:463
  17.1 0.8 %collective-permute-start.10 = (f32[96,128]{1,0:T(8,128)S(1)}, f32[96,128]{1,0:T(8,128)S(1)}, u32[]{:S(2)}, u32[]{:S(2)}) collective-permute-start(f32[96,128]{1,0:T(8,128)S(1)} %answer.1.after_ref.refs_0_), channel_id=1, source_target_pairs={{0,3},{1,2},{2,1},{3,0},{4,7},{5,6},{6,5},{7,4},{8,11},{9,10},{10,... | collective-permute-start | bytes 147464 | tf_op jit(solution)/shard_map/ppermute | solution.py:391
  17.9 0.9 %collective-permute-start.9 = (f32[96,128]{1,0:T(8,128)S(1)}, f32[96,128]{1,0:T(8,128)S(1)}, u32[]{:S(2)}, u32[]{:S(2)}) collective-permute-start(f32[96,128]{1,0:T(8,128)S(1)} %answer.1.after_ref.refs_0_), channel_id=1, source_target_pairs={{0,2},{1,3},{2,0},{3,1},{4,6},{5,7},{6,4},{7,5},{8,10},{9,11},{10,... | collective-permute-start | bytes 147464 | tf_op jit(solution)/shard_map/ppermute | solution.py:391
  19.1 1.9 %scores.1 = (f32[384,128]{1,0:T(8,128)S(1)}, f32[384,128]{1,0:T(8,128)S(1)}, f32[2,96,128]{2,1,0:T(8,128)S(1)}, f32[1024,128]{1,0:T(8,128)S(1)}) custom-call(s32[80,128]{1,0:T(8,128)S(1)} %get-tuple-element.24.near_ref.facts_ref, bf16[384,128]{1,0:T(8,128)(2,1)S(1)} %bitcast.27, bf16[384,128]{1,0:T(8,128)(2,1)S(1)} %bitcast.29, ...), custom_call_target="tpu_custom_call" | custom-call | tf_op jit(solution)/shard_map/scores/pallas_call | solution.py:476
  21.1 1.2 %collective-permute-done.9.refs_2_ = f32[96,128]{1,0:T(8,128)S(1)} collective-permute-done((f32[96,128]{1,0:T(8,128)S(1)}, f32[96,128]{1,0:T(8,128)S(1)}, u32[]{:S(2)}, u32[]{:S(2)}) %collective-permute-start.9) | collective-permute-done | bytes 49184 | tf_op jit(solution)/shard_map/ppermute | solution.py:391
  22.3 1.5 %collective-permute-start.11 = (f32[96,128]{1,0:T(8,128)S(1)}, f32[96,128]{1,0:T(8,128)S(1)}, u32[]{:S(2)}, u32[]{:S(2)}) collective-permute-start(f32[96,128]{1,0:T(8,128)S(1)} %get-tuple-element.40), channel_id=1, source_target_pairs={{0,8},{1,9},{2,10},{3,11},{4,12},{5,13},{6,14},{7,15},{8,0},{9,1},... | collective-permute-start | bytes 147464 | tf_op jit(solution)/shard_map/ppermute | solution.py:396
  23.9 1.3 %collective-permute-start.12 = (f32[96,128]{1,0:T(8,128)S(1)}, f32[96,128]{1,0:T(8,128)S(1)}, u32[]{:S(2)}, u32[]{:S(2)}) collective-permute-start(f32[96,128]{1,0:T(8,128)S(1)} %get-tuple-element.41), channel_id=1, source_target_pairs={{0,12},{1,13},{2,14},{3,15},{4,8},{5,9},{6,10},{7,11},{8,4},{9,5},... | collective-permute-start | bytes 147464 | tf_op jit(solution)/shard_map/ppermute | solution.py:396
  25.2 0.7 %collective-permute-start.13 = (f32[96,128]{1,0:T(8,128)S(1)}, f32[96,128]{1,0:T(8,128)S(1)}, u32[]{:S(2)}, u32[]{:S(2)}) collective-permute-start(f32[96,128]{1,0:T(8,128)S(1)} %get-tuple-element.42), channel_id=1, source_target_pairs={{0,4},{1,5},{2,6},{3,7},{4,0},{5,1},{6,2},{7,3},{8,12},{9,13},{10,... | collective-permute-start | bytes 147464 | tf_op jit(solution)/shard_map/ppermute | solution.py:396
  25.9 2.7 %local.1 = (bf16[384,128]{1,0:T(8,128)(2,1)}, bf16[192,128]{1,0:T(8,128)(2,1)S(1)}) custom-call(f32[384,128]{1,0:T(8,128)S(1)} %get-tuple-element.33.mixed_ref, f32[384,128]{1,0:T(8,128)S(1)} %get-tuple-element.34.scale_ref, f32[1024,128]{1,0:T(8,128)S(1)} %get-tuple-element.35.lhs, f32[96,128]{1,0:T(8,128)S(1)} %get-tuple-element.37.after_ref.refs_0_, ...), custom_call_target="tpu_custom_call" | custom-call | tf_op jit(solution)/shard_map/local/pallas_call | solution.py:499
  28.6 0.3 collective-permute-done.11.refs_1_
  28.8 1.0 %collective-permute-done.12.refs_2_ = f32[96,128]{1,0:T(8,128)S(1)} collective-permute-done((f32[96,128]{1,0:T(8,128)S(1)}, f32[96,128]{1,0:T(8,128)S(1)}, u32[]{:S(2)}, u32[]{:S(2)}) %collective-permute-start.12) | collective-permute-done | bytes 49184 | tf_op jit(solution)/shard_map/ppermute | solution.py:396
  29.9 0.8 %finish.1 = bf16[384,128]{1,0:T(8,128)(2,1)} custom-call(s32[80,128]{1,0:T(8,128)S(1)} %get-tuple-element.24.near_ref.facts_ref, bf16[384,128]{1,0:T(8,128)(2,1)} %get-tuple-element.38.base_ref, bf16[192,128]{1,0:T(8,128)(2,1)S(1)} %get-tuple-element.39.last_ref, ...), custom_call_target="tpu_custom_call", output_to_operand_aliasing={{}: (1, {})} | custom-call | tf_op jit(solution)/shard_map/finish/pallas_call | solution.py:511
  (24 shorter events, 0.4 us)
Async XLA Ops:
  0.0 19.0 %copy-start = (bf16[2,6,4096]{2,0,1:T(2,128)(2,1)S(1)}, bf16[2,6,4096]{2,0,1:T(2,128)(2,1)}, u32[]{:S(2)}) copy-start(bf16[2,6,4096]{2,0,1:T(2,128)(2,1)} %param.7) | copy-start | bytes 294916
  0.0 19.1 %copy-start.2 = (bf16[2,6,4096]{2,0,1:T(2,128)(2,1)S(1)}, bf16[2,6,4096]{2,0,1:T(2,128)(2,1)}, u32[]{:S(2)}) copy-start(bf16[2,6,4096]{2,0,1:T(2,128)(2,1)} %param.9) | copy-start | bytes 294916
  0.0 19.1 %copy-start.1 = (bf16[2,6,4096]{2,0,1:T(2,128)(2,1)S(1)}, bf16[2,6,4096]{2,0,1:T(2,128)(2,1)}, u32[]{:S(2)}) copy-start(bf16[2,6,4096]{2,0,1:T(2,128)(2,1)} %param.8) | copy-start | bytes 294916
  0.0 19.1 %copy-start.4 = (f32[4096]{0:T(1024)S(1)}, f32[4096]{0:T(1024)}, u32[]{:S(2)}) copy-start(f32[4096]{0:T(1024)} %param.13) | copy-start | bytes 49156
  0.0 19.1 %copy-start.3 = (bf16[2,6,4096]{2,0,1:T(2,128)(2,1)S(1)}, bf16[2,6,4096]{2,0,1:T(2,128)(2,1)}, u32[]{:S(2)}) copy-start(bf16[2,6,4096]{2,0,1:T(2,128)(2,1)} %param.10) | copy-start | bytes 294916
  0.9 10.3 %collective-permute-start.4 = (f32[104,128]{1,0:T(8,128)S(1)}, f32[104,128]{1,0:T(8,128)S(1)}, u32[]{:S(2)}, u32[]{:S(2)}) collective-permute-start(f32[104,128]{1,0:T(8,128)S(1)} %get-tuple-element.26), channel_id=1, source_target_pairs={{0,12},{1,13},{2,14},{3,15},{4,8},{5,9},{6,10},{7,11},{8,4},{9,5},... | collective-permute-start | bytes 159752 | tf_op jit(solution)/shard_map/ppermute | solution.py:396
  6.1 1.2 %collective-permute-start = (s32[80,128]{1,0:T(8,128)S(1)}, s32[80,128]{1,0:T(8,128)S(1)}, u32[]{:S(2)}, u32[]{:S(2)}) collective-permute-start(s32[80,128]{1,0:T(8,128)S(1)} %get-tuple-element.24.near_ref.facts_ref), channel_id=1, source_target_pairs={{0,1},{1,0},{2,3},{3,2},{4,5},{5,4},{6,7},{7,6},{8,9},{9,8},{10,11... | collective-permute-start | bytes 122888 | tf_op jit(solution)/shard_map/ppermute | solution.py:391
  6.1 5.2 %collective-permute-start.3 = (f32[96,128]{1,0:T(8,128)S(1)}, f32[96,128]{1,0:T(8,128)S(1)}, u32[]{:S(2)}, u32[]{:S(2)}) collective-permute-start(f32[96,128]{1,0:T(8,128)S(1)} %get-tuple-element.25.refs_0_), channel_id=1, source_target_pairs={{0,8},{1,9},{2,10},{3,11},{4,12},{5,13},{6,14},{7,15},{8,0},{9,1},... | collective-permute-start | bytes 147464 | tf_op jit(solution)/shard_map/ppermute | solution.py:396
  6.1 5.2 %collective-permute-start.2 = (f32[96,128]{1,0:T(8,128)S(1)}, f32[96,128]{1,0:T(8,128)S(1)}, u32[]{:S(2)}, u32[]{:S(2)}) collective-permute-start(f32[96,128]{1,0:T(8,128)S(1)} %get-tuple-element.25.refs_0_), channel_id=1, source_target_pairs={{0,4},{1,5},{2,6},{3,7},{4,0},{5,1},{6,2},{7,3},{8,12},{9,13},{10,... | collective-permute-start | bytes 147464 | tf_op jit(solution)/shard_map/ppermute | solution.py:396
  7.3 3.7 %collective-permute-start.1 = (s32[16,128]{1,0:T(8,128)S(1)}, s32[16,128]{1,0:T(8,128)S(1)}, u32[]{:S(2)}, u32[]{:S(2)}) collective-permute-start(s32[16,128]{1,0:T(8,128)S(1)} %pair.2.near_ref), channel_id=1, source_target_pairs={{0,2},{1,3},{2,0},{3,1},{4,6},{5,7},{6,4},{7,5},{8,10},{9,11},{10,... | collective-permute-start | bytes 24584 | tf_op jit(solution)/shard_map/ppermute | solution.py:391
  11.3 4.3 %collective-permute-start.5 = (f32[96,128]{1,0:T(8,128)S(1)}, f32[96,128]{1,0:T(8,128)S(1)}, u32[]{:S(2)}, u32[]{:S(2)}) collective-permute-start(f32[96,128]{1,0:T(8,128)S(1)} %get-tuple-element.28), channel_id=1, source_target_pairs={{0,3},{1,2},{2,1},{3,0},{4,7},{5,6},{6,5},{7,4},{8,11},{9,10},{10,... | collective-permute-start | bytes 147464 | tf_op jit(solution)/shard_map/ppermute | solution.py:391
  12.2 4.5 %collective-permute-start.6 = (f32[96,128]{1,0:T(8,128)S(1)}, f32[96,128]{1,0:T(8,128)S(1)}, u32[]{:S(2)}, u32[]{:S(2)}) collective-permute-start(f32[96,128]{1,0:T(8,128)S(1)} %get-tuple-element.29), channel_id=1, source_target_pairs={{0,2},{1,3},{2,0},{3,1},{4,6},{5,7},{6,4},{7,5},{8,10},{9,11},{10,... | collective-permute-start | bytes 147464 | tf_op jit(solution)/shard_map/ppermute | solution.py:391
  13.0 3.7 %collective-permute-start.7 = (f32[96,128]{1,0:T(8,128)S(1)}, f32[96,128]{1,0:T(8,128)S(1)}, u32[]{:S(2)}, u32[]{:S(2)}) collective-permute-start(f32[96,128]{1,0:T(8,128)S(1)} %get-tuple-element.30), channel_id=1, source_target_pairs={{0,1},{1,0},{2,3},{3,2},{4,5},{5,4},{6,7},{7,6},{8,9},{9,8},{10,11... | collective-permute-start | bytes 147464 | tf_op jit(solution)/shard_map/ppermute | solution.py:391
  17.1 3.9 %collective-permute-start.10 = (f32[96,128]{1,0:T(8,128)S(1)}, f32[96,128]{1,0:T(8,128)S(1)}, u32[]{:S(2)}, u32[]{:S(2)}) collective-permute-start(f32[96,128]{1,0:T(8,128)S(1)} %answer.1.after_ref.refs_0_), channel_id=1, source_target_pairs={{0,3},{1,2},{2,1},{3,0},{4,7},{5,6},{6,5},{7,4},{8,11},{9,10},{10,... | collective-permute-start | bytes 147464 | tf_op jit(solution)/shard_map/ppermute | solution.py:391
  17.9 4.4 %collective-permute-start.9 = (f32[96,128]{1,0:T(8,128)S(1)}, f32[96,128]{1,0:T(8,128)S(1)}, u32[]{:S(2)}, u32[]{:S(2)}) collective-permute-start(f32[96,128]{1,0:T(8,128)S(1)} %answer.1.after_ref.refs_0_), channel_id=1, source_target_pairs={{0,2},{1,3},{2,0},{3,1},{4,6},{5,7},{6,4},{7,5},{8,10},{9,11},{10,... | collective-permute-start | bytes 147464 | tf_op jit(solution)/shard_map/ppermute | solution.py:391
  18.8 3.5 %collective-permute-start.8 = (f32[96,128]{1,0:T(8,128)S(1)}, f32[96,128]{1,0:T(8,128)S(1)}, u32[]{:S(2)}, u32[]{:S(2)}) collective-permute-start(f32[96,128]{1,0:T(8,128)S(1)} %answer.1.after_ref.refs_0_), channel_id=1, source_target_pairs={{0,1},{1,0},{2,3},{3,2},{4,5},{5,4},{6,7},{7,6},{8,9},{9,8},{10,11... | collective-permute-start | bytes 147464 | tf_op jit(solution)/shard_map/ppermute | solution.py:391
  22.3 6.5 %collective-permute-start.11 = (f32[96,128]{1,0:T(8,128)S(1)}, f32[96,128]{1,0:T(8,128)S(1)}, u32[]{:S(2)}, u32[]{:S(2)}) collective-permute-start(f32[96,128]{1,0:T(8,128)S(1)} %get-tuple-element.40), channel_id=1, source_target_pairs={{0,8},{1,9},{2,10},{3,11},{4,12},{5,13},{6,14},{7,15},{8,0},{9,1},... | collective-permute-start | bytes 147464 | tf_op jit(solution)/shard_map/ppermute | solution.py:396
  23.9 6.0 %collective-permute-start.12 = (f32[96,128]{1,0:T(8,128)S(1)}, f32[96,128]{1,0:T(8,128)S(1)}, u32[]{:S(2)}, u32[]{:S(2)}) collective-permute-start(f32[96,128]{1,0:T(8,128)S(1)} %get-tuple-element.41), channel_id=1, source_target_pairs={{0,12},{1,13},{2,14},{3,15},{4,8},{5,9},{6,10},{7,11},{8,4},{9,5},... | collective-permute-start | bytes 147464 | tf_op jit(solution)/shard_map/ppermute | solution.py:396
  25.2 4.7 %collective-permute-start.13 = (f32[96,128]{1,0:T(8,128)S(1)}, f32[96,128]{1,0:T(8,128)S(1)}, u32[]{:S(2)}, u32[]{:S(2)}) collective-permute-start(f32[96,128]{1,0:T(8,128)S(1)} %get-tuple-element.42), channel_id=1, source_target_pairs={{0,4},{1,5},{2,6},{3,7},{4,0},{5,1},{6,2},{7,3},{8,12},{9,13},{10,... | collective-permute-start | bytes 147464 | tf_op jit(solution)/shard_map/ppermute | solution.py:396

commit v10 on v9

--- a/solution.py
+++ b/solution.py
@@ -93,6 +93,10 @@
     return position ^ step if size & (size - 1) == 0 else (position - step) % size
 
 
+def shift(position, step, size):
+    return lax.rem(position + step, size)
+
+
 def inverse_step(step, size):
     return step if size & (size - 1) == 0 else (size - step) % size
 
@@ -104,11 +108,11 @@
     return result
 
 
-def choose(options, index, mine, size):
+def choose(options, index, sources):
     rows = index.shape[0]
     result = options[0][:rows, :]
-    for k in range(1, size):
-        result = jnp.where(unturn(mine, k, size) == index, options[k][:rows, :], result)
+    for option, source in zip(options[1:], sources[1:]):
+        result = jnp.where(source == index, option[:rows, :], result)
     return result
 
 
@@ -174,7 +178,7 @@
     for k in range(inner):
         back = wish_steps(inner).index(inverse_step(k, inner))
         wish = fact(wishes_ref, back, OUTER, outs[k].shape[0])
-        outs[k][...] = choose(column, wish, my_outer, outer)
+        outs[k][...] = choose(column, wish, [unturn(my_outer, k, outer) for k in range(outer)])
 
 
 def answer_kernel(facts_ref, *refs, inner, late, heads, width, order):
@@ -182,7 +186,8 @@
     found = in_steps(found, order)
     my_inner = lax.rem(lax.axis_index("req"), inner)
     block = lambda ref, t: ref[t * heads:(t + 1) * heads, :]
-    rows = choose(found, fact(facts_ref, 0, INNER, late * heads), my_inner, inner)
+    sources = [unturn(my_inner, k, inner) for k in range(inner)]
+    rows = choose(found, fact(facts_ref, 0, INNER, late * heads), sources)
     q = [rows[t * heads:(t + 1) * heads, :] for t in range(late)]
     slope = head_slope(heads, width)
     for t in range(late):
@@ -215,7 +220,7 @@
     for k in range(outer):
         result = 0.0
         for n in range(inner):
-            result = jnp.where(owner[n] == turn(my_outer, k, outer), replies[n][...], result)
+            result = jnp.where(owner[n] == shift(my_outer, k, outer), replies[n][...], result)
         outs[k][...] = result
 
 
@@ -411,6 +416,11 @@
             step *= 2
         return result
 
+    def shift_outer(x, k):
+        return lax.ppermute(x, "req", [
+            (o * inner + i, (o + k) % outer * inner + i)
+            for o in range(outer) for i in range(inner)])
+
     def params(limit):
         return pltpu.CompilerParams(vmem_limit_bytes=limit * MIB)
 
@@ -432,8 +442,7 @@
         compiler_params=params(4), name="ask",
     )(in_hbm(new_slot), in_hbm(queries))
 
-    up, half = list(range(1, outer)), outer // 2
-    z1, z2 = up, up[half - 1:] + up[:half - 1]
+    z1, z2 = list(range(1, outer)), list(range(1, outer))
     q1, q2 = list(range(inner - 1, 0, -1)), list(range(1, inner))
     column = [ask] + [send_outer(ask_long if k == outer - 1 else ask, k) for k in z1]
     wishes = gather_inner(facts)
@@ -493,7 +502,7 @@
         in_specs=[VMEM, ANY] + [VMEM] * inner, out_specs=(VMEM,) * outer,
         compiler_params=params(4), name="reply",
     )(wishes, partial, *replies)
-    parts = [send_outer(sorted_replies[k], k) for k in z2]
+    parts = [shift_outer(sorted_replies[k], k) for k in z2]
 
     output = jax.ShapeDtypeStruct((packed_rows, width), BF16)
     base, last = pl.pallas_call(

time: 30.8 us -> 30.8 us (level)
  waiting for transfers between devices: 6.54 us -> 5.56 us
  starting transfers between devices: 14.8 us -> 15.7 us
    ppermute x0 -> x3, starting transfers between devices: none -> 4.44 us  [shift_outer(): lax.ppermute(x, 'req', [(o * inner + i, (o + k) % outer * inner + i) for...]
    ppermute x6 -> x3, starting transfers between devices: 9.39 us -> 5.84 us  [send_outer(): lax.ppermute(x, 'req', [(o * inner + i, int(turn(o, k, outer)) * inner +...]
    ppermute x6 -> x3, waiting for transfers between devices: 1.64 us -> 0.34 us  [send_outer(): lax.ppermute(x, 'req', [(o * inner + i, int(turn(o, k, outer)) * inner +...]
    ppermute x0 -> x3, waiting for transfers between devices: none -> 0.32 us  [shift_outer(): lax.ppermute(x, 'req', [(o * inner + i, (o + k) % outer * inner + i) for...]
  transfers between devices with their start and end apart: 14 -> 14, of which waited for: 7 -> 6; matrix products, arithmetic and copies ran while one was open for 0% -> 0% of each run, Pallas kernels for 23% -> 23%
where the time goes in v10:
time: 30.8 us; the launch traced here: 30.5 us
  starting transfers between devices  15.7 us (51%)
  Pallas kernels  9.21 us (30%)
  waiting for transfers between devices  5.56 us (18%)
    ppermute x3, starting transfers between devices, send_outer(): lax.ppermute(x, 'req', [(o * inner + i, int(turn(o, k, outer)) * inner +...  5.84 us
    ppermute x8, starting transfers between devices, send_inner(): lax.ppermute(x, 'req', [(o * inner + i, o * inner + int(turn(i, k, inner)...  5.37 us
    ppermute x8, waiting for transfers between devices, send_inner(): lax.ppermute(x, 'req', [(o * inner + i, o * inner + int(turn(i, k, inner)...  4.9 us
    ppermute x3, starting transfers between devices, shift_outer(): lax.ppermute(x, 'req', [(o * inner + i, (o + k) % outer * inner + i) for...  4.44 us
    pallas_call x1, Pallas kernels, on_device(): pl.pallas_call(functools.partial(local_kernel, slots=last_slots, count=co...  2.67 us
    pallas_call x1, Pallas kernels, on_device(): pl.pallas_call(functools.partial(prepare_kernel, count=count, chunks=chun...  2.41 us
    pallas_call x1, Pallas kernels, on_device(): pl.pallas_call(functools.partial(scores_kernel, slots=first_slots, count=...  1.93 us
    pallas_call x1, Pallas kernels, on_device(): pl.pallas_call(functools.partial(ask_kernel, count=count, inner=inner), o...  0.91 us
  transfers between devices with their start and end apart: 14, of which 6 were waited for; matrix products, arithmetic and copies ran while one was open for 0% of the time, Pallas kernels for 23%

profile of v10, /device:TPU:0, one launch (start us, length us, event | category | flops | bytes accessed | tf_op | source)
XLA Modules:
  0.0 30.5 jit_solution(15390722013847907629)
XLA Ops:
  0.0 0.9 %ask.1 = (f32[96,128]{1,0:T(8,128)S(1)}, f32[104,128]{1,0:T(8,128)S(1)}, s32[80,128]{1,0:T(8,128)S(1)}) custom-call(s32[2]{0:T(128)} %slots_ref.1, bf16[384,128]{1,0:T(8,128)(2,1)} %bitcast.26), custom_call_target="tpu_custom_call" | custom-call | tf_op jit(solution)/shard_map/ask/pallas_call | solution.py:436
  0.9 5.1 %collective-permute-start.4 = (f32[104,128]{1,0:T(8,128)S(1)}, f32[104,128]{1,0:T(8,128)S(1)}, u32[]{:S(2)}, u32[]{:S(2)}) collective-permute-start(f32[104,128]{1,0:T(8,128)S(1)} %get-tuple-element.26), channel_id=1, source_target_pairs={{0,12},{1,13},{2,14},{3,15},{4,8},{5,9},{6,10},{7,11},{8,4},{9,5},... | collective-permute-start | bytes 159752 | tf_op jit(solution)/shard_map/ppermute | solution.py:401
  6.1 0.7 %collective-permute-start.2 = (f32[96,128]{1,0:T(8,128)S(1)}, f32[96,128]{1,0:T(8,128)S(1)}, u32[]{:S(2)}, u32[]{:S(2)}) collective-permute-start(f32[96,128]{1,0:T(8,128)S(1)} %get-tuple-element.25.refs_0_), channel_id=1, source_target_pairs={{0,4},{1,5},{2,6},{3,7},{4,0},{5,1},{6,2},{7,3},{8,12},{9,13},{10,... | collective-permute-start | bytes 147464 | tf_op jit(solution)/shard_map/ppermute | solution.py:401
  6.8 0.5 %collective-permute-done.far_ref = s32[80,128]{1,0:T(8,128)S(1)} collective-permute-done((s32[80,128]{1,0:T(8,128)S(1)}, s32[80,128]{1,0:T(8,128)S(1)}, u32[]{:S(2)}, u32[]{:S(2)}) %collective-permute-start) | collective-permute-done | bytes 40992 | tf_op jit(solution)/shard_map/ppermute | solution.py:396
  7.3 1.5 %collective-permute-start.1 = (s32[16,128]{1,0:T(8,128)S(1)}, s32[16,128]{1,0:T(8,128)S(1)}, u32[]{:S(2)}, u32[]{:S(2)}) collective-permute-start(s32[16,128]{1,0:T(8,128)S(1)} %pair.2.near_ref), channel_id=1, source_target_pairs={{0,2},{1,3},{2,0},{3,1},{4,6},{5,7},{6,4},{7,5},{8,10},{9,11},{10,... | collective-permute-start | bytes 24584 | tf_op jit(solution)/shard_map/ppermute | solution.py:396
  8.8 2.1 %collective-permute-done.1.far_ref = s32[16,128]{1,0:T(8,128)S(1)} collective-permute-done((s32[16,128]{1,0:T(8,128)S(1)}, s32[16,128]{1,0:T(8,128)S(1)}, u32[]{:S(2)}, u32[]{:S(2)}) %collective-permute-start.1) | collective-permute-done | bytes 8224 | tf_op jit(solution)/shard_map/ppermute | solution.py:396
  10.9 0.3 %collective-permute-done.3.refs_2_ = f32[96,128]{1,0:T(8,128)S(1)} collective-permute-done((f32[96,128]{1,0:T(8,128)S(1)}, f32[96,128]{1,0:T(8,128)S(1)}, u32[]{:S(2)}, u32[]{:S(2)}) %collective-permute-start.3) | collective-permute-done | bytes 49184 | tf_op jit(solution)/shard_map/ppermute | solution.py:401
  11.3 0.8 %collective-permute-start.5 = (f32[96,128]{1,0:T(8,128)S(1)}, f32[96,128]{1,0:T(8,128)S(1)}, u32[]{:S(2)}, u32[]{:S(2)}) collective-permute-start(f32[96,128]{1,0:T(8,128)S(1)} %get-tuple-element.28), channel_id=1, source_target_pairs={{0,3},{1,2},{2,1},{3,0},{4,7},{5,6},{6,5},{7,4},{8,11},{9,10},{10,... | collective-permute-start | bytes 147464 | tf_op jit(solution)/shard_map/ppermute | solution.py:396
  12.2 0.8 %collective-permute-start.6 = (f32[96,128]{1,0:T(8,128)S(1)}, f32[96,128]{1,0:T(8,128)S(1)}, u32[]{:S(2)}, u32[]{:S(2)}) collective-permute-start(f32[96,128]{1,0:T(8,128)S(1)} %get-tuple-element.29), channel_id=1, source_target_pairs={{0,2},{1,3},{2,0},{3,1},{4,6},{5,7},{6,4},{7,5},{8,10},{9,11},{10,... | collective-permute-start | bytes 147464 | tf_op jit(solution)/shard_map/ppermute | solution.py:396
  13.0 0.3 collective-permute-start.7
  13.2 2.4 %prepare.1 = (bf16[32,256,128]{2,1,0:T(8,128)(2,1)S(1)}, f32[2,96,128]{2,1,0:T(8,128)S(1)}) custom-call(s32[2]{0:T(128)} %slots_ref.1, bf16[384,128]{1,0:T(8,128)(2,1)} %bitcast.28, bf16[384,128]{1,0:T(8,128)(2,1)} %bitcast.30, f32[2,32,128,128]{3,2,1,0:T(8,128)} %states_ref.5), custom_call_target="tpu_custom_call" | custom-call | tf_op jit(solution)/shard_map/prepare/pallas_call | solution.py:451
  15.7 1.0 %collective-permute-done.6.refs_2_ = f32[96,128]{1,0:T(8,128)S(1)} collective-permute-done((f32[96,128]{1,0:T(8,128)S(1)}, f32[96,128]{1,0:T(8,128)S(1)}, u32[]{:S(2)}, u32[]{:S(2)}) %collective-permute-start.6) | collective-permute-done | bytes 49184 | tf_op jit(solution)/shard_map/ppermute | solution.py:396
  16.7 0.5 %answer.1.after_ref.refs_0_ = f32[96,128]{1,0:T(8,128)S(1)} custom-call(s32[80,128]{1,0:T(8,128)S(1)} %get-tuple-element.24.near_ref.facts_ref, f32[96,128]{1,0:T(8,128)S(1)} %get-tuple-element.27.refs_0_, f32[96,128]{1,0:T(8,128)S(1)} %collective-permute-done.5.refs_1_, f32[96,128]{1,0:T(8,128)S(1)} %collective-permute-done.6.refs_2_, ...), custom_call_target="tpu_custom_call" | custom-call | tf_op jit(solution)/shard_map/answer/pallas_call | solution.py:472
  17.1 0.8 %collective-permute-start.10 = (f32[96,128]{1,0:T(8,128)S(1)}, f32[96,128]{1,0:T(8,128)S(1)}, u32[]{:S(2)}, u32[]{:S(2)}) collective-permute-start(f32[96,128]{1,0:T(8,128)S(1)} %answer.1.after_ref.refs_0_), channel_id=1, source_target_pairs={{0,3},{1,2},{2,1},{3,0},{4,7},{5,6},{6,5},{7,4},{8,11},{9,10},{10,... | collective-permute-start | bytes 147464 | tf_op jit(solution)/shard_map/ppermute | solution.py:396
  17.9 0.9 %collective-permute-start.9 = (f32[96,128]{1,0:T(8,128)S(1)}, f32[96,128]{1,0:T(8,128)S(1)}, u32[]{:S(2)}, u32[]{:S(2)}) collective-permute-start(f32[96,128]{1,0:T(8,128)S(1)} %answer.1.after_ref.refs_0_), channel_id=1, source_target_pairs={{0,2},{1,3},{2,0},{3,1},{4,6},{5,7},{6,4},{7,5},{8,10},{9,11},{10,... | collective-permute-start | bytes 147464 | tf_op jit(solution)/shard_map/ppermute | solution.py:396
  18.8 0.2 collective-permute-start.8
  19.1 1.9 %scores.1 = (f32[384,128]{1,0:T(8,128)S(1)}, f32[384,128]{1,0:T(8,128)S(1)}, f32[2,96,128]{2,1,0:T(8,128)S(1)}, f32[1024,128]{1,0:T(8,128)S(1)}) custom-call(s32[80,128]{1,0:T(8,128)S(1)} %get-tuple-element.24.near_ref.facts_ref, bf16[384,128]{1,0:T(8,128)(2,1)S(1)} %bitcast.27, bf16[384,128]{1,0:T(8,128)(2,1)S(1)} %bitcast.29, ...), custom_call_target="tpu_custom_call" | custom-call | tf_op jit(solution)/shard_map/scores/pallas_call | solution.py:485
  21.1 1.2 %collective-permute-done.9.refs_2_ = f32[96,128]{1,0:T(8,128)S(1)} collective-permute-done((f32[96,128]{1,0:T(8,128)S(1)}, f32[96,128]{1,0:T(8,128)S(1)}, u32[]{:S(2)}, u32[]{:S(2)}) %collective-permute-start.9) | collective-permute-done | bytes 49184 | tf_op jit(solution)/shard_map/ppermute | solution.py:396
  22.3 0.5 %collective-permute-start.11 = (f32[96,128]{1,0:T(8,128)S(1)}, f32[96,128]{1,0:T(8,128)S(1)}, u32[]{:S(2)}, u32[]{:S(2)}) collective-permute-start(f32[96,128]{1,0:T(8,128)S(1)} %get-tuple-element.40), channel_id=1, source_target_pairs={{0,4},{1,5},{2,6},{3,7},{4,8},{5,9},{6,10},{7,11},{8,12},{9,13},{1... | collective-permute-start | bytes 147464 | tf_op jit(solution)/shard_map/ppermute | solution.py:420
  22.8 2.7 %collective-permute-start.12 = (f32[96,128]{1,0:T(8,128)S(1)}, f32[96,128]{1,0:T(8,128)S(1)}, u32[]{:S(2)}, u32[]{:S(2)}) collective-permute-start(f32[96,128]{1,0:T(8,128)S(1)} %get-tuple-element.41), channel_id=1, source_target_pairs={{0,8},{1,9},{2,10},{3,11},{4,12},{5,13},{6,14},{7,15},{8,0},{9,1},... | collective-permute-start | bytes 147464 | tf_op jit(solution)/shard_map/ppermute | solution.py:420
  25.6 1.2 %collective-permute-start.13 = (f32[96,128]{1,0:T(8,128)S(1)}, f32[96,128]{1,0:T(8,128)S(1)}, u32[]{:S(2)}, u32[]{:S(2)}) collective-permute-start(f32[96,128]{1,0:T(8,128)S(1)} %get-tuple-element.42), channel_id=1, source_target_pairs={{0,12},{1,13},{2,14},{3,15},{4,0},{5,1},{6,2},{7,3},{8,4},{9,5},{1... | collective-permute-start | bytes 147464 | tf_op jit(solution)/shard_map/ppermute | solution.py:420
  26.8 2.7 %local.1 = (bf16[384,128]{1,0:T(8,128)(2,1)}, bf16[192,128]{1,0:T(8,128)(2,1)S(1)}) custom-call(f32[384,128]{1,0:T(8,128)S(1)} %get-tuple-element.33.mixed_ref, f32[384,128]{1,0:T(8,128)S(1)} %get-tuple-element.34.scale_ref, f32[1024,128]{1,0:T(8,128)S(1)} %get-tuple-element.35.lhs, f32[96,128]{1,0:T(8,128)S(1)} %get-tuple-element.37.after_ref.refs_0_, ...), custom_call_target="tpu_custom_call" | custom-call | tf_op jit(solution)/shard_map/local/pallas_call | solution.py:508
  29.5 0.3 collective-permute-done.13.refs_3_
  29.8 0.8 %finish.1 = bf16[384,128]{1,0:T(8,128)(2,1)} custom-call(s32[80,128]{1,0:T(8,128)S(1)} %get-tuple-element.24.near_ref.facts_ref, bf16[384,128]{1,0:T(8,128)(2,1)} %get-tuple-element.38.base_ref, bf16[192,128]{1,0:T(8,128)(2,1)S(1)} %get-tuple-element.39.last_ref, ...), custom_call_target="tpu_custom_call", output_to_operand_aliasing={{}: (1, {})} | custom-call | tf_op jit(solution)/shard_map/finish/pallas_call | solution.py:520
  (24 shorter events, 0.2 us)
Async XLA Ops:
  0.0 19.0 %copy-start = (bf16[2,6,4096]{2,0,1:T(2,128)(2,1)S(1)}, bf16[2,6,4096]{2,0,1:T(2,128)(2,1)}, u32[]{:S(2)}) copy-start(bf16[2,6,4096]{2,0,1:T(2,128)(2,1)} %param.7) | copy-start | bytes 294916
  0.0 19.1 %copy-start.2 = (bf16[2,6,4096]{2,0,1:T(2,128)(2,1)S(1)}, bf16[2,6,4096]{2,0,1:T(2,128)(2,1)}, u32[]{:S(2)}) copy-start(bf16[2,6,4096]{2,0,1:T(2,128)(2,1)} %param.9) | copy-start | bytes 294916
  0.0 19.1 %copy-start.1 = (bf16[2,6,4096]{2,0,1:T(2,128)(2,1)S(1)}, bf16[2,6,4096]{2,0,1:T(2,128)(2,1)}, u32[]{:S(2)}) copy-start(bf16[2,6,4096]{2,0,1:T(2,128)(2,1)} %param.8) | copy-start | bytes 294916
  0.0 19.1 %copy-start.4 = (f32[4096]{0:T(1024)S(1)}, f32[4096]{0:T(1024)}, u32[]{:S(2)}) copy-start(f32[4096]{0:T(1024)} %param.13) | copy-start | bytes 49156
  0.0 19.1 %copy-start.3 = (bf16[2,6,4096]{2,0,1:T(2,128)(2,1)S(1)}, bf16[2,6,4096]{2,0,1:T(2,128)(2,1)}, u32[]{:S(2)}) copy-start(bf16[2,6,4096]{2,0,1:T(2,128)(2,1)} %param.10) | copy-start | bytes 294916
  0.9 10.3 %collective-permute-start.4 = (f32[104,128]{1,0:T(8,128)S(1)}, f32[104,128]{1,0:T(8,128)S(1)}, u32[]{:S(2)}, u32[]{:S(2)}) collective-permute-start(f32[104,128]{1,0:T(8,128)S(1)} %get-tuple-element.26), channel_id=1, source_target_pairs={{0,12},{1,13},{2,14},{3,15},{4,8},{5,9},{6,10},{7,11},{8,4},{9,5},... | collective-permute-start | bytes 159752 | tf_op jit(solution)/shard_map/ppermute | solution.py:401
  6.1 1.2 %collective-permute-start = (s32[80,128]{1,0:T(8,128)S(1)}, s32[80,128]{1,0:T(8,128)S(1)}, u32[]{:S(2)}, u32[]{:S(2)}) collective-permute-start(s32[80,128]{1,0:T(8,128)S(1)} %get-tuple-element.24.near_ref.facts_ref), channel_id=1, source_target_pairs={{0,1},{1,0},{2,3},{3,2},{4,5},{5,4},{6,7},{7,6},{8,9},{9,8},{10,11... | collective-permute-start | bytes 122888 | tf_op jit(solution)/shard_map/ppermute | solution.py:396
  6.1 5.2 %collective-permute-start.3 = (f32[96,128]{1,0:T(8,128)S(1)}, f32[96,128]{1,0:T(8,128)S(1)}, u32[]{:S(2)}, u32[]{:S(2)}) collective-permute-start(f32[96,128]{1,0:T(8,128)S(1)} %get-tuple-element.25.refs_0_), channel_id=1, source_target_pairs={{0,8},{1,9},{2,10},{3,11},{4,12},{5,13},{6,14},{7,15},{8,0},{9,1},... | collective-permute-start | bytes 147464 | tf_op jit(solution)/shard_map/ppermute | solution.py:401
  6.1 5.2 %collective-permute-start.2 = (f32[96,128]{1,0:T(8,128)S(1)}, f32[96,128]{1,0:T(8,128)S(1)}, u32[]{:S(2)}, u32[]{:S(2)}) collective-permute-start(f32[96,128]{1,0:T(8,128)S(1)} %get-tuple-element.25.refs_0_), channel_id=1, source_target_pairs={{0,4},{1,5},{2,6},{3,7},{4,0},{5,1},{6,2},{7,3},{8,12},{9,13},{10,... | collective-permute-start | bytes 147464 | tf_op jit(solution)/shard_map/ppermute | solution.py:401
  7.3 3.7 %collective-permute-start.1 = (s32[16,128]{1,0:T(8,128)S(1)}, s32[16,128]{1,0:T(8,128)S(1)}, u32[]{:S(2)}, u32[]{:S(2)}) collective-permute-start(s32[16,128]{1,0:T(8,128)S(1)} %pair.2.near_ref), channel_id=1, source_target_pairs={{0,2},{1,3},{2,0},{3,1},{4,6},{5,7},{6,4},{7,5},{8,10},{9,11},{10,... | collective-permute-start | bytes 24584 | tf_op jit(solution)/shard_map/ppermute | solution.py:396
  11.3 4.3 %collective-permute-start.5 = (f32[96,128]{1,0:T(8,128)S(1)}, f32[96,128]{1,0:T(8,128)S(1)}, u32[]{:S(2)}, u32[]{:S(2)}) collective-permute-start(f32[96,128]{1,0:T(8,128)S(1)} %get-tuple-element.28), channel_id=1, source_target_pairs={{0,3},{1,2},{2,1},{3,0},{4,7},{5,6},{6,5},{7,4},{8,11},{9,10},{10,... | collective-permute-start | bytes 147464 | tf_op jit(solution)/shard_map/ppermute | solution.py:396
  12.2 4.5 %collective-permute-start.6 = (f32[96,128]{1,0:T(8,128)S(1)}, f32[96,128]{1,0:T(8,128)S(1)}, u32[]{:S(2)}, u32[]{:S(2)}) collective-permute-start(f32[96,128]{1,0:T(8,128)S(1)} %get-tuple-element.29), channel_id=1, source_target_pairs={{0,2},{1,3},{2,0},{3,1},{4,6},{5,7},{6,4},{7,5},{8,10},{9,11},{10,... | collective-permute-start | bytes 147464 | tf_op jit(solution)/shard_map/ppermute | solution.py:396
  13.0 3.7 %collective-permute-start.7 = (f32[96,128]{1,0:T(8,128)S(1)}, f32[96,128]{1,0:T(8,128)S(1)}, u32[]{:S(2)}, u32[]{:S(2)}) collective-permute-start(f32[96,128]{1,0:T(8,128)S(1)} %get-tuple-element.30), channel_id=1, source_target_pairs={{0,1},{1,0},{2,3},{3,2},{4,5},{5,4},{6,7},{7,6},{8,9},{9,8},{10,11... | collective-permute-start | bytes 147464 | tf_op jit(solution)/shard_map/ppermute | solution.py:396
  17.1 3.9 %collective-permute-start.10 = (f32[96,128]{1,0:T(8,128)S(1)}, f32[96,128]{1,0:T(8,128)S(1)}, u32[]{:S(2)}, u32[]{:S(2)}) collective-permute-start(f32[96,128]{1,0:T(8,128)S(1)} %answer.1.after_ref.refs_0_), channel_id=1, source_target_pairs={{0,3},{1,2},{2,1},{3,0},{4,7},{5,6},{6,5},{7,4},{8,11},{9,10},{10,... | collective-permute-start | bytes 147464 | tf_op jit(solution)/shard_map/ppermute | solution.py:396
  17.9 4.4 %collective-permute-start.9 = (f32[96,128]{1,0:T(8,128)S(1)}, f32[96,128]{1,0:T(8,128)S(1)}, u32[]{:S(2)}, u32[]{:S(2)}) collective-permute-start(f32[96,128]{1,0:T(8,128)S(1)} %answer.1.after_ref.refs_0_), channel_id=1, source_target_pairs={{0,2},{1,3},{2,0},{3,1},{4,6},{5,7},{6,4},{7,5},{8,10},{9,11},{10,... | collective-permute-start | bytes 147464 | tf_op jit(solution)/shard_map/ppermute | solution.py:396
  18.8 3.5 %collective-permute-start.8 = (f32[96,128]{1,0:T(8,128)S(1)}, f32[96,128]{1,0:T(8,128)S(1)}, u32[]{:S(2)}, u32[]{:S(2)}) collective-permute-start(f32[96,128]{1,0:T(8,128)S(1)} %answer.1.after_ref.refs_0_), channel_id=1, source_target_pairs={{0,1},{1,0},{2,3},{3,2},{4,5},{5,4},{6,7},{7,6},{8,9},{9,8},{10,11... | collective-permute-start | bytes 147464 | tf_op jit(solution)/shard_map/ppermute | solution.py:396
  22.3 7.1 %collective-permute-start.11 = (f32[96,128]{1,0:T(8,128)S(1)}, f32[96,128]{1,0:T(8,128)S(1)}, u32[]{:S(2)}, u32[]{:S(2)}) collective-permute-start(f32[96,128]{1,0:T(8,128)S(1)} %get-tuple-element.40), channel_id=1, source_target_pairs={{0,4},{1,5},{2,6},{3,7},{4,8},{5,9},{6,10},{7,11},{8,12},{9,13},{1... | collective-permute-start | bytes 147464 | tf_op jit(solution)/shard_map/ppermute | solution.py:420
  22.8 6.7 %collective-permute-start.12 = (f32[96,128]{1,0:T(8,128)S(1)}, f32[96,128]{1,0:T(8,128)S(1)}, u32[]{:S(2)}, u32[]{:S(2)}) collective-permute-start(f32[96,128]{1,0:T(8,128)S(1)} %get-tuple-element.41), channel_id=1, source_target_pairs={{0,8},{1,9},{2,10},{3,11},{4,12},{5,13},{6,14},{7,15},{8,0},{9,1},... | collective-permute-start | bytes 147464 | tf_op jit(solution)/shard_map/ppermute | solution.py:420
  25.6 4.2 %collective-permute-start.13 = (f32[96,128]{1,0:T(8,128)S(1)}, f32[96,128]{1,0:T(8,128)S(1)}, u32[]{:S(2)}, u32[]{:S(2)}) collective-permute-start(f32[96,128]{1,0:T(8,128)S(1)} %get-tuple-element.42), channel_id=1, source_target_pairs={{0,12},{1,13},{2,14},{3,15},{4,0},{5,1},{6,2},{7,3},{8,4},{9,5},{1... | collective-permute-start | bytes 147464 | tf_op jit(solution)/shard_map/ppermute | solution.py:420

commit v11 on v10

--- a/solution.py
+++ b/solution.py
@@ -144,32 +144,38 @@
     out_ref[rows:, :] = far_ref[:rows, :]
 
 
-def prepare_kernel(slots_ref, keys_ref, values_ref, states_ref, weight_ref, early_ref,
-                   state, rows_ref, wide, sems, row_sems, *, count, chunks):
+def prepare_kernel(slots_ref, queries_ref, keys_ref, values_ref, gates_ref, gain_ref, states_ref,
+                   weight_ref, early_ref, rows_ref, gain_rows_ref, state, wide, sems, row_sems,
+                   *, count, chunks):
     heads = states_ref.shape[1]
     size = heads // chunks
     place, _ = moving_slot(slots_ref, count)
+    sources = (keys_ref, values_ref, queries_ref, gates_ref)
     copies = [
-        pltpu.make_async_copy(
-            ref.at[pl.ds(0, wide.shape[0])], rows_ref.at[n], row_sems.at[n])
-        for n, ref in enumerate((keys_ref, values_ref))]
-    for copy in copies:
-        copy.start()
+        pltpu.make_async_copy(ref, rows_ref.at[n], row_sems.at[n])
+        for n, ref in enumerate(sources)]
+    copies.append(pltpu.make_async_copy(gain_ref, gain_rows_ref, row_sems.at[len(sources)]))
 
     def load(c):
         part = pl.ds(c * size, size)
         return pltpu.make_async_copy(states_ref.at[place, part], state.at[part], sems.at[c])
 
+    for copy in copies[:2]:
+        copy.start()
     for c in range(chunks):
         load(c).start()
-    for n, copy in enumerate(copies):
+    for copy in copies[2:]:
+        copy.start()
+    for n, copy in enumerate(copies[:2]):
         copy.wait()
-        wide[...] = rows_ref[n].astype(F32)
+        wide[...] = rows_ref[n, :wide.shape[0], :].astype(F32)
         early_ref[n] = silu(extract(wide, place, count))
     for c in range(chunks):
         load(c).wait()
         for h in range(c * size, (c + 1) * size):
             weight_ref[h] = jnp.concatenate(split(state[h]), axis=0)
+    for copy in copies[2:]:
+        copy.wait()
 
 
 def route_kernel(wishes_ref, *refs, inner, outer, order):
@@ -261,12 +267,12 @@
     return ref[t * rows:(t + 1) * rows, :]
 
 
-def scores_kernel(facts_ref, queries_ref, keys_ref, values_ref, gates_ref, gain_ref, after_ref,
-                  states_ref, mixed_ref, scale_ref, late_ref, lhs, state, prod, wide, sems,
+def scores_kernel(facts_ref, rows_ref, gain_ref, after_ref, states_ref, mixed_ref, scale_ref, late_ref, lhs, state, prod, wide, sems,
                   *, slots, count, chunks):
     heads, width = states_ref.shape[1], states_ref.shape[2]
     span = heads * count
-    steps = queries_ref.shape[0] // span
+    keys_ref, values_ref, queries_ref, gates_ref = [rows_ref.at[n] for n in range(4)]
+    steps = rows_ref.shape[1] // span
     late = steps - BEFORE
     place = fact(facts_ref, 0, SLOT, late * heads)
     load = load_states(states_ref, state, sems, slots, chunks)
@@ -448,18 +454,20 @@
     wishes = gather_inner(facts)
 
     chunks = 8
-    weight, early = pl.pallas_call(
+    gain = norm_gain.reshape(heads, width)
+    weight, early, rows, gain_rows = pl.pallas_call(
         functools.partial(prepare_kernel, count=count, chunks=chunks),
         out_shape=(jax.ShapeDtypeStruct((heads, 2 * width, width), BF16),
-                   jax.ShapeDtypeStruct((2, BEFORE * heads, width), F32)),
-        in_specs=[SMEM, HBM, HBM, HBM], out_specs=(VMEM, VMEM),
+                   jax.ShapeDtypeStruct((2, BEFORE * heads, width), F32),
+                   jax.ShapeDtypeStruct((4, packed_rows, width), BF16),
+                   jax.ShapeDtypeStruct(gain.shape, F32)),
+        in_specs=[SMEM] + [HBM] * 6, out_specs=(VMEM,) * 4,
         scratch_shapes=[pltpu.VMEM((heads, width, width), F32),
-                        pltpu.VMEM((2, BEFORE * heads * count, width), BF16),
                         pltpu.VMEM((BEFORE * heads * count, width), F32),
                         pltpu.SemaphoreType.DMA((chunks,)),
-                        pltpu.SemaphoreType.DMA((2,))],
+                        pltpu.SemaphoreType.DMA((5,))],
         compiler_params=params(12), name="prepare",
-    )(in_hbm(new_slot), in_hbm(keys), in_hbm(values), in_hbm(states))
+    )(*map(in_hbm, (new_slot, queries, keys, values, gates, gain, states)))
 
     asked = pl.pallas_call(
         functools.partial(route_kernel, inner=inner, outer=outer, order=z1),
@@ -485,7 +493,7 @@
     mixed, scale, partial, lhs = pl.pallas_call(
         functools.partial(scores_kernel, slots=first_slots, count=count, chunks=chunks),
         out_shape=(packed, packed, jax.ShapeDtypeStruct((2, single_rows, width), F32), products),
-        in_specs=[VMEM] * 6 + [ANY, HBM], out_specs=(VMEM,) * 4,
+        in_specs=[VMEM] * 3 + [ANY, HBM], out_specs=(VMEM,) * 4,
         scratch_shapes=[
             pltpu.VMEM((max(len(first_slots), 1), heads, width, width), F32),
             pltpu.VMEM(products.shape, F32),
@@ -493,8 +501,7 @@
             pltpu.SemaphoreType.DMA((max(len(first_slots), 1), chunks)),
         ],
         compiler_params=params(16), name="scores",
-    )(facts, queries, keys, values, gates, norm_gain.reshape(heads, width), answer,
-      in_hbm(states))
+    )(facts, rows, gain_rows, answer, in_hbm(states))
 
     sorted_replies = pl.pallas_call(
         functools.partial(reply_kernel, inner=inner, outer=outer, order=q2),

time: 30.8 us -> 30.7 us (level)
  transfers between devices with their start and end apart: 14 -> 14, of which waited for: 6 -> 6; matrix products, arithmetic and copies ran while one was open for 0% -> 0% of each run, Pallas kernels for 23% -> 24%
where the time goes in v11:
time: 30.7 us; the launch traced here: 30.5 us
  starting transfers between devices  15.7 us (51%)
  Pallas kernels  9.41 us (31%)
  waiting for transfers between devices  5.3 us (17%)
    ppermute x3, starting transfers between devices, send_outer(): lax.ppermute(x, 'req', [(o * inner + i, int(turn(o, k, outer)) * inner +...  5.83 us
    ppermute x8, starting transfers between devices, send_inner(): lax.ppermute(x, 'req', [(o * inner + i, o * inner + int(turn(i, k, inner)...  5.37 us
    ppermute x8, waiting for transfers between devices, send_inner(): lax.ppermute(x, 'req', [(o * inner + i, o * inner + int(turn(i, k, inner)...  4.65 us
    ppermute x3, starting transfers between devices, shift_outer(): lax.ppermute(x, 'req', [(o * inner + i, (o + k) % outer * inner + i) for...  4.44 us
    pallas_call x1, Pallas kernels, on_device(): pl.pallas_call(functools.partial(local_kernel, slots=last_slots, count=co...  2.67 us
    pallas_call x1, Pallas kernels, on_device(): pl.pallas_call(functools.partial(prepare_kernel, count=count, chunks=chun...  2.48 us
    pallas_call x1, Pallas kernels, on_device(): pl.pallas_call(functools.partial(scores_kernel, slots=first_slots, count=...  2.13 us
    pallas_call x1, Pallas kernels, on_device(): pl.pallas_call(functools.partial(ask_kernel, count=count, inner=inner), o...  0.85 us
  transfers between devices with their start and end apart: 14, of which 6 were waited for; matrix products, arithmetic and copies ran while one was open for 0% of the time, Pallas kernels for 24%

profile of v11, /device:TPU:0, one launch (start us, length us, event | category | flops | bytes accessed | tf_op | source)
XLA Modules:
  0.0 30.5 jit_solution(4802478064687814968)
XLA Ops:
  0.0 0.9 %ask.1 = (f32[96,128]{1,0:T(8,128)S(1)}, f32[104,128]{1,0:T(8,128)S(1)}, s32[80,128]{1,0:T(8,128)S(1)}) custom-call(s32[2]{0:T(128)} %slots_ref.1, bf16[384,128]{1,0:T(8,128)(2,1)} %bitcast.26), custom_call_target="tpu_custom_call" | custom-call | tf_op jit(solution)/shard_map/ask/pallas_call | solution.py:442
  0.9 5.1 %collective-permute-start.4 = (f32[104,128]{1,0:T(8,128)S(1)}, f32[104,128]{1,0:T(8,128)S(1)}, u32[]{:S(2)}, u32[]{:S(2)}) collective-permute-start(f32[104,128]{1,0:T(8,128)S(1)} %get-tuple-element.30), channel_id=1, source_target_pairs={{0,12},{1,13},{2,14},{3,15},{4,8},{5,9},{6,10},{7,11},{8,4},{9,5},... | collective-permute-start | bytes 159752 | tf_op jit(solution)/shard_map/ppermute | solution.py:407
  6.0 0.7 %collective-permute-start.2 = (f32[96,128]{1,0:T(8,128)S(1)}, f32[96,128]{1,0:T(8,128)S(1)}, u32[]{:S(2)}, u32[]{:S(2)}) collective-permute-start(f32[96,128]{1,0:T(8,128)S(1)} %get-tuple-element.29.refs_0_), channel_id=1, source_target_pairs={{0,4},{1,5},{2,6},{3,7},{4,0},{5,1},{6,2},{7,3},{8,12},{9,13},{10,... | collective-permute-start | bytes 147464 | tf_op jit(solution)/shard_map/ppermute | solution.py:407
  6.7 0.5 %collective-permute-done.far_ref = s32[80,128]{1,0:T(8,128)S(1)} collective-permute-done((s32[80,128]{1,0:T(8,128)S(1)}, s32[80,128]{1,0:T(8,128)S(1)}, u32[]{:S(2)}, u32[]{:S(2)}) %collective-permute-start) | collective-permute-done | bytes 40992 | tf_op jit(solution)/shard_map/ppermute | solution.py:402
  7.2 1.5 %collective-permute-start.1 = (s32[16,128]{1,0:T(8,128)S(1)}, s32[16,128]{1,0:T(8,128)S(1)}, u32[]{:S(2)}, u32[]{:S(2)}) collective-permute-start(s32[16,128]{1,0:T(8,128)S(1)} %pair.2.near_ref), channel_id=1, source_target_pairs={{0,2},{1,3},{2,0},{3,1},{4,6},{5,7},{6,4},{7,5},{8,10},{9,11},{10,... | collective-permute-start | bytes 24584 | tf_op jit(solution)/shard_map/ppermute | solution.py:402
  8.7 2.1 %collective-permute-done.1.far_ref = s32[16,128]{1,0:T(8,128)S(1)} collective-permute-done((s32[16,128]{1,0:T(8,128)S(1)}, s32[16,128]{1,0:T(8,128)S(1)}, u32[]{:S(2)}, u32[]{:S(2)}) %collective-permute-start.1) | collective-permute-done | bytes 8224 | tf_op jit(solution)/shard_map/ppermute | solution.py:402
  10.9 0.3 %collective-permute-done.3.refs_2_ = f32[96,128]{1,0:T(8,128)S(1)} collective-permute-done((f32[96,128]{1,0:T(8,128)S(1)}, f32[96,128]{1,0:T(8,128)S(1)}, u32[]{:S(2)}, u32[]{:S(2)}) %collective-permute-start.3) | collective-permute-done | bytes 49184 | tf_op jit(solution)/shard_map/ppermute | solution.py:407
  11.2 0.8 %collective-permute-start.5 = (f32[96,128]{1,0:T(8,128)S(1)}, f32[96,128]{1,0:T(8,128)S(1)}, u32[]{:S(2)}, u32[]{:S(2)}) collective-permute-start(f32[96,128]{1,0:T(8,128)S(1)} %get-tuple-element.32), channel_id=1, source_target_pairs={{0,3},{1,2},{2,1},{3,0},{4,7},{5,6},{6,5},{7,4},{8,11},{9,10},{10,... | collective-permute-start | bytes 147464 | tf_op jit(solution)/shard_map/ppermute | solution.py:402
  12.1 0.8 %collective-permute-start.6 = (f32[96,128]{1,0:T(8,128)S(1)}, f32[96,128]{1,0:T(8,128)S(1)}, u32[]{:S(2)}, u32[]{:S(2)}) collective-permute-start(f32[96,128]{1,0:T(8,128)S(1)} %get-tuple-element.33), channel_id=1, source_target_pairs={{0,2},{1,3},{2,0},{3,1},{4,6},{5,7},{6,4},{7,5},{8,10},{9,11},{10,... | collective-permute-start | bytes 147464 | tf_op jit(solution)/shard_map/ppermute | solution.py:402
  12.9 0.3 collective-permute-start.7
  13.2 2.5 %prepare.1 = (bf16[32,256,128]{2,1,0:T(8,128)(2,1)S(1)}, f32[2,96,128]{2,1,0:T(8,128)S(1)}, bf16[4,384,128]{2,1,0:T(8,128)(2,1)S(1)}, f32[32,128]{1,0:T(8,128)S(1)}) custom-call(s32[2]{0:T(128)} %slots_ref.1, bf16[384,128]{1,0:T(8,128)(2,1)} %bitcast.27, bf16[384,128]{1,0:T(8,128)(2,1)} %bitcast.28, bf16[384,128]{1,0:T(8,128)(2,1)} %bitcast.29, ...), custom_call_target="tpu_custom_call" | custom-call | tf_op jit(solution)/shard_map/prepare/pallas_call | solution.py:458
  15.7 0.9 %collective-permute-done.6.refs_2_ = f32[96,128]{1,0:T(8,128)S(1)} collective-permute-done((f32[96,128]{1,0:T(8,128)S(1)}, f32[96,128]{1,0:T(8,128)S(1)}, u32[]{:S(2)}, u32[]{:S(2)}) %collective-permute-start.6) | collective-permute-done | bytes 49184 | tf_op jit(solution)/shard_map/ppermute | solution.py:402
  16.6 0.5 %answer.1.after_ref.refs_0_ = f32[96,128]{1,0:T(8,128)S(1)} custom-call(s32[80,128]{1,0:T(8,128)S(1)} %get-tuple-element.26.near_ref.facts_ref, f32[96,128]{1,0:T(8,128)S(1)} %get-tuple-element.31.refs_0_, f32[96,128]{1,0:T(8,128)S(1)} %collective-permute-done.5.refs_1_, f32[96,128]{1,0:T(8,128)S(1)} %collective-permute-done.6.refs_2_, ...), custom_call_target="tpu_custom_call" | custom-call | tf_op jit(solution)/shard_map/answer/pallas_call | solution.py:480
  17.0 0.8 %collective-permute-start.10 = (f32[96,128]{1,0:T(8,128)S(1)}, f32[96,128]{1,0:T(8,128)S(1)}, u32[]{:S(2)}, u32[]{:S(2)}) collective-permute-start(f32[96,128]{1,0:T(8,128)S(1)} %answer.1.after_ref.refs_0_), channel_id=1, source_target_pairs={{0,3},{1,2},{2,1},{3,0},{4,7},{5,6},{6,5},{7,4},{8,11},{9,10},{10,... | collective-permute-start | bytes 147464 | tf_op jit(solution)/shard_map/ppermute | solution.py:402
  17.8 0.9 %collective-permute-start.9 = (f32[96,128]{1,0:T(8,128)S(1)}, f32[96,128]{1,0:T(8,128)S(1)}, u32[]{:S(2)}, u32[]{:S(2)}) collective-permute-start(f32[96,128]{1,0:T(8,128)S(1)} %answer.1.after_ref.refs_0_), channel_id=1, source_target_pairs={{0,2},{1,3},{2,0},{3,1},{4,6},{5,7},{6,4},{7,5},{8,10},{9,11},{10,... | collective-permute-start | bytes 147464 | tf_op jit(solution)/shard_map/ppermute | solution.py:402
  18.7 0.2 collective-permute-start.8
  19.0 2.1 %scores.1 = (f32[384,128]{1,0:T(8,128)S(1)}, f32[384,128]{1,0:T(8,128)S(1)}, f32[2,96,128]{2,1,0:T(8,128)S(1)}, f32[1024,128]{1,0:T(8,128)S(1)}) custom-call(s32[80,128]{1,0:T(8,128)S(1)} %get-tuple-element.26.near_ref.facts_ref, bf16[4,384,128]{2,1,0:T(8,128)(2,1)S(1)} %get-tuple-element.27.rows_ref, f32[32,128]{1,0:T(8,128)S(1)} %get-tuple-element.28.gain_ref, ...), custom_call_target="tpu_custom_call" | custom-call | tf_op jit(solution)/shard_map/scores/pallas_call | solution.py:493
  21.1 1.1 %collective-permute-done.9.refs_2_ = f32[96,128]{1,0:T(8,128)S(1)} collective-permute-done((f32[96,128]{1,0:T(8,128)S(1)}, f32[96,128]{1,0:T(8,128)S(1)}, u32[]{:S(2)}, u32[]{:S(2)}) %collective-permute-start.9) | collective-permute-done | bytes 49184 | tf_op jit(solution)/shard_map/ppermute | solution.py:402
  22.2 0.5 %collective-permute-start.11 = (f32[96,128]{1,0:T(8,128)S(1)}, f32[96,128]{1,0:T(8,128)S(1)}, u32[]{:S(2)}, u32[]{:S(2)}) collective-permute-start(f32[96,128]{1,0:T(8,128)S(1)} %get-tuple-element.44), channel_id=1, source_target_pairs={{0,4},{1,5},{2,6},{3,7},{4,8},{5,9},{6,10},{7,11},{8,12},{9,13},{1... | collective-permute-start | bytes 147464 | tf_op jit(solution)/shard_map/ppermute | solution.py:426
  22.8 2.7 %collective-permute-start.12 = (f32[96,128]{1,0:T(8,128)S(1)}, f32[96,128]{1,0:T(8,128)S(1)}, u32[]{:S(2)}, u32[]{:S(2)}) collective-permute-start(f32[96,128]{1,0:T(8,128)S(1)} %get-tuple-element.45), channel_id=1, source_target_pairs={{0,8},{1,9},{2,10},{3,11},{4,12},{5,13},{6,14},{7,15},{8,0},{9,1},... | collective-permute-start | bytes 147464 | tf_op jit(solution)/shard_map/ppermute | solution.py:426
  25.5 1.2 %collective-permute-start.13 = (f32[96,128]{1,0:T(8,128)S(1)}, f32[96,128]{1,0:T(8,128)S(1)}, u32[]{:S(2)}, u32[]{:S(2)}) collective-permute-start(f32[96,128]{1,0:T(8,128)S(1)} %get-tuple-element.46), channel_id=1, source_target_pairs={{0,12},{1,13},{2,14},{3,15},{4,0},{5,1},{6,2},{7,3},{8,4},{9,5},{1... | collective-permute-start | bytes 147464 | tf_op jit(solution)/shard_map/ppermute | solution.py:426
  26.7 2.7 %local.1 = (bf16[384,128]{1,0:T(8,128)(2,1)}, bf16[192,128]{1,0:T(8,128)(2,1)S(1)}) custom-call(f32[384,128]{1,0:T(8,128)S(1)} %get-tuple-element.37.mixed_ref, f32[384,128]{1,0:T(8,128)S(1)} %get-tuple-element.38.scale_ref, f32[1024,128]{1,0:T(8,128)S(1)} %get-tuple-element.39.lhs, f32[96,128]{1,0:T(8,128)S(1)} %get-tuple-element.41.after_ref.refs_0_, ...), custom_call_target="tpu_custom_call" | custom-call | tf_op jit(solution)/shard_map/local/pallas_call | solution.py:515
  29.4 0.3 collective-permute-done.13.refs_3_
  29.7 0.8 %finish.1 = bf16[384,128]{1,0:T(8,128)(2,1)} custom-call(s32[80,128]{1,0:T(8,128)S(1)} %get-tuple-element.26.near_ref.facts_ref, bf16[384,128]{1,0:T(8,128)(2,1)} %get-tuple-element.42.base_ref, bf16[192,128]{1,0:T(8,128)(2,1)S(1)} %get-tuple-element.43.last_ref, ...), custom_call_target="tpu_custom_call", output_to_operand_aliasing={{}: (1, {})} | custom-call | tf_op jit(solution)/shard_map/finish/pallas_call | solution.py:527
  (14 shorter events, 0.2 us)
Async XLA Ops:
  0.9 10.3 %collective-permute-start.4 = (f32[104,128]{1,0:T(8,128)S(1)}, f32[104,128]{1,0:T(8,128)S(1)}, u32[]{:S(2)}, u32[]{:S(2)}) collective-permute-start(f32[104,128]{1,0:T(8,128)S(1)} %get-tuple-element.30), channel_id=1, source_target_pairs={{0,12},{1,13},{2,14},{3,15},{4,8},{5,9},{6,10},{7,11},{8,4},{9,5},... | collective-permute-start | bytes 159752 | tf_op jit(solution)/shard_map/ppermute | solution.py:407
  6.0 1.2 %collective-permute-start = (s32[80,128]{1,0:T(8,128)S(1)}, s32[80,128]{1,0:T(8,128)S(1)}, u32[]{:S(2)}, u32[]{:S(2)}) collective-permute-start(s32[80,128]{1,0:T(8,128)S(1)} %get-tuple-element.26.near_ref.facts_ref), channel_id=1, source_target_pairs={{0,1},{1,0},{2,3},{3,2},{4,5},{5,4},{6,7},{7,6},{8,9},{9,8},{10,11... | collective-permute-start | bytes 122888 | tf_op jit(solution)/shard_map/ppermute | solution.py:402
  6.0 5.2 %collective-permute-start.3 = (f32[96,128]{1,0:T(8,128)S(1)}, f32[96,128]{1,0:T(8,128)S(1)}, u32[]{:S(2)}, u32[]{:S(2)}) collective-permute-start(f32[96,128]{1,0:T(8,128)S(1)} %get-tuple-element.29.refs_0_), channel_id=1, source_target_pairs={{0,8},{1,9},{2,10},{3,11},{4,12},{5,13},{6,14},{7,15},{8,0},{9,1},... | collective-permute-start | bytes 147464 | tf_op jit(solution)/shard_map/ppermute | solution.py:407
  6.0 5.2 %collective-permute-start.2 = (f32[96,128]{1,0:T(8,128)S(1)}, f32[96,128]{1,0:T(8,128)S(1)}, u32[]{:S(2)}, u32[]{:S(2)}) collective-permute-start(f32[96,128]{1,0:T(8,128)S(1)} %get-tuple-element.29.refs_0_), channel_id=1, source_target_pairs={{0,4},{1,5},{2,6},{3,7},{4,0},{5,1},{6,2},{7,3},{8,12},{9,13},{10,... | collective-permute-start | bytes 147464 | tf_op jit(solution)/shard_map/ppermute | solution.py:407
  7.2 3.7 %collective-permute-start.1 = (s32[16,128]{1,0:T(8,128)S(1)}, s32[16,128]{1,0:T(8,128)S(1)}, u32[]{:S(2)}, u32[]{:S(2)}) collective-permute-start(s32[16,128]{1,0:T(8,128)S(1)} %pair.2.near_ref), channel_id=1, source_target_pairs={{0,2},{1,3},{2,0},{3,1},{4,6},{5,7},{6,4},{7,5},{8,10},{9,11},{10,... | collective-permute-start | bytes 24584 | tf_op jit(solution)/shard_map/ppermute | solution.py:402
  11.2 4.4 %collective-permute-start.5 = (f32[96,128]{1,0:T(8,128)S(1)}, f32[96,128]{1,0:T(8,128)S(1)}, u32[]{:S(2)}, u32[]{:S(2)}) collective-permute-start(f32[96,128]{1,0:T(8,128)S(1)} %get-tuple-element.32), channel_id=1, source_target_pairs={{0,3},{1,2},{2,1},{3,0},{4,7},{5,6},{6,5},{7,4},{8,11},{9,10},{10,... | collective-permute-start | bytes 147464 | tf_op jit(solution)/shard_map/ppermute | solution.py:402
  12.1 4.5 %collective-permute-start.6 = (f32[96,128]{1,0:T(8,128)S(1)}, f32[96,128]{1,0:T(8,128)S(1)}, u32[]{:S(2)}, u32[]{:S(2)}) collective-permute-start(f32[96,128]{1,0:T(8,128)S(1)} %get-tuple-element.33), channel_id=1, source_target_pairs={{0,2},{1,3},{2,0},{3,1},{4,6},{5,7},{6,4},{7,5},{8,10},{9,11},{10,... | collective-permute-start | bytes 147464 | tf_op jit(solution)/shard_map/ppermute | solution.py:402
  12.9 3.7 %collective-permute-start.7 = (f32[96,128]{1,0:T(8,128)S(1)}, f32[96,128]{1,0:T(8,128)S(1)}, u32[]{:S(2)}, u32[]{:S(2)}) collective-permute-start(f32[96,128]{1,0:T(8,128)S(1)} %get-tuple-element.34), channel_id=1, source_target_pairs={{0,1},{1,0},{2,3},{3,2},{4,5},{5,4},{6,7},{7,6},{8,9},{9,8},{10,11... | collective-permute-start | bytes 147464 | tf_op jit(solution)/shard_map/ppermute | solution.py:402
  17.0 4.1 %collective-permute-start.10 = (f32[96,128]{1,0:T(8,128)S(1)}, f32[96,128]{1,0:T(8,128)S(1)}, u32[]{:S(2)}, u32[]{:S(2)}) collective-permute-start(f32[96,128]{1,0:T(8,128)S(1)} %answer.1.after_ref.refs_0_), channel_id=1, source_target_pairs={{0,3},{1,2},{2,1},{3,0},{4,7},{5,6},{6,5},{7,4},{8,11},{9,10},{10,... | collective-permute-start | bytes 147464 | tf_op jit(solution)/shard_map/ppermute | solution.py:402
  17.8 4.4 %collective-permute-start.9 = (f32[96,128]{1,0:T(8,128)S(1)}, f32[96,128]{1,0:T(8,128)S(1)}, u32[]{:S(2)}, u32[]{:S(2)}) collective-permute-start(f32[96,128]{1,0:T(8,128)S(1)} %answer.1.after_ref.refs_0_), channel_id=1, source_target_pairs={{0,2},{1,3},{2,0},{3,1},{4,6},{5,7},{6,4},{7,5},{8,10},{9,11},{10,... | collective-permute-start | bytes 147464 | tf_op jit(solution)/shard_map/ppermute | solution.py:402
  18.7 3.5 %collective-permute-start.8 = (f32[96,128]{1,0:T(8,128)S(1)}, f32[96,128]{1,0:T(8,128)S(1)}, u32[]{:S(2)}, u32[]{:S(2)}) collective-permute-start(f32[96,128]{1,0:T(8,128)S(1)} %answer.1.after_ref.refs_0_), channel_id=1, source_target_pairs={{0,1},{1,0},{2,3},{3,2},{4,5},{5,4},{6,7},{7,6},{8,9},{9,8},{10,11... | collective-permute-start | bytes 147464 | tf_op jit(solution)/shard_map/ppermute | solution.py:402
  22.2 7.1 %collective-permute-start.11 = (f32[96,128]{1,0:T(8,128)S(1)}, f32[96,128]{1,0:T(8,128)S(1)}, u32[]{:S(2)}, u32[]{:S(2)}) collective-permute-start(f32[96,128]{1,0:T(8,128)S(1)} %get-tuple-element.44), channel_id=1, source_target_pairs={{0,4},{1,5},{2,6},{3,7},{4,8},{5,9},{6,10},{7,11},{8,12},{9,13},{1... | collective-permute-start | bytes 147464 | tf_op jit(solution)/shard_map/ppermute | solution.py:426
  22.8 6.7 %collective-permute-start.12 = (f32[96,128]{1,0:T(8,128)S(1)}, f32[96,128]{1,0:T(8,128)S(1)}, u32[]{:S(2)}, u32[]{:S(2)}) collective-permute-start(f32[96,128]{1,0:T(8,128)S(1)} %get-tuple-element.45), channel_id=1, source_target_pairs={{0,8},{1,9},{2,10},{3,11},{4,12},{5,13},{6,14},{7,15},{8,0},{9,1},... | collective-permute-start | bytes 147464 | tf_op jit(solution)/shard_map/ppermute | solution.py:426
  25.5 4.2 %collective-permute-start.13 = (f32[96,128]{1,0:T(8,128)S(1)}, f32[96,128]{1,0:T(8,128)S(1)}, u32[]{:S(2)}, u32[]{:S(2)}) collective-permute-start(f32[96,128]{1,0:T(8,128)S(1)} %get-tuple-element.46), channel_id=1, source_target_pairs={{0,12},{1,13},{2,14},{3,15},{4,0},{5,1},{6,2},{7,3},{8,4},{9,5},{1... | collective-permute-start | bytes 147464 | tf_op jit(solution)/shard_map/ppermute | solution.py:426

commit v12 on v11

--- a/solution.py
+++ b/solution.py
@@ -173,7 +173,9 @@
     for c in range(chunks):
         load(c).wait()
         for h in range(c * size, (c + 1) * size):
-            weight_ref[h] = jnp.concatenate(split(state[h]), axis=0)
+            group, n = divmod(h, weight_ref.shape[2] // state.shape[2])
+            lanes = slice(n * state.shape[2], (n + 1) * state.shape[2])
+            weight_ref[group, :, lanes] = jnp.concatenate(split(state[h]), axis=0)
     for copy in copies[2:]:
         copy.wait()
 
@@ -201,10 +203,15 @@
         high = x.astype(BF16).astype(F32)
         lhs[t * heads:(t + 1) * heads, :] = high
         lhs[(late + t) * heads:(late + t + 1) * heads, :] = x - high
-    for h in range(heads):
-        x = lhs[pl.ds(h, 2 * late, stride=heads), :].astype(BF16)
-        prod[pl.ds(h, 2 * late, stride=heads), :] = jnp.dot(
-            jnp.concatenate([x, x], axis=1), weight_ref[h], preferred_element_type=F32)
+    depth = lhs.shape[0] // heads
+    joint = weight_ref.shape[2] // width
+    for group in range(heads // joint):
+        rows = [pl.ds(group * joint + n, depth, stride=heads) for n in range(joint)]
+        x = jnp.concatenate([lhs[r, :] for r in rows], axis=0).astype(BF16)
+        result = jnp.dot(
+            jnp.concatenate([x, x], axis=1), weight_ref[group], preferred_element_type=F32)
+        for n in range(joint):
+            prod[rows[n], :] = result[n * depth:(n + 1) * depth, n * width:(n + 1) * width]
     for t in range(late):
         total = block(prod, t) + block(prod, late + t)
         for s in range(BEFORE):
@@ -454,10 +461,11 @@
     wishes = gather_inner(facts)
 
     chunks = 8
+    joint = 2 - heads % 2
     gain = norm_gain.reshape(heads, width)
     weight, early, rows, gain_rows = pl.pallas_call(
         functools.partial(prepare_kernel, count=count, chunks=chunks),
-        out_shape=(jax.ShapeDtypeStruct((heads, 2 * width, width), BF16),
+        out_shape=(jax.ShapeDtypeStruct((heads // joint, 2 * width, joint * width), BF16),
                    jax.ShapeDtypeStruct((2, BEFORE * heads, width), F32),
                    jax.ShapeDtypeStruct((4, packed_rows, width), BF16),
                    jax.ShapeDtypeStruct(gain.shape, F32)),
@@ -481,7 +489,7 @@
         functools.partial(answer_kernel, inner=inner, late=late, heads=heads, width=width,
                           order=q1),
         out_shape=single, in_specs=[VMEM] * (inner + 3), out_specs=VMEM,
-        scratch_shapes=[pltpu.VMEM((2 * late * heads, width), F32)] * 2,
+        scratch_shapes=[pltpu.VMEM((-(-2 * late // 8) * 8 * heads, width), F32)] * 2,
         compiler_params=params(8), name="answer",
     )(facts, *found, weight, early)
     replies = [answer] + [send_inner(answer, k) for k in q2]

time: 30.7 us -> 30.7 us (level)
  no operation moved by 1% of the time
where the time goes in v12:
time: 30.7 us; the launch traced here: 30.4 us
  starting transfers between devices  15.7 us (51%)
  Pallas kernels  9.41 us (31%)
  waiting for transfers between devices  5.29 us (17%)
    ppermute x3, starting transfers between devices, send_outer(): lax.ppermute(x, 'req', [(o * inner + i, int(turn(o, k, outer)) * inner +...  5.83 us
    ppermute x8, starting transfers between devices, send_inner(): lax.ppermute(x, 'req', [(o * inner + i, o * inner + int(turn(i, k, inner)...  5.37 us
    ppermute x8, waiting for transfers between devices, send_inner(): lax.ppermute(x, 'req', [(o * inner + i, o * inner + int(turn(i, k, inner)...  4.63 us
    ppermute x3, starting transfers between devices, shift_outer(): lax.ppermute(x, 'req', [(o * inner + i, (o + k) % outer * inner + i) for...  4.44 us
    pallas_call x1, Pallas kernels, on_device(): pl.pallas_call(functools.partial(local_kernel, slots=last_slots, count=co...  2.67 us
    pallas_call x1, Pallas kernels, on_device(): pl.pallas_call(functools.partial(prepare_kernel, count=count, chunks=chun...  2.49 us
    pallas_call x1, Pallas kernels, on_device(): pl.pallas_call(functools.partial(scores_kernel, slots=first_slots, count=...  2.13 us
    pallas_call x1, Pallas kernels, on_device(): pl.pallas_call(functools.partial(ask_kernel, count=count, inner=inner), o...  0.85 us
  transfers between devices with their start and end apart: 14, of which 6 were waited for; matrix products, arithmetic and copies ran while one was open for 0% of the time, Pallas kernels for 24%

profile of v12, /device:TPU:0, one launch (start us, length us, event | category | flops | bytes accessed | tf_op | source)
XLA Modules:
  0.0 30.4 jit_solution(13887823600830627197)
XLA Ops:
  0.0 0.9 %ask.1 = (f32[96,128]{1,0:T(8,128)S(1)}, f32[104,128]{1,0:T(8,128)S(1)}, s32[80,128]{1,0:T(8,128)S(1)}) custom-call(s32[2]{0:T(128)} %slots_ref.1, bf16[384,128]{1,0:T(8,128)(2,1)} %bitcast.26), custom_call_target="tpu_custom_call" | custom-call | tf_op jit(solution)/shard_map/ask/pallas_call | solution.py:449
  0.9 5.1 %collective-permute-start.4 = (f32[104,128]{1,0:T(8,128)S(1)}, f32[104,128]{1,0:T(8,128)S(1)}, u32[]{:S(2)}, u32[]{:S(2)}) collective-permute-start(f32[104,128]{1,0:T(8,128)S(1)} %get-tuple-element.30), channel_id=1, source_target_pairs={{0,12},{1,13},{2,14},{3,15},{4,8},{5,9},{6,10},{7,11},{8,4},{9,5},... | collective-permute-start | bytes 159752 | tf_op jit(solution)/shard_map/ppermute | solution.py:414
  6.0 0.7 %collective-permute-start.2 = (f32[96,128]{1,0:T(8,128)S(1)}, f32[96,128]{1,0:T(8,128)S(1)}, u32[]{:S(2)}, u32[]{:S(2)}) collective-permute-start(f32[96,128]{1,0:T(8,128)S(1)} %get-tuple-element.29.refs_0_), channel_id=1, source_target_pairs={{0,4},{1,5},{2,6},{3,7},{4,0},{5,1},{6,2},{7,3},{8,12},{9,13},{10,... | collective-permute-start | bytes 147464 | tf_op jit(solution)/shard_map/ppermute | solution.py:414
  6.7 0.5 %collective-permute-done.far_ref = s32[80,128]{1,0:T(8,128)S(1)} collective-permute-done((s32[80,128]{1,0:T(8,128)S(1)}, s32[80,128]{1,0:T(8,128)S(1)}, u32[]{:S(2)}, u32[]{:S(2)}) %collective-permute-start) | collective-permute-done | bytes 40992 | tf_op jit(solution)/shard_map/ppermute | solution.py:409
  7.2 1.5 %collective-permute-start.1 = (s32[16,128]{1,0:T(8,128)S(1)}, s32[16,128]{1,0:T(8,128)S(1)}, u32[]{:S(2)}, u32[]{:S(2)}) collective-permute-start(s32[16,128]{1,0:T(8,128)S(1)} %pair.2.near_ref), channel_id=1, source_target_pairs={{0,2},{1,3},{2,0},{3,1},{4,6},{5,7},{6,4},{7,5},{8,10},{9,11},{10,... | collective-permute-start | bytes 24584 | tf_op jit(solution)/shard_map/ppermute | solution.py:409
  8.7 2.1 %collective-permute-done.1.far_ref = s32[16,128]{1,0:T(8,128)S(1)} collective-permute-done((s32[16,128]{1,0:T(8,128)S(1)}, s32[16,128]{1,0:T(8,128)S(1)}, u32[]{:S(2)}, u32[]{:S(2)}) %collective-permute-start.1) | collective-permute-done | bytes 8224 | tf_op jit(solution)/shard_map/ppermute | solution.py:409
  10.9 0.3 %collective-permute-done.3.refs_2_ = f32[96,128]{1,0:T(8,128)S(1)} collective-permute-done((f32[96,128]{1,0:T(8,128)S(1)}, f32[96,128]{1,0:T(8,128)S(1)}, u32[]{:S(2)}, u32[]{:S(2)}) %collective-permute-start.3) | collective-permute-done | bytes 49184 | tf_op jit(solution)/shard_map/ppermute | solution.py:414
  11.2 0.8 %collective-permute-start.5 = (f32[96,128]{1,0:T(8,128)S(1)}, f32[96,128]{1,0:T(8,128)S(1)}, u32[]{:S(2)}, u32[]{:S(2)}) collective-permute-start(f32[96,128]{1,0:T(8,128)S(1)} %get-tuple-element.32), channel_id=1, source_target_pairs={{0,3},{1,2},{2,1},{3,0},{4,7},{5,6},{6,5},{7,4},{8,11},{9,10},{10,... | collective-permute-start | bytes 147464 | tf_op jit(solution)/shard_map/ppermute | solution.py:409
  12.1 0.8 %collective-permute-start.6 = (f32[96,128]{1,0:T(8,128)S(1)}, f32[96,128]{1,0:T(8,128)S(1)}, u32[]{:S(2)}, u32[]{:S(2)}) collective-permute-start(f32[96,128]{1,0:T(8,128)S(1)} %get-tuple-element.33), channel_id=1, source_target_pairs={{0,2},{1,3},{2,0},{3,1},{4,6},{5,7},{6,4},{7,5},{8,10},{9,11},{10,... | collective-permute-start | bytes 147464 | tf_op jit(solution)/shard_map/ppermute | solution.py:409
  12.9 0.3 collective-permute-start.7
  13.2 2.5 %prepare.1 = (bf16[16,256,256]{2,1,0:T(8,128)(2,1)S(1)}, f32[2,96,128]{2,1,0:T(8,128)S(1)}, bf16[4,384,128]{2,1,0:T(8,128)(2,1)S(1)}, f32[32,128]{1,0:T(8,128)S(1)}) custom-call(s32[2]{0:T(128)} %slots_ref.1, bf16[384,128]{1,0:T(8,128)(2,1)} %bitcast.27, bf16[384,128]{1,0:T(8,128)(2,1)} %bitcast.28, bf16[384,128]{1,0:T(8,128)(2,1)} %bitcast.29, ...), custom_call_target="tpu_custom_call" | custom-call | tf_op jit(solution)/shard_map/prepare/pallas_call | solution.py:466
  15.7 0.9 %collective-permute-done.6.refs_2_ = f32[96,128]{1,0:T(8,128)S(1)} collective-permute-done((f32[96,128]{1,0:T(8,128)S(1)}, f32[96,128]{1,0:T(8,128)S(1)}, u32[]{:S(2)}, u32[]{:S(2)}) %collective-permute-start.6) | collective-permute-done | bytes 49184 | tf_op jit(solution)/shard_map/ppermute | solution.py:409
  16.6 0.4 %answer.1.after_ref.refs_0_ = f32[96,128]{1,0:T(8,128)S(1)} custom-call(s32[80,128]{1,0:T(8,128)S(1)} %get-tuple-element.26.near_ref.facts_ref, f32[96,128]{1,0:T(8,128)S(1)} %get-tuple-element.31.refs_0_, f32[96,128]{1,0:T(8,128)S(1)} %collective-permute-done.5.refs_1_, f32[96,128]{1,0:T(8,128)S(1)} %collective-permute-done.6.refs_2_, ...), custom_call_target="tpu_custom_call" | custom-call | tf_op jit(solution)/shard_map/answer/pallas_call | solution.py:488
  17.0 0.8 %collective-permute-start.10 = (f32[96,128]{1,0:T(8,128)S(1)}, f32[96,128]{1,0:T(8,128)S(1)}, u32[]{:S(2)}, u32[]{:S(2)}) collective-permute-start(f32[96,128]{1,0:T(8,128)S(1)} %answer.1.after_ref.refs_0_), channel_id=1, source_target_pairs={{0,3},{1,2},{2,1},{3,0},{4,7},{5,6},{6,5},{7,4},{8,11},{9,10},{10,... | collective-permute-start | bytes 147464 | tf_op jit(solution)/shard_map/ppermute | solution.py:409
  17.8 0.9 %collective-permute-start.9 = (f32[96,128]{1,0:T(8,128)S(1)}, f32[96,128]{1,0:T(8,128)S(1)}, u32[]{:S(2)}, u32[]{:S(2)}) collective-permute-start(f32[96,128]{1,0:T(8,128)S(1)} %answer.1.after_ref.refs_0_), channel_id=1, source_target_pairs={{0,2},{1,3},{2,0},{3,1},{4,6},{5,7},{6,4},{7,5},{8,10},{9,11},{10,... | collective-permute-start | bytes 147464 | tf_op jit(solution)/shard_map/ppermute | solution.py:409
  18.7 0.2 collective-permute-start.8
  18.9 2.1 %scores.1 = (f32[384,128]{1,0:T(8,128)S(1)}, f32[384,128]{1,0:T(8,128)S(1)}, f32[2,96,128]{2,1,0:T(8,128)S(1)}, f32[1024,128]{1,0:T(8,128)S(1)}) custom-call(s32[80,128]{1,0:T(8,128)S(1)} %get-tuple-element.26.near_ref.facts_ref, bf16[4,384,128]{2,1,0:T(8,128)(2,1)S(1)} %get-tuple-element.27.rows_ref, f32[32,128]{1,0:T(8,128)S(1)} %get-tuple-element.28.gain_ref, ...), custom_call_target="tpu_custom_call" | custom-call | tf_op jit(solution)/shard_map/scores/pallas_call | solution.py:501
  21.1 1.1 %collective-permute-done.9.refs_2_ = f32[96,128]{1,0:T(8,128)S(1)} collective-permute-done((f32[96,128]{1,0:T(8,128)S(1)}, f32[96,128]{1,0:T(8,128)S(1)}, u32[]{:S(2)}, u32[]{:S(2)}) %collective-permute-start.9) | collective-permute-done | bytes 49184 | tf_op jit(solution)/shard_map/ppermute | solution.py:409
  22.2 0.5 %collective-permute-start.11 = (f32[96,128]{1,0:T(8,128)S(1)}, f32[96,128]{1,0:T(8,128)S(1)}, u32[]{:S(2)}, u32[]{:S(2)}) collective-permute-start(f32[96,128]{1,0:T(8,128)S(1)} %get-tuple-element.44), channel_id=1, source_target_pairs={{0,4},{1,5},{2,6},{3,7},{4,8},{5,9},{6,10},{7,11},{8,12},{9,13},{1... | collective-permute-start | bytes 147464 | tf_op jit(solution)/shard_map/ppermute | solution.py:433
  22.7 2.7 %collective-permute-start.12 = (f32[96,128]{1,0:T(8,128)S(1)}, f32[96,128]{1,0:T(8,128)S(1)}, u32[]{:S(2)}, u32[]{:S(2)}) collective-permute-start(f32[96,128]{1,0:T(8,128)S(1)} %get-tuple-element.45), channel_id=1, source_target_pairs={{0,8},{1,9},{2,10},{3,11},{4,12},{5,13},{6,14},{7,15},{8,0},{9,1},... | collective-permute-start | bytes 147464 | tf_op jit(solution)/shard_map/ppermute | solution.py:433
  25.4 1.2 %collective-permute-start.13 = (f32[96,128]{1,0:T(8,128)S(1)}, f32[96,128]{1,0:T(8,128)S(1)}, u32[]{:S(2)}, u32[]{:S(2)}) collective-permute-start(f32[96,128]{1,0:T(8,128)S(1)} %get-tuple-element.46), channel_id=1, source_target_pairs={{0,12},{1,13},{2,14},{3,15},{4,0},{5,1},{6,2},{7,3},{8,4},{9,5},{1... | collective-permute-start | bytes 147464 | tf_op jit(solution)/shard_map/ppermute | solution.py:433
  26.7 2.7 %local.1 = (bf16[384,128]{1,0:T(8,128)(2,1)}, bf16[192,128]{1,0:T(8,128)(2,1)S(1)}) custom-call(f32[384,128]{1,0:T(8,128)S(1)} %get-tuple-element.37.mixed_ref, f32[384,128]{1,0:T(8,128)S(1)} %get-tuple-element.38.scale_ref, f32[1024,128]{1,0:T(8,128)S(1)} %get-tuple-element.39.lhs, f32[96,128]{1,0:T(8,128)S(1)} %get-tuple-element.41.after_ref.refs_0_, ...), custom_call_target="tpu_custom_call" | custom-call | tf_op jit(solution)/shard_map/local/pallas_call | solution.py:523
  29.4 0.3 collective-permute-done.13.refs_3_
  29.7 0.8 %finish.1 = bf16[384,128]{1,0:T(8,128)(2,1)} custom-call(s32[80,128]{1,0:T(8,128)S(1)} %get-tuple-element.26.near_ref.facts_ref, bf16[384,128]{1,0:T(8,128)(2,1)} %get-tuple-element.42.base_ref, bf16[192,128]{1,0:T(8,128)(2,1)S(1)} %get-tuple-element.43.last_ref, ...), custom_call_target="tpu_custom_call", output_to_operand_aliasing={{}: (1, {})} | custom-call | tf_op jit(solution)/shard_map/finish/pallas_call | solution.py:535
  (14 shorter events, 0.2 us)
Async XLA Ops:
  0.9 10.3 %collective-permute-start.4 = (f32[104,128]{1,0:T(8,128)S(1)}, f32[104,128]{1,0:T(8,128)S(1)}, u32[]{:S(2)}, u32[]{:S(2)}) collective-permute-start(f32[104,128]{1,0:T(8,128)S(1)} %get-tuple-element.30), channel_id=1, source_target_pairs={{0,12},{1,13},{2,14},{3,15},{4,8},{5,9},{6,10},{7,11},{8,4},{9,5},... | collective-permute-start | bytes 159752 | tf_op jit(solution)/shard_map/ppermute | solution.py:414
  6.0 1.2 %collective-permute-start = (s32[80,128]{1,0:T(8,128)S(1)}, s32[80,128]{1,0:T(8,128)S(1)}, u32[]{:S(2)}, u32[]{:S(2)}) collective-permute-start(s32[80,128]{1,0:T(8,128)S(1)} %get-tuple-element.26.near_ref.facts_ref), channel_id=1, source_target_pairs={{0,1},{1,0},{2,3},{3,2},{4,5},{5,4},{6,7},{7,6},{8,9},{9,8},{10,11... | collective-permute-start | bytes 122888 | tf_op jit(solution)/shard_map/ppermute | solution.py:409
  6.0 5.2 %collective-permute-start.3 = (f32[96,128]{1,0:T(8,128)S(1)}, f32[96,128]{1,0:T(8,128)S(1)}, u32[]{:S(2)}, u32[]{:S(2)}) collective-permute-start(f32[96,128]{1,0:T(8,128)S(1)} %get-tuple-element.29.refs_0_), channel_id=1, source_target_pairs={{0,8},{1,9},{2,10},{3,11},{4,12},{5,13},{6,14},{7,15},{8,0},{9,1},... | collective-permute-start | bytes 147464 | tf_op jit(solution)/shard_map/ppermute | solution.py:414
  6.0 5.2 %collective-permute-start.2 = (f32[96,128]{1,0:T(8,128)S(1)}, f32[96,128]{1,0:T(8,128)S(1)}, u32[]{:S(2)}, u32[]{:S(2)}) collective-permute-start(f32[96,128]{1,0:T(8,128)S(1)} %get-tuple-element.29.refs_0_), channel_id=1, source_target_pairs={{0,4},{1,5},{2,6},{3,7},{4,0},{5,1},{6,2},{7,3},{8,12},{9,13},{10,... | collective-permute-start | bytes 147464 | tf_op jit(solution)/shard_map/ppermute | solution.py:414
  7.2 3.7 %collective-permute-start.1 = (s32[16,128]{1,0:T(8,128)S(1)}, s32[16,128]{1,0:T(8,128)S(1)}, u32[]{:S(2)}, u32[]{:S(2)}) collective-permute-start(s32[16,128]{1,0:T(8,128)S(1)} %pair.2.near_ref), channel_id=1, source_target_pairs={{0,2},{1,3},{2,0},{3,1},{4,6},{5,7},{6,4},{7,5},{8,10},{9,11},{10,... | collective-permute-start | bytes 24584 | tf_op jit(solution)/shard_map/ppermute | solution.py:409
  11.2 4.4 %collective-permute-start.5 = (f32[96,128]{1,0:T(8,128)S(1)}, f32[96,128]{1,0:T(8,128)S(1)}, u32[]{:S(2)}, u32[]{:S(2)}) collective-permute-start(f32[96,128]{1,0:T(8,128)S(1)} %get-tuple-element.32), channel_id=1, source_target_pairs={{0,3},{1,2},{2,1},{3,0},{4,7},{5,6},{6,5},{7,4},{8,11},{9,10},{10,... | collective-permute-start | bytes 147464 | tf_op jit(solution)/shard_map/ppermute | solution.py:409
  12.1 4.5 %collective-permute-start.6 = (f32[96,128]{1,0:T(8,128)S(1)}, f32[96,128]{1,0:T(8,128)S(1)}, u32[]{:S(2)}, u32[]{:S(2)}) collective-permute-start(f32[96,128]{1,0:T(8,128)S(1)} %get-tuple-element.33), channel_id=1, source_target_pairs={{0,2},{1,3},{2,0},{3,1},{4,6},{5,7},{6,4},{7,5},{8,10},{9,11},{10,... | collective-permute-start | bytes 147464 | tf_op jit(solution)/shard_map/ppermute | solution.py:409
  12.9 3.7 %collective-permute-start.7 = (f32[96,128]{1,0:T(8,128)S(1)}, f32[96,128]{1,0:T(8,128)S(1)}, u32[]{:S(2)}, u32[]{:S(2)}) collective-permute-start(f32[96,128]{1,0:T(8,128)S(1)} %get-tuple-element.34), channel_id=1, source_target_pairs={{0,1},{1,0},{2,3},{3,2},{4,5},{5,4},{6,7},{7,6},{8,9},{9,8},{10,11... | collective-permute-start | bytes 147464 | tf_op jit(solution)/shard_map/ppermute | solution.py:409
  17.0 4.1 %collective-permute-start.10 = (f32[96,128]{1,0:T(8,128)S(1)}, f32[96,128]{1,0:T(8,128)S(1)}, u32[]{:S(2)}, u32[]{:S(2)}) collective-permute-start(f32[96,128]{1,0:T(8,128)S(1)} %answer.1.after_ref.refs_0_), channel_id=1, source_target_pairs={{0,3},{1,2},{2,1},{3,0},{4,7},{5,6},{6,5},{7,4},{8,11},{9,10},{10,... | collective-permute-start | bytes 147464 | tf_op jit(solution)/shard_map/ppermute | solution.py:409
  17.8 4.4 %collective-permute-start.9 = (f32[96,128]{1,0:T(8,128)S(1)}, f32[96,128]{1,0:T(8,128)S(1)}, u32[]{:S(2)}, u32[]{:S(2)}) collective-permute-start(f32[96,128]{1,0:T(8,128)S(1)} %answer.1.after_ref.refs_0_), channel_id=1, source_target_pairs={{0,2},{1,3},{2,0},{3,1},{4,6},{5,7},{6,4},{7,5},{8,10},{9,11},{10,... | collective-permute-start | bytes 147464 | tf_op jit(solution)/shard_map/ppermute | solution.py:409
  18.7 3.5 %collective-permute-start.8 = (f32[96,128]{1,0:T(8,128)S(1)}, f32[96,128]{1,0:T(8,128)S(1)}, u32[]{:S(2)}, u32[]{:S(2)}) collective-permute-start(f32[96,128]{1,0:T(8,128)S(1)} %answer.1.after_ref.refs_0_), channel_id=1, source_target_pairs={{0,1},{1,0},{2,3},{3,2},{4,5},{5,4},{6,7},{7,6},{8,9},{9,8},{10,11... | collective-permute-start | bytes 147464 | tf_op jit(solution)/shard_map/ppermute | solution.py:409
  22.2 7.1 %collective-permute-start.11 = (f32[96,128]{1,0:T(8,128)S(1)}, f32[96,128]{1,0:T(8,128)S(1)}, u32[]{:S(2)}, u32[]{:S(2)}) collective-permute-start(f32[96,128]{1,0:T(8,128)S(1)} %get-tuple-element.44), channel_id=1, source_target_pairs={{0,4},{1,5},{2,6},{3,7},{4,8},{5,9},{6,10},{7,11},{8,12},{9,13},{1... | collective-permute-start | bytes 147464 | tf_op jit(solution)/shard_map/ppermute | solution.py:433
  22.7 6.7 %collective-permute-start.12 = (f32[96,128]{1,0:T(8,128)S(1)}, f32[96,128]{1,0:T(8,128)S(1)}, u32[]{:S(2)}, u32[]{:S(2)}) collective-permute-start(f32[96,128]{1,0:T(8,128)S(1)} %get-tuple-element.45), channel_id=1, source_target_pairs={{0,8},{1,9},{2,10},{3,11},{4,12},{5,13},{6,14},{7,15},{8,0},{9,1},... | collective-permute-start | bytes 147464 | tf_op jit(solution)/shard_map/ppermute | solution.py:433
  25.4 4.2 %collective-permute-start.13 = (f32[96,128]{1,0:T(8,128)S(1)}, f32[96,128]{1,0:T(8,128)S(1)}, u32[]{:S(2)}, u32[]{:S(2)}) collective-permute-start(f32[96,128]{1,0:T(8,128)S(1)} %get-tuple-element.46), channel_id=1, source_target_pairs={{0,12},{1,13},{2,14},{3,15},{4,0},{5,1},{6,2},{7,3},{8,4},{9,5},{1... | collective-permute-start | bytes 147464 | tf_op jit(solution)/shard_map/ppermute | solution.py:433

commit v13 on v11

--- a/solution.py
+++ b/solution.py
@@ -450,7 +450,7 @@
 
     z1, z2 = list(range(1, outer)), list(range(1, outer))
     q1, q2 = list(range(inner - 1, 0, -1)), list(range(1, inner))
-    column = [ask] + [send_outer(ask_long if k == outer - 1 else ask, k) for k in z1]
+    column = [ask] + [send_outer(ask_long if k == outer // 2 else ask, k) for k in z1]
     wishes = gather_inner(facts)
 
     chunks = 8

time: 30.7 us -> 30.7 us (level)
    ppermute x8, waiting for transfers between devices: 4.65 us -> 3.72 us  [send_inner(): lax.ppermute(x, 'req', [(o * inner + i, o * inner + int(turn(i, k, inner)...]
    ppermute x3, waiting for transfers between devices: 0.34 us -> 1.24 us  [send_outer(): lax.ppermute(x, 'req', [(o * inner + i, int(turn(o, k, outer)) * inner +...]
where the time goes in v13:
time: 30.7 us; the launch traced here: 30.4 us
  starting transfers between devices  15.7 us (51%)
  Pallas kernels  9.41 us (31%)
  waiting for transfers between devices  5.28 us (17%)
    ppermute x3, starting transfers between devices, send_outer(): lax.ppermute(x, 'req', [(o * inner + i, int(turn(o, k, outer)) * inner +...  5.68 us
    ppermute x8, starting transfers between devices, send_inner(): lax.ppermute(x, 'req', [(o * inner + i, o * inner + int(turn(i, k, inner)...  5.41 us
    ppermute x3, starting transfers between devices, shift_outer(): lax.ppermute(x, 'req', [(o * inner + i, (o + k) % outer * inner + i) for...  4.57 us
    ppermute x8, waiting for transfers between devices, send_inner(): lax.ppermute(x, 'req', [(o * inner + i, o * inner + int(turn(i, k, inner)...  3.72 us
    pallas_call x1, Pallas kernels, on_device(): pl.pallas_call(functools.partial(local_kernel, slots=last_slots, count=co...  2.67 us
    pallas_call x1, Pallas kernels, on_device(): pl.pallas_call(functools.partial(prepare_kernel, count=count, chunks=chun...  2.48 us
    pallas_call x1, Pallas kernels, on_device(): pl.pallas_call(functools.partial(scores_kernel, slots=first_slots, count=...  2.13 us
    ppermute x3, waiting for transfers between devices, send_outer(): lax.ppermute(x, 'req', [(o * inner + i, int(turn(o, k, outer)) * inner +...  1.24 us
  transfers between devices with their start and end apart: 14, of which 6 were waited for; matrix products, arithmetic and copies ran while one was open for 0% of the time, Pallas kernels for 24%

profile of v13, /device:TPU:0, one launch (start us, length us, event | category | flops | bytes accessed | tf_op | source)
XLA Modules:
  0.0 30.4 jit_solution(16849378570517030717)
XLA Ops:
  0.0 0.9 %ask.1 = (f32[96,128]{1,0:T(8,128)S(1)}, f32[104,128]{1,0:T(8,128)S(1)}, s32[80,128]{1,0:T(8,128)S(1)}) custom-call(s32[2]{0:T(128)} %slots_ref.1, bf16[384,128]{1,0:T(8,128)(2,1)} %bitcast.26), custom_call_target="tpu_custom_call" | custom-call | tf_op jit(solution)/shard_map/ask/pallas_call | solution.py:442
  0.9 4.1 %collective-permute-start.3 = (f32[104,128]{1,0:T(8,128)S(1)}, f32[104,128]{1,0:T(8,128)S(1)}, u32[]{:S(2)}, u32[]{:S(2)}) collective-permute-start(f32[104,128]{1,0:T(8,128)S(1)} %get-tuple-element.30), channel_id=1, source_target_pairs={{0,8},{1,9},{2,10},{3,11},{4,12},{5,13},{6,14},{7,15},{8,0},{9,1},... | collective-permute-start | bytes 159752 | tf_op jit(solution)/shard_map/ppermute | solution.py:407
  5.0 1.3 %collective-permute-start.4 = (f32[96,128]{1,0:T(8,128)S(1)}, f32[96,128]{1,0:T(8,128)S(1)}, u32[]{:S(2)}, u32[]{:S(2)}) collective-permute-start(f32[96,128]{1,0:T(8,128)S(1)} %get-tuple-element.29.refs_0_), channel_id=1, source_target_pairs={{0,12},{1,13},{2,14},{3,15},{4,8},{5,9},{6,10},{7,11},{8,4},{9,5},... | collective-permute-start | bytes 147464 | tf_op jit(solution)/shard_map/ppermute | solution.py:407
  6.3 0.2 collective-permute-start.2
  6.6 1.5 %collective-permute-start.1 = (s32[16,128]{1,0:T(8,128)S(1)}, s32[16,128]{1,0:T(8,128)S(1)}, u32[]{:S(2)}, u32[]{:S(2)}) collective-permute-start(s32[16,128]{1,0:T(8,128)S(1)} %pair.2.near_ref), channel_id=1, source_target_pairs={{0,2},{1,3},{2,0},{3,1},{4,6},{5,7},{6,4},{7,5},{8,10},{9,11},{10,... | collective-permute-start | bytes 24584 | tf_op jit(solution)/shard_map/ppermute | solution.py:402
  8.1 2.1 %collective-permute-done.1.far_ref = s32[16,128]{1,0:T(8,128)S(1)} collective-permute-done((s32[16,128]{1,0:T(8,128)S(1)}, s32[16,128]{1,0:T(8,128)S(1)}, u32[]{:S(2)}, u32[]{:S(2)}) %collective-permute-start.1) | collective-permute-done | bytes 8224 | tf_op jit(solution)/shard_map/ppermute | solution.py:402
  10.2 1.1 %collective-permute-done.4.refs_3_ = f32[96,128]{1,0:T(8,128)S(1)} collective-permute-done((f32[96,128]{1,0:T(8,128)S(1)}, f32[96,128]{1,0:T(8,128)S(1)}, u32[]{:S(2)}, u32[]{:S(2)}) %collective-permute-start.4) | collective-permute-done | bytes 49184 | tf_op jit(solution)/shard_map/ppermute | solution.py:407
  11.5 0.4 %collective-permute-start.5 = (f32[96,128]{1,0:T(8,128)S(1)}, f32[96,128]{1,0:T(8,128)S(1)}, u32[]{:S(2)}, u32[]{:S(2)}) collective-permute-start(f32[96,128]{1,0:T(8,128)S(1)} %get-tuple-element.32), channel_id=1, source_target_pairs={{0,3},{1,2},{2,1},{3,0},{4,7},{5,6},{6,5},{7,4},{8,11},{9,10},{10,... | collective-permute-start | bytes 147464 | tf_op jit(solution)/shard_map/ppermute | solution.py:402
  11.9 1.3 %collective-permute-start.6 = (f32[96,128]{1,0:T(8,128)S(1)}, f32[96,128]{1,0:T(8,128)S(1)}, u32[]{:S(2)}, u32[]{:S(2)}) collective-permute-start(f32[96,128]{1,0:T(8,128)S(1)} %get-tuple-element.33), channel_id=1, source_target_pairs={{0,2},{1,3},{2,0},{3,1},{4,6},{5,7},{6,4},{7,5},{8,10},{9,11},{10,... | collective-permute-start | bytes 147464 | tf_op jit(solution)/shard_map/ppermute | solution.py:402
  13.2 0.3 collective-permute-start.7
  13.4 2.5 %prepare.1 = (bf16[32,256,128]{2,1,0:T(8,128)(2,1)S(1)}, f32[2,96,128]{2,1,0:T(8,128)S(1)}, bf16[4,384,128]{2,1,0:T(8,128)(2,1)S(1)}, f32[32,128]{1,0:T(8,128)S(1)}) custom-call(s32[2]{0:T(128)} %slots_ref.1, bf16[384,128]{1,0:T(8,128)(2,1)} %bitcast.27, bf16[384,128]{1,0:T(8,128)(2,1)} %bitcast.28, bf16[384,128]{1,0:T(8,128)(2,1)} %bitcast.29, ...), custom_call_target="tpu_custom_call" | custom-call | tf_op jit(solution)/shard_map/prepare/pallas_call | solution.py:458
  15.9 0.5 %collective-permute-done.6.refs_2_ = f32[96,128]{1,0:T(8,128)S(1)} collective-permute-done((f32[96,128]{1,0:T(8,128)S(1)}, f32[96,128]{1,0:T(8,128)S(1)}, u32[]{:S(2)}, u32[]{:S(2)}) %collective-permute-start.6) | collective-permute-done | bytes 49184 | tf_op jit(solution)/shard_map/ppermute | solution.py:402
  16.4 0.5 %answer.1.after_ref.refs_0_ = f32[96,128]{1,0:T(8,128)S(1)} custom-call(s32[80,128]{1,0:T(8,128)S(1)} %get-tuple-element.26.near_ref.facts_ref, f32[96,128]{1,0:T(8,128)S(1)} %get-tuple-element.31.refs_0_, f32[96,128]{1,0:T(8,128)S(1)} %collective-permute-done.5.refs_1_, f32[96,128]{1,0:T(8,128)S(1)} %collective-permute-done.6.refs_2_, ...), custom_call_target="tpu_custom_call" | custom-call | tf_op jit(solution)/shard_map/answer/pallas_call | solution.py:480
  16.9 0.9 %collective-permute-start.10 = (f32[96,128]{1,0:T(8,128)S(1)}, f32[96,128]{1,0:T(8,128)S(1)}, u32[]{:S(2)}, u32[]{:S(2)}) collective-permute-start(f32[96,128]{1,0:T(8,128)S(1)} %answer.1.after_ref.refs_0_), channel_id=1, source_target_pairs={{0,3},{1,2},{2,1},{3,0},{4,7},{5,6},{6,5},{7,4},{8,11},{9,10},{10,... | collective-permute-start | bytes 147464 | tf_op jit(solution)/shard_map/ppermute | solution.py:402
  17.8 0.9 %collective-permute-start.9 = (f32[96,128]{1,0:T(8,128)S(1)}, f32[96,128]{1,0:T(8,128)S(1)}, u32[]{:S(2)}, u32[]{:S(2)}) collective-permute-start(f32[96,128]{1,0:T(8,128)S(1)} %answer.1.after_ref.refs_0_), channel_id=1, source_target_pairs={{0,2},{1,3},{2,0},{3,1},{4,6},{5,7},{6,4},{7,5},{8,10},{9,11},{10,... | collective-permute-start | bytes 147464 | tf_op jit(solution)/shard_map/ppermute | solution.py:402
  18.7 0.1 collective-permute-start.8
  18.9 2.1 %scores.1 = (f32[384,128]{1,0:T(8,128)S(1)}, f32[384,128]{1,0:T(8,128)S(1)}, f32[2,96,128]{2,1,0:T(8,128)S(1)}, f32[1024,128]{1,0:T(8,128)S(1)}) custom-call(s32[80,128]{1,0:T(8,128)S(1)} %get-tuple-element.26.near_ref.facts_ref, bf16[4,384,128]{2,1,0:T(8,128)(2,1)S(1)} %get-tuple-element.27.rows_ref, f32[32,128]{1,0:T(8,128)S(1)} %get-tuple-element.28.gain_ref, ...), custom_call_target="tpu_custom_call" | custom-call | tf_op jit(solution)/shard_map/scores/pallas_call | solution.py:493
  21.0 1.1 %collective-permute-done.9.refs_2_ = f32[96,128]{1,0:T(8,128)S(1)} collective-permute-done((f32[96,128]{1,0:T(8,128)S(1)}, f32[96,128]{1,0:T(8,128)S(1)}, u32[]{:S(2)}, u32[]{:S(2)}) %collective-permute-start.9) | collective-permute-done | bytes 49184 | tf_op jit(solution)/shard_map/ppermute | solution.py:402
  22.1 0.6 %collective-permute-start.11 = (f32[96,128]{1,0:T(8,128)S(1)}, f32[96,128]{1,0:T(8,128)S(1)}, u32[]{:S(2)}, u32[]{:S(2)}) collective-permute-start(f32[96,128]{1,0:T(8,128)S(1)} %get-tuple-element.44), channel_id=1, source_target_pairs={{0,4},{1,5},{2,6},{3,7},{4,8},{5,9},{6,10},{7,11},{8,12},{9,13},{1... | collective-permute-start | bytes 147464 | tf_op jit(solution)/shard_map/ppermute | solution.py:426
  22.7 2.7 %collective-permute-start.12 = (f32[96,128]{1,0:T(8,128)S(1)}, f32[96,128]{1,0:T(8,128)S(1)}, u32[]{:S(2)}, u32[]{:S(2)}) collective-permute-start(f32[96,128]{1,0:T(8,128)S(1)} %get-tuple-element.45), channel_id=1, source_target_pairs={{0,8},{1,9},{2,10},{3,11},{4,12},{5,13},{6,14},{7,15},{8,0},{9,1},... | collective-permute-start | bytes 147464 | tf_op jit(solution)/shard_map/ppermute | solution.py:426
  25.5 1.2 %collective-permute-start.13 = (f32[96,128]{1,0:T(8,128)S(1)}, f32[96,128]{1,0:T(8,128)S(1)}, u32[]{:S(2)}, u32[]{:S(2)}) collective-permute-start(f32[96,128]{1,0:T(8,128)S(1)} %get-tuple-element.46), channel_id=1, source_target_pairs={{0,12},{1,13},{2,14},{3,15},{4,0},{5,1},{6,2},{7,3},{8,4},{9,5},{1... | collective-permute-start | bytes 147464 | tf_op jit(solution)/shard_map/ppermute | solution.py:426
  26.7 2.7 %local.1 = (bf16[384,128]{1,0:T(8,128)(2,1)}, bf16[192,128]{1,0:T(8,128)(2,1)S(1)}) custom-call(f32[384,128]{1,0:T(8,128)S(1)} %get-tuple-element.37.mixed_ref, f32[384,128]{1,0:T(8,128)S(1)} %get-tuple-element.38.scale_ref, f32[1024,128]{1,0:T(8,128)S(1)} %get-tuple-element.39.lhs, f32[96,128]{1,0:T(8,128)S(1)} %get-tuple-element.41.after_ref.refs_0_, ...), custom_call_target="tpu_custom_call" | custom-call | tf_op jit(solution)/shard_map/local/pallas_call | solution.py:515
  29.4 0.3 %collective-permute-done.13.refs_3_ = f32[96,128]{1,0:T(8,128)S(1)} collective-permute-done((f32[96,128]{1,0:T(8,128)S(1)}, f32[96,128]{1,0:T(8,128)S(1)}, u32[]{:S(2)}, u32[]{:S(2)}) %collective-permute-start.13) | collective-permute-done | bytes 49184 | tf_op jit(solution)/shard_map/ppermute | solution.py:426
  29.7 0.8 %finish.1 = bf16[384,128]{1,0:T(8,128)(2,1)} custom-call(s32[80,128]{1,0:T(8,128)S(1)} %get-tuple-element.26.near_ref.facts_ref, bf16[384,128]{1,0:T(8,128)(2,1)} %get-tuple-element.42.base_ref, bf16[192,128]{1,0:T(8,128)(2,1)S(1)} %get-tuple-element.43.last_ref, ...), custom_call_target="tpu_custom_call", output_to_operand_aliasing={{}: (1, {})} | custom-call | tf_op jit(solution)/shard_map/finish/pallas_call | solution.py:527
  (14 shorter events, 0.2 us)
Async XLA Ops:
  0.9 10.6 %collective-permute-start.3 = (f32[104,128]{1,0:T(8,128)S(1)}, f32[104,128]{1,0:T(8,128)S(1)}, u32[]{:S(2)}, u32[]{:S(2)}) collective-permute-start(f32[104,128]{1,0:T(8,128)S(1)} %get-tuple-element.30), channel_id=1, source_target_pairs={{0,8},{1,9},{2,10},{3,11},{4,12},{5,13},{6,14},{7,15},{8,0},{9,1},... | collective-permute-start | bytes 159752 | tf_op jit(solution)/shard_map/ppermute | solution.py:407
  5.0 1.6 %collective-permute-start = (s32[80,128]{1,0:T(8,128)S(1)}, s32[80,128]{1,0:T(8,128)S(1)}, u32[]{:S(2)}, u32[]{:S(2)}) collective-permute-start(s32[80,128]{1,0:T(8,128)S(1)} %get-tuple-element.26.near_ref.facts_ref), channel_id=1, source_target_pairs={{0,1},{1,0},{2,3},{3,2},{4,5},{5,4},{6,7},{7,6},{8,9},{9,8},{10,11... | collective-permute-start | bytes 122888 | tf_op jit(solution)/shard_map/ppermute | solution.py:402
  5.0 6.3 %collective-permute-start.4 = (f32[96,128]{1,0:T(8,128)S(1)}, f32[96,128]{1,0:T(8,128)S(1)}, u32[]{:S(2)}, u32[]{:S(2)}) collective-permute-start(f32[96,128]{1,0:T(8,128)S(1)} %get-tuple-element.29.refs_0_), channel_id=1, source_target_pairs={{0,12},{1,13},{2,14},{3,15},{4,8},{5,9},{6,10},{7,11},{8,4},{9,5},... | collective-permute-start | bytes 147464 | tf_op jit(solution)/shard_map/ppermute | solution.py:407
  6.3 5.1 %collective-permute-start.2 = (f32[96,128]{1,0:T(8,128)S(1)}, f32[96,128]{1,0:T(8,128)S(1)}, u32[]{:S(2)}, u32[]{:S(2)}) collective-permute-start(f32[96,128]{1,0:T(8,128)S(1)} %get-tuple-element.29.refs_0_), channel_id=1, source_target_pairs={{0,4},{1,5},{2,6},{3,7},{4,0},{5,1},{6,2},{7,3},{8,12},{9,13},{10,... | collective-permute-start | bytes 147464 | tf_op jit(solution)/shard_map/ppermute | solution.py:407
  6.6 3.7 %collective-permute-start.1 = (s32[16,128]{1,0:T(8,128)S(1)}, s32[16,128]{1,0:T(8,128)S(1)}, u32[]{:S(2)}, u32[]{:S(2)}) collective-permute-start(s32[16,128]{1,0:T(8,128)S(1)} %pair.2.near_ref), channel_id=1, source_target_pairs={{0,2},{1,3},{2,0},{3,1},{4,6},{5,7},{6,4},{7,5},{8,10},{9,11},{10,... | collective-permute-start | bytes 24584 | tf_op jit(solution)/shard_map/ppermute | solution.py:402
  11.5 4.4 %collective-permute-start.5 = (f32[96,128]{1,0:T(8,128)S(1)}, f32[96,128]{1,0:T(8,128)S(1)}, u32[]{:S(2)}, u32[]{:S(2)}) collective-permute-start(f32[96,128]{1,0:T(8,128)S(1)} %get-tuple-element.32), channel_id=1, source_target_pairs={{0,3},{1,2},{2,1},{3,0},{4,7},{5,6},{6,5},{7,4},{8,11},{9,10},{10,... | collective-permute-start | bytes 147464 | tf_op jit(solution)/shard_map/ppermute | solution.py:402
  11.9 4.6 %collective-permute-start.6 = (f32[96,128]{1,0:T(8,128)S(1)}, f32[96,128]{1,0:T(8,128)S(1)}, u32[]{:S(2)}, u32[]{:S(2)}) collective-permute-start(f32[96,128]{1,0:T(8,128)S(1)} %get-tuple-element.33), channel_id=1, source_target_pairs={{0,2},{1,3},{2,0},{3,1},{4,6},{5,7},{6,4},{7,5},{8,10},{9,11},{10,... | collective-permute-start | bytes 147464 | tf_op jit(solution)/shard_map/ppermute | solution.py:402
  13.2 3.3 %collective-permute-start.7 = (f32[96,128]{1,0:T(8,128)S(1)}, f32[96,128]{1,0:T(8,128)S(1)}, u32[]{:S(2)}, u32[]{:S(2)}) collective-permute-start(f32[96,128]{1,0:T(8,128)S(1)} %get-tuple-element.34), channel_id=1, source_target_pairs={{0,1},{1,0},{2,3},{3,2},{4,5},{5,4},{6,7},{7,6},{8,9},{9,8},{10,11... | collective-permute-start | bytes 147464 | tf_op jit(solution)/shard_map/ppermute | solution.py:402
  16.9 4.1 %collective-permute-start.10 = (f32[96,128]{1,0:T(8,128)S(1)}, f32[96,128]{1,0:T(8,128)S(1)}, u32[]{:S(2)}, u32[]{:S(2)}) collective-permute-start(f32[96,128]{1,0:T(8,128)S(1)} %answer.1.after_ref.refs_0_), channel_id=1, source_target_pairs={{0,3},{1,2},{2,1},{3,0},{4,7},{5,6},{6,5},{7,4},{8,11},{9,10},{10,... | collective-permute-start | bytes 147464 | tf_op jit(solution)/shard_map/ppermute | solution.py:402
  17.8 4.3 %collective-permute-start.9 = (f32[96,128]{1,0:T(8,128)S(1)}, f32[96,128]{1,0:T(8,128)S(1)}, u32[]{:S(2)}, u32[]{:S(2)}) collective-permute-start(f32[96,128]{1,0:T(8,128)S(1)} %answer.1.after_ref.refs_0_), channel_id=1, source_target_pairs={{0,2},{1,3},{2,0},{3,1},{4,6},{5,7},{6,4},{7,5},{8,10},{9,11},{10,... | collective-permute-start | bytes 147464 | tf_op jit(solution)/shard_map/ppermute | solution.py:402
  18.7 3.4 %collective-permute-start.8 = (f32[96,128]{1,0:T(8,128)S(1)}, f32[96,128]{1,0:T(8,128)S(1)}, u32[]{:S(2)}, u32[]{:S(2)}) collective-permute-start(f32[96,128]{1,0:T(8,128)S(1)} %answer.1.after_ref.refs_0_), channel_id=1, source_target_pairs={{0,1},{1,0},{2,3},{3,2},{4,5},{5,4},{6,7},{7,6},{8,9},{9,8},{10,11... | collective-permute-start | bytes 147464 | tf_op jit(solution)/shard_map/ppermute | solution.py:402
  22.1 7.2 %collective-permute-start.11 = (f32[96,128]{1,0:T(8,128)S(1)}, f32[96,128]{1,0:T(8,128)S(1)}, u32[]{:S(2)}, u32[]{:S(2)}) collective-permute-start(f32[96,128]{1,0:T(8,128)S(1)} %get-tuple-element.44), channel_id=1, source_target_pairs={{0,4},{1,5},{2,6},{3,7},{4,8},{5,9},{6,10},{7,11},{8,12},{9,13},{1... | collective-permute-start | bytes 147464 | tf_op jit(solution)/shard_map/ppermute | solution.py:426
  22.7 6.6 %collective-permute-start.12 = (f32[96,128]{1,0:T(8,128)S(1)}, f32[96,128]{1,0:T(8,128)S(1)}, u32[]{:S(2)}, u32[]{:S(2)}) collective-permute-start(f32[96,128]{1,0:T(8,128)S(1)} %get-tuple-element.45), channel_id=1, source_target_pairs={{0,8},{1,9},{2,10},{3,11},{4,12},{5,13},{6,14},{7,15},{8,0},{9,1},... | collective-permute-start | bytes 147464 | tf_op jit(solution)/shard_map/ppermute | solution.py:426
  25.5 4.2 %collective-permute-start.13 = (f32[96,128]{1,0:T(8,128)S(1)}, f32[96,128]{1,0:T(8,128)S(1)}, u32[]{:S(2)}, u32[]{:S(2)}) collective-permute-start(f32[96,128]{1,0:T(8,128)S(1)} %get-tuple-element.46), channel_id=1, source_target_pairs={{0,12},{1,13},{2,14},{3,15},{4,0},{5,1},{6,2},{7,3},{8,4},{9,5},{1... | collective-permute-start | bytes 147464 | tf_op jit(solution)/shard_map/ppermute | solution.py:426

commit v14 on v13

--- a/solution.py
+++ b/solution.py
@@ -449,7 +449,7 @@
     )(in_hbm(new_slot), in_hbm(queries))
 
     z1, z2 = list(range(1, outer)), list(range(1, outer))
-    q1, q2 = list(range(inner - 1, 0, -1)), list(range(1, inner))
+    q1, q2 = list(range(inner - 1, 0, -1)), [inner - 1, *range(1, inner - 1)]
     column = [ask] + [send_outer(ask_long if k == outer // 2 else ask, k) for k in z1]
     wishes = gather_inner(facts)
 

time: 30.7 us -> 30.9 us (level)
    ppermute x8, waiting for transfers between devices: 3.72 us -> 3.09 us  [send_inner(): lax.ppermute(x, 'req', [(o * inner + i, o * inner + int(turn(i, k, inner)...]
    ppermute x3, waiting for transfers between devices: 0.31 us -> 0.89 us  [shift_outer(): lax.ppermute(x, 'req', [(o * inner + i, (o + k) % outer * inner + i) for...]
where the time goes in v14:
time: 30.9 us; the launch traced here: 30.6 us
  starting transfers between devices  15.9 us (51%)
  Pallas kernels  9.41 us (30%)
  waiting for transfers between devices  5.23 us (17%)
    ppermute x3, starting transfers between devices, send_outer(): lax.ppermute(x, 'req', [(o * inner + i, int(turn(o, k, outer)) * inner +...  5.68 us
    ppermute x8, starting transfers between devices, send_inner(): lax.ppermute(x, 'req', [(o * inner + i, o * inner + int(turn(i, k, inner)...  5.65 us
    ppermute x3, starting transfers between devices, shift_outer(): lax.ppermute(x, 'req', [(o * inner + i, (o + k) % outer * inner + i) for...  4.57 us
    ppermute x8, waiting for transfers between devices, send_inner(): lax.ppermute(x, 'req', [(o * inner + i, o * inner + int(turn(i, k, inner)...  3.09 us
    pallas_call x1, Pallas kernels, on_device(): pl.pallas_call(functools.partial(local_kernel, slots=last_slots, count=co...  2.67 us
    pallas_call x1, Pallas kernels, on_device(): pl.pallas_call(functools.partial(prepare_kernel, count=count, chunks=chun...  2.48 us
    pallas_call x1, Pallas kernels, on_device(): pl.pallas_call(functools.partial(scores_kernel, slots=first_slots, count=...  2.13 us
    ppermute x3, waiting for transfers between devices, send_outer(): lax.ppermute(x, 'req', [(o * inner + i, int(turn(o, k, outer)) * inner +...  1.24 us
  transfers between devices with their start and end apart: 14, of which 6 were waited for; matrix products, arithmetic and copies ran while one was open for 0% of the time, Pallas kernels for 24%

profile of v14, /device:TPU:0, one launch (start us, length us, event | category | flops | bytes accessed | tf_op | source)
XLA Modules:
  0.0 30.6 jit_solution(11171233068749632199)
XLA Ops:
  0.0 0.9 %ask.1 = (f32[96,128]{1,0:T(8,128)S(1)}, f32[104,128]{1,0:T(8,128)S(1)}, s32[80,128]{1,0:T(8,128)S(1)}) custom-call(s32[2]{0:T(128)} %slots_ref.1, bf16[384,128]{1,0:T(8,128)(2,1)} %bitcast.26), custom_call_target="tpu_custom_call" | custom-call | tf_op jit(solution)/shard_map/ask/pallas_call | solution.py:442
  0.9 4.1 %collective-permute-start.3 = (f32[104,128]{1,0:T(8,128)S(1)}, f32[104,128]{1,0:T(8,128)S(1)}, u32[]{:S(2)}, u32[]{:S(2)}) collective-permute-start(f32[104,128]{1,0:T(8,128)S(1)} %get-tuple-element.30), channel_id=1, source_target_pairs={{0,8},{1,9},{2,10},{3,11},{4,12},{5,13},{6,14},{7,15},{8,0},{9,1},... | collective-permute-start | bytes 159752 | tf_op jit(solution)/shard_map/ppermute | solution.py:407
  5.0 1.3 %collective-permute-start.4 = (f32[96,128]{1,0:T(8,128)S(1)}, f32[96,128]{1,0:T(8,128)S(1)}, u32[]{:S(2)}, u32[]{:S(2)}) collective-permute-start(f32[96,128]{1,0:T(8,128)S(1)} %get-tuple-element.29.refs_0_), channel_id=1, source_target_pairs={{0,12},{1,13},{2,14},{3,15},{4,8},{5,9},{6,10},{7,11},{8,4},{9,5},... | collective-permute-start | bytes 147464 | tf_op jit(solution)/shard_map/ppermute | solution.py:407
  6.3 0.2 collective-permute-start.2
  6.6 1.5 %collective-permute-start.1 = (s32[16,128]{1,0:T(8,128)S(1)}, s32[16,128]{1,0:T(8,128)S(1)}, u32[]{:S(2)}, u32[]{:S(2)}) collective-permute-start(s32[16,128]{1,0:T(8,128)S(1)} %pair.2.near_ref), channel_id=1, source_target_pairs={{0,2},{1,3},{2,0},{3,1},{4,6},{5,7},{6,4},{7,5},{8,10},{9,11},{10,... | collective-permute-start | bytes 24584 | tf_op jit(solution)/shard_map/ppermute | solution.py:402
  8.1 2.1 %collective-permute-done.1.far_ref = s32[16,128]{1,0:T(8,128)S(1)} collective-permute-done((s32[16,128]{1,0:T(8,128)S(1)}, s32[16,128]{1,0:T(8,128)S(1)}, u32[]{:S(2)}, u32[]{:S(2)}) %collective-permute-start.1) | collective-permute-done | bytes 8224 | tf_op jit(solution)/shard_map/ppermute | solution.py:402
  10.2 1.1 %collective-permute-done.4.refs_3_ = f32[96,128]{1,0:T(8,128)S(1)} collective-permute-done((f32[96,128]{1,0:T(8,128)S(1)}, f32[96,128]{1,0:T(8,128)S(1)}, u32[]{:S(2)}, u32[]{:S(2)}) %collective-permute-start.4) | collective-permute-done | bytes 49184 | tf_op jit(solution)/shard_map/ppermute | solution.py:407
  11.3 0.1 collective-permute-done.2.refs_1_
  11.5 0.4 %collective-permute-start.5 = (f32[96,128]{1,0:T(8,128)S(1)}, f32[96,128]{1,0:T(8,128)S(1)}, u32[]{:S(2)}, u32[]{:S(2)}) collective-permute-start(f32[96,128]{1,0:T(8,128)S(1)} %get-tuple-element.32), channel_id=1, source_target_pairs={{0,3},{1,2},{2,1},{3,0},{4,7},{5,6},{6,5},{7,4},{8,11},{9,10},{10,... | collective-permute-start | bytes 147464 | tf_op jit(solution)/shard_map/ppermute | solution.py:402
  11.9 1.3 %collective-permute-start.6 = (f32[96,128]{1,0:T(8,128)S(1)}, f32[96,128]{1,0:T(8,128)S(1)}, u32[]{:S(2)}, u32[]{:S(2)}) collective-permute-start(f32[96,128]{1,0:T(8,128)S(1)} %get-tuple-element.33), channel_id=1, source_target_pairs={{0,2},{1,3},{2,0},{3,1},{4,6},{5,7},{6,4},{7,5},{8,10},{9,11},{10,... | collective-permute-start | bytes 147464 | tf_op jit(solution)/shard_map/ppermute | solution.py:402
  13.2 0.3 collective-permute-start.7
  13.4 2.5 %prepare.1 = (bf16[32,256,128]{2,1,0:T(8,128)(2,1)S(1)}, f32[2,96,128]{2,1,0:T(8,128)S(1)}, bf16[4,384,128]{2,1,0:T(8,128)(2,1)S(1)}, f32[32,128]{1,0:T(8,128)S(1)}) custom-call(s32[2]{0:T(128)} %slots_ref.1, bf16[384,128]{1,0:T(8,128)(2,1)} %bitcast.27, bf16[384,128]{1,0:T(8,128)(2,1)} %bitcast.28, bf16[384,128]{1,0:T(8,128)(2,1)} %bitcast.29, ...), custom_call_target="tpu_custom_call" | custom-call | tf_op jit(solution)/shard_map/prepare/pallas_call | solution.py:458
  15.9 0.5 %collective-permute-done.6.refs_2_ = f32[96,128]{1,0:T(8,128)S(1)} collective-permute-done((f32[96,128]{1,0:T(8,128)S(1)}, f32[96,128]{1,0:T(8,128)S(1)}, u32[]{:S(2)}, u32[]{:S(2)}) %collective-permute-start.6) | collective-permute-done | bytes 49184 | tf_op jit(solution)/shard_map/ppermute | solution.py:402
  16.4 0.5 %answer.1.after_ref.refs_0_ = f32[96,128]{1,0:T(8,128)S(1)} custom-call(s32[80,128]{1,0:T(8,128)S(1)} %get-tuple-element.26.near_ref.facts_ref, f32[96,128]{1,0:T(8,128)S(1)} %get-tuple-element.31.refs_0_, f32[96,128]{1,0:T(8,128)S(1)} %collective-permute-done.5.refs_1_, f32[96,128]{1,0:T(8,128)S(1)} %collective-permute-done.6.refs_2_, ...), custom_call_target="tpu_custom_call" | custom-call | tf_op jit(solution)/shard_map/answer/pallas_call | solution.py:480
  16.9 1.3 %collective-permute-start.10 = (f32[96,128]{1,0:T(8,128)S(1)}, f32[96,128]{1,0:T(8,128)S(1)}, u32[]{:S(2)}, u32[]{:S(2)}) collective-permute-start(f32[96,128]{1,0:T(8,128)S(1)} %answer.1.after_ref.refs_0_), channel_id=1, source_target_pairs={{0,2},{1,3},{2,0},{3,1},{4,6},{5,7},{6,4},{7,5},{8,10},{9,11},{10,... | collective-permute-start | bytes 147464 | tf_op jit(solution)/shard_map/ppermute | solution.py:402
  18.2 0.9 %collective-permute-start.8 = (f32[96,128]{1,0:T(8,128)S(1)}, f32[96,128]{1,0:T(8,128)S(1)}, u32[]{:S(2)}, u32[]{:S(2)}) collective-permute-start(f32[96,128]{1,0:T(8,128)S(1)} %answer.1.after_ref.refs_0_), channel_id=1, source_target_pairs={{0,3},{1,2},{2,1},{3,0},{4,7},{5,6},{6,5},{7,4},{8,11},{9,10},{10,... | collective-permute-start | bytes 147464 | tf_op jit(solution)/shard_map/ppermute | solution.py:402
  19.1 2.1 %scores.1 = (f32[384,128]{1,0:T(8,128)S(1)}, f32[384,128]{1,0:T(8,128)S(1)}, f32[2,96,128]{2,1,0:T(8,128)S(1)}, f32[1024,128]{1,0:T(8,128)S(1)}) custom-call(s32[80,128]{1,0:T(8,128)S(1)} %get-tuple-element.26.near_ref.facts_ref, bf16[4,384,128]{2,1,0:T(8,128)(2,1)S(1)} %get-tuple-element.27.rows_ref, f32[32,128]{1,0:T(8,128)S(1)} %get-tuple-element.28.gain_ref, ...), custom_call_target="tpu_custom_call" | custom-call | tf_op jit(solution)/shard_map/scores/pallas_call | solution.py:493
  21.3 0.4 %collective-permute-done.8.refs_1_ = f32[96,128]{1,0:T(8,128)S(1)} collective-permute-done((f32[96,128]{1,0:T(8,128)S(1)}, f32[96,128]{1,0:T(8,128)S(1)}, u32[]{:S(2)}, u32[]{:S(2)}) %collective-permute-start.8) | collective-permute-done | bytes 49184 | tf_op jit(solution)/shard_map/ppermute | solution.py:402
  21.7 0.6 %collective-permute-start.11 = (f32[96,128]{1,0:T(8,128)S(1)}, f32[96,128]{1,0:T(8,128)S(1)}, u32[]{:S(2)}, u32[]{:S(2)}) collective-permute-start(f32[96,128]{1,0:T(8,128)S(1)} %get-tuple-element.44), channel_id=1, source_target_pairs={{0,4},{1,5},{2,6},{3,7},{4,8},{5,9},{6,10},{7,11},{8,12},{9,13},{1... | collective-permute-start | bytes 147464 | tf_op jit(solution)/shard_map/ppermute | solution.py:426
  22.4 2.9 %collective-permute-start.12 = (f32[96,128]{1,0:T(8,128)S(1)}, f32[96,128]{1,0:T(8,128)S(1)}, u32[]{:S(2)}, u32[]{:S(2)}) collective-permute-start(f32[96,128]{1,0:T(8,128)S(1)} %get-tuple-element.45), channel_id=1, source_target_pairs={{0,8},{1,9},{2,10},{3,11},{4,12},{5,13},{6,14},{7,15},{8,0},{9,1},... | collective-permute-start | bytes 147464 | tf_op jit(solution)/shard_map/ppermute | solution.py:426
  25.2 1.1 %collective-permute-start.13 = (f32[96,128]{1,0:T(8,128)S(1)}, f32[96,128]{1,0:T(8,128)S(1)}, u32[]{:S(2)}, u32[]{:S(2)}) collective-permute-start(f32[96,128]{1,0:T(8,128)S(1)} %get-tuple-element.46), channel_id=1, source_target_pairs={{0,12},{1,13},{2,14},{3,15},{4,0},{5,1},{6,2},{7,3},{8,4},{9,5},{1... | collective-permute-start | bytes 147464 | tf_op jit(solution)/shard_map/ppermute | solution.py:426
  26.3 2.7 %local.1 = (bf16[384,128]{1,0:T(8,128)(2,1)}, bf16[192,128]{1,0:T(8,128)(2,1)S(1)}) custom-call(f32[384,128]{1,0:T(8,128)S(1)} %get-tuple-element.37.mixed_ref, f32[384,128]{1,0:T(8,128)S(1)} %get-tuple-element.38.scale_ref, f32[1024,128]{1,0:T(8,128)S(1)} %get-tuple-element.39.lhs, f32[96,128]{1,0:T(8,128)S(1)} %get-tuple-element.41.after_ref.refs_0_, ...), custom_call_target="tpu_custom_call" | custom-call | tf_op jit(solution)/shard_map/local/pallas_call | solution.py:515
  29.0 0.9 %collective-permute-done.12.refs_2_ = f32[96,128]{1,0:T(8,128)S(1)} collective-permute-done((f32[96,128]{1,0:T(8,128)S(1)}, f32[96,128]{1,0:T(8,128)S(1)}, u32[]{:S(2)}, u32[]{:S(2)}) %collective-permute-start.12) | collective-permute-done | bytes 49184 | tf_op jit(solution)/shard_map/ppermute | solution.py:426
  29.9 0.8 %finish.1 = bf16[384,128]{1,0:T(8,128)(2,1)} custom-call(s32[80,128]{1,0:T(8,128)S(1)} %get-tuple-element.26.near_ref.facts_ref, bf16[384,128]{1,0:T(8,128)(2,1)} %get-tuple-element.42.base_ref, bf16[192,128]{1,0:T(8,128)(2,1)S(1)} %get-tuple-element.43.last_ref, ...), custom_call_target="tpu_custom_call", output_to_operand_aliasing={{}: (1, {})} | custom-call | tf_op jit(solution)/shard_map/finish/pallas_call | solution.py:527
  (14 shorter events, 0.1 us)
Async XLA Ops:
  0.9 10.6 %collective-permute-start.3 = (f32[104,128]{1,0:T(8,128)S(1)}, f32[104,128]{1,0:T(8,128)S(1)}, u32[]{:S(2)}, u32[]{:S(2)}) collective-permute-start(f32[104,128]{1,0:T(8,128)S(1)} %get-tuple-element.30), channel_id=1, source_target_pairs={{0,8},{1,9},{2,10},{3,11},{4,12},{5,13},{6,14},{7,15},{8,0},{9,1},... | collective-permute-start | bytes 159752 | tf_op jit(solution)/shard_map/ppermute | solution.py:407
  5.0 1.6 %collective-permute-start = (s32[80,128]{1,0:T(8,128)S(1)}, s32[80,128]{1,0:T(8,128)S(1)}, u32[]{:S(2)}, u32[]{:S(2)}) collective-permute-start(s32[80,128]{1,0:T(8,128)S(1)} %get-tuple-element.26.near_ref.facts_ref), channel_id=1, source_target_pairs={{0,1},{1,0},{2,3},{3,2},{4,5},{5,4},{6,7},{7,6},{8,9},{9,8},{10,11... | collective-permute-start | bytes 122888 | tf_op jit(solution)/shard_map/ppermute | solution.py:402
  5.0 6.3 %collective-permute-start.4 = (f32[96,128]{1,0:T(8,128)S(1)}, f32[96,128]{1,0:T(8,128)S(1)}, u32[]{:S(2)}, u32[]{:S(2)}) collective-permute-start(f32[96,128]{1,0:T(8,128)S(1)} %get-tuple-element.29.refs_0_), channel_id=1, source_target_pairs={{0,12},{1,13},{2,14},{3,15},{4,8},{5,9},{6,10},{7,11},{8,4},{9,5},... | collective-permute-start | bytes 147464 | tf_op jit(solution)/shard_map/ppermute | solution.py:407
  6.3 5.1 %collective-permute-start.2 = (f32[96,128]{1,0:T(8,128)S(1)}, f32[96,128]{1,0:T(8,128)S(1)}, u32[]{:S(2)}, u32[]{:S(2)}) collective-permute-start(f32[96,128]{1,0:T(8,128)S(1)} %get-tuple-element.29.refs_0_), channel_id=1, source_target_pairs={{0,4},{1,5},{2,6},{3,7},{4,0},{5,1},{6,2},{7,3},{8,12},{9,13},{10,... | collective-permute-start | bytes 147464 | tf_op jit(solution)/shard_map/ppermute | solution.py:407
  6.6 3.7 %collective-permute-start.1 = (s32[16,128]{1,0:T(8,128)S(1)}, s32[16,128]{1,0:T(8,128)S(1)}, u32[]{:S(2)}, u32[]{:S(2)}) collective-permute-start(s32[16,128]{1,0:T(8,128)S(1)} %pair.2.near_ref), channel_id=1, source_target_pairs={{0,2},{1,3},{2,0},{3,1},{4,6},{5,7},{6,4},{7,5},{8,10},{9,11},{10,... | collective-permute-start | bytes 24584 | tf_op jit(solution)/shard_map/ppermute | solution.py:402
  11.5 4.4 %collective-permute-start.5 = (f32[96,128]{1,0:T(8,128)S(1)}, f32[96,128]{1,0:T(8,128)S(1)}, u32[]{:S(2)}, u32[]{:S(2)}) collective-permute-start(f32[96,128]{1,0:T(8,128)S(1)} %get-tuple-element.32), channel_id=1, source_target_pairs={{0,3},{1,2},{2,1},{3,0},{4,7},{5,6},{6,5},{7,4},{8,11},{9,10},{10,... | collective-permute-start | bytes 147464 | tf_op jit(solution)/shard_map/ppermute | solution.py:402
  11.9 4.6 %collective-permute-start.6 = (f32[96,128]{1,0:T(8,128)S(1)}, f32[96,128]{1,0:T(8,128)S(1)}, u32[]{:S(2)}, u32[]{:S(2)}) collective-permute-start(f32[96,128]{1,0:T(8,128)S(1)} %get-tuple-element.33), channel_id=1, source_target_pairs={{0,2},{1,3},{2,0},{3,1},{4,6},{5,7},{6,4},{7,5},{8,10},{9,11},{10,... | collective-permute-start | bytes 147464 | tf_op jit(solution)/shard_map/ppermute | solution.py:402
  13.2 3.3 %collective-permute-start.7 = (f32[96,128]{1,0:T(8,128)S(1)}, f32[96,128]{1,0:T(8,128)S(1)}, u32[]{:S(2)}, u32[]{:S(2)}) collective-permute-start(f32[96,128]{1,0:T(8,128)S(1)} %get-tuple-element.34), channel_id=1, source_target_pairs={{0,1},{1,0},{2,3},{3,2},{4,5},{5,4},{6,7},{7,6},{8,9},{9,8},{10,11... | collective-permute-start | bytes 147464 | tf_op jit(solution)/shard_map/ppermute | solution.py:402
  16.9 4.3 %collective-permute-start.10 = (f32[96,128]{1,0:T(8,128)S(1)}, f32[96,128]{1,0:T(8,128)S(1)}, u32[]{:S(2)}, u32[]{:S(2)}) collective-permute-start(f32[96,128]{1,0:T(8,128)S(1)} %answer.1.after_ref.refs_0_), channel_id=1, source_target_pairs={{0,2},{1,3},{2,0},{3,1},{4,6},{5,7},{6,4},{7,5},{8,10},{9,11},{10,... | collective-permute-start | bytes 147464 | tf_op jit(solution)/shard_map/ppermute | solution.py:402
  18.2 3.1 %collective-permute-start.9 = (f32[96,128]{1,0:T(8,128)S(1)}, f32[96,128]{1,0:T(8,128)S(1)}, u32[]{:S(2)}, u32[]{:S(2)}) collective-permute-start(f32[96,128]{1,0:T(8,128)S(1)} %answer.1.after_ref.refs_0_), channel_id=1, source_target_pairs={{0,1},{1,0},{2,3},{3,2},{4,5},{5,4},{6,7},{7,6},{8,9},{9,8},{10,11... | collective-permute-start | bytes 147464 | tf_op jit(solution)/shard_map/ppermute | solution.py:402
  18.2 3.5 %collective-permute-start.8 = (f32[96,128]{1,0:T(8,128)S(1)}, f32[96,128]{1,0:T(8,128)S(1)}, u32[]{:S(2)}, u32[]{:S(2)}) collective-permute-start(f32[96,128]{1,0:T(8,128)S(1)} %answer.1.after_ref.refs_0_), channel_id=1, source_target_pairs={{0,3},{1,2},{2,1},{3,0},{4,7},{5,6},{6,5},{7,4},{8,11},{9,10},{10,... | collective-permute-start | bytes 147464 | tf_op jit(solution)/shard_map/ppermute | solution.py:402
  21.7 7.2 %collective-permute-start.11 = (f32[96,128]{1,0:T(8,128)S(1)}, f32[96,128]{1,0:T(8,128)S(1)}, u32[]{:S(2)}, u32[]{:S(2)}) collective-permute-start(f32[96,128]{1,0:T(8,128)S(1)} %get-tuple-element.44), channel_id=1, source_target_pairs={{0,4},{1,5},{2,6},{3,7},{4,8},{5,9},{6,10},{7,11},{8,12},{9,13},{1... | collective-permute-start | bytes 147464 | tf_op jit(solution)/shard_map/ppermute | solution.py:426
  22.4 7.5 %collective-permute-start.12 = (f32[96,128]{1,0:T(8,128)S(1)}, f32[96,128]{1,0:T(8,128)S(1)}, u32[]{:S(2)}, u32[]{:S(2)}) collective-permute-start(f32[96,128]{1,0:T(8,128)S(1)} %get-tuple-element.45), channel_id=1, source_target_pairs={{0,8},{1,9},{2,10},{3,11},{4,12},{5,13},{6,14},{7,15},{8,0},{9,1},... | collective-permute-start | bytes 147464 | tf_op jit(solution)/shard_map/ppermute | solution.py:426
  25.2 4.7 %collective-permute-start.13 = (f32[96,128]{1,0:T(8,128)S(1)}, f32[96,128]{1,0:T(8,128)S(1)}, u32[]{:S(2)}, u32[]{:S(2)}) collective-permute-start(f32[96,128]{1,0:T(8,128)S(1)} %get-tuple-element.46), channel_id=1, source_target_pairs={{0,12},{1,13},{2,14},{3,15},{4,0},{5,1},{6,2},{7,3},{8,4},{9,5},{1... | collective-permute-start | bytes 147464 | tf_op jit(solution)/shard_map/ppermute | solution.py:426
